TPU v7x, 32 devices: a whole 2x2x4 slice. The times are simulated.
32 devices in a mesh: fsdp: 4 (over y, core), ctx: 4 (over z), tp: 2 (over x).
Axes of the slice: x: 2, y: 2, z: 4, core: 2. Of those that a mesh axis runs over, the one named last changes fastest.
Arguments:
- latents: bfloat16 [3, 4, 1024, 1152], P(None, 'fsdp', 'ctx'), may hold values from -6 to 6
- condition: bfloat16 [3, 4, 1152], P(None, 'fsdp'), may hold values from -6 to 6
- grad_out: bfloat16 [3, 4, 1024, 1152], P(None, 'fsdp', 'ctx'), may hold values from -6 to 6
- ada_weight: bfloat16 [1152, 6, 1152], P(('fsdp', 'ctx'), None, 'tp'), may hold values from -0.375 to 0.375
- ada_bias: bfloat16 [6, 1152], replicated, may hold values from -3 to 3
- qkv_weight: bfloat16 [1152, 3, 1152], P(('fsdp', 'ctx'), None, 'tp'), may hold values from -0.09375 to 0.09375
- qv_bias: bfloat16 [2, 1152], replicated, may hold values from -3 to 3
- proj_weight: bfloat16 [1152, 1152], P('tp', ('fsdp', 'ctx')), may hold values from -3 to 3
- proj_bias: bfloat16 [1152], replicated, may hold values from -3 to 3
- up_weight: bfloat16 [1152, 4608], P(('fsdp', 'ctx'), 'tp'), may hold values from -0.1875 to 0.1875
- up_bias: bfloat16 [4608], replicated, may hold values from -3 to 3
- down_weight: bfloat16 [4608, 1152], P('tp', ('fsdp', 'ctx')), may hold values from -0.09375 to 0.09375
- down_bias: bfloat16 [1152], replicated, may hold values from -3 to 3
Outputs:
- output: bfloat16 [3, 4, 1024, 1152], P(None, 'fsdp', 'ctx')
- grad_latents: float32 [3, 4, 1024, 1152], P(None, 'fsdp', 'ctx')
- grad_condition: float32 [3, 4, 1152], P(None, 'fsdp')
- grad_ada_weight: float32 [1152, 6, 1152], P(('fsdp', 'ctx'), None, 'tp')
- grad_ada_bias: float32 [6, 1152], replicated
- grad_qkv_weight: float32 [1152, 3, 1152], P(('fsdp', 'ctx'), None, 'tp')
- grad_qv_bias: float32 [2, 1152], replicated
- grad_proj_weight: float32 [1152, 1152], P('tp', ('fsdp', 'ctx'))
- grad_proj_bias: float32 [1152], replicated
- grad_up_weight: float32 [1152, 4608], P(('fsdp', 'ctx'), 'tp')
- grad_up_bias: float32 [4608], replicated
- grad_down_weight: float32 [4608, 1152], P('tp', ('fsdp', 'ctx'))
- grad_down_bias: float32 [1152], replicated
All inputs are finite; a program needn't handle non-finite values.
Results may differ from a plain program's by a relative error of at most 0.01.
The roundings to bfloat16 on the way count: a program that leaves them out, or rounds other values in their place, can miss the bound.
Values may be sent and summed in bfloat16 or wider, within the bound.
No kernel may reach another device: no remote copies, remote signals or barrier semaphores. Data moves between devices by JAX's collectives and lax.ppermute only.
A program may use at most 256 MiB of HBM per device.

v0:
```python
from functools import partial

import jax
import jax.numpy as jnp
from jax import lax
from jax.sharding import PartitionSpec as P

HEADS = 16
HEAD_DIM = 72


def normalize(values):
    centre = values - jnp.mean(values, -1, keepdims=True)
    inverse = lax.rsqrt(jnp.mean(centre * centre, -1, keepdims=True) + 1e-06)
    return (centre * inverse, inverse)


def norm_back(incoming, normed, inverse):
    return inverse * (
        incoming
        - jnp.mean(incoming, -1, keepdims=True)
        - normed * jnp.mean(incoming * normed, -1, keepdims=True)
    )


def gelu_tanh(values):
    return jax.nn.gelu(values, approximate=True)


def gather_weights(shard_tuple):
    return (
        lax.all_gather(shard_tuple[0], ("fsdp", "ctx"), axis=0, tiled=True),
        lax.all_gather(shard_tuple[1], ("fsdp", "ctx"), axis=0, tiled=True),
        lax.all_gather(shard_tuple[2], ("fsdp", "ctx"), axis=1, tiled=True),
        lax.all_gather(shard_tuple[3], ("fsdp", "ctx"), axis=0, tiled=True),
        lax.all_gather(shard_tuple[4], ("fsdp", "ctx"), axis=1, tiled=True),
    )


def scatter_grads(term_tuple):
    return (
        lax.psum_scatter(term_tuple[0], ("fsdp", "ctx"), scatter_dimension=0, tiled=True),
        lax.psum_scatter(term_tuple[1], ("fsdp", "ctx"), scatter_dimension=0, tiled=True),
        lax.psum_scatter(term_tuple[2], ("fsdp", "ctx"), scatter_dimension=1, tiled=True),
        lax.psum_scatter(term_tuple[3], ("fsdp", "ctx"), scatter_dimension=0, tiled=True),
        lax.psum_scatter(term_tuple[4], ("fsdp", "ctx"), scatter_dimension=1, tiled=True),
    )


def scores_of(queries, key_rows, heads_here):
    query_heads = queries.reshape(queries.shape[0], heads_here, HEAD_DIM)
    key_heads = key_rows.reshape(key_rows.shape[0], heads_here, HEAD_DIM)
    raw_scores = jnp.einsum(
        "qhe,khe->hqk", query_heads, key_heads, preferred_element_type=jnp.float32
    )
    return raw_scores * HEAD_DIM ** (-0.5)


def attend(sequence_items, heads_here):
    queries, key_rows, value_rows = sequence_items
    scores = scores_of(queries, key_rows, heads_here)
    highest = jnp.max(scores, -1, keepdims=True)
    exponent = jnp.exp(scores - highest)
    summed = jnp.sum(exponent, -1, keepdims=True)
    chances = (exponent / summed).astype(jnp.bfloat16)
    value_heads = value_rows.reshape(value_rows.shape[0], heads_here, HEAD_DIM)
    blended = jnp.einsum("hqk,khe->qhe", chances, value_heads, preferred_element_type=jnp.float32)
    return (blended.reshape(queries.shape[0], -1), highest[..., 0] + jnp.log(summed[..., 0]))


def attend_back(sequence_items, heads_here):
    queries, key_rows, value_rows, grad_blended, logsum = sequence_items
    scaling = HEAD_DIM ** (-0.5)
    row_count = queries.shape[0]
    key_count = key_rows.shape[0]
    scores = scores_of(queries, key_rows, heads_here)
    chances = jnp.exp(scores - logsum[..., None])
    query_heads = queries.reshape(row_count, heads_here, HEAD_DIM)
    key_heads = key_rows.reshape(key_count, heads_here, HEAD_DIM)
    value_heads = value_rows.reshape(key_count, heads_here, HEAD_DIM)
    grad_heads = grad_blended.reshape(row_count, heads_here, HEAD_DIM)
    grad_chances = jnp.einsum(
        "qhe,khe->hqk", grad_heads, value_heads, preferred_element_type=jnp.float32
    )
    weighted = jnp.sum(chances * grad_chances, -1, keepdims=True)
    grad_scores = (chances * (grad_chances - weighted)).astype(jnp.bfloat16)
    grad_query = (
        jnp.einsum("hqk,khe->qhe", grad_scores, key_heads, preferred_element_type=jnp.float32)
        * scaling
    )
    grad_key = (
        jnp.einsum("hqk,qhe->khe", grad_scores, query_heads, preferred_element_type=jnp.float32)
        * scaling
    )
    grad_value = jnp.einsum(
        "hqk,qhe->khe", chances.astype(jnp.bfloat16), grad_heads, preferred_element_type=jnp.float32
    )
    key_pair = jnp.stack([grad_key.reshape(key_count, -1), grad_value.reshape(key_count, -1)], 1)
    return (grad_query.reshape(row_count, -1), key_pair)


def body(
    latents,
    condition,
    grad_out,
    ada_weight,
    ada_bias,
    qkv_weight,
    qv_bias,
    proj_weight,
    proj_bias,
    up_weight,
    up_bias,
    down_weight,
    down_bias,
):
    tp_rank = lax.axis_index("tp")
    heads_here = HEADS // lax.axis_size("tp")
    half_width = qkv_weight.shape[2]
    hidden_here = up_weight.shape[1]
    first_column = tp_rank * half_width
    lead_tp = (tp_rank == 0).astype(jnp.float32)
    lead_ctx = (lax.axis_index("ctx") == 0).astype(jnp.float32)
    bias_pair = lax.dynamic_slice_in_dim(qv_bias.astype(jnp.float32), first_column, half_width, 1)
    bias_up = lax.dynamic_slice_in_dim(
        up_bias.astype(jnp.float32), tp_rank * hidden_here, hidden_here, 0
    )
    bias_mod = lax.dynamic_slice_in_dim(ada_bias.astype(jnp.float32), first_column, half_width, 1)
    bias_proj = proj_bias.astype(jnp.float32)
    bias_down = down_bias.astype(jnp.float32)
    shards = (ada_weight, qkv_weight, proj_weight, up_weight, down_weight)
    grad_shards = tuple((jnp.zeros(shard_piece.shape, jnp.float32) for shard_piece in shards))
    bias_totals = tuple(
        (
            jnp.zeros(bias_piece.shape, jnp.float32)
            for bias_piece in (ada_bias, qv_bias, proj_bias, up_bias, down_bias)
        )
    )
    outputs, input_grads, cond_grads = ([], [], [])
    for batch_index in range(latents.shape[0]):
        gathered = gather_weights(shards)
        ada_full, qkv_full, proj_full, up_full, down_full = gathered
        latent = latents[batch_index].astype(jnp.float32)
        cond_value = condition[batch_index].astype(jnp.float32)
        silu_cond = jax.nn.silu(cond_value).astype(jnp.bfloat16)
        mod_part = (
            jnp.einsum("bd,dke->bke", silu_cond, ada_full, preferred_element_type=jnp.float32)
            + bias_mod
        )
        modulation = lax.all_gather(mod_part.astype(jnp.bfloat16), "tp", axis=2, tiled=True).astype(
            jnp.float32
        )
        shift_one = modulation[:, 0:1]
        scale_one = modulation[:, 1:2]
        gate_one = modulation[:, 2:3]
        shift_two = modulation[:, 3:4]
        scale_two = modulation[:, 4:5]
        gate_two = modulation[:, 5:6]
        normed_one, inverse_one = normalize(latent)
        in_first = (normed_one * (1.0 + scale_one) + shift_one).astype(jnp.bfloat16)
        projected = jnp.einsum(
            "btd,dke->btke", in_first, qkv_full, preferred_element_type=jnp.float32
        )
        queries = (projected[:, :, 0] + bias_pair[0]).astype(jnp.bfloat16)
        key_rows = projected[:, :, 1].astype(jnp.bfloat16)
        value_rows = (projected[:, :, 2] + bias_pair[1]).astype(jnp.bfloat16)
        key_all, value_all = (
            lax.all_gather(key_rows, "ctx", axis=1, tiled=True),
            lax.all_gather(value_rows, "ctx", axis=1, tiled=True),
        )
        blended, logsum = lax.map(
            partial(attend, heads_here=heads_here), (queries, key_all, value_all)
        )
        blended_low = blended.astype(jnp.bfloat16)
        attn_part = jnp.einsum(
            "bte,ed->btd", blended_low, proj_full, preferred_element_type=jnp.float32
        )
        attended = lax.psum(attn_part, "tp") + bias_proj
        residual = latent + gate_one * attended
        normed_two, inverse_two = normalize(residual)
        in_second = (normed_two * (1.0 + scale_two) + shift_two).astype(jnp.bfloat16)
        upward = (
            jnp.einsum("btd,df->btf", in_second, up_full, preferred_element_type=jnp.float32)
            + bias_up
        )
        activated = gelu_tanh(upward).astype(jnp.bfloat16)
        feed_part = jnp.einsum(
            "btf,fd->btd", activated, down_full, preferred_element_type=jnp.float32
        )
        feed_out = lax.psum(feed_part, "tp") + bias_down
        outputs.append((residual + gate_two * feed_out).astype(jnp.bfloat16))
        cotangent = grad_out[batch_index].astype(jnp.float32)
        grad_feed = (cotangent * gate_two).astype(jnp.bfloat16)
        grad_gate_two = jnp.sum(cotangent * feed_out, 1)
        grad_act = jnp.einsum(
            "btd,fd->btf", grad_feed, down_full, preferred_element_type=jnp.float32
        )
        gelu_value, gelu_pull = jax.vjp(gelu_tanh, upward)
        grad_upward = gelu_pull(grad_act)[0].astype(jnp.bfloat16)
        in_second_part = jnp.einsum(
            "btf,df->btd", grad_upward, up_full, preferred_element_type=jnp.float32
        )
        grad_in_second = lax.psum(in_second_part, "tp")
        grad_shift_two = jnp.sum(grad_in_second, 1)
        grad_scale_two = jnp.sum(grad_in_second * normed_two, 1)
        grad_residual = cotangent + norm_back(
            grad_in_second * (1.0 + scale_two), normed_two, inverse_two
        )
        grad_attended = (grad_residual * gate_one).astype(jnp.bfloat16)
        grad_gate_one = jnp.sum(grad_residual * attended, 1)
        grad_blended = jnp.einsum(
            "btd,ed->bte", grad_attended, proj_full, preferred_element_type=jnp.float32
        ).astype(jnp.bfloat16)
        grad_queries, key_terms = lax.map(
            partial(attend_back, heads_here=heads_here),
            (queries, key_all, value_all, grad_blended, logsum),
        )
        key_grads = lax.psum_scatter(key_terms, "ctx", scatter_dimension=1, tiled=True)
        grad_projected = jnp.concatenate([grad_queries[:, :, None], key_grads], 2).astype(
            jnp.bfloat16
        )
        in_first_part = jnp.einsum(
            "btke,dke->btd", grad_projected, qkv_full, preferred_element_type=jnp.float32
        )
        grad_in_first = lax.psum(in_first_part, "tp")
        grad_shift_one = jnp.sum(grad_in_first, 1)
        grad_scale_one = jnp.sum(grad_in_first * normed_one, 1)
        input_grads.append(
            grad_residual + norm_back(grad_in_first * (1.0 + scale_one), normed_one, inverse_one)
        )
        mod_terms = jnp.stack(
            [
                grad_shift_one,
                grad_scale_one,
                grad_gate_one,
                grad_shift_two,
                grad_scale_two,
                grad_gate_two,
            ],
            1,
        )
        grad_mod = lax.psum(mod_terms, "ctx").astype(jnp.bfloat16)
        grad_mod_here = lax.dynamic_slice_in_dim(grad_mod, first_column, half_width, 2)
        cond_term = jnp.einsum(
            "bke,dke->bd", grad_mod_here, ada_full, preferred_element_type=jnp.float32
        )
        silu_value, silu_pull = jax.vjp(jax.nn.silu, cond_value)
        cond_grads.append(silu_pull(lax.psum(cond_term, "tp"))[0])
        terms = (
            lead_ctx
            * jnp.einsum(
                "bd,bke->dke", silu_cond, grad_mod_here, preferred_element_type=jnp.float32
            ),
            jnp.einsum(
                "btd,btke->dke", in_first, grad_projected, preferred_element_type=jnp.float32
            ),
            jnp.einsum(
                "bte,btd->ed", blended_low, grad_attended, preferred_element_type=jnp.float32
            ),
            jnp.einsum("btd,btf->df", in_second, grad_upward, preferred_element_type=jnp.float32),
            jnp.einsum("btf,btd->fd", activated, grad_feed, preferred_element_type=jnp.float32),
        )
        pair_sum = jnp.sum(grad_projected[:, :, 0::2].astype(jnp.float32), (0, 1))
        up_sum = jnp.sum(grad_upward.astype(jnp.float32), (0, 1))
        bias_terms = (
            lead_tp * lead_ctx * jnp.sum(grad_mod.astype(jnp.float32), 0),
            lax.dynamic_update_slice_in_dim(
                jnp.zeros(qv_bias.shape, jnp.float32), pair_sum, first_column, 1
            ),
            lead_tp * jnp.sum(grad_attended.astype(jnp.float32), (0, 1)),
            lax.dynamic_update_slice_in_dim(
                jnp.zeros(up_bias.shape, jnp.float32), up_sum, tp_rank * hidden_here, 0
            ),
            lead_tp * jnp.sum(grad_feed.astype(jnp.float32), (0, 1)),
        )
        bias_totals = tuple((earlier + later for earlier, later in zip(bias_totals, bias_terms)))
        grad_shards = tuple(
            (earlier + later for earlier, later in zip(grad_shards, scatter_grads(terms)))
        )
    bias_done = lax.psum(bias_totals, ("fsdp", "ctx", "tp"))
    return (
        jnp.stack(outputs),
        jnp.stack(input_grads),
        jnp.stack(cond_grads),
        grad_shards[0],
        bias_done[0],
        grad_shards[1],
        bias_done[1],
        grad_shards[2],
        bias_done[2],
        grad_shards[3],
        bias_done[3],
        grad_shards[4],
        bias_done[4],
    )


def solution(mesh):
    in_specs = (
        P(None, "fsdp", "ctx", None),
        P(None, "fsdp", None),
        P(None, "fsdp", "ctx", None),
        P(("fsdp", "ctx"), None, "tp"),
        P(),
        P(("fsdp", "ctx"), None, "tp"),
        P(),
        P("tp", ("fsdp", "ctx")),
        P(),
        P(("fsdp", "ctx"), "tp"),
        P(),
        P("tp", ("fsdp", "ctx")),
        P(),
    )
    out_specs = (
        P(None, "fsdp", "ctx", None),
        P(None, "fsdp", "ctx", None),
        P(None, "fsdp", None),
        P(("fsdp", "ctx"), None, "tp"),
        P(),
        P(("fsdp", "ctx"), None, "tp"),
        P(),
        P("tp", ("fsdp", "ctx")),
        P(),
        P(("fsdp", "ctx"), "tp"),
        P(),
        P("tp", ("fsdp", "ctx")),
        P(),
    )
    return jax.shard_map(body, mesh=mesh, in_specs=in_specs, out_specs=out_specs, check_vma=False)
```

profile of v0, /device:TPU:0, one launch (start us, length us, event | category | flops | bytes accessed | tf_op | source)
XLA Modules:
  0.0 1814.5 jit_solution(17322543694355994409)
XLA Ops:
  15.0 75.7 %all-gather.21.cloned.1.call-done = bf16[1152,6,576]{2,0,1:T(8,128)(2,1)} async-done(((bf16[72,6,576]{2,0,1:T(8,128)(2,1)}), bf16[1152,6,576]{2,0,1:T(8,128)(2,1)}) %all-gather.21.cloned.1.call-update) | async-done | bytes 7962640 | tf_op jit(solution)/shard_map/all_gather | solution.py:32
  90.7 4.9 fusion.272
  100.0 4.4 all-gather.8
  105.2 37.8 %all-gather.23.cloned.1.call-done = bf16[1152,3,576]{2,0,1:T(8,128)(2,1)} async-done(((bf16[72,3,576]{2,0,1:T(8,128)(2,1)}), bf16[1152,3,576]{2,0,1:T(8,128)(2,1)}) %all-gather.23.cloned.1.call-update) | async-done | bytes 3981328 | tf_op jit(solution)/shard_map/all_gather | solution.py:33
  142.9 4.2 convolution_bitcast_fusion.15
  150.1 4.6 all-gather.7
  156.8 4.6 all-gather.6
  166.9 4.2 convolution_bitcast_fusion.17
  171.1 4.8 convolution_bitcast_fusion.16
  187.7 2.9 multiply_reduce_fusion.3
  190.7 3.2 copy-done.3
  195.9 14.1 all-gather.35.cloned.1.call-done
  210.0 5.6 fusion.72
  215.6 25.9 %all-gather.39.cloned.1.call-done = bf16[1,1024,1,576]{1,3,2,0:T(8,128)(2,1)} async-done(((bf16[1,256,1,576]{1,3,2,0:T(8,128)(2,1)}), bf16[1,1024,1,576]{1,3,2,0:T(8,128)(2,1)}) %all-gather.39.cloned.1.call-update) | async-done | bytes 1179664 | tf_op jit(solution)/shard_map/all_gather | solution.py:168
  244.2 3.2 copy-done.1
  249.9 23.2 %all-gather.37.cloned.1.call-done = bf16[1,1024,1,576]{1,3,2,0:T(8,128)(2,1)} async-done(((bf16[1,256,1,576]{1,3,2,0:T(8,128)(2,1)}), bf16[1,1024,1,576]{1,3,2,0:T(8,128)(2,1)}) %all-gather.37.cloned.1.call-update) | async-done | bytes 1179664 | tf_op jit(solution)/shard_map/all_gather | solution.py:168
  275.8 3.2 copy-done.2
  281.0 24.3 %all-gather.33.cloned.1.call-done = bf16[1,1024,576]{1,2,0:T(8,128)(2,1)} async-done(((bf16[1,256,576]{1,2,0:T(8,128)(2,1)}), bf16[1,1024,576]{1,2,0:T(8,128)(2,1)}) %all-gather.33.cloned.1.call-update) | async-done | bytes 1179664 | tf_op jit(solution)/shard_map/all_gather | solution.py:169
  305.3 5.7 fusion.73
  311.1 26.5 %all-gather.25.cloned.1.call-done = bf16[1,1024,576]{1,2,0:T(8,128)(2,1)} async-done(((bf16[1,256,576]{1,2,0:T(8,128)(2,1)}), bf16[1,1024,576]{1,2,0:T(8,128)(2,1)}) %all-gather.25.cloned.1.call-update) | async-done | bytes 1179664 | tf_op jit(solution)/shard_map/all_gather | solution.py:169
  337.6 5.7 fusion.74
  343.3 34.3 %all-gather.27.cloned.1.call-done = bf16[576,1152]{0,1:T(8,128)(2,1)} async-done(((bf16[576,72]{0,1:T(8,128)(2,1)}), bf16[576,1152]{0,1:T(8,128)(2,1)}) %all-gather.27.cloned.1.call-update) | async-done | bytes 1327120 | tf_op jit(solution)/shard_map/all_gather | solution.py:34
  377.6 3.2 convolution_bitcast_fusion
  387.0 91.0 %all-reduce.15.cloned.1.call-done = (f32[1,256,1152]{2,1,0:T(8,128)}, f32[1,256,1152]{2,1,0:T(8,128)}, f32[1,256,1152]{2,1,0:T(8,128)}) async-done(((f32[1,256,1152]{2,1,0:T(8,128)}, f32[1,256,1152]{2,1,0:T(8,128)}, f32[1,256,1152]{2,1,0:T(8,128)}), (f32[1,256,1152]{2,1,0:T(8,128)}, f32[1,256,1152]{2,1,0:T(8,128)}, f32[1,256,1152]{2,1,0:T(8,128)})) %all-reduce.15.cloned.1.call-update) | async-done | bytes 3538960 | tf_op jit(solution)/shard_map/psum | solution.py:178
  483.9 52.9 %all-gather.29.cloned.1.call-done = bf16[1152,2304]{1,0:T(8,128)(2,1)} async-done(((bf16[72,2304]{1,0:T(8,128)(2,1)}), bf16[1152,2304]{1,0:T(8,128)(2,1)}) %all-gather.29.cloned.1.call-update) | async-done | bytes 5308432 | tf_op jit(solution)/shard_map/all_gather | solution.py:35
  536.9 6.2 convolution_add_fusion.4
  543.1 51.0 %all-gather.31.cloned.1.call-done = bf16[2304,1152]{0,1:T(8,128)(2,1)} async-done(((bf16[2304,72]{0,1:T(8,128)(2,1)}), bf16[2304,1152]{0,1:T(8,128)(2,1)}) %all-gather.31.cloned.1.call-update) | async-done | bytes 5308432 | tf_op jit(solution)/shard_map/all_gather | solution.py:36
  594.1 6.8 convert_reduce_fusion
  605.6 3.8 convert_reduce_fusion.2
  614.1 3.8 convert_reduce_fusion.1
  623.0 92.2 %all-reduce.13.cloned.1.call-done = (f32[1,256,1152]{2,1,0:T(8,128)}, f32[1,256,1152]{2,1,0:T(8,128)}, f32[1,256,1152]{2,1,0:T(8,128)}) async-done(((f32[1,256,1152]{2,1,0:T(8,128)}, f32[1,256,1152]{2,1,0:T(8,128)}, f32[1,256,1152]{2,1,0:T(8,128)}), (f32[1,256,1152]{2,1,0:T(8,128)}, f32[1,256,1152]{2,1,0:T(8,128)}, f32[1,256,1152]{2,1,0:T(8,128)})) %all-reduce.13.cloned.1.call-update) | async-done | bytes 3538960 | tf_op jit(solution)/shard_map/psum | solution.py:203
  717.8 3.5 convert_reduce_fusion.9
  722.0 4.5 fusion.6
  741.3 4.3 convert_reduce_fusion.10
  756.1 2.9 maximum_bitcast_fusion
  762.2 5.8 multiply_reduce_fusion.1
  777.1 6.5 convolution_bitcast_fusion.9
  783.7 5.8 convolution_bitcast_fusion.10
  789.5 3.1 convolution_bitcast_fusion.11
  799.4 22.6 %reduce-scatter.15.cloned.1.call-done = f32[1,256,2,576]{1,3,2,0:T(8,128)} async-done(((f32[1,1024,2,576]{1,3,2,0:T(8,128)}), f32[1,256,2,576]{1,3,2,0:T(8,128)}) %reduce-scatter.15.cloned.1.call-update) | async-done | bytes 1179664 | tf_op jit(solution)/shard_map/reduce_scatter | solution.py:218
  824.1 85.8 %reduce-scatter.11.cloned.1.call-done = f32[1,256,2,576]{1,3,2,0:T(8,128)} async-done(((f32[1,1024,2,576]{1,3,2,0:T(8,128)}), f32[1,256,2,576]{1,3,2,0:T(8,128)}) %reduce-scatter.11.cloned.1.call-update) | async-done | bytes 1179664 | tf_op jit(solution)/shard_map/reduce_scatter | solution.py:218
  912.1 85.8 %reduce-scatter.13.cloned.1.call-done = f32[1,256,2,576]{1,3,2,0:T(8,128)} async-done(((f32[1,1024,2,576]{1,3,2,0:T(8,128)}), f32[1,256,2,576]{1,3,2,0:T(8,128)}) %reduce-scatter.13.cloned.1.call-update) | async-done | bytes 1179664 | tf_op jit(solution)/shard_map/reduce_scatter | solution.py:218
  999.4 5.2 convolution_bitcast_fusion.3
  1004.5 5.0 convolution_bitcast_fusion.7
  1018.4 3.9 fusion.260
  1024.2 5.8 convolution_add_fusion.2
  1031.6 3.7 fusion.160
  1037.3 6.0 convolution_add_fusion
  1049.4 5.0 add_add_fusion
  1063.7 121.3 %all-reduce.11.cloned.1.call-done = (f32[1,256,1152]{2,1,0:T(8,128)}, f32[1,256,1152]{2,1,0:T(8,128)}, f32[1,256,1152]{2,1,0:T(8,128)}, f32[1,256,1152]{2,1,0:T(...) async-done(((f32[1,256,1152]{2,1,0:T(8,128)}, f32[1,256,1152]{2,1,0:T(8,128)}, f32[1,256,1152]{2,1,0:T(8,128)}, f32[1,256,1152]{2,1,0:T(8,128)}, ...) | async-done | bytes 7077904 | tf_op jit(solution)/shard_map/psum | solution.py:190
  1185.1 3.8 fusion.83
  1190.3 3.8 multiply_reduce_fusion.11
  1200.0 20.9 %all-reduce.2 = (bf16[1,6,1152]{2,1,0:T(8,128)(2,1)S(1)}, bf16[1,6,1152]{2,1,0:T(8,128)(2,1)S(1)}, bf16[1,6,1152]{2,1,0:T(8,128)(2,1)S(1)}) all-reduce(f32[1,6,1152]{2,1,0:T(8,128)S(1)} %stack.144, f32[1,6,1152]{2,1,0:T(8,128)S(1)} %stack.136, f32[1,6,1152]{2,1,0:T(8,128)S(1)} %stack.128), channel_id=1, replica_groups=mesh['fsdp'=4,'ctx'=4,'tp'=2] {'ctx'}, use_global_device_ids=true, to_apply=%region_70.71 | all-reduce | flops 20736 | bytes 124416 | tf_op jit(solution)/shard_map/psum | solution.py:242
  1223.0 8.2 add_multiply_fusion
  1246.6 6.7 convolution_bitcast_fusion.12
  1253.3 6.6 convolution_bitcast_fusion.13
  1260.0 3.0 convolution_bitcast_fusion.14
  1263.0 8.6 all-reduce.3
  1274.3 43.5 %all-reduce.1 = (f32[6,1152]{1,0:T(8,128)}, f32[2,1152]{1,0:T(2,128)}, f32[1152]{0:T(1024)}, f32[4608]{0:T(1024)}, f32[1152]{0:T(1024)}) all-reduce(f32[6,1152]{1,0:T(8,128)} %multiply_bitcast_fusion, f32[2,1152]{1,0:T(2,128)} %add.729, f32[1152]{0:T(1024)} %add_multiply_fusion.2, ...), channel_id=1, replica_groups=mesh['fsdp'=4,'ctx'=4,'tp'=2] {'fsdp','ctx','tp'}, use_global_device_ids=true, to_apply=%region_75.76 | all-reduce | flops 16128 | bytes 129024 | tf_op jit(solution)/shard_map/psum | solution.py:280
  1321.9 2.9 pad_maximum_fusion.1
  1328.1 52.1 %reduce-scatter.21.cloned.1.call-done = f32[72,2304]{1,0:T(8,128)} async-done(((f32[1152,2304]{1,0:T(8,128)}), f32[72,2304]{1,0:T(8,128)}) %reduce-scatter.21.cloned.1.call-update) | async-done | bytes 663568 | tf_op jit(solution)/shard_map/reduce_scatter | solution.py:45
  1380.2 125.0 %reduce-scatter.23.cloned.1.call-done = f32[2304,72]{0,1:T(8,128)} async-done(((f32[2304,1152]{0,1:T(8,128)}), f32[2304,72]{0,1:T(8,128)}) %reduce-scatter.23.cloned.1.call-update) | async-done | bytes 663568 | tf_op jit(solution)/shard_map/reduce_scatter | solution.py:46
  1505.2 112.0 %reduce-scatter.19.cloned.1.call-done = f32[72,3,576]{2,0,1:T(8,128)} async-done(((f32[1152,3,576]{2,0,1:T(8,128)}), f32[72,3,576]{2,0,1:T(8,128)}) %reduce-scatter.19.cloned.1.call-update) | async-done | bytes 497680 | tf_op jit(solution)/shard_map/reduce_scatter | solution.py:43
  1617.3 190.2 %reduce-scatter.17.cloned.1.call-done = f32[72,6,576]{2,0,1:T(8,128)} async-done(((f32[1152,6,576]{2,0,1:T(8,128)}), f32[72,6,576]{2,0,1:T(8,128)}) %reduce-scatter.17.cloned.1.call-update) | async-done | bytes 995344 | tf_op jit(solution)/shard_map/reduce_scatter | solution.py:42
  (586 shorter events, 190.0 us)
Async XLA Ops:
  7.2 83.5 %all-gather.21.cloned.1.call-start = ((), (), s32[]{:S(2)}) async-start(), calls=%async_computation.8 | async-start | bytes 9400320 | tf_op jit(solution)/shard_map/all_gather | solution.py:32
  7.9 135.0 %all-gather.23.cloned.1.call-start = ((), (), s32[]{:S(2)}) async-start(), calls=%async_computation.9 | async-start | bytes 4700160 | tf_op jit(solution)/shard_map/all_gather | solution.py:33
  8.7 179.1 %all-gather.41.cloned.1.call-start = ((), (), s32[]{:S(2)}) async-start(), calls=%async_computation.21 | async-start | bytes 1474560 | tf_op jit(solution)/shard_map/all_gather | solution.py:168
  90.7 6.0 copy-start
  105.1 42.0 %copy-start.93 = (f32[1152]{0:T(1024)}, f32[1152]{0:T(1024)S(1)}, u32[]{:S(2)}) copy-start(f32[1152]{0:T(1024)S(1)} %get-tuple-element.198) | copy-start | bytes 13828
  105.1 42.0 %copy-start.132 = (f32[1152]{0:T(1024)}, f32[1152]{0:T(1024)S(1)}, u32[]{:S(2)}) copy-start(f32[1152]{0:T(1024)S(1)} %get-tuple-element.197) | copy-start | bytes 13828
  147.1 28.8 %copy-start.67 = (f32[1,256,3,576]{1,3,2,0:T(8,128)}, f32[1,256,3,576]{1,3,2,0:T(8,128)S(1)}, u32[]{:S(2)}) copy-start(f32[1,256,3,576]{1,3,2,0:T(8,128)S(1)} %convolution_bitcast_fusion.15) | copy-start | bytes 5308420
  148.0 62.0 %all-gather.35.cloned.1.call-start = ((), (), s32[]{:S(2)}) async-start(), calls=%async_computation.15 | async-start | bytes 1474560 | tf_op jit(solution)/shard_map/all_gather | solution.py:169
  150.1 21.0 %copy-start.165 = (f32[256]{0:T(256)}, f32[256]{0:T(256)S(1)}, u32[]{:S(2)}) copy-start(f32[256]{0:T(256)S(1)} %add_rsqrt_fusion.3) | copy-start | bytes 3076
  165.2 5.9 copy-start.137
  177.4 6.6 copy-start.168
  177.5 64.0 %all-gather.39.cloned.1.call-start = ((), (), s32[]{:S(2)}) async-start(), calls=%async_computation.20 | async-start | bytes 1474560 | tf_op jit(solution)/shard_map/all_gather | solution.py:168
  179.3 93.7 %all-gather.37.cloned.1.call-start = ((), (), s32[]{:S(2)}) async-start(), calls=%async_computation.19 | async-start | bytes 1474560 | tf_op jit(solution)/shard_map/all_gather | solution.py:168
  181.2 124.1 %all-gather.33.cloned.1.call-start = ((), (), s32[]{:S(2)}) async-start(), calls=%async_computation.14 | async-start | bytes 1474560 | tf_op jit(solution)/shard_map/all_gather | solution.py:169
  182.0 155.6 %all-gather.25.cloned.1.call-start = ((), (), s32[]{:S(2)}) async-start(), calls=%async_computation.10 | async-start | bytes 1474560 | tf_op jit(solution)/shard_map/all_gather | solution.py:169
  182.7 194.9 %all-gather.27.cloned.1.call-start = ((), (), s32[]{:S(2)}) async-start(), calls=%async_computation.11 | async-start | bytes 1566720 | tf_op jit(solution)/shard_map/all_gather | solution.py:34
  183.4 294.6 %all-reduce.15.cloned.1.call-start = ((), (), s32[]{:S(2)}) async-start(), calls=%async_computation.29 | async-start | bytes 7077888 | tf_op jit(solution)/shard_map/psum | solution.py:178
  187.7 85.4 %copy-start.34 = (f32[1,256,1,576]{1,3,2,0:T(8,128)}, f32[1,256,1,576]{1,3,2,0:T(8,128)S(1)}, u32[]{:S(2)}) copy-start(f32[1,256,1,576]{1,3,2,0:T(8,128)S(1)} %slice.176) | copy-start | bytes 1769476
  195.9 19.7 %copy-start.142 = (f32[8,256]{1,0:T(8,128)}, f32[8,256]{1,0:T(8,128)S(1)}, u32[]{:S(2)}) copy-start(f32[8,256]{1,0:T(8,128)S(1)} %fusion.2) | copy-start | bytes 24580
  215.6 162.1 %copy-start.74 = (bf16[8,72,256]{2,1,0:T(8,128)(2,1)}, bf16[8,72,256]{2,1,0:T(8,128)(2,1)S(1)}, u32[]{:S(2)}) copy-start(bf16[8,72,256]{2,1,0:T(8,128)(2,1)S(1)} %fusion.72) | copy-start | bytes 884740
  279.0 26.3 %copy-start.108 = (f32[8,256]{1,0:T(8,128)S(1)}, f32[8,256]{1,0:T(8,128)}, u32[]{:S(2)}) copy-start(f32[8,256]{1,0:T(8,128)} %copy-done.107) | copy-start | bytes 24580
  279.0 26.3 %copy-start.140 = (f32[8,256]{1,0:T(8,128)S(1)}, f32[8,256]{1,0:T(8,128)}, u32[]{:S(2)}) copy-start(f32[8,256]{1,0:T(8,128)} %fusion.1) | copy-start | bytes 24580
  281.0 56.6 %copy-start.141 = (f32[8,256]{1,0:T(8,128)}, f32[8,256]{1,0:T(8,128)S(1)}, u32[]{:S(2)}) copy-start(f32[8,256]{1,0:T(8,128)S(1)} %fusion) | copy-start | bytes 24580
  305.3 32.3 %copy-start.110 = (f32[8,256]{1,0:T(8,128)S(1)}, f32[8,256]{1,0:T(8,128)}, u32[]{:S(2)}) copy-start(f32[8,256]{1,0:T(8,128)} %copy-done.109) | copy-start | bytes 24580
  311.1 69.8 %copy-start.76 = (bf16[8,72,256]{2,1,0:T(8,128)(2,1)}, bf16[8,72,256]{2,1,0:T(8,128)(2,1)S(1)}, u32[]{:S(2)}) copy-start(bf16[8,72,256]{2,1,0:T(8,128)(2,1)S(1)} %fusion.73) | copy-start | bytes 884740
  343.3 39.2 %copy-start.82 = (bf16[8,72,256]{2,1,0:T(8,128)(2,1)}, bf16[8,72,256]{2,1,0:T(8,128)(2,1)S(1)}, u32[]{:S(2)}) copy-start(bf16[8,72,256]{2,1,0:T(8,128)(2,1)S(1)} %fusion.74) | copy-start | bytes 884740
  384.3 152.5 %all-gather.29.cloned.1.call-start = ((), (), s32[]{:S(2)}) async-start(), calls=%async_computation.12 | async-start | bytes 5640192 | tf_op jit(solution)/shard_map/all_gather | solution.py:35
  385.1 209.0 %all-gather.31.cloned.1.call-start = ((), (), s32[]{:S(2)}) async-start(), calls=%async_computation.13 | async-start | bytes 5640192 | tf_op jit(solution)/shard_map/all_gather | solution.py:36
  385.7 329.6 %all-reduce.13.cloned.1.call-start = ((), (), s32[]{:S(2)}) async-start(), calls=%async_computation.28 | async-start | bytes 7077888 | tf_op jit(solution)/shard_map/psum | solution.py:203
  536.9 57.2 %copy-start.22 = (bf16[3,1,256,1152]{3,2,1,0:T(8,128)(2,1)S(1)}, bf16[3,1,256,1152]{3,2,1,0:T(8,128)(2,1)}, u32[]{:S(2)}) copy-start(bf16[3,1,256,1152]{3,2,1,0:T(8,128)(2,1)} %param.15) | copy-start | bytes 5308420
  594.1 6.8 copy-start.173
  621.7 93.5 %copy-start.7 = (f32[1,256,1152]{2,1,0:T(8,128)S(1)}, f32[1,256,1152]{2,1,0:T(8,128)}, u32[]{:S(2)}) copy-start(f32[1,256,1152]{2,1,0:T(8,128)} %copy-done.6) | copy-start | bytes 3538948
  621.7 93.5 %copy-start.86 = (f32[1152]{0:T(1024)S(1)}, f32[1152]{0:T(1024)}, u32[]{:S(2)}) copy-start(f32[1152]{0:T(1024)} %get-tuple-element.196) | copy-start | bytes 13828
  621.7 93.5 %copy-start.154 = (f32[256]{0:T(256)S(1)}, f32[256]{0:T(256)}, u32[]{:S(2)}) copy-start(f32[256]{0:T(256)} %add_rsqrt_fusion) | copy-start | bytes 3076
  621.8 200.2 %reduce-scatter.15.cloned.1.call-start = ((), (), s32[]{:S(2)}) async-start(), calls=%async_computation.18 | async-start | bytes 5898240 | tf_op jit(solution)/shard_map/reduce_scatter | solution.py:218
  715.2 6.0 copy-start.10
  717.8 8.8 slice-start.7
  736.6 173.4 %reduce-scatter.11.cloned.1.call-start = ((), (), s32[]{:S(2)}) async-start(), calls=%async_computation.16 | async-start | bytes 5898240 | tf_op jit(solution)/shard_map/reduce_scatter | solution.py:218
  737.6 8.9 slice-start.5
  759.0 238.9 %reduce-scatter.13.cloned.1.call-start = ((), (), s32[]{:S(2)}) async-start(), calls=%async_computation.17 | async-start | bytes 5898240 | tf_op jit(solution)/shard_map/reduce_scatter | solution.py:218
  762.2 6.0 slice-start.4
  776.9 408.1 %all-reduce.11.cloned.1.call-start = ((), (), s32[]{:S(2)}) async-start(), calls=%async_computation.27 | async-start | bytes 14155776 | tf_op jit(solution)/shard_map/psum | solution.py:190
  777.1 6.5 copy-start.32
  777.1 12.3 slice-start.11
  795.2 204.1 %copy-start.54 = (bf16[8,72,256]{2,1,0:T(8,128)(2,1)}, bf16[8,72,256]{2,1,0:T(8,128)(2,1)S(1)}, u32[]{:S(2)}) copy-start(bf16[8,72,256]{2,1,0:T(8,128)(2,1)S(1)} %fusion.77) | copy-start | bytes 884740
  799.4 210.1 %copy-start.56 = (bf16[8,72,256]{2,1,0:T(8,128)(2,1)}, bf16[8,72,256]{2,1,0:T(8,128)(2,1)S(1)}, u32[]{:S(2)}) copy-start(bf16[8,72,256]{2,1,0:T(8,128)(2,1)S(1)} %fusion.76) | copy-start | bytes 884740
  999.3 10.2 copy-start.62
  999.4 10.2 slice-start.13
  1012.4 315.7 %reduce-scatter.25.cloned.1.call-start = ((), (), s32[]{:S(2)}) async-start(), calls=%async_computation.26 | async-start | bytes 3133440
  1017.8 362.5 %reduce-scatter.21.cloned.1.call-start = ((), (), s32[]{:S(2)}) async-start(), calls=%async_computation.24 | async-start | bytes 11280384 | tf_op jit(solution)/shard_map/reduce_scatter | solution.py:45
  1030.1 475.1 %reduce-scatter.23.cloned.1.call-start = ((), (), s32[]{:S(2)}) async-start(), calls=%async_computation.25 | async-start | bytes 11280384 | tf_op jit(solution)/shard_map/reduce_scatter | solution.py:46
  1043.3 573.9 %reduce-scatter.19.cloned.1.call-start = ((), (), s32[]{:S(2)}) async-start(), calls=%async_computation.23 | async-start | bytes 9400320 | tf_op jit(solution)/shard_map/reduce_scatter | solution.py:43
  1054.5 753.0 %reduce-scatter.17.cloned.1.call-start = ((), (), s32[]{:S(2)}) async-start(), calls=%async_computation.22 | async-start | bytes 18800640 | tf_op jit(solution)/shard_map/reduce_scatter | solution.py:42
  1221.0 10.3 copy-start.121
  1221.0 10.2 copy-start.122
  1221.0 10.2 copy-start.123
  1231.2 6.6 copy-start.45
  1246.6 6.7 copy-start.119
  1246.6 13.3 slice-start
  1246.6 13.3 slice-start.1
  1253.3 6.6 slice-start.2
  1253.3 6.6 copy-start.120
  1260.0 61.9 %copy-start.64 = (bf16[1,1,256,1152]{3,2,1,0:T(8,128)(2,1)S(1)}, bf16[1,1,256,1152]{3,2,1,0:T(8,128)(2,1)}, u32[]{:S(2)}) copy-start(bf16[1,1,256,1152]{3,2,1,0:T(8,128)(2,1)} %get-tuple-element.258) | copy-start | bytes 1769476
  1260.0 64.8 %copy-start.43 = (f32[1,256,1152]{2,1,0:T(8,128)S(1)}, f32[1,256,1152]{2,1,0:T(8,128)}, u32[]{:S(2)}) copy-start(f32[1,256,1152]{2,1,0:T(8,128)} %get-tuple-element.227) | copy-start | bytes 3538948
  (147 other events, 462.7 us)
Sparse Core Ops, SparseCore 0:
  10.2 80.4 all-gather.20
  92.9 49.9 all-gather.22
  148.1 30.2 all-gather.40
  179.8 30.0 all-gather.34
  211.4 30.0 all-gather.38
  242.9 30.0 all-gather.36
  275.2 30.1 all-gather.32
  307.5 30.0 all-gather.24
  339.8 37.7 all-gather.26
  384.5 93.5 all-reduce.14
  480.5 56.3 all-gather.28
  539.1 54.9 all-gather.30
  621.9 93.2 all-reduce.12
  736.7 85.2 reduce-scatter.14
  824.1 85.7 reduce-scatter.10
  912.1 85.7 reduce-scatter.12
  1012.5 172.4 all-reduce.10
  1189.9 65.2 reduce-scatter.24
  1260.4 119.7 reduce-scatter.20
  1385.2 119.9 reduce-scatter.22
  1510.5 106.6 reduce-scatter.18
  1622.0 185.3 reduce-scatter.16
where the time goes:
time: 1830 us; the launch traced here: 1810 us
  waiting for transfers between devices  1350 us (74%)
  matrix products  198 us (11%)
  other arithmetic  105 us (6%)
  blocking collectives  86.6 us (5%)
  local copies, waits for them, and re-layouts  56 us (3%)
    reduce_scatter x3, waiting for transfers between devices, body(): lax.psum_scatter(key_terms, 'ctx', scatter_dimension=1, tiled=True)  194 us
    reduce_scatter x1, waiting for transfers between devices, scatter_grads(): lax.psum_scatter(term_tuple[0], ('fsdp', 'ctx'), scatter_dimension=0, til...  190 us
    reduce_scatter x1, waiting for transfers between devices, scatter_grads(): lax.psum_scatter(term_tuple[4], ('fsdp', 'ctx'), scatter_dimension=1, til...  125 us
    psum x1, waiting for transfers between devices, body(): feed_out = lax.psum(feed_part, 'tp') + bias_down  121 us
    reduce_scatter x1, waiting for transfers between devices, scatter_grads(): lax.psum_scatter(term_tuple[1], ('fsdp', 'ctx'), scatter_dimension=0, til...  112 us
    psum x1, waiting for transfers between devices, body(): grad_in_second = lax.psum(in_second_part, 'tp')  92.2 us
    psum x1, waiting for transfers between devices, body(): attended = lax.psum(attn_part, 'tp') + bias_proj  91 us
    all_gather x1, waiting for transfers between devices, gather_weights(): lax.all_gather(shard_tuple[0], ('fsdp', 'ctx'), axis=0, tiled=True)  75.7 us
  transfers between devices with their start and end apart: 22, of which 20 were waited for; matrix products, arithmetic and copies ran while one was open for 15% of the time, Pallas kernels for 0%

commit v1 on v0

v1 whole, which is shorter than its diff:
```python
from functools import partial

import jax
import jax.numpy as jnp
from jax import lax
from jax.experimental import pallas as pl
from jax.experimental.pallas import tpu as pltpu
from jax.sharding import PartitionSpec as P

HEADS = 16
HEAD_DIM = 72
LOG2E = 1.4426950408889634
F32 = jnp.float32
BF16 = jnp.bfloat16


def dot(a, b, dims):
    return lax.dot_general(a, b, (dims, ((), ())), preferred_element_type=F32)


def normalize(values):
    centre = values - jnp.mean(values, -1, keepdims=True)
    inverse = lax.rsqrt(jnp.mean(centre * centre, -1, keepdims=True) + 1e-06)
    return (centre * inverse, inverse)


def norm_back(incoming, normed, inverse):
    return inverse * (
        incoming
        - jnp.mean(incoming, -1, keepdims=True)
        - normed * jnp.mean(incoming * normed, -1, keepdims=True)
    )


def shift(x, k):
    size = lax.axis_size("ctx")
    return lax.ppermute(x, "ctx", [(i, (i + k) % size) for i in range(size)])


def flip(x, axis, bit):
    size = lax.axis_size(axis)
    return lax.ppermute(x, axis, [(i, i ^ (1 << bit)) for i in range(size)])


def bits_of(axis):
    return lax.axis_size(axis).bit_length() - 1


def ring_gather(x):
    size = lax.axis_size("ctx")
    blocks = [x] * size
    moving = x
    for step in range(1, size // 2 + 1):
        moving = shift(moving, 1)
        blocks[step] = moving
    moving = x
    for step in range(1, (size - 1) // 2 + 1):
        moving = shift(moving, -1)
        blocks[size - step] = moving
    return blocks


def butterfly_sum(x, axis):
    for bit in range(bits_of(axis)):
        x = x + flip(x, axis, bit)
    return x


def cube_gather(x):
    x = x[None]
    for bit in range(bits_of("fsdp")):
        x = jnp.concatenate([x, flip(x, "fsdp", bit)], 0)
    return x


def cube_reduce(x):
    for bit in reversed(range(bits_of("fsdp"))):
        half = x.shape[0] // 2
        x = x[:half] + flip(x[half:], "fsdp", bit)
    return x[0]


def pick(entries, which):
    return lax.select_n(which, *entries) if len(entries) > 2 else jnp.where(which == 0, *entries)


def absolute(entries, rank, sign):
    size = len(entries)
    return jnp.stack([pick(entries, (sign * (place - rank)) % size) for place in range(size)])


def gather_pieces(shard):
    blocks = ring_gather(shard)
    size = len(blocks)
    if size * lax.axis_size("fsdp") > 16:
        pieces = [(0, tuple(range(size)), jnp.stack(blocks))]
    else:
        pieces = [(0, (k,), block[None]) for k, block in enumerate(blocks)]
    for bit in reversed(range(bits_of("fsdp"))):
        pieces = pieces + [
            (offset ^ (1 << bit), places, flip(block, "fsdp", bit))
            for offset, places, block in pieces
        ]
    return pieces


def place_kernel(targets, widths, *refs):
    count = len(targets)
    ins, outs = refs[:count], refs[count : count + len(widths)]
    held, in_sem, out_sem = refs[count + len(widths) :]
    own_f = lax.axis_index("fsdp")
    own_c = lax.axis_index("ctx")
    size_c = lax.axis_size("ctx")
    arriving, leaving = [], []
    for (offset, places), ref in zip(targets, ins):
        row = jnp.bitwise_xor(own_f, offset)
        for at, spot in enumerate(places):
            column = lax.rem(own_c + size_c - spot, size_c)
            slot = len(arriving)
            arriving.append(pltpu.make_async_copy(ref.at[at], held.at[slot], in_sem.at[slot]))
            first = 0
            for width, out in zip(widths, outs):
                leaving.append(
                    pltpu.make_async_copy(
                        held.at[slot, :, pl.ds(first, width)],
                        out.at[row, column],
                        out_sem.at[len(leaving)],
                    )
                )
                first += width
    for copy in arriving:
        copy.start()
    each = len(widths)
    for slot, copy in enumerate(arriving):
        copy.wait()
        for out_copy in leaving[slot * each : (slot + 1) * each]:
            out_copy.start()
    for copy in leaving:
        copy.wait()


def place(pieces, widths):
    size_f, size_c = lax.axis_size("fsdp"), lax.axis_size("ctx")
    rows, total = pieces[0][2].shape[1:]
    count = size_f * size_c
    outs = pl.pallas_call(
        partial(place_kernel, [piece[:2] for piece in pieces], widths),
        out_shape=[jax.ShapeDtypeStruct((size_f, size_c, rows, width), BF16) for width in widths],
        in_specs=[pl.BlockSpec(memory_space=pl.ANY)] * len(pieces),
        out_specs=[pl.BlockSpec(memory_space=pl.ANY)] * len(widths),
        scratch_shapes=[
            pltpu.VMEM((count, rows, total), BF16),
            pltpu.SemaphoreType.DMA((count,)),
            pltpu.SemaphoreType.DMA((count * len(widths),)),
        ],
        compiler_params=pltpu.CompilerParams(vmem_limit_bytes=40 << 20),
        cost_estimate=pl.CostEstimate(
            flops=0, bytes_accessed=4 * count * rows * total, transcendentals=0
        ),
    )(*[piece[2] for piece in pieces])
    return [out.reshape(-1, width) for out, width in zip(outs, widths)]


def reduce_rows(features, others, dims):
    size_f, size_c = lax.axis_size("fsdp"), lax.axis_size("ctx")
    own_f = lax.axis_index("fsdp")
    width = features.shape[-1] // size_f
    split = features.reshape(*features.shape[:-1], size_f // 2, 2, width)
    low = own_f % 2
    evens = split[..., 0, :].reshape(*features.shape[:-1], -1)
    odds = split[..., 1, :].reshape(*features.shape[:-1], -1)
    mine = jnp.where(low == 0, evens, odds)
    theirs = jnp.where(low == 0, odds, evens)
    there = flip(dot(theirs, others, dims), "fsdp", 0)
    total = dot(mine, others, dims) + there
    columns = total.shape[-1]
    for bit in range(1, bits_of("fsdp")):
        own_bit = (own_f >> bit) % 2
        pairs = total.reshape(-1, 2, width, columns)
        send = lax.dynamic_index_in_dim(pairs, 1 - own_bit, 1, False)
        keep = lax.dynamic_index_in_dim(pairs, own_bit, 1, False)
        total = keep + flip(send.astype(BF16), "fsdp", bit).astype(F32)
    return total.reshape(size_c, width // size_c, columns)


def ring_reduce(blocks):
    size = lax.axis_size("ctx")
    own = lax.axis_index("ctx")

    def block(offset):
        return lax.dynamic_index_in_dim(blocks, (own + offset) % size, 0, False)

    total = block(0)
    for sign, reach in ((1, size // 2), (-1, (size - 1) // 2)):
        moving = None
        for distance in range(reach, 0, -1):
            term = block(sign * distance)
            if moving is not None:
                term = term + moving
            moving = shift(term.astype(BF16), sign).astype(F32)
        if moving is not None:
            total = total + moving
    return total


def head_rows(ref, head):
    values = ref[...].astype(F32)
    row = lax.broadcasted_iota(jnp.int32, values.shape, 0)
    inside = (row >= head * HEAD_DIM) & (row < (head + 1) * HEAD_DIM)
    return jnp.where(inside, values, 0.0).astype(BF16), inside


def attend_kernel(heads, q_ref, k_ref, vt_ref, out_ref, log_ref):
    factor = HEAD_DIM ** (-0.5) * LOG2E
    total = None
    for head in range(heads):
        q_head, inside = head_rows(q_ref, head)
        scores = dot(k_ref[...], q_head, ((1,), (0,)))
        highest = jnp.max(scores, 0, keepdims=True)
        exponent = jnp.exp2((scores - highest) * factor)
        summed = jnp.sum(exponent, 0, keepdims=True)
        chances = (exponent * (1.0 / summed)).astype(BF16)
        mixed = dot(vt_ref[...], chances, ((1,), (0,)))
        total = mixed if total is None else jnp.where(inside, mixed, total)
        log_ref[pl.ds(head, 1), :] = highest * factor + jnp.log2(summed)
    out_ref[...] = total.astype(BF16)


def attend(qkv_t, keys, block):
    width = keys.shape[1]
    tokens = keys.shape[0]
    heads = width // HEAD_DIM
    return pl.pallas_call(
        partial(attend_kernel, heads),
        grid=(tokens // block,),
        in_specs=[
            pl.BlockSpec((None, width, block), lambda i: (0, 0, i)),
            pl.BlockSpec((tokens, width), lambda i: (0, 0)),
            pl.BlockSpec((None, width, tokens), lambda i: (2, 0, 0)),
        ],
        out_specs=[
            pl.BlockSpec((width, block), lambda i: (0, i)),
            pl.BlockSpec((heads, block), lambda i: (0, i)),
        ],
        out_shape=[
            jax.ShapeDtypeStruct((width, tokens), BF16),
            jax.ShapeDtypeStruct((heads, tokens), F32),
        ],
        compiler_params=pltpu.CompilerParams(vmem_limit_bytes=40 << 20),
        cost_estimate=pl.CostEstimate(
            flops=heads * tokens * tokens * 1600,
            bytes_accessed=8 * width * tokens,
            transcendentals=heads * tokens * tokens,
        ),
    )(qkv_t, keys, qkv_t)


def attend_back_kernel(
    heads, q_ref, k_ref, kt_ref, v_ref, do_ref, log_ref, out_ref, dk_ref, dv_ref
):
    step = pl.program_id(0)
    scaling = HEAD_DIM ** (-0.5)
    block = q_ref.shape[1]

    @pl.when(step == 0)
    def _():
        dk_ref[...] = jnp.zeros_like(dk_ref)
        dv_ref[...] = jnp.zeros_like(dv_ref)

    grad_query = None
    for head in range(heads):
        q_head, inside = head_rows(q_ref, head)
        do_head, _ = head_rows(do_ref, head)
        scores = dot(k_ref[...], q_head, ((1,), (0,)))
        chances = jnp.exp2(scores * (scaling * LOG2E) - log_ref[pl.ds(head, 1), :])
        grad_chances = dot(v_ref[...], do_head, ((1,), (0,)))
        weighted = jnp.sum(chances * grad_chances, 0, keepdims=True)
        grad_scores = (chances * (grad_chances - weighted)).astype(BF16)
        term = dot(kt_ref[...], grad_scores, ((1,), (0,)))
        grad_query = term if grad_query is None else jnp.where(inside, term, grad_query)
        dk_ref[...] += dot(q_head, grad_scores, ((1,), (1,)))
        dv_ref[...] += dot(do_head, chances.astype(BF16), ((1,), (1,)))
    columns = pl.ds(pl.multiple_of(step * block, block), block)
    out_ref[0, :, columns] = (grad_query * scaling).astype(BF16)

    @pl.when(step == pl.num_programs(0) - 1)
    def _():
        out_ref[1] = (dk_ref[...] * scaling).astype(BF16)
        out_ref[2] = dv_ref[...].astype(BF16)


def attend_back(qkv_t, keys, values, grad_t, logs, block):
    width = keys.shape[1]
    tokens = keys.shape[0]
    heads = width // HEAD_DIM
    return pl.pallas_call(
        partial(attend_back_kernel, heads),
        grid=(tokens // block,),
        in_specs=[
            pl.BlockSpec((None, width, block), lambda i: (0, 0, i)),
            pl.BlockSpec((tokens, width), lambda i: (0, 0)),
            pl.BlockSpec((None, width, tokens), lambda i: (1, 0, 0)),
            pl.BlockSpec((tokens, width), lambda i: (0, 0)),
            pl.BlockSpec((width, block), lambda i: (0, i)),
            pl.BlockSpec((heads, block), lambda i: (0, i)),
        ],
        out_specs=pl.BlockSpec((3, width, tokens), lambda i: (0, 0, 0)),
        out_shape=jax.ShapeDtypeStruct((3, width, tokens), BF16),
        scratch_shapes=[pltpu.VMEM((width, tokens), F32), pltpu.VMEM((width, tokens), F32)],
        compiler_params=pltpu.CompilerParams(vmem_limit_bytes=40 << 20),
        cost_estimate=pl.CostEstimate(
            flops=heads * tokens * tokens * 4000,
            bytes_accessed=16 * width * tokens,
            transcendentals=heads * tokens * tokens,
        ),
    )(qkv_t, keys, qkv_t, values, grad_t, logs)


def body(
    latents,
    condition,
    grad_out,
    ada_weight,
    ada_bias,
    qkv_weight,
    qv_bias,
    proj_weight,
    proj_bias,
    up_weight,
    up_bias,
    down_weight,
    down_bias,
):
    t = lax.axis_index("tp")
    c = lax.axis_index("ctx")
    f = lax.axis_index("fsdp")
    size_c = lax.axis_size("ctx")
    size_f = lax.axis_size("fsdp")
    micro, batch, here, model = latents.shape
    items = micro * batch
    half = here // 2
    half_width = qkv_weight.shape[2]
    group = half_width // size_c
    hidden = up_weight.shape[1]
    rows = qkv_weight.shape[0]
    first_column = t * half_width

    def swap(x):
        return flip(x, "tp", 0)

    def both(own, peer, axis):
        return jnp.where(
            t == 0,
            jnp.concatenate([own, peer], axis),
            jnp.concatenate([peer, own], axis),
        )

    def own_first(x):
        ahead, behind = x[:, :half], x[:, half:]
        return jnp.concatenate(
            [jnp.where(t == 0, ahead, behind), jnp.where(t == 0, behind, ahead)], 1
        )

    latent = own_first(latents.reshape(items, here, model))
    cotangent = own_first(grad_out.reshape(items, here, model))
    cond = condition.reshape(items, model).astype(F32)

    silu_all = cube_gather(jax.nn.silu(cond).astype(BF16))
    first_row = (f * size_c + c) * rows
    silu_here = lax.dynamic_slice_in_dim(silu_all, first_row, rows, 2).reshape(-1, rows)
    mod_part = dot(silu_here, ada_weight.reshape(rows, -1), ((1,), (0,)))
    mod_part = butterfly_sum(cube_reduce(mod_part.reshape(size_f, items, -1)), "ctx")
    bias_mod = lax.dynamic_slice_in_dim(ada_bias.astype(F32), first_column, half_width, 1)
    mod_half = (mod_part.reshape(items, 6, half_width) + bias_mod).astype(BF16)
    modulation = both(mod_half, swap(mod_half), 2).astype(F32)
    shift_one, scale_one, gate_one, shift_two, scale_two, gate_two = (
        modulation[:, k : k + 1] for k in range(6)
    )

    qkv_groups = (
        qkv_weight.reshape(rows, 3, size_c, group)
        .transpose(2, 0, 1, 3)
        .reshape(size_c, rows, 3 * group)
    )
    blocks = [
        shift(lax.dynamic_index_in_dim(qkv_groups, (c + k) % size_c, 0, False), k) if k
        else lax.dynamic_index_in_dim(qkv_groups, c, 0, False)
        for k in range(size_c)
    ]
    pieces = [(0, tuple(range(size_c)), jnp.stack(blocks))]
    for bit in reversed(range(bits_of("fsdp"))):
        pieces = pieces + [
            (offset ^ (1 << bit), places, flip(block, "fsdp", bit))
            for offset, places, block in pieces
        ]
    (qkv_mine,) = place(pieces, [3 * group])
    bias_pair = lax.dynamic_slice_in_dim(
        qv_bias.astype(F32), first_column + c * group, group, 1
    )
    bias_mine = jnp.concatenate([bias_pair[0], jnp.zeros((group,), F32), bias_pair[1]])

    tokens_all = []
    for item in range(items):
        pairs = [latent[item]]
        for block in ring_gather(latent[item, :half])[1:]:
            pairs += [block, swap(block)]
        tokens_all.append(jnp.concatenate(pairs, 0))

    proj_t = proj_weight.T
    down_t = down_weight.T
    (proj_full,) = place(gather_pieces(proj_t), [half_width])
    up_full, down_full = place(
        gather_pieces(jnp.concatenate([up_weight, down_t], 1)), [hidden, hidden]
    )
    (qkv_full,) = place(
        gather_pieces(qkv_groups.transpose(1, 0, 2).reshape(rows, -1)), [3 * half_width]
    )

    bias_proj = proj_bias.astype(F32)
    bias_down = down_bias.astype(F32)
    bias_up = lax.dynamic_slice_in_dim(up_bias.astype(F32), t * hidden, hidden, 0)
    block = min(256, here * size_c)

    saved = []
    outputs = []
    for item in range(items):
        in_first = (
            normalize(tokens_all[item].astype(F32))[0] * (1.0 + scale_one[item])
            + shift_one[item]
        ).astype(BF16)
        qkv = (dot(in_first, qkv_mine, ((1,), (0,))) + bias_mine).astype(BF16)
        keys = qkv[:, group : 2 * group]
        values = qkv[:, 2 * group :]
        qkv_t = qkv.T.reshape(3, group, -1)
        mixed_t, logs = attend(qkv_t, keys, block)
        sent = [
            shift(mixed_t[:, k * here : (k + 1) * here], -k) if k else mixed_t[:, :here]
            for k in range(size_c)
        ]
        mixed = absolute(sent, c, 1).reshape(half_width, here)
        part = dot(mixed, proj_full, ((0,), (1,)))
        attended = part[:half] + swap(part[half:].astype(BF16)).astype(F32) + bias_proj
        residual = latent[item, :half].astype(F32) + gate_one[item] * attended
        normed, inverse = normalize(residual)
        in_second_half = (normed * (1.0 + scale_two[item]) + shift_two[item]).astype(BF16)
        in_second = jnp.concatenate([in_second_half, swap(in_second_half)], 0)
        saved.append(
            dict(
                in_first=in_first,
                keys=keys,
                values=values,
                qkv_t=qkv_t,
                logs=logs,
                mixed=mixed,
                attended=attended,
                residual=residual,
                normed=normed,
                inverse=inverse,
                in_second=in_second,
            )
        )

    for item, kept in enumerate(saved):
        upward = dot(kept["in_second"], up_full, ((1,), (0,))) + bias_up
        grad_feed = (cotangent[item].astype(F32) * gate_two[item]).astype(BF16)
        grad_act = dot(grad_feed, down_full, ((1,), (0,)))
        activated, pull = jax.vjp(partial(jax.nn.gelu, approximate=True), upward)
        activated = activated.astype(BF16)
        grad_upward = pull(grad_act)[0].astype(BF16)
        part = dot(grad_upward, up_full, ((1,), (1,)))
        kept["grad_in_second"] = part[:half] + swap(part[half:].astype(BF16)).astype(F32)
        part = dot(activated, down_full, ((1,), (1,)))
        kept["feed_out"] = (
            part[:half] + swap(part[half:].astype(BF16)).astype(F32) + bias_down
        )
        out_half = (kept["residual"] + gate_two[item] * kept["feed_out"]).astype(BF16)
        outputs.append(both(out_half, swap(out_half), 0))
        kept.update(activated=activated, grad_upward=grad_upward, grad_feed=grad_feed)

    input_grads = []
    mod_terms = []
    for item, kept in enumerate(saved):
        cot = cotangent[item, :half].astype(F32)
        grad_in_second = kept["grad_in_second"]
        grad_residual = cot + norm_back(
            grad_in_second * (1.0 + scale_two[item]), kept["normed"], kept["inverse"]
        )
        grad_attended_half = (grad_residual * gate_one[item]).astype(BF16)
        grad_attended = jnp.concatenate([grad_attended_half, swap(grad_attended_half)], 0)
        grad_mixed = (
            dot(proj_full, grad_attended, ((0,), (1,)))
            .astype(BF16)
            .reshape(size_c, group, here)
        )
        grad_mixed = [
            shift(lax.dynamic_index_in_dim(grad_mixed, (c + k) % size_c, 0, False), k) if k
            else lax.dynamic_index_in_dim(grad_mixed, c, 0, False)
            for k in range(size_c)
        ]
        grad_qkv = attend_back(
            kept["qkv_t"],
            kept["keys"],
            kept["values"],
            jnp.concatenate(grad_mixed, 1),
            kept["logs"],
            block,
        ).reshape(3 * group, -1)
        sent = [
            shift(grad_qkv[:, k * here : (k + 1) * here], -k) if k else grad_qkv[:, :here]
            for k in range(size_c)
        ]
        grad_here = absolute(sent, c, 1).reshape(3 * half_width, here)
        part = dot(grad_here, qkv_full, ((0,), (1,)))
        grad_in_first = part[:half] + swap(part[half:].astype(BF16)).astype(F32)
        normed_one, inverse_one = normalize(latent[item, :half].astype(F32))
        grad_latent = grad_residual + norm_back(
            grad_in_first * (1.0 + scale_one[item]), normed_one, inverse_one
        )
        input_grads.append(both(grad_latent, swap(grad_latent), 0))
        mod_terms.append(
            jnp.stack(
                [
                    jnp.sum(grad_in_first, 0),
                    jnp.sum(grad_in_first * normed_one, 0),
                    jnp.sum(grad_residual * kept["attended"], 0),
                    jnp.sum(grad_in_second, 0),
                    jnp.sum(grad_in_second * kept["normed"], 0),
                    jnp.sum(cot * kept["feed_out"], 0),
                ]
            )
        )
        kept.update(grad_attended=grad_attended, grad_qkv=grad_qkv)

    def rows_of(name):
        return jnp.concatenate([kept[name] for kept in saved], 0)

    def columns_of(name):
        return jnp.concatenate([kept[name] for kept in saved], 1)

    grad_feed = rows_of("grad_feed")
    grad_upward = rows_of("grad_upward")
    grad_attended = rows_of("grad_attended")
    grad_qkv = columns_of("grad_qkv")
    by_rows = ((0,), (0,))
    grad_down = ring_reduce(reduce_rows(grad_feed, rows_of("activated"), by_rows)).T
    grad_up = ring_reduce(reduce_rows(rows_of("in_second"), grad_upward, by_rows))
    grad_proj = ring_reduce(reduce_rows(grad_attended, columns_of("mixed"), ((0,), (1,)))).T
    qkv_rows = reduce_rows(rows_of("in_first"), grad_qkv, ((0,), (1,)))
    sent = [
        shift(lax.dynamic_index_in_dim(qkv_rows, (c + k) % size_c, 0, False), k) if k
        else lax.dynamic_index_in_dim(qkv_rows, c, 0, False)
        for k in range(size_c)
    ]
    grad_qkv_weight = (
        absolute(sent, c, -1)
        .reshape(size_c, rows, 3, group)
        .transpose(1, 2, 0, 3)
        .reshape(rows, 3, half_width)
    )

    own_rows = [kept["grad_attended"][:half] for kept in saved]
    proj_sum = sum(jnp.sum(piece.astype(F32), 0) for piece in own_rows)
    down_sum = sum(jnp.sum(kept["grad_feed"][:half].astype(F32), 0) for kept in saved)
    up_sum = jnp.sum(grad_upward.astype(F32), 0)
    qkv_sum = jnp.sum(grad_qkv.astype(F32), 1).reshape(3, group)
    pair_sum = jnp.stack([qkv_sum[0], qkv_sum[2]])
    up_total = lax.dynamic_update_slice_in_dim(
        jnp.zeros(up_bias.shape, F32), up_sum, t * hidden, 0
    )
    pair_total = lax.dynamic_update_slice_in_dim(
        jnp.zeros(qv_bias.shape, F32), pair_sum, first_column + c * group, 1
    )
    sums = jnp.concatenate([up_total, pair_total.reshape(-1), proj_sum, down_sum])
    sums = sums.reshape(-1, 128)
    for axis in ("fsdp", "ctx", "tp"):
        sums = butterfly_sum(sums, axis)
    sums = sums.reshape(-1)
    ends = [up_bias.shape[0], up_bias.shape[0] + qv_bias.size]
    grad_up_bias = sums[: ends[0]]
    grad_qv_bias = sums[ends[0] : ends[1]].reshape(qv_bias.shape)
    grad_proj_bias = sums[ends[1] : ends[1] + model]
    grad_down_bias = sums[ends[1] + model :]

    grad_mod = jnp.stack(mod_terms)
    grad_mod = butterfly_sum(butterfly_sum(grad_mod, "tp"), "ctx").astype(BF16)
    grad_mod_all = cube_gather(grad_mod)
    grad_ada_bias = jnp.sum(
        absolute_xor(grad_mod_all, f).astype(F32), (0, 1)
    )
    mod_here = lax.dynamic_slice_in_dim(grad_mod_all, first_column, half_width, 3).reshape(
        size_f * items, -1
    )
    grad_ada = dot(silu_here, mod_here, ((0,), (0,))).reshape(rows, 6, half_width)
    cond_part = dot(mod_here, ada_weight.reshape(rows, -1), ((1,), (1,)))
    cond_part = lax.dynamic_update_slice_in_dim(
        jnp.zeros((size_f * items, model), F32), cond_part, first_row, 1
    ).reshape(size_f, items, model)
    cond_total = butterfly_sum(butterfly_sum(cube_reduce(cond_part), "ctx"), "tp")
    grad_cond = jax.vjp(jax.nn.silu, cond)[1](cond_total)[0]

    return (
        jnp.stack(outputs).reshape(latents.shape),
        jnp.stack(input_grads).reshape(latents.shape),
        grad_cond.reshape(condition.shape),
        grad_ada,
        grad_ada_bias,
        grad_qkv_weight,
        grad_qv_bias,
        grad_proj,
        grad_proj_bias,
        grad_up,
        grad_up_bias,
        grad_down,
        grad_down_bias,
    )


def absolute_xor(entries, rank):
    size = entries.shape[0]
    for bit in range(size.bit_length() - 1):
        pairs = entries.reshape(-1, 2, 1 << bit, *entries.shape[1:])
        turned = jnp.flip(pairs, 1)
        entries = jnp.where((rank >> bit) % 2 == 0, pairs, turned).reshape(entries.shape)
    return entries


def solution(mesh):
    in_specs = (
        P(None, "fsdp", "ctx", None),
        P(None, "fsdp", None),
        P(None, "fsdp", "ctx", None),
        P(("fsdp", "ctx"), None, "tp"),
        P(),
        P(("fsdp", "ctx"), None, "tp"),
        P(),
        P("tp", ("fsdp", "ctx")),
        P(),
        P(("fsdp", "ctx"), "tp"),
        P(),
        P("tp", ("fsdp", "ctx")),
        P(),
    )
    out_specs = (
        P(None, "fsdp", "ctx", None),
        P(None, "fsdp", "ctx", None),
        P(None, "fsdp", None),
        P(("fsdp", "ctx"), None, "tp"),
        P(),
        P(("fsdp", "ctx"), None, "tp"),
        P(),
        P("tp", ("fsdp", "ctx")),
        P(),
        P(("fsdp", "ctx"), "tp"),
        P(),
        P("tp", ("fsdp", "ctx")),
        P(),
    )
    return jax.shard_map(body, mesh=mesh, in_specs=in_specs, out_specs=out_specs, check_vma=False)
```

time: 1830 us -> 919 us (0.50)
  waiting for transfers between devices: 1350 us -> 249 us
  starting transfers between devices: 2.63 us -> 174 us
  local copies, waits for them, and re-layouts: 56 us -> 208 us
  matrix products: 198 us -> 82.9 us
  blocking collectives: 86.6 us -> 0 us
  Pallas kernels: 0 us -> 75.3 us
    reduce_scatter x7 -> x0, waiting for transfers between devices: 674 us -> none  [the longest x3 194 us: body(): lax.psum_scatter(key_terms, 'ctx', scatter_dimension=1, tiled=True)]
    all_gather x11 -> x0, waiting for transfers between devices: 366 us -> none  [the longest x1 75.7 us: gather_weights(): lax.all_gather(shard_tuple[0], ('fsdp', 'ctx'), axis=0, tiled=True)]
    psum x3 -> x0, waiting for transfers between devices: 305 us -> none  [the longest x1 121 us: body(): feed_out = lax.psum(feed_part, 'tp') + bias_down]
    ppermute x0 -> x162, waiting for transfers between devices: none -> 249 us  [the longest x102 148 us: flip(): return lax.ppermute(x, axis, [(i, i ^ 1 << bit) for i in range(size)])]
    ppermute x0 -> x162, starting transfers between devices: none -> 174 us  [the longest x60 95 us: shift(): return lax.ppermute(x, 'ctx', [(i, (i + k) % size) for i in range(size)])]
    dot_general x60 -> x35, matrix products: 198 us -> 82.9 us  [dot(): return lax.dot_general(a, b, (dims, ((), ())), preferred_element_type=F32)]
    pallas_call x0 -> x10, Pallas kernels: none -> 75.3 us  [the longest x3 28.7 us: attend_back(): pl.pallas_call(partial(attend_back_kernel, heads), grid=(tokens // block,...]
    psum x3 -> x0, blocking collectives: 73 us -> none  [the longest x1 43.5 us: body(): bias_done = lax.psum(bias_totals, ('fsdp', 'ctx', 'tp'))]
  transfers between devices with their start and end apart: 22 -> 162, of which waited for: 20 -> 55; matrix products, arithmetic and copies ran while one was open for 15% -> 40% of each run, Pallas kernels for 0% -> 7%
where the time goes in v1:
time: 919 us; the launch traced here: 906 us
  waiting for transfers between devices  249 us (27%)
  local copies, waits for them, and re-layouts  208 us (23%)
  starting transfers between devices  174 us (19%)
  other arithmetic  112 us (12%)
  matrix products  82.9 us (9%)
  Pallas kernels  75.3 us (8%)
    ppermute x102, waiting for transfers between devices, flip(): return lax.ppermute(x, axis, [(i, i ^ 1 << bit) for i in range(size)])  148 us
    ppermute x60, waiting for transfers between devices, shift(): return lax.ppermute(x, 'ctx', [(i, (i + k) % size) for i in range(size)])  101 us
    ppermute x60, starting transfers between devices, shift(): return lax.ppermute(x, 'ctx', [(i, (i + k) % size) for i in range(size)])  95 us
    dot_general x35, matrix products, dot(): return lax.dot_general(a, b, (dims, ((), ())), preferred_element_type=F32)  82.9 us
    unnamed x584, local copies, waits for them, and re-layouts  80.5 us
    ppermute x102, starting transfers between devices, flip(): return lax.ppermute(x, axis, [(i, i ^ 1 << bit) for i in range(size)])  79 us
    pallas_call x3, Pallas kernels, attend_back(): pl.pallas_call(partial(attend_back_kernel, heads), grid=(tokens // block,...  28.7 us
    pallas_call x4, Pallas kernels, place(): pl.pallas_call(partial(place_kernel, [piece[:2] for piece in pieces], wid...  25.6 us
  transfers between devices with their start and end apart: 162, of which 55 were waited for; matrix products, arithmetic and copies ran while one was open for 40% of the time, Pallas kernels for 7%

profile of v1, /device:TPU:0, one launch (start us, length us, event | category | flops | bytes accessed | tf_op | source)
XLA Modules:
  0.0 905.6 jit_solution(11062869279983570845)
XLA Ops:
  0.6 3.1 collective-permute-start.22
  25.8 4.1 fusion.125
  39.6 3.3 collective-permute-done.2
  60.6 3.7 collective-permute-start.15
  78.1 3.8 collective-permute-start.7
  93.9 3.5 collective-permute-start.60
  108.3 5.8 collective-permute-done.73
  141.9 4.2 shard_map.230
  146.1 3.3 collective-permute-start.92
  149.4 3.4 shard_map.228
  208.2 7.0 shard_map.232
  216.0 3.8 collective-permute-start.62
  228.5 3.2 add_convert_fusion.5
  238.9 7.0 shard_map.229
  257.6 3.2 add_convert_fusion.3
  285.3 7.1 shard_map.233
  321.5 3.2 collective-permute-done.78
  335.1 3.0 collective-permute-start.41
  344.2 11.4 %collective-permute-done.39 = bf16[72,4608]{1,0:T(8,128)(2,1)S(1)} collective-permute-done((bf16[72,4608]{1,0:T(8,128)(2,1)S(1)}, bf16[72,4608]{1,0:T(8,128)(2,1)S(1)}, u32[]{:S(2)}, u32[]{:S(2)}) %collective-permute-start.39) | collective-permute-done | bytes 663584 | tf_op jit(solution)/shard_map/ppermute | solution.py:37
  357.1 11.9 %collective-permute-done.41 = bf16[72,4608]{1,0:T(8,128)(2,1)S(1)} collective-permute-done((bf16[72,4608]{1,0:T(8,128)(2,1)S(1)}, bf16[72,4608]{1,0:T(8,128)(2,1)S(1)}, u32[]{:S(2)}, u32[]{:S(2)}) %collective-permute-start.41) | collective-permute-done | bytes 663584 | tf_op jit(solution)/shard_map/ppermute | solution.py:37
  374.9 13.5 %collective-permute-done.40 = bf16[72,4608]{1,0:T(8,128)(2,1)} collective-permute-done((bf16[72,4608]{1,0:T(8,128)(2,1)S(1)}, bf16[72,4608]{1,0:T(8,128)(2,1)}, u32[]{:S(2)}, u32[]{:S(2)}) %collective-permute-start.40) | collective-permute-done | bytes 663584 | tf_op jit(solution)/shard_map/ppermute | solution.py:37
  391.0 3.2 broadcast_select_fusion.1
  394.2 10.6 %shard_map.235 = bf16[4,4,72,1728]{3,2,1,0:T(8,128)(2,1)S(1)} custom-call(bf16[1,72,1728]{2,1,0:T(8,128)(2,1)S(1)} %copy-done.4, bf16[1,72,1728]{2,1,0:T(8,128)(2,1)} %bitcast.82.refs_1_, bf16[1,72,1728]{2,1,0:T(8,128)(2,1)S(1)} %bitcast.536, bf16[1,72,1728]{2,1,0:T(8,128)(2,1)} %bitcast.85.refs_3_, ...), custom_call_target="tpu_custom_call" | custom-call | bytes 7962624 | tf_op jit(solution)/shard_map/pallas_call | solution.py:146
  408.7 9.6 %collective-permute-done.44.refs_6_ = bf16[1,72,4608]{2,1,0:T(8,128)(2,1)} collective-permute-done((bf16[1,72,4608]{2,1,0:T(8,128)(2,1)}, bf16[1,72,4608]{2,1,0:T(8,128)(2,1)}, u32[]{:S(2)}, u32[]{:S(2)}) %collective-permute-start.44) | collective-permute-done | bytes 663584 | tf_op jit(solution)/shard_map/ppermute | solution.py:42
  420.2 3.8 copy.134
  426.7 7.5 shard_map.231
  434.3 4.7 multiply_convert_fusion
  450.9 3.6 fusion.31
  462.0 3.2 fusion.24
  466.9 4.6 fusion.224
  471.5 4.6 fusion.63
  492.4 4.0 collective-permute-done.82
  510.8 20.0 %collective-permute-done.83 = bf16[128,1152]{1,0:T(8,128)(2,1)S(1)} collective-permute-done((bf16[128,1152]{1,0:T(8,128)(2,1)S(1)}, bf16[128,1152]{1,0:T(8,128)(2,1)S(1)}, u32[]{:S(2)}, u32[]{:S(2)}) %collective-permute-start.83) | collective-permute-done | bytes 294944 | tf_op jit(solution)/shard_map/ppermute | solution.py:42
  531.5 3.3 collective-permute-start.86
  544.0 9.5 %shard_map.234 = bf16[3,144,1024]{2,1,0:T(8,128)(2,1)S(1)} custom-call(bf16[3,144,1024]{2,1,0:T(8,128)(2,1)S(1)} %bitcast.526, bf16[1024,144]{1,0:T(8,128)(2,1)S(1)} %copy-done.25, bf16[3,144,1024]{2,1,0:T(8,128)(2,1)S(1)} %bitcast.527, bf16[1024,144]{1,0:T(8,128)(2,1)S(1)} %copy-done.23, bf16[144,1024]{1,0:T(8,128)(2,1)S(1)} %pad_maximum_fusion.20.do_ref, ...), custom_call_target="tpu_custom_call" | custom-call | flops 8388608000 | bytes 2359296 | tf_op jit(solution)/shard_map/pallas_call | solution.py:296
  564.6 6.6 collective-permute-start.110
  578.7 9.7 %shard_map.236 = bf16[3,144,1024]{2,1,0:T(8,128)(2,1)S(1)} custom-call(bf16[3,144,1024]{2,1,0:T(8,128)(2,1)S(1)} %bitcast.522, bf16[1024,144]{1,0:T(8,128)(2,1)S(1)} %copy-done.22, bf16[3,144,1024]{2,1,0:T(8,128)(2,1)S(1)} %bitcast.523, bf16[1024,144]{1,0:T(8,128)(2,1)S(1)} %copy-done.20, bf16[144,1024]{1,0:T(8,128)(2,1)S(1)} %pad_maximum_fusion.21.do_ref, ...), custom_call_target="tpu_custom_call" | custom-call | flops 8388608000 | bytes 2359296 | tf_op jit(solution)/shard_map/pallas_call | solution.py:296
  588.5 4.4 collective-permute-start.112
  594.1 2.9 collective-permute-done.112
  598.0 3.1 collective-permute-done.114
  601.1 6.1 collective-permute-done.113
  612.1 3.9 copy.133
  627.6 9.5 %shard_map.237 = bf16[3,144,1024]{2,1,0:T(8,128)(2,1)S(1)} custom-call(bf16[3,144,1024]{2,1,0:T(8,128)(2,1)S(1)} %bitcast.518, bf16[1024,144]{1,0:T(8,128)(2,1)S(1)} %copy-done.19, bf16[3,144,1024]{2,1,0:T(8,128)(2,1)S(1)} %bitcast.519, bf16[1024,144]{1,0:T(8,128)(2,1)S(1)} %copy-done.17, bf16[144,1024]{1,0:T(8,128)(2,1)S(1)} %pad_maximum_fusion.22.do_ref, ...), custom_call_target="tpu_custom_call" | custom-call | flops 8388608000 | bytes 2359296 | tf_op jit(solution)/shard_map/pallas_call | solution.py:296
  654.5 13.9 %collective-permute-done.145 = f32[72,128]{1,0:T(8,128)S(1)} collective-permute-done((f32[72,128]{1,0:T(8,128)S(1)}, f32[72,128]{1,0:T(8,128)S(1)}, u32[]{:S(2)}, u32[]{:S(2)}) %collective-permute-start.145) | collective-permute-done | bytes 36896 | tf_op jit(solution)/shard_map/ppermute | solution.py:42
  671.9 3.7 fusion.259
  677.5 3.2 fusion.223
  686.0 3.5 fusion.90
  695.4 3.1 collective-permute-done.127
  710.4 3.9 collective-permute-done.129
  736.4 3.3 fusion.95
  751.0 5.1 collective-permute-done.136
  759.4 5.6 convolution_add_fusion.6
  768.6 4.0 collective-permute-done.126
  775.5 8.6 collective-permute-done.106
  796.4 5.5 collective-permute-done.140
  809.5 6.0 convolution_add_fusion
  817.3 4.6 convolution_add_fusion.1
  824.2 23.5 %collective-permute-done.158 = bf16[1,288,2304]{2,1,0:T(8,128)(2,1)S(1)} collective-permute-done((bf16[1,288,2304]{2,1,0:T(8,128)(2,1)S(1)}, bf16[1,288,2304]{2,1,0:T(8,128)(2,1)S(1)}, u32[]{:S(2)}, u32[]{:S(2)}) %collective-permute-start.158) | collective-permute-done | bytes 1327136 | tf_op jit(solution)/shard_map/ppermute | solution.py:42
  848.1 3.8 collective-permute-start.161
  851.9 21.7 %collective-permute-done.153 = bf16[1,288,2304]{2,1,0:T(8,128)(2,1)S(1)} collective-permute-done((bf16[1,288,2304]{2,1,0:T(8,128)(2,1)S(1)}, bf16[1,288,2304]{2,1,0:T(8,128)(2,1)S(1)}, u32[]{:S(2)}, u32[]{:S(2)}) %collective-permute-start.153) | collective-permute-done | bytes 1327136 | tf_op jit(solution)/shard_map/ppermute | solution.py:42
  874.2 3.6 collective-permute-start.156
  878.0 8.6 collective-permute-done.154
  886.6 4.5 collective-permute-start.155
  891.2 9.6 %collective-permute-done.160 = bf16[72,2304]{1,0:T(8,128)(2,1)S(1)} collective-permute-done((bf16[72,2304]{1,0:T(8,128)(2,1)S(1)}, bf16[72,2304]{1,0:T(8,128)(2,1)S(1)}, u32[]{:S(2)}, u32[]{:S(2)}) %collective-permute-start.160) | collective-permute-done | bytes 331808 | tf_op jit(solution)/shard_map/ppermute | solution.py:37
  (1184 shorter events, 500.9 us)
Async XLA Ops:
  0.6 68.2 %collective-permute-start.22 = (bf16[72,576]{1,0:T(8,128)(2,1)}, bf16[72,576]{1,0:T(8,128)(2,1)S(1)}, u32[]{:S(2)}, u32[]{:S(2)}) collective-permute-start(bf16[72,576]{1,0:T(8,128)(2,1)} %bitcast.537), channel_id=1, source_target_pairs={{0,2},{2,4},{4,6},{6,0},{1,3},{3,5},{5,7},{7,1},{8,10},{10,12},{12... | collective-permute-start | bytes 248840 | tf_op jit(solution)/shard_map/ppermute | solution.py:37
  3.7 73.5 %collective-permute-start.24 = (bf16[72,576]{1,0:T(8,128)(2,1)}, bf16[72,576]{1,0:T(8,128)(2,1)S(1)}, u32[]{:S(2)}, u32[]{:S(2)}) collective-permute-start(bf16[72,576]{1,0:T(8,128)(2,1)} %bitcast.538), channel_id=1, source_target_pairs={{0,6},{2,0},{4,2},{6,4},{1,7},{3,1},{5,3},{7,5},{8,14},{10,8},{12,... | collective-permute-start | bytes 248840 | tf_op jit(solution)/shard_map/ppermute | solution.py:37
  6.5 25.5 %collective-permute-start = (bf16[1,3,1152]{2,1,0:T(4,128)(2,1)S(1)}, bf16[1,3,1152]{2,1,0:T(4,128)(2,1)S(1)}, u32[]{:S(2)}, u32[]{:S(2)}) collective-permute-start(bf16[1,3,1152]{2,1,0:T(4,128)(2,1)S(1)} %fusion.193), channel_id=1, source_target_pairs={{0,8},{8,0},{16,24},{24,16},{1,9},{9,1},{17,25},{25,17},{2,10},{10... | collective-permute-start | bytes 20744 | tf_op jit(solution)/shard_map/ppermute | solution.py:42
  9.7 54.7 %collective-permute-start.13 = (bf16[72,432]{1,0:T(8,128)(2,1)}, bf16[72,432]{1,0:T(8,128)(2,1)S(1)}, u32[]{:S(2)}, u32[]{:S(2)}) collective-permute-start(bf16[72,432]{1,0:T(8,128)(2,1)} %bitcast.8), channel_id=1, source_target_pairs={{0,2},{2,4},{4,6},{6,0},{1,3},{3,5},{5,7},{7,1},{8,10},{10,12},{12... | collective-permute-start | bytes 186632 | tf_op jit(solution)/shard_map/ppermute | solution.py:37
  10.5 54.1 %collective-permute-start.14 = (bf16[72,432]{1,0:T(8,128)(2,1)}, bf16[72,432]{1,0:T(8,128)(2,1)}, u32[]{:S(2)}, u32[]{:S(2)}) collective-permute-start(bf16[72,432]{1,0:T(8,128)(2,1)} %bitcast.10), channel_id=1, source_target_pairs={{0,4},{2,6},{4,0},{6,2},{1,5},{3,7},{5,1},{7,3},{8,12},{10,14},{12... | collective-permute-start | bytes 186632 | tf_op jit(solution)/shard_map/ppermute | solution.py:37
  68.8 23.4 %collective-permute-start.56 = (bf16[128,1152]{1,0:T(8,128)(2,1)}, bf16[128,1152]{1,0:T(8,128)(2,1)}, u32[]{:S(2)}, u32[]{:S(2)}) collective-permute-start(bf16[128,1152]{1,0:T(8,128)(2,1)} %get-tuple-element.220), channel_id=1, source_target_pairs={{0,2},{2,4},{4,6},{6,0},{1,3},{3,5},{5,7},{7,1},{8,10},{10,12},{12... | collective-permute-start | bytes 884744 | tf_op jit(solution)/shard_map/ppermute | solution.py:37
  78.1 20.1 %collective-permute-start.7 = (bf16[128,1152]{1,0:T(8,128)(2,1)}, bf16[128,1152]{1,0:T(8,128)(2,1)S(1)}, u32[]{:S(2)}, u32[]{:S(2)}) collective-permute-start(bf16[128,1152]{1,0:T(8,128)(2,1)} %get-tuple-element.222), channel_id=1, source_target_pairs={{0,2},{2,4},{4,6},{6,0},{1,3},{3,5},{5,7},{7,1},{8,10},{10,12},{12... | collective-permute-start | bytes 884744 | tf_op jit(solution)/shard_map/ppermute | solution.py:37
  99.5 21.7 %collective-permute-start.11 = (bf16[128,1152]{1,0:T(8,128)(2,1)}, bf16[128,1152]{1,0:T(8,128)(2,1)S(1)}, u32[]{:S(2)}, u32[]{:S(2)}) collective-permute-start(bf16[128,1152]{1,0:T(8,128)(2,1)} %get-tuple-element.222), channel_id=1, source_target_pairs={{0,6},{2,0},{4,2},{6,4},{1,7},{3,1},{5,3},{7,5},{8,14},{10,8},{12,... | collective-permute-start | bytes 884744 | tf_op jit(solution)/shard_map/ppermute | solution.py:37
  101.9 21.6 %collective-permute-start.17 = (bf16[4,72,432]{2,1,0:T(8,128)(2,1)S(1)}, bf16[4,72,432]{2,1,0:T(8,128)(2,1)S(1)}, u32[]{:S(2)}, u32[]{:S(2)}) collective-permute-start(bf16[4,72,432]{2,1,0:T(8,128)(2,1)S(1)} %pad_maximum_fusion.16.refs_0_), channel_id=1, source_target_pairs={{0,8},{8,0},{16,24},{24,16},{1,9},{9,1},{17,25},{25,17},{2,10},{10... | collective-permute-start | bytes 746504 | tf_op jit(solution)/shard_map/ppermute | solution.py:42
  107.7 46.1 %collective-permute-start.71 = (bf16[128,1152]{1,0:T(8,128)(2,1)}, bf16[128,1152]{1,0:T(8,128)(2,1)}, u32[]{:S(2)}, u32[]{:S(2)}) collective-permute-start(bf16[128,1152]{1,0:T(8,128)(2,1)} %copy-done.141), channel_id=1, source_target_pairs={{0,2},{2,4},{4,6},{6,0},{1,3},{3,5},{5,7},{7,1},{8,10},{10,12},{12... | collective-permute-start | bytes 884744 | tf_op jit(solution)/shard_map/ppermute | solution.py:37
  114.0 41.0 %collective-permute-start.70 = (bf16[128,1152]{1,0:T(8,128)(2,1)}, bf16[128,1152]{1,0:T(8,128)(2,1)}, u32[]{:S(2)}, u32[]{:S(2)}) collective-permute-start(bf16[128,1152]{1,0:T(8,128)(2,1)} %copy-done.141), channel_id=1, source_target_pairs={{0,1},{1,0},{2,3},{3,2},{4,5},{5,4},{6,7},{7,6},{8,9},{9,8},{10,11... | collective-permute-start | bytes 884744 | tf_op jit(solution)/shard_map/ppermute | solution.py:42
  115.7 30.4 %collective-permute-start.18 = (bf16[4,72,432]{2,1,0:T(8,128)(2,1)S(1)}, bf16[4,72,432]{2,1,0:T(8,128)(2,1)S(1)}, u32[]{:S(2)}, u32[]{:S(2)}) collective-permute-start(bf16[4,72,432]{2,1,0:T(8,128)(2,1)S(1)} %collective-permute-done.16.refs_1_), channel_id=1, source_target_pairs={{0,8},{8,0},{16,24},{24,16},{1,9},{9,1},{17,25},{25,17},{2,10},{10... | collective-permute-start | bytes 746504 | tf_op jit(solution)/shard_map/ppermute | solution.py:42
  123.5 35.5 %collective-permute-start.9 = (bf16[128,1152]{1,0:T(8,128)(2,1)}, bf16[128,1152]{1,0:T(8,128)(2,1)}, u32[]{:S(2)}, u32[]{:S(2)}) collective-permute-start(bf16[128,1152]{1,0:T(8,128)(2,1)} %copy-done.139), channel_id=1, source_target_pairs={{0,2},{2,4},{4,6},{6,0},{1,3},{3,5},{5,7},{7,1},{8,10},{10,12},{12... | collective-permute-start | bytes 884744 | tf_op jit(solution)/shard_map/ppermute | solution.py:37
  124.2 36.8 %collective-permute-start.8 = (bf16[128,1152]{1,0:T(8,128)(2,1)}, bf16[128,1152]{1,0:T(8,128)(2,1)}, u32[]{:S(2)}, u32[]{:S(2)}) collective-permute-start(bf16[128,1152]{1,0:T(8,128)(2,1)} %copy-done.139), channel_id=1, source_target_pairs={{0,1},{1,0},{2,3},{3,2},{4,5},{5,4},{6,7},{7,6},{8,9},{9,8},{10,11... | collective-permute-start | bytes 884744 | tf_op jit(solution)/shard_map/ppermute | solution.py:42
  146.1 169.3 %collective-permute-start.92 = (bf16[72,1728]{1,0:T(8,128)(2,1)}, bf16[72,1728]{1,0:T(8,128)(2,1)}, u32[]{:S(2)}, u32[]{:S(2)}) collective-permute-start(bf16[72,1728]{1,0:T(8,128)(2,1)} %copy.145), channel_id=1, source_target_pairs={{0,6},{2,0},{4,2},{6,4},{1,7},{3,1},{5,3},{7,5},{8,14},{10,8},{12,... | collective-permute-start | bytes 746504 | tf_op jit(solution)/shard_map/ppermute | solution.py:37
  159.0 24.4 %collective-permute-start.61 = (bf16[128,1152]{1,0:T(8,128)(2,1)}, bf16[128,1152]{1,0:T(8,128)(2,1)}, u32[]{:S(2)}, u32[]{:S(2)}) collective-permute-start(bf16[128,1152]{1,0:T(8,128)(2,1)} %copy-done.137), channel_id=1, source_target_pairs={{0,1},{1,0},{2,3},{3,2},{4,5},{5,4},{6,7},{7,6},{8,9},{9,8},{10,11... | collective-permute-start | bytes 884744 | tf_op jit(solution)/shard_map/ppermute | solution.py:42
  161.0 24.3 %collective-permute-start.74 = (bf16[128,1152]{1,0:T(8,128)(2,1)}, bf16[128,1152]{1,0:T(8,128)(2,1)S(1)}, u32[]{:S(2)}, u32[]{:S(2)}) collective-permute-start(bf16[128,1152]{1,0:T(8,128)(2,1)} %copy-done.132), channel_id=1, source_target_pairs={{0,1},{1,0},{2,3},{3,2},{4,5},{5,4},{6,7},{7,6},{8,9},{9,8},{10,11... | collective-permute-start | bytes 884744 | tf_op jit(solution)/shard_map/ppermute | solution.py:42
  166.6 20.4 %collective-permute-start.12 = (bf16[128,1152]{1,0:T(8,128)(2,1)S(1)}, bf16[128,1152]{1,0:T(8,128)(2,1)}, u32[]{:S(2)}, u32[]{:S(2)}) collective-permute-start(bf16[128,1152]{1,0:T(8,128)(2,1)S(1)} %copy-done.135), channel_id=1, source_target_pairs={{0,1},{1,0},{2,3},{3,2},{4,5},{5,4},{6,7},{7,6},{8,9},{9,8},{10,11... | collective-permute-start | bytes 884744 | tf_op jit(solution)/shard_map/ppermute | solution.py:42
  167.4 24.3 %collective-permute-start.59 = (bf16[128,1152]{1,0:T(8,128)(2,1)}, bf16[128,1152]{1,0:T(8,128)(2,1)S(1)}, u32[]{:S(2)}, u32[]{:S(2)}) collective-permute-start(bf16[128,1152]{1,0:T(8,128)(2,1)} %collective-permute-done.58), channel_id=1, source_target_pairs={{0,1},{1,0},{2,3},{3,2},{4,5},{5,4},{6,7},{7,6},{8,9},{9,8},{10,11... | collective-permute-start | bytes 884744 | tf_op jit(solution)/shard_map/ppermute | solution.py:42
  183.4 144.8 %collective-permute-start.90 = (bf16[72,1728]{1,0:T(8,128)(2,1)}, bf16[72,1728]{1,0:T(8,128)(2,1)}, u32[]{:S(2)}, u32[]{:S(2)}) collective-permute-start(bf16[72,1728]{1,0:T(8,128)(2,1)} %copy.145), channel_id=1, source_target_pairs={{0,2},{2,4},{4,6},{6,0},{1,3},{3,5},{5,7},{7,1},{8,10},{10,12},{12... | collective-permute-start | bytes 746504 | tf_op jit(solution)/shard_map/ppermute | solution.py:37
  185.3 61.4 %collective-permute-start.72 = (bf16[128,1152]{1,0:T(8,128)(2,1)}, bf16[128,1152]{1,0:T(8,128)(2,1)}, u32[]{:S(2)}, u32[]{:S(2)}) collective-permute-start(bf16[128,1152]{1,0:T(8,128)(2,1)} %collective-permute-done.71), channel_id=1, source_target_pairs={{0,1},{1,0},{2,3},{3,2},{4,5},{5,4},{6,7},{7,6},{8,9},{9,8},{10,11... | collective-permute-start | bytes 884744 | tf_op jit(solution)/shard_map/ppermute | solution.py:42
  187.0 32.8 %collective-permute-start.10 = (bf16[128,1152]{1,0:T(8,128)(2,1)}, bf16[128,1152]{1,0:T(8,128)(2,1)}, u32[]{:S(2)}, u32[]{:S(2)}) collective-permute-start(bf16[128,1152]{1,0:T(8,128)(2,1)} %collective-permute-done.9), channel_id=1, source_target_pairs={{0,1},{1,0},{2,3},{3,2},{4,5},{5,4},{6,7},{7,6},{8,9},{9,8},{10,11... | collective-permute-start | bytes 884744 | tf_op jit(solution)/shard_map/ppermute | solution.py:42
  216.0 80.8 %collective-permute-start.62 = (bf16[144,256]{1,0:T(8,128)(2,1)}, bf16[144,256]{1,0:T(8,128)(2,1)}, u32[]{:S(2)}, u32[]{:S(2)}) collective-permute-start(bf16[144,256]{1,0:T(8,128)(2,1)} %get-tuple-element.258), channel_id=1, source_target_pairs={{0,6},{2,0},{4,2},{6,4},{1,7},{3,1},{5,3},{7,5},{8,14},{10,8},{12,... | collective-permute-start | bytes 221192 | tf_op jit(solution)/shard_map/ppermute | solution.py:37
  219.8 78.3 %collective-permute-start.64 = (bf16[144,256]{1,0:T(8,128)(2,1)}, bf16[144,256]{1,0:T(8,128)(2,1)}, u32[]{:S(2)}, u32[]{:S(2)}) collective-permute-start(bf16[144,256]{1,0:T(8,128)(2,1)} %get-tuple-element.259), channel_id=1, source_target_pairs={{0,2},{2,4},{4,6},{6,0},{1,3},{3,5},{5,7},{7,1},{8,10},{10,12},{12... | collective-permute-start | bytes 221192 | tf_op jit(solution)/shard_map/ppermute | solution.py:37
  246.7 52.1 %collective-permute-start.63 = (bf16[144,256]{1,0:T(8,128)(2,1)}, bf16[144,256]{1,0:T(8,128)(2,1)}, u32[]{:S(2)}, u32[]{:S(2)}) collective-permute-start(bf16[144,256]{1,0:T(8,128)(2,1)} %get-tuple-element.260), channel_id=1, source_target_pairs={{0,4},{2,6},{4,0},{6,2},{1,5},{3,7},{5,1},{7,3},{8,12},{10,14},{12... | collective-permute-start | bytes 221192 | tf_op jit(solution)/shard_map/ppermute | solution.py:37
  333.1 22.5 %collective-permute-start.39 = (bf16[72,4608]{1,0:T(8,128)(2,1)S(1)}, bf16[72,4608]{1,0:T(8,128)(2,1)S(1)}, u32[]{:S(2)}, u32[]{:S(2)}) collective-permute-start(bf16[72,4608]{1,0:T(8,128)(2,1)S(1)} %copy-done.160), channel_id=1, source_target_pairs={{0,2},{2,4},{4,6},{6,0},{1,3},{3,5},{5,7},{7,1},{8,10},{10,12},{12... | collective-permute-start | bytes 1990664 | tf_op jit(solution)/shard_map/ppermute | solution.py:37
  335.1 33.9 %collective-permute-start.41 = (bf16[72,4608]{1,0:T(8,128)(2,1)S(1)}, bf16[72,4608]{1,0:T(8,128)(2,1)S(1)}, u32[]{:S(2)}, u32[]{:S(2)}) collective-permute-start(bf16[72,4608]{1,0:T(8,128)(2,1)S(1)} %copy-done.160), channel_id=1, source_target_pairs={{0,6},{2,0},{4,2},{6,4},{1,7},{3,1},{5,3},{7,5},{8,14},{10,8},{12,... | collective-permute-start | bytes 1990664 | tf_op jit(solution)/shard_map/ppermute | solution.py:37
  338.8 30.2 %collective-permute-start.46 = (bf16[1,72,4608]{2,1,0:T(8,128)(2,1)S(1)}, bf16[1,72,4608]{2,1,0:T(8,128)(2,1)S(1)}, u32[]{:S(2)}, u32[]{:S(2)}) collective-permute-start(bf16[1,72,4608]{2,1,0:T(8,128)(2,1)S(1)} %get-tuple-element.226.refs_0_), channel_id=1, source_target_pairs={{0,8},{8,0},{16,24},{24,16},{1,9},{9,1},{17,25},{25,17},{2,10},{10... | collective-permute-start | bytes 1990664 | tf_op jit(solution)/shard_map/ppermute | solution.py:42
  338.8 32.1 %collective-permute-start.42 = (bf16[1,72,4608]{2,1,0:T(8,128)(2,1)S(1)}, bf16[1,72,4608]{2,1,0:T(8,128)(2,1)}, u32[]{:S(2)}, u32[]{:S(2)}) collective-permute-start(bf16[1,72,4608]{2,1,0:T(8,128)(2,1)S(1)} %get-tuple-element.226.refs_0_), channel_id=1, source_target_pairs={{0,16},{8,24},{16,0},{24,8},{1,17},{9,25},{17,1},{25,9},{2,18},{10... | collective-permute-start | bytes 1990664 | tf_op jit(solution)/shard_map/ppermute | solution.py:42
  343.0 26.6 %collective-permute-start.66 = (bf16[128,1152]{1,0:T(8,128)(2,1)S(1)}, bf16[128,1152]{1,0:T(8,128)(2,1)S(1)}, u32[]{:S(2)}, u32[]{:S(2)}) collective-permute-start(bf16[128,1152]{1,0:T(8,128)(2,1)S(1)} %get-tuple-element.124), channel_id=1, source_target_pairs={{0,1},{1,0},{2,3},{3,2},{4,5},{5,4},{6,7},{7,6},{8,9},{9,8},{10,11... | collective-permute-start | bytes 884744 | tf_op jit(solution)/shard_map/ppermute | solution.py:42
  369.1 20.9 %collective-permute-start.47 = (bf16[1,72,4608]{2,1,0:T(8,128)(2,1)S(1)}, bf16[1,72,4608]{2,1,0:T(8,128)(2,1)S(1)}, u32[]{:S(2)}, u32[]{:S(2)}) collective-permute-start(bf16[1,72,4608]{2,1,0:T(8,128)(2,1)S(1)} %bitcast.528), channel_id=1, source_target_pairs={{0,8},{8,0},{16,24},{24,16},{1,9},{9,1},{17,25},{25,17},{2,10},{10... | collective-permute-start | bytes 1990664 | tf_op jit(solution)/shard_map/ppermute | solution.py:42
  369.6 18.8 %collective-permute-start.40 = (bf16[72,4608]{1,0:T(8,128)(2,1)S(1)}, bf16[72,4608]{1,0:T(8,128)(2,1)}, u32[]{:S(2)}, u32[]{:S(2)}) collective-permute-start(bf16[72,4608]{1,0:T(8,128)(2,1)S(1)} %collective-permute-done.39), channel_id=1, source_target_pairs={{0,2},{2,4},{4,6},{6,0},{1,3},{3,5},{5,7},{7,1},{8,10},{10,12},{12... | collective-permute-start | bytes 1990664 | tf_op jit(solution)/shard_map/ppermute | solution.py:37
  372.8 34.5 %collective-permute-start.43 = (bf16[1,72,4608]{2,1,0:T(8,128)(2,1)S(1)}, bf16[1,72,4608]{2,1,0:T(8,128)(2,1)}, u32[]{:S(2)}, u32[]{:S(2)}) collective-permute-start(bf16[1,72,4608]{2,1,0:T(8,128)(2,1)S(1)} %bitcast.529), channel_id=1, source_target_pairs={{0,16},{8,24},{16,0},{24,8},{1,17},{9,25},{17,1},{25,9},{2,18},{10... | collective-permute-start | bytes 1990664 | tf_op jit(solution)/shard_map/ppermute | solution.py:42
  374.4 33.0 %collective-permute-start.49 = (bf16[1,72,4608]{2,1,0:T(8,128)(2,1)S(1)}, bf16[1,72,4608]{2,1,0:T(8,128)(2,1)S(1)}, u32[]{:S(2)}, u32[]{:S(2)}) collective-permute-start(bf16[1,72,4608]{2,1,0:T(8,128)(2,1)S(1)} %bitcast.531), channel_id=1, source_target_pairs={{0,8},{8,0},{16,24},{24,16},{1,9},{9,1},{17,25},{25,17},{2,10},{10... | collective-permute-start | bytes 1990664 | tf_op jit(solution)/shard_map/ppermute | solution.py:42
  374.4 34.3 %collective-permute-start.45 = (bf16[1,72,4608]{2,1,0:T(8,128)(2,1)S(1)}, bf16[1,72,4608]{2,1,0:T(8,128)(2,1)}, u32[]{:S(2)}, u32[]{:S(2)}) collective-permute-start(bf16[1,72,4608]{2,1,0:T(8,128)(2,1)S(1)} %bitcast.532), channel_id=1, source_target_pairs={{0,16},{8,24},{16,0},{24,8},{1,17},{9,25},{17,1},{25,9},{2,18},{10... | collective-permute-start | bytes 1990664 | tf_op jit(solution)/shard_map/ppermute | solution.py:42
  388.4 29.9 %collective-permute-start.44 = (bf16[1,72,4608]{2,1,0:T(8,128)(2,1)}, bf16[1,72,4608]{2,1,0:T(8,128)(2,1)}, u32[]{:S(2)}, u32[]{:S(2)}) collective-permute-start(bf16[1,72,4608]{2,1,0:T(8,128)(2,1)} %bitcast.34.refs_2_), channel_id=1, source_target_pairs={{0,16},{8,24},{16,0},{24,8},{1,17},{9,25},{17,1},{25,9},{2,18},{10... | collective-permute-start | bytes 1990664 | tf_op jit(solution)/shard_map/ppermute | solution.py:42
  389.9 28.4 %collective-permute-start.79 = (bf16[128,1152]{1,0:T(8,128)(2,1)S(1)}, bf16[128,1152]{1,0:T(8,128)(2,1)S(1)}, u32[]{:S(2)}, u32[]{:S(2)}) collective-permute-start(bf16[128,1152]{1,0:T(8,128)(2,1)S(1)} %get-tuple-element.122), channel_id=1, source_target_pairs={{0,1},{1,0},{2,3},{3,2},{4,5},{5,4},{6,7},{7,6},{8,9},{9,8},{10,11... | collective-permute-start | bytes 884744 | tf_op jit(solution)/shard_map/ppermute | solution.py:42
  407.3 19.3 %collective-permute-start.50 = (bf16[1,72,4608]{2,1,0:T(8,128)(2,1)}, bf16[1,72,4608]{2,1,0:T(8,128)(2,1)}, u32[]{:S(2)}, u32[]{:S(2)}) collective-permute-start(bf16[1,72,4608]{2,1,0:T(8,128)(2,1)} %collective-permute-done.42.refs_4_), channel_id=1, source_target_pairs={{0,8},{8,0},{16,24},{24,16},{1,9},{9,1},{17,25},{25,17},{2,10},{10... | collective-permute-start | bytes 1990664 | tf_op jit(solution)/shard_map/ppermute | solution.py:42
  444.2 41.5 %collective-permute-start.117 = (bf16[128,1152]{1,0:T(8,128)(2,1)}, bf16[128,1152]{1,0:T(8,128)(2,1)}, u32[]{:S(2)}, u32[]{:S(2)}) collective-permute-start(bf16[128,1152]{1,0:T(8,128)(2,1)} %slice.979), channel_id=1, source_target_pairs={{0,1},{1,0},{2,3},{3,2},{4,5},{5,4},{6,7},{7,6},{8,9},{9,8},{10,11... | collective-permute-start | bytes 884744 | tf_op jit(solution)/shard_map/ppermute | solution.py:42
  447.8 50.8 %collective-permute-start.80 = (bf16[128,1152]{1,0:T(8,128)(2,1)}, bf16[128,1152]{1,0:T(8,128)(2,1)}, u32[]{:S(2)}, u32[]{:S(2)}) collective-permute-start(bf16[128,1152]{1,0:T(8,128)(2,1)} %slice.984), channel_id=1, source_target_pairs={{0,1},{1,0},{2,3},{3,2},{4,5},{5,4},{6,7},{7,6},{8,9},{9,8},{10,11... | collective-permute-start | bytes 884744 | tf_op jit(solution)/shard_map/ppermute | solution.py:42
  457.1 32.6 %collective-permute-start.107 = (bf16[128,1152]{1,0:T(8,128)(2,1)}, bf16[128,1152]{1,0:T(8,128)(2,1)}, u32[]{:S(2)}, u32[]{:S(2)}) collective-permute-start(bf16[128,1152]{1,0:T(8,128)(2,1)} %slice.981), channel_id=1, source_target_pairs={{0,1},{1,0},{2,3},{3,2},{4,5},{5,4},{6,7},{7,6},{8,9},{9,8},{10,11... | collective-permute-start | bytes 884744 | tf_op jit(solution)/shard_map/ppermute | solution.py:42
  479.9 18.7 %collective-permute-start.67 = (bf16[128,1152]{1,0:T(8,128)(2,1)}, bf16[128,1152]{1,0:T(8,128)(2,1)}, u32[]{:S(2)}, u32[]{:S(2)}) collective-permute-start(bf16[128,1152]{1,0:T(8,128)(2,1)} %slice.986), channel_id=1, source_target_pairs={{0,1},{1,0},{2,3},{3,2},{4,5},{5,4},{6,7},{7,6},{8,9},{9,8},{10,11... | collective-permute-start | bytes 884744 | tf_op jit(solution)/shard_map/ppermute | solution.py:42
  489.7 319.7 %collective-permute-start.157 = (f32[576,2304]{1,0:T(8,128)}, f32[576,2304]{1,0:T(8,128)}, u32[]{:S(2)}, u32[]{:S(2)}) collective-permute-start(f32[576,2304]{1,0:T(8,128)} %fusion.63), channel_id=1, source_target_pairs={{0,8},{8,0},{16,24},{24,16},{1,9},{9,1},{17,25},{25,17},{2,10},{10... | collective-permute-start | bytes 15925256 | tf_op jit(solution)/shard_map/ppermute | solution.py:42
  504.6 33.0 %collective-permute-start.68 = (bf16[128,1152]{1,0:T(8,128)(2,1)S(1)}, bf16[128,1152]{1,0:T(8,128)(2,1)S(1)}, u32[]{:S(2)}, u32[]{:S(2)}) collective-permute-start(bf16[128,1152]{1,0:T(8,128)(2,1)S(1)} %get-tuple-element.185), channel_id=1, source_target_pairs={{0,1},{1,0},{2,3},{3,2},{4,5},{5,4},{6,7},{7,6},{8,9},{9,8},{10,11... | collective-permute-start | bytes 884744 | tf_op jit(solution)/shard_map/ppermute | solution.py:42
  505.6 32.1 %collective-permute-start.81 = (bf16[128,1152]{1,0:T(8,128)(2,1)S(1)}, bf16[128,1152]{1,0:T(8,128)(2,1)S(1)}, u32[]{:S(2)}, u32[]{:S(2)}) collective-permute-start(bf16[128,1152]{1,0:T(8,128)(2,1)S(1)} %get-tuple-element.186), channel_id=1, source_target_pairs={{0,1},{1,0},{2,3},{3,2},{4,5},{5,4},{6,7},{7,6},{8,9},{9,8},{10,11... | collective-permute-start | bytes 884744 | tf_op jit(solution)/shard_map/ppermute | solution.py:42
  506.6 32.9 %collective-permute-start.55 = (bf16[128,1152]{1,0:T(8,128)(2,1)S(1)}, bf16[128,1152]{1,0:T(8,128)(2,1)S(1)}, u32[]{:S(2)}, u32[]{:S(2)}) collective-permute-start(bf16[128,1152]{1,0:T(8,128)(2,1)S(1)} %get-tuple-element.187), channel_id=1, source_target_pairs={{0,1},{1,0},{2,3},{3,2},{4,5},{5,4},{6,7},{7,6},{8,9},{9,8},{10,11... | collective-permute-start | bytes 884744 | tf_op jit(solution)/shard_map/ppermute | solution.py:42
  509.6 21.1 %collective-permute-start.83 = (bf16[128,1152]{1,0:T(8,128)(2,1)S(1)}, bf16[128,1152]{1,0:T(8,128)(2,1)S(1)}, u32[]{:S(2)}, u32[]{:S(2)}) collective-permute-start(bf16[128,1152]{1,0:T(8,128)(2,1)S(1)} %get-tuple-element.134), channel_id=1, source_target_pairs={{0,1},{1,0},{2,3},{3,2},{4,5},{5,4},{6,7},{7,6},{8,9},{9,8},{10,11... | collective-permute-start | bytes 884744 | tf_op jit(solution)/shard_map/ppermute | solution.py:42
  555.7 19.1 %collective-permute-start.88 = (bf16[432,256]{1,0:T(8,128)(2,1)S(1)}, bf16[432,256]{1,0:T(8,128)(2,1)S(1)}, u32[]{:S(2)}, u32[]{:S(2)}) collective-permute-start(bf16[432,256]{1,0:T(8,128)(2,1)S(1)} %get-tuple-element.213), channel_id=1, source_target_pairs={{0,4},{2,6},{4,0},{6,2},{1,5},{3,7},{5,1},{7,3},{8,12},{10,14},{12... | collective-permute-start | bytes 663560 | tf_op jit(solution)/shard_map/ppermute | solution.py:37
  574.8 35.8 %collective-permute-start.118 = (bf16[128,1152]{1,0:T(8,128)(2,1)S(1)}, bf16[128,1152]{1,0:T(8,128)(2,1)S(1)}, u32[]{:S(2)}, u32[]{:S(2)}) collective-permute-start(bf16[128,1152]{1,0:T(8,128)(2,1)S(1)} %get-tuple-element.128), channel_id=1, source_target_pairs={{0,1},{1,0},{2,3},{3,2},{4,5},{5,4},{6,7},{7,6},{8,9},{9,8},{10,11... | collective-permute-start | bytes 884744 | tf_op jit(solution)/shard_map/ppermute | solution.py:42
  597.0 27.1 %collective-permute-start.105 = (bf16[128,1152]{1,0:T(8,128)(2,1)}, bf16[128,1152]{1,0:T(8,128)(2,1)}, u32[]{:S(2)}, u32[]{:S(2)}) collective-permute-start(bf16[128,1152]{1,0:T(8,128)(2,1)} %slice.982), channel_id=1, source_target_pairs={{0,1},{1,0},{2,3},{3,2},{4,5},{5,4},{6,7},{7,6},{8,9},{9,8},{10,11... | collective-permute-start | bytes 884744 | tf_op jit(solution)/shard_map/ppermute | solution.py:42
  646.5 21.8 %collective-permute-start.122 = (bf16[432,256]{1,0:T(8,128)(2,1)}, bf16[432,256]{1,0:T(8,128)(2,1)S(1)}, u32[]{:S(2)}, u32[]{:S(2)}) collective-permute-start(bf16[432,256]{1,0:T(8,128)(2,1)} %get-tuple-element.208), channel_id=1, source_target_pairs={{0,6},{2,0},{4,2},{6,4},{1,7},{3,1},{5,3},{7,5},{8,14},{10,8},{12,... | collective-permute-start | bytes 663560 | tf_op jit(solution)/shard_map/ppermute | solution.py:37
  647.5 22.0 %collective-permute-start.124 = (bf16[432,256]{1,0:T(8,128)(2,1)}, bf16[432,256]{1,0:T(8,128)(2,1)S(1)}, u32[]{:S(2)}, u32[]{:S(2)}) collective-permute-start(bf16[432,256]{1,0:T(8,128)(2,1)} %get-tuple-element.209), channel_id=1, source_target_pairs={{0,2},{2,4},{4,6},{6,0},{1,3},{3,5},{5,7},{7,1},{8,10},{10,12},{12... | collective-permute-start | bytes 663560 | tf_op jit(solution)/shard_map/ppermute | solution.py:37
  648.9 21.5 %collective-permute-start.123 = (bf16[432,256]{1,0:T(8,128)(2,1)}, bf16[432,256]{1,0:T(8,128)(2,1)}, u32[]{:S(2)}, u32[]{:S(2)}) collective-permute-start(bf16[432,256]{1,0:T(8,128)(2,1)} %get-tuple-element.210), channel_id=1, source_target_pairs={{0,4},{2,6},{4,0},{6,2},{1,5},{3,7},{5,1},{7,3},{8,12},{10,14},{12... | collective-permute-start | bytes 663560 | tf_op jit(solution)/shard_map/ppermute | solution.py:37
  668.3 148.9 %collective-permute-start.152 = (f32[576,2304]{1,0:T(8,128)}, f32[576,2304]{1,0:T(8,128)}, u32[]{:S(2)}, u32[]{:S(2)}) collective-permute-start(f32[576,2304]{1,0:T(8,128)} %fusion.224), channel_id=1, source_target_pairs={{0,8},{8,0},{16,24},{24,16},{1,9},{9,1},{17,25},{25,17},{2,10},{10... | collective-permute-start | bytes 15925256 | tf_op jit(solution)/shard_map/ppermute | solution.py:42
  680.8 77.6 %collective-permute-start.137 = (f32[576,432]{0,1:T(8,128)}, f32[576,432]{0,1:T(8,128)}, u32[]{:S(2)}, u32[]{:S(2)}) collective-permute-start(f32[576,432]{0,1:T(8,128)} %fusion.223), channel_id=1, source_target_pairs={{0,8},{8,0},{16,24},{24,16},{1,9},{9,1},{17,25},{25,17},{2,10},{10... | collective-permute-start | bytes 2985992 | tf_op jit(solution)/shard_map/ppermute | solution.py:42
  739.7 27.0 %collective-permute-start.116 = (f32[128,1152]{1,0:T(8,128)}, f32[128,1152]{1,0:T(8,128)}, u32[]{:S(2)}, u32[]{:S(2)}) collective-permute-start(f32[128,1152]{1,0:T(8,128)} %get-tuple-element.203), channel_id=1, source_target_pairs={{0,1},{1,0},{2,3},{3,2},{4,5},{5,4},{6,7},{7,6},{8,9},{9,8},{10,11... | collective-permute-start | bytes 1769480 | tf_op jit(solution)/shard_map/ppermute | solution.py:42
  758.4 25.6 %collective-permute-start.106 = (f32[128,1152]{1,0:T(8,128)}, f32[128,1152]{1,0:T(8,128)}, u32[]{:S(2)}, u32[]{:S(2)}) collective-permute-start(f32[128,1152]{1,0:T(8,128)} %get-tuple-element.202), channel_id=1, source_target_pairs={{0,1},{1,0},{2,3},{3,2},{4,5},{5,4},{6,7},{7,6},{8,9},{9,8},{10,11... | collective-permute-start | bytes 1769480 | tf_op jit(solution)/shard_map/ppermute | solution.py:42
  766.8 23.9 %collective-permute-start.147 = (f32[576,576]{1,0:T(8,128)}, f32[576,576]{1,0:T(8,128)S(1)}, u32[]{:S(2)}, u32[]{:S(2)}) collective-permute-start(f32[576,576]{1,0:T(8,128)} %fusion.160), channel_id=1, source_target_pairs={{0,8},{8,0},{16,24},{24,16},{1,9},{9,1},{17,25},{25,17},{2,10},{10... | collective-permute-start | bytes 3981320 | tf_op jit(solution)/shard_map/ppermute | solution.py:42
  815.6 32.1 %collective-permute-start.158 = (bf16[1,288,2304]{2,1,0:T(8,128)(2,1)S(1)}, bf16[1,288,2304]{2,1,0:T(8,128)(2,1)S(1)}, u32[]{:S(2)}, u32[]{:S(2)}) collective-permute-start(bf16[1,288,2304]{2,1,0:T(8,128)(2,1)S(1)} %fusion.65), channel_id=1, source_target_pairs={{0,16},{8,24},{16,0},{24,8},{1,17},{9,25},{17,1},{25,9},{2,18},{10... | collective-permute-start | bytes 3981320 | tf_op jit(solution)/shard_map/ppermute | solution.py:42
  822.0 51.6 %collective-permute-start.153 = (bf16[1,288,2304]{2,1,0:T(8,128)(2,1)S(1)}, bf16[1,288,2304]{2,1,0:T(8,128)(2,1)S(1)}, u32[]{:S(2)}, u32[]{:S(2)}) collective-permute-start(bf16[1,288,2304]{2,1,0:T(8,128)(2,1)S(1)} %fusion.64), channel_id=1, source_target_pairs={{0,16},{8,24},{16,0},{24,8},{1,17},{9,25},{17,1},{25,9},{2,18},{10... | collective-permute-start | bytes 3981320 | tf_op jit(solution)/shard_map/ppermute | solution.py:42
  848.1 29.8 %collective-permute-start.159 = (bf16[72,2304]{1,0:T(8,128)(2,1)S(1)}, bf16[72,2304]{1,0:T(8,128)(2,1)S(1)}, u32[]{:S(2)}, u32[]{:S(2)}) collective-permute-start(bf16[72,2304]{1,0:T(8,128)(2,1)S(1)} %get-tuple-element.150), channel_id=1, source_target_pairs={{0,2},{2,4},{4,6},{6,0},{1,3},{3,5},{5,7},{7,1},{8,10},{10,12},{12... | collective-permute-start | bytes 995336 | tf_op jit(solution)/shard_map/ppermute | solution.py:37
  848.1 43.1 %collective-permute-start.161 = (bf16[72,2304]{1,0:T(8,128)(2,1)S(1)}, bf16[72,2304]{1,0:T(8,128)(2,1)S(1)}, u32[]{:S(2)}, u32[]{:S(2)}) collective-permute-start(bf16[72,2304]{1,0:T(8,128)(2,1)S(1)} %get-tuple-element.151), channel_id=1, source_target_pairs={{0,6},{2,0},{4,2},{6,4},{1,7},{3,1},{5,3},{7,5},{8,14},{10,8},{12,... | collective-permute-start | bytes 995336 | tf_op jit(solution)/shard_map/ppermute | solution.py:37
  874.2 27.5 %collective-permute-start.156 = (bf16[72,2304]{1,0:T(8,128)(2,1)S(1)}, bf16[72,2304]{1,0:T(8,128)(2,1)S(1)}, u32[]{:S(2)}, u32[]{:S(2)}) collective-permute-start(bf16[72,2304]{1,0:T(8,128)(2,1)S(1)} %get-tuple-element.153), channel_id=1, source_target_pairs={{0,6},{2,0},{4,2},{6,4},{1,7},{3,1},{5,3},{7,5},{8,14},{10,8},{12,... | collective-permute-start | bytes 995336 | tf_op jit(solution)/shard_map/ppermute | solution.py:37
  877.9 22.9 %collective-permute-start.160 = (bf16[72,2304]{1,0:T(8,128)(2,1)S(1)}, bf16[72,2304]{1,0:T(8,128)(2,1)S(1)}, u32[]{:S(2)}, u32[]{:S(2)}) collective-permute-start(bf16[72,2304]{1,0:T(8,128)(2,1)S(1)} %fusion.81), channel_id=1, source_target_pairs={{0,2},{2,4},{4,6},{6,0},{1,3},{3,5},{5,7},{7,1},{8,10},{10,12},{12... | collective-permute-start | bytes 995336 | tf_op jit(solution)/shard_map/ppermute | solution.py:37
  (370 other events, 3840.6 us)

commit v2 on v1

v2 whole, which is shorter than its diff:
```python
from functools import partial

import jax
import jax.numpy as jnp
from jax import lax
from jax.experimental import pallas as pl
from jax.experimental.pallas import tpu as pltpu
from jax.sharding import PartitionSpec as P

HEADS = 16
HEAD_DIM = 72
LOG2E = 1.4426950408889634
F32 = jnp.float32
BF16 = jnp.bfloat16


def dot(a, b, dims):
    return lax.dot_general(a, b, (dims, ((), ())), preferred_element_type=F32)


def normalize(values):
    centre = values - jnp.mean(values, -1, keepdims=True)
    inverse = lax.rsqrt(jnp.mean(centre * centre, -1, keepdims=True) + 1e-06)
    return (centre * inverse, inverse)


def norm_back(incoming, normed, inverse):
    return inverse * (
        incoming
        - jnp.mean(incoming, -1, keepdims=True)
        - normed * jnp.mean(incoming * normed, -1, keepdims=True)
    )


def shift(x, k, name="shift"):
    size = lax.axis_size("ctx")
    with jax.named_scope(name):
        return lax.ppermute(x, "ctx", [(i, (i + k) % size) for i in range(size)])


def flip(x, axis, bit, name="flip"):
    size = lax.axis_size(axis)
    with jax.named_scope(name):
        return lax.ppermute(x, axis, [(i, i ^ (1 << bit)) for i in range(size)])


def exchange(x, name):
    with jax.named_scope(name):
        return lax.all_to_all(x, "ctx", 0, 0)


def gather_rows(x, name):
    with jax.named_scope(name):
        return lax.all_gather(x, ("fsdp", "ctx"), tiled=True)


def bits_of(axis):
    return lax.axis_size(axis).bit_length() - 1


def ring_gather(x, name):
    size = lax.axis_size("ctx")
    blocks = [x] * size
    moving = x
    for step in range(1, size // 2 + 1):
        moving = shift(moving, 1, name + "_right")
        blocks[step] = moving
    moving = x
    for step in range(1, (size - 1) // 2 + 1):
        moving = shift(moving, -1, name + "_left")
        blocks[size - step] = moving
    return blocks


def butterfly_sum(x, axis, name):
    for bit in range(bits_of(axis)):
        x = x + flip(x, axis, bit, name)
    return x


def butterfly_max(x, axis, name):
    for bit in range(bits_of(axis)):
        x = jnp.maximum(x, flip(x, axis, bit, name))
    return x


def cube_gather(x, name):
    x = x[None]
    for bit in range(bits_of("fsdp")):
        x = jnp.concatenate([x, flip(x, "fsdp", bit, name)], 0)
    return x


def cube_reduce(x, name):
    for bit in reversed(range(bits_of("fsdp"))):
        half = x.shape[0] // 2
        x = x[:half] + flip(x[half:], "fsdp", bit, name)
    return x[0]


def spread(pieces, name):
    for bit in reversed(range(bits_of("fsdp"))):
        pieces = pieces + [
            (offset ^ (1 << bit), places, flip(block, "fsdp", bit, name + "_%d" % bit))
            for offset, places, block in pieces
        ]
    return pieces


def gather_stacked(shard, name):
    blocks = ring_gather(shard, name)
    return spread([(0, "before", jnp.stack(blocks))], name)


def place_kernel(targets, widths, *refs):
    count = len(targets)
    ins, outs = refs[:count], refs[-3 - len(widths) : -3]
    held, in_sem, out_sem = refs[-3:]
    own_f = lax.axis_index("fsdp")
    own_c = lax.axis_index("ctx")
    size_c = lax.axis_size("ctx")
    arriving, leaving = [], []
    for (offset, places), ref in zip(targets, ins):
        row = jnp.bitwise_xor(own_f, offset)
        for at in range(size_c):
            column = at if places == "own" else lax.rem(own_c + size_c - at, size_c)
            slot = len(arriving)
            arriving.append(pltpu.make_async_copy(ref.at[at], held.at[slot], in_sem.at[slot]))
            first = 0
            for width, out in zip(widths, outs):
                leaving.append(
                    pltpu.make_async_copy(
                        held.at[slot, :, pl.ds(first, width)],
                        out.at[row, column],
                        out_sem.at[len(leaving)],
                    )
                )
                first += width
    for copy in arriving:
        copy.start()
    each = len(widths)
    for slot, copy in enumerate(arriving):
        copy.wait()
        for out_copy in leaving[slot * each : (slot + 1) * each]:
            out_copy.start()
    for copy in leaving:
        copy.wait()


def place(pieces, widths, after=()):
    size_f, size_c = lax.axis_size("fsdp"), lax.axis_size("ctx")
    rows, total = pieces[0][2].shape[1:]
    count = size_f * size_c
    outs = pl.pallas_call(
        partial(place_kernel, [piece[:2] for piece in pieces], widths),
        out_shape=[jax.ShapeDtypeStruct((size_f, size_c, rows, width), BF16) for width in widths],
        in_specs=[ANYWHERE] * (len(pieces) + len(after)),
        out_specs=[ANYWHERE] * len(widths),
        scratch_shapes=[
            pltpu.VMEM((count, rows, total), BF16),
            pltpu.SemaphoreType.DMA((count,)),
            pltpu.SemaphoreType.DMA((count * len(widths),)),
        ],
        compiler_params=pltpu.CompilerParams(vmem_limit_bytes=40 << 20),
        cost_estimate=pl.CostEstimate(
            flops=0, bytes_accessed=4 * count * rows * total, transcendentals=0
        ),
    )(*[piece[2] for piece in pieces], *after)
    return [out.reshape(-1, width) for out, width in zip(outs, widths)]


def lower(x, scale):
    return x if scale is None else (x * scale).astype(jnp.float16)


def higher(x, scale):
    return x if scale is None else x.astype(F32) * (1.0 / scale)


def reduce_rows(send, keep, name, scale=None):
    size_c = lax.axis_size("ctx")
    own_f = lax.axis_index("fsdp")
    _, width, columns = keep.shape
    parts = [keep, flip(send, "fsdp", 0, name + "_0")]
    for bit in range(1, bits_of("fsdp")):
        own_bit = (own_f >> bit) % 2
        pairs = [part.reshape(-1, 2, width, columns) for part in parts]
        got = sum(lax.dynamic_index_in_dim(pair, 1 - own_bit, 1, False) for pair in pairs)
        got = flip(lower(got, scale), "fsdp", bit, name + "_%d" % bit)
        parts = [lax.dynamic_index_in_dim(pair, own_bit, 1, False) for pair in pairs]
        parts.append(higher(got, scale))
    return sum(parts).reshape(size_c, width // size_c, columns)


def ring_reduce(blocks, name, scale=None):
    size = lax.axis_size("ctx")
    own = lax.axis_index("ctx")

    def block(offset):
        return lax.dynamic_index_in_dim(blocks, (own + offset) % size, 0, False)

    total = block(0)
    for sign, reach in ((1, size // 2), (-1, (size - 1) // 2)):
        moving = None
        for distance in range(reach, 0, -1):
            term = block(sign * distance)
            if moving is not None:
                term = term + moving
            moving = higher(shift(lower(term, scale), sign, name + "_ring"), scale)
        if moving is not None:
            total = total + moving
    return total


def whole(shape):
    return pl.BlockSpec(tuple(shape), lambda *_: (0,) * len(shape))


def struct(shape, dtype):
    return jax.ShapeDtypeStruct(tuple(shape), dtype)


ANYWHERE = pl.BlockSpec(memory_space=pltpu.HBM)
PARAMS = pltpu.CompilerParams(vmem_limit_bytes=48 << 20)


def cost(flops, nbytes, exps=0):
    return pl.CostEstimate(flops=int(flops), bytes_accessed=int(nbytes), transcendentals=int(exps))


def mods_spec(mods, item):
    return pl.BlockSpec((None,) + mods.shape[1:], lambda *_: (item, 0, 0))


def largest(x):
    return jnp.full((8, 128), jnp.max(jnp.abs(x)), F32)


def slab_call(kernel, args, in_specs, helds, after=(), **options):
    taken = [held for held in helds if held is not None]
    count = len(args)
    more = len(taken) + len(after)

    def run(*refs):
        kernel(*refs[:count], *refs[count + more :])

    return pl.pallas_call(
        run,
        in_specs=in_specs + [ANYWHERE] * more,
        input_output_aliases={count + at: at for at in range(len(taken))},
        compiler_params=PARAMS,
        **options,
    )(*args, *taken, *after)


def halves_kernel(first, both_ref, own_ref, peer_ref):
    count, half, _ = own_ref.shape
    t = lax.axis_index("tp")
    for rank, out in ((t, own_ref), (1 - t, peer_ref)):
        rows = pl.ds(pl.multiple_of(rank * half, half), half)
        for at in range(count):
            out[at] = both_ref[first + at, rows, :]


def halves(x, first, count, after=()):
    items, here, model = x.shape
    shape = (count, here // 2, model)
    return slab_call(
        partial(halves_kernel, first),
        [x],
        [whole(x.shape)],
        [],
        after,
        grid=(1,),
        out_specs=[whole(shape)] * 2,
        out_shape=[struct(shape, x.dtype)] * 2,
        cost_estimate=cost(0, 4 * count * here * model),
    )


def wait_kernel(in_ref, out_ref):
    out_ref[...] = in_ref[...]


def once_after(x, after):
    return slab_call(
        wait_kernel,
        [x],
        [whole(x.shape)],
        [],
        after,
        grid=(1,),
        out_specs=whole(x.shape),
        out_shape=struct(x.shape, x.dtype),
        cost_estimate=cost(0, 4 * x.size),
    )


def project_kernel(count, *refs):
    pieces = refs[:count]
    mods_ref, weight_ref, bias_ref, in_ref, out_ref = refs[count:]
    for pair in range(count // 2):
        rows = jnp.concatenate([pieces[2 * pair][...], pieces[2 * pair + 1][...]], 0)
        here = rows.shape[0]
        normed, _ = normalize(rows.astype(F32))
        in_first = (normed * (1.0 + mods_ref[1:2, :]) + mods_ref[0:1, :]).astype(BF16)
        in_ref[pl.ds(pair * here, here), :] = in_first
        product = dot(weight_ref[...], in_first, ((1,), (1,))) + bias_ref[...]
        out_ref[:, pl.ds(pair * here, here)] = product.astype(BF16)


def project(pieces, place_in, mods, item, items, weight_t, bias, held, after=()):
    _, half, model = pieces[0].shape
    total = half * len(pieces)
    piece_spec = pl.BlockSpec((None, half, model), lambda i: (place_in, 0, 0))
    width = weight_t.shape[0]
    return slab_call(
        partial(project_kernel, len(pieces)),
        [*pieces, mods, weight_t, bias],
        [piece_spec] * len(pieces)
        + [mods_spec(mods, item), whole(weight_t.shape), whole(bias.shape)],
        [held],
        after,
        grid=(1,),
        out_specs=[
            pl.BlockSpec((total, model), lambda i: (item, 0)),
            whole((width, total)),
        ],
        out_shape=[struct((items * total, model), BF16), struct((width, total), BF16)],
        cost_estimate=cost(2 * total * model * width, 6 * total * model),
    )


def head_rows(values, head):
    values = values.astype(F32)
    row = lax.broadcasted_iota(jnp.int32, values.shape, 0)
    inside = (row >= head * HEAD_DIM) & (row < (head + 1) * HEAD_DIM)
    return jnp.where(inside, values, 0.0).astype(BF16), inside


def attend_kernel(heads, steps, q_ref, kt_ref, vt_ref, out_ref, log_ref, k_ref):
    step = pl.program_id(0)
    factor = HEAD_DIM ** (-0.5) * LOG2E

    @pl.when(step == 0)
    def _():
        k_ref[...] = kt_ref[...].T

    total = None
    for head in range(heads):
        q_head, inside = head_rows(q_ref[...], head)
        scores = dot(k_ref[...], q_head, ((1,), (0,)))
        highest = jnp.max(scores, 0, keepdims=True)
        exponent = jnp.exp2((scores - highest) * factor)
        summed = jnp.sum(exponent, 0, keepdims=True)
        chances = (exponent * (1.0 / summed)).astype(BF16)
        mixed = dot(vt_ref[...], chances, ((1,), (0,)))
        total = mixed if total is None else jnp.where(inside, mixed, total)
        log_ref[pl.ds(head, 1), :] = highest * factor + jnp.log2(summed)
    out_ref[lax.rem(lax.axis_index("ctx") + steps - step, steps)] = total.astype(BF16)


def attend(qkv_t, here, after=()):
    group, total = qkv_t.shape[0] // 3, qkv_t.shape[1]
    heads, steps = group // HEAD_DIM, total // here
    thirds = qkv_t.reshape(3, group, total)
    return slab_call(
        partial(attend_kernel, heads, steps),
        [thirds, thirds, thirds],
        [
            pl.BlockSpec((None, group, here), lambda i: (0, 0, i)),
            pl.BlockSpec((None, group, total), lambda i: (1, 0, 0)),
            pl.BlockSpec((None, group, total), lambda i: (2, 0, 0)),
        ],
        [],
        after,
        grid=(steps,),
        out_specs=[
            whole((steps, group, here)),
            pl.BlockSpec((heads, here), lambda i: (0, i)),
        ],
        out_shape=[struct((steps, group, here), BF16), struct((heads, total), F32)],
        scratch_shapes=[pltpu.VMEM((total, group), BF16)],
        cost_estimate=cost(heads * total * total * 1600, 8 * group * total, heads * total * total),
    )


def attend_back_kernel(
    heads,
    steps,
    q_ref,
    kt_ref,
    vt_ref,
    log_ref,
    grad_ref,
    all_ref,
    out_ref,
    k_ref,
    v_ref,
    dk_ref,
    dv_ref,
):
    step = pl.program_id(0)
    own_c = lax.axis_index("ctx")
    scaling = HEAD_DIM ** (-0.5)
    group, block = q_ref.shape

    @pl.when(step == 0)
    def _():
        dk_ref[...] = jnp.zeros_like(dk_ref)
        dv_ref[...] = jnp.zeros_like(dv_ref)
        k_ref[...] = kt_ref[...].T
        v_ref[...] = vt_ref[...].T

    grad = grad_ref[lax.rem(own_c + steps - step, steps)]
    grad_query = None
    for head in range(heads):
        q_head, inside = head_rows(q_ref[...], head)
        do_head, _ = head_rows(grad, head)
        scores = dot(k_ref[...], q_head, ((1,), (0,)))
        chances = jnp.exp2(scores * (scaling * LOG2E) - log_ref[pl.ds(head, 1), :])
        grad_chances = dot(v_ref[...], do_head, ((1,), (0,)))
        weighted = jnp.sum(chances * grad_chances, 0, keepdims=True)
        grad_scores = (chances * (grad_chances - weighted)).astype(BF16)
        term = dot(kt_ref[...], grad_scores, ((1,), (0,)))
        grad_query = term if grad_query is None else jnp.where(inside, term, grad_query)
        dk_ref[...] += dot(q_head, grad_scores, ((1,), (1,)))
        dv_ref[...] += dot(do_head, chances.astype(BF16), ((1,), (1,)))
    columns = pl.ds(pl.multiple_of(step * block, block), block)
    all_ref[0, :, columns] = (grad_query * scaling).astype(BF16)

    @pl.when(step == steps - 1)
    def _():
        all_ref[1] = (dk_ref[...] * scaling).astype(BF16)
        all_ref[2] = dv_ref[...].astype(BF16)
        for at in range(steps):
            out_ref[lax.rem(own_c + steps - at, steps)] = all_ref[
                :, :, at * block : (at + 1) * block
            ]


def attend_back(qkv_t, grads, logs, held, item, items, after=()):
    group, total = qkv_t.shape[0] // 3, qkv_t.shape[1]
    heads, steps = group // HEAD_DIM, grads.shape[0]
    here = total // steps
    thirds = qkv_t.reshape(3, group, total)
    return slab_call(
        partial(attend_back_kernel, heads, steps),
        [thirds, thirds, thirds, logs, grads],
        [
            pl.BlockSpec((None, group, here), lambda i: (0, 0, i)),
            pl.BlockSpec((None, group, total), lambda i: (1, 0, 0)),
            pl.BlockSpec((None, group, total), lambda i: (2, 0, 0)),
            pl.BlockSpec((heads, here), lambda i: (0, i)),
            whole(grads.shape),
        ],
        [held],
        after,
        grid=(steps,),
        out_specs=[
            pl.BlockSpec((3, group, total), lambda i: (0, 0, item)),
            whole((steps, 3, group, here)),
        ],
        out_shape=[
            struct((3, group, items * total), BF16),
            struct((steps, 3, group, here), BF16),
        ],
        scratch_shapes=[
            pltpu.VMEM((total, group), BF16),
            pltpu.VMEM((total, group), BF16),
            pltpu.VMEM((group, total), F32),
            pltpu.VMEM((group, total), F32),
        ],
        cost_estimate=cost(heads * total * total * 4000, 16 * group * total, heads * total * total),
    )


def back_to_rows_kernel(contract, keep, blocks_ref, weight_ref, *outs):
    own_ref, peer_ref = outs[-2:]
    rows = blocks_ref[...].reshape(-1, blocks_ref.shape[-1])
    if keep:
        outs[0][...] = rows
    total = dot(rows, weight_ref[...], ((0,), (contract,)))
    half = own_ref.shape[0]
    own_ref[...] = total[:half]
    peer_ref[...] = total[half:]


def back_to_rows(blocks, weight, contract, keep=False, held=None, item=0, items=1, after=()):
    here = blocks.shape[-1]
    features, model = weight.shape[contract], weight.shape[1 - contract]
    half = here // 2
    out_specs = [whole((half, model))] * 2
    out_shape = [struct((half, model), F32)] * 2
    if keep:
        out_specs = [pl.BlockSpec((features, here), lambda i: (0, item))] + out_specs
        out_shape = [struct((features, items * here), BF16)] + out_shape
    return slab_call(
        partial(back_to_rows_kernel, contract, keep),
        [blocks, weight],
        [whole(blocks.shape), whole(weight.shape)],
        [held],
        after,
        grid=(1,),
        out_specs=out_specs,
        out_shape=out_shape,
        cost_estimate=cost(
            2 * here * features * model, 2 * features * model + 8 * here * model
        ),
    )


def second_kernel(own_ref, peer_ref, bias_ref, latent_ref, mods_ref, att_ref, res_ref, in_ref):
    attended = own_ref[...] + peer_ref[...] + bias_ref[...]
    residual = latent_ref[...].astype(F32) + mods_ref[2:3, :] * attended
    normed, _ = normalize(residual)
    att_ref[...] = attended
    res_ref[...] = residual
    in_ref[...] = (normed * (1.0 + mods_ref[4:5, :]) + mods_ref[3:4, :]).astype(BF16)


def second(own, peer, bias, latent, place_in, mods, item, after=()):
    shape = own.shape
    return slab_call(
        second_kernel,
        [own, peer, bias, latent, mods],
        [
            whole(shape),
            whole(shape),
            whole(bias.shape),
            pl.BlockSpec((None,) + shape, lambda i: (place_in, 0, 0)),
            mods_spec(mods, item),
        ],
        [],
        after,
        grid=(1,),
        out_specs=[whole(shape)] * 3,
        out_shape=[struct(shape, F32), struct(shape, F32), struct(shape, BF16)],
        cost_estimate=cost(20 * own.size, 20 * own.size),
    )


def feed_kernel(
    steps,
    own_ref,
    peer_ref,
    cot_own,
    cot_peer,
    mods_ref,
    up_ref,
    down_ref,
    bias_ref,
    in_all,
    grad_all,
    act_ref,
    gup_ref,
    out_own,
    out_peer,
    gin_own,
    gin_peer,
    sum_ref,
    highs,
    in_ref,
    grad_ref,
    out_acc,
    gin_acc,
):
    step = pl.program_id(0)
    half = own_ref.shape[0]

    @pl.when(step == 0)
    def _():
        in_ref[:half, :] = own_ref[...]
        in_ref[half:, :] = peer_ref[...]
        in_all[...] = in_ref[...]
        gate = mods_ref[5:6, :]
        grad_ref[:half, :] = (cot_own[...].astype(F32) * gate).astype(BF16)
        grad_ref[half:, :] = (cot_peer[...].astype(F32) * gate).astype(BF16)
        grad_all[...] = grad_ref[...]
        highs[0] = largest(in_ref[...].astype(F32))
        highs[1] = largest(grad_ref[...].astype(F32))
        highs[2] = jnp.zeros((8, 128), F32)
        highs[3] = jnp.zeros((8, 128), F32)

    upward = dot(in_ref[...], up_ref[...], ((1,), (0,))) + bias_ref[...]
    grad_act = dot(grad_ref[...], down_ref[...], ((1,), (0,)))
    inner = 0.7978845608028654
    squared = upward * upward
    curve = jnp.tanh(inner * upward * (1.0 + 0.044715 * squared))
    activated = (0.5 * upward * (1.0 + curve)).astype(BF16)
    slope = 0.5 * (1.0 + curve) + (0.5 * inner) * upward * (1.0 - curve * curve) * (
        1.0 + (3.0 * 0.044715) * squared
    )
    grad_up = (slope * grad_act).astype(BF16)
    act_ref[...] = activated
    gup_ref[...] = grad_up
    wide = grad_up.astype(F32)
    sum_ref[...] = jnp.sum(wide, 0, keepdims=True)
    highs[2] = jnp.maximum(highs[2], largest(activated.astype(F32)))
    highs[3] = jnp.maximum(highs[3], largest(wide))
    out_term = dot(activated, down_ref[...], ((1,), (1,)))
    gin_term = dot(grad_up, up_ref[...], ((1,), (1,)))

    @pl.when(step == 0)
    def _():
        out_acc[...] = out_term
        gin_acc[...] = gin_term

    @pl.when(step > 0)
    def _():
        out_acc[...] += out_term
        gin_acc[...] += gin_term

    @pl.when(step == steps - 1)
    def _():
        out_own[...] = out_acc[:half, :]
        out_peer[...] = out_acc[half:, :].astype(BF16)
        gin_own[...] = gin_acc[:half, :]
        gin_peer[...] = gin_acc[half:, :]


def feed(own, peer, cots, mods, weights, bias, helds, item, items, after=()):
    half, model = own.shape
    here, hidden = 2 * half, weights.shape[1] // 2
    cot = pl.BlockSpec((None, half, model), lambda j: (item, 0, 0))
    tile = 768
    steps = hidden // tile
    rows = pl.BlockSpec((here, model), lambda j: (item, 0))
    slab = pl.BlockSpec((here, tile), lambda j: (item, j))
    return slab_call(
        partial(feed_kernel, steps),
        [own, peer, *cots, mods, weights, weights, bias],
        [whole(own.shape)] * 2
        + [cot] * 2
        + [
            mods_spec(mods, item),
            pl.BlockSpec((model, tile), lambda j: (0, j)),
            pl.BlockSpec((model, tile), lambda j: (0, j + steps)),
            pl.BlockSpec((1, tile), lambda j: (0, j)),
        ],
        helds,
        after,
        grid=(steps,),
        out_specs=[rows, rows, slab, slab]
        + [pl.BlockSpec((half, model), lambda j: (item, 0))] * 2
        + [whole(own.shape)] * 2
        + [pl.BlockSpec((1, tile), lambda j: (0, j)), whole((4, 8, 128))],
        out_shape=[
            struct((items * here, model), BF16),
            struct((items * here, model), BF16),
            struct((items * here, hidden), BF16),
            struct((items * here, hidden), BF16),
            struct((items * half, model), F32),
            struct((items * half, model), BF16),
            struct(own.shape, F32),
            struct(own.shape, F32),
            struct((1, hidden), F32),
            struct((4, 8, 128), F32),
        ],
        scratch_shapes=[
            pltpu.VMEM((here, model), BF16),
            pltpu.VMEM((here, model), BF16),
            pltpu.VMEM((here, model), F32),
            pltpu.VMEM((here, model), F32),
        ],
        cost_estimate=cost(8 * here * model * hidden, 4 * model * hidden + 4 * here * hidden),
    )


def finish_kernel(own_ref, peer_ref, bias_ref, res_ref, cot_ref, mods_ref, out_ref, sum_ref):
    feed_out = own_ref[...] + peer_ref[...].astype(F32) + bias_ref[...]
    out_ref[...] = (res_ref[...] + mods_ref[5:6, :] * feed_out).astype(BF16)
    sum_ref[...] = jnp.sum(cot_ref[...].astype(F32) * feed_out, 0, keepdims=True)


def finish(own, peer, bias, residual, cots, mods, held, item, after=()):
    items, half, model = cots.shape
    part = pl.BlockSpec((half, model), lambda i: (item, 0))
    return slab_call(
        finish_kernel,
        [own, peer, bias, residual, cots, mods],
        [
            part,
            part,
            whole(bias.shape),
            whole((half, model)),
            pl.BlockSpec((None, half, model), lambda i: (item, 0, 0)),
            mods_spec(mods, item),
        ],
        [held],
        after,
        grid=(1,),
        out_specs=[part, whole(bias.shape)],
        out_shape=[struct((items * half, model), BF16), struct(bias.shape, F32)],
        cost_estimate=cost(8 * half * model, 16 * half * model),
    )


def second_back_kernel(
    own_ref, peer_ref, res_ref, att_ref, cot_ref, mods_ref, grad_ref, low_ref, sum_ref
):
    incoming = own_ref[...] + peer_ref[...]
    normed, inverse = normalize(res_ref[...])
    grad = cot_ref[...].astype(F32) + norm_back(
        incoming * (1.0 + mods_ref[4:5, :]), normed, inverse
    )
    low = (grad * mods_ref[2:3, :]).astype(BF16)
    grad_ref[...] = grad
    low_ref[...] = low
    sum_ref[0:1, :] = jnp.sum(grad * att_ref[...], 0, keepdims=True)
    sum_ref[1:2, :] = jnp.sum(incoming, 0, keepdims=True)
    sum_ref[2:3, :] = jnp.sum(incoming * normed, 0, keepdims=True)
    sum_ref[3:4, :] = jnp.sum(low.astype(F32), 0, keepdims=True)


def second_back(own, peer, residual, attended, cots, mods, item, after=()):
    shape = own.shape
    return slab_call(
        second_back_kernel,
        [own, peer, residual, attended, cots, mods],
        [whole(shape)] * 4
        + [pl.BlockSpec((None,) + shape, lambda i: (item, 0, 0)), mods_spec(mods, item)],
        [],
        after,
        grid=(1,),
        out_specs=[whole(shape), whole(shape), whole((4, shape[1]))],
        out_shape=[struct(shape, F32), struct(shape, BF16), struct((4, shape[1]), F32)],
        cost_estimate=cost(30 * own.size, 24 * own.size),
    )


def grad_mixed_kernel(own_ref, peer_ref, weight_ref, all_ref, out_ref):
    rows = jnp.concatenate([own_ref[...], peer_ref[...]], 0)
    all_ref[...] = rows
    out_ref[...] = dot(weight_ref[...], rows, ((1,), (1,))).astype(BF16)


def grad_mixed_of(own, peer, weight, held, item, items, after=()):
    features, model = weight.shape
    here = 2 * own.shape[0]
    return slab_call(
        grad_mixed_kernel,
        [own, peer, weight],
        [whole(own.shape), whole(own.shape), whole(weight.shape)],
        [held],
        after,
        grid=(1,),
        out_specs=[
            pl.BlockSpec((here, model), lambda i: (item, 0)),
            whole((features, here)),
        ],
        out_shape=[struct((items * here, model), BF16), struct((features, here), BF16)],
        cost_estimate=cost(2 * here * features * model, 2 * features * model),
    )


def first_back_kernel(own_ref, peer_ref, latent_ref, res_ref, mods_ref, grad_ref, sum_ref):
    incoming = own_ref[...] + peer_ref[...]
    normed, inverse = normalize(latent_ref[...].astype(F32))
    grad_ref[...] = res_ref[...] + norm_back(
        incoming * (1.0 + mods_ref[1:2, :]), normed, inverse
    )
    sum_ref[0:1, :] = jnp.sum(incoming, 0, keepdims=True)
    sum_ref[1:2, :] = jnp.sum(incoming * normed, 0, keepdims=True)


def first_back(own, peer, latent, place_in, grad_residual, mods, item, after=()):
    shape = own.shape
    return slab_call(
        first_back_kernel,
        [own, peer, latent, grad_residual, mods],
        [
            whole(shape),
            whole(shape),
            pl.BlockSpec((None,) + shape, lambda i: (place_in, 0, 0)),
            whole(shape),
            mods_spec(mods, item),
        ],
        [],
        after,
        grid=(1,),
        out_specs=[whole(shape), whole((2, shape[1]))],
        out_shape=[struct(shape, F32), struct((2, shape[1]), F32)],
        cost_estimate=cost(30 * own.size, 20 * own.size),
    )


def split_rows(product_ref, send_ref, keep_ref):
    width = keep_ref.shape[1]
    core = lax.rem(lax.axis_index("fsdp"), 2)
    for high in range(keep_ref.shape[0]):
        theirs = pl.multiple_of((2 * high + 1 - core) * width, 8)
        mine = pl.multiple_of((2 * high + core) * width, 8)
        send_ref[high] = product_ref[pl.ds(theirs, width), :]
        keep_ref[high] = product_ref[pl.ds(mine, width), :]


def outer_kernel(right, left_ref, right_ref, send_ref, keep_ref, left_t, *product):
    @pl.when(pl.program_id(0) == 0)
    def _():
        left_t[...] = left_ref[...].T

    if product:
        product[0][...] = dot(left_t[...], right_ref[...], ((1,), (right,)))
        split_rows(product[0], send_ref, keep_ref)
        return
    width = keep_ref.shape[1]
    core = lax.rem(lax.axis_index("fsdp"), 2)
    for high in range(keep_ref.shape[0]):
        for out, which in ((send_ref, 1 - core), (keep_ref, core)):
            rows = pl.ds(pl.multiple_of((2 * high + which) * width, 8), width)
            out[high] = dot(left_t[rows, :], right_ref[...], ((1,), (right,)))


def outer(left, right, contract, tile, first, columns, helds, after=()):
    rows, model = left.shape
    size_f = lax.axis_size("fsdp")
    wide = right.shape[1 - contract]
    shape = (size_f // 2, model // size_f, columns)
    block = pl.BlockSpec(shape[:2] + (tile,), lambda j: (0, 0, j + first))
    right_spec = (
        pl.BlockSpec((rows, tile), lambda j: (0, j))
        if contract == 0
        else pl.BlockSpec((tile, rows), lambda j: (j, 0))
    )
    return slab_call(
        partial(outer_kernel, contract),
        [left, right],
        [whole(left.shape), right_spec],
        helds,
        after,
        grid=(wide // tile,),
        out_specs=[block] * 2,
        out_shape=[struct(shape, F32)] * 2,
        scratch_shapes=[pltpu.VMEM((model, rows), BF16)]
        + ([pltpu.VMEM((model, tile), F32)] if shape[1] % 16 else []),
        cost_estimate=cost(2 * rows * model * wide, 2 * rows * wide + 4 * model * wide),
    )


def long_outer_kernel(steps, left_ref, right_ref, send_ref, keep_ref, product):
    step = pl.program_id(0)
    term = dot(left_ref[...], right_ref[...], ((0,), (1,)))

    @pl.when(step == 0)
    def _():
        product[...] = term

    @pl.when(step > 0)
    def _():
        product[...] += term

    @pl.when(step == steps - 1)
    def _():
        split_rows(product, send_ref, keep_ref)


def long_outer(left, right, steps, after=()):
    rows, model = left.shape
    wide = right.shape[0]
    size_f = lax.axis_size("fsdp")
    shape = (size_f // 2, model // size_f, wide)
    return slab_call(
        partial(long_outer_kernel, steps),
        [left, right],
        [
            pl.BlockSpec((rows // steps, model), lambda j: (j, 0)),
            pl.BlockSpec((wide, rows // steps), lambda j: (0, j)),
        ],
        [],
        after,
        grid=(steps,),
        out_specs=[whole(shape)] * 2,
        out_shape=[struct(shape, F32)] * 2,
        scratch_shapes=[pltpu.VMEM((model, wide), F32)],
        cost_estimate=cost(2 * rows * model * wide, 2 * rows * (model + wide)),
    )


def order_kernel(count, *refs):
    out_ref = refs[-1]
    half = out_ref.shape[1] // 2
    items = out_ref.shape[0]
    t = lax.axis_index("tp")
    for rank, parts in ((t, refs[:count]), (1 - t, refs[count : 2 * count])):
        rows = pl.ds(pl.multiple_of(rank * half, half), half)
        for item in range(items):
            part = parts[0][item * half : (item + 1) * half, :] if count == 1 else parts[item][...]
            out_ref[item, rows, :] = part


def order(owns, peers, items, after=()):
    model = owns[0].shape[1]
    half = sum(own.shape[0] for own in owns) // items
    return slab_call(
        partial(order_kernel, len(owns)),
        [*owns, *peers],
        [whole(part.shape) for part in (*owns, *peers)],
        [],
        after,
        grid=(1,),
        out_specs=whole((items, 2 * half, model)),
        out_shape=struct((items, 2 * half, model), owns[0].dtype),
        cost_estimate=cost(0, 16 * items * half * model),
    )


def body(
    latents,
    condition,
    grad_out,
    ada_weight,
    ada_bias,
    qkv_weight,
    qv_bias,
    proj_weight,
    proj_bias,
    up_weight,
    up_bias,
    down_weight,
    down_bias,
):
    t = lax.axis_index("tp")
    c = lax.axis_index("ctx")
    f = lax.axis_index("fsdp")
    size_c = lax.axis_size("ctx")
    size_f = lax.axis_size("fsdp")
    micro, batch, here, model = latents.shape
    items = micro * batch
    half = here // 2
    half_width = qkv_weight.shape[2]
    group = half_width // size_c
    hidden = up_weight.shape[1]
    rows = qkv_weight.shape[0]
    first_column = t * half_width

    def swap(x, name):
        return flip(x, "tp", 0, name)

    def both(own, peer, axis):
        return jnp.where(
            t == 0,
            jnp.concatenate([own, peer], axis),
            jnp.concatenate([peer, own], axis),
        )

    qkv_groups = (
        qkv_weight.reshape(rows, 3, size_c, group)
        .transpose(2, 0, 1, 3)
        .reshape(size_c, rows, 3 * group)
    )
    qkv_came = exchange(qkv_groups, "qkv_c")

    flat_latents = latents.reshape(items, here, model)

    def swapped_ring(first, count, after=()):
        own, peer = halves(flat_latents, first, count, after)
        pairs = [own, peer]
        for piece in ring_gather(own, "latent%d" % first)[1:]:
            pairs += [piece, swap(piece, "latent%d_t" % first)]
        return pairs

    rings = [swapped_ring(0, 1)]

    cond = condition.reshape(items, model).astype(F32)
    silu_all = cube_gather(jax.nn.silu(cond).astype(BF16), "cond")
    first_row = (f * size_c + c) * rows
    silu_here = lax.dynamic_slice_in_dim(silu_all, first_row, rows, 2).reshape(-1, rows)
    silu_here = once_after(silu_here, [rings[0][2], rings[0][-2]])
    mod_part = dot(silu_here, ada_weight.reshape(rows, -1), ((1,), (0,)))
    mod_part = cube_reduce(mod_part.reshape(size_f, items, -1), "mod_f")
    mod_part = butterfly_sum(mod_part, "ctx", "mod_c")
    bias_mod = lax.dynamic_slice_in_dim(ada_bias.astype(F32), first_column, half_width, 1)
    mod_half = (mod_part.reshape(items, 6, half_width) + bias_mod).astype(BF16)
    mods = both(mod_half, swap(mod_half, "mod_t"), 2).astype(F32)
    mods = once_after(mods, [qkv_came])

    pieces = spread([(0, "own", qkv_came)], "qkv")
    (qkv_mine,) = place(pieces, [3 * group])
    bias_pair = lax.dynamic_slice_in_dim(
        qv_bias.astype(F32), first_column + c * group, group, 1
    )
    bias_mine = jnp.concatenate([bias_pair[0], jnp.zeros((group,), F32), bias_pair[1]])
    bias_mine = bias_mine.reshape(-1, 1)
    qkv_mine = qkv_mine.T

    in_first, qkv_t = project(rings[0], 0, mods, 0, items, qkv_mine, bias_mine, None)
    qkv_ts = [qkv_t]
    rings.append(swapped_ring(1, items - 1, [qkv_t]))
    latent = [(pairs[0], at) for pairs in rings for at in range(pairs[0].shape[0])]

    hop = [rings[1][2], rings[1][-2]]
    (proj_full,) = place(gather_stacked(once_after(proj_weight.T, hop), "proj"), [half_width])
    proj_full = proj_full.T
    feed_shard = jnp.concatenate([up_weight, down_weight.T], 1)
    feed_full = gather_rows(once_after(feed_shard, [mods]), "feed_weights")
    cots = halves(grad_out.reshape(items, here, model), 0, items)

    bias_proj = proj_bias.astype(F32).reshape(1, -1)
    bias_down = down_bias.astype(F32).reshape(1, -1)
    bias_up = lax.dynamic_slice_in_dim(up_bias.astype(F32), t * hidden, hidden, 0)
    bias_up = bias_up.reshape(1, -1)
    mixed = in_second = grad_feed = activated = grad_upward = None
    grad_attended = grad_qkv = out_own = out_peer = out_half = None

    kept = []
    for item in range(items):
        if item:
            in_first, qkv_t = project(
                rings[1], item - 1, mods, item, items, qkv_mine, bias_mine, in_first
            )
            qkv_ts.append(qkv_t)
        qkv_t = qkv_ts[item]
        outs, logs = attend(qkv_t, here)
        mixed, own, peer = back_to_rows(
            exchange(outs, "mixed%d" % item), proj_full, 0, True, mixed, item, items
        )
        attended, residual, in_half = second(
            own, swap(peer, "attended%d" % item), bias_proj, *latent[item], mods, item
        )
        in_peer = swap(in_half, "in_second%d" % item)
        kept.append((qkv_t, logs, attended, residual, in_half, in_peer))

    qkv_rows = once_after(qkv_groups.transpose(1, 0, 2).reshape(rows, -1), [kept[0][5]])
    qkv_full = gather_rows(qkv_rows, "qkv_weights")

    up_sums, grads_in, highs = [], [], []
    for item in range(items):
        _, _, _, _, in_half, in_peer = kept[item]
        (
            in_second,
            grad_feed,
            activated,
            grad_upward,
            out_own,
            out_peer,
            gin_own,
            gin_peer,
            up_sum,
            high,
        ) = feed(
            in_half,
            in_peer,
            cots,
            mods,
            feed_full,
            bias_up,
            (in_second, grad_feed, activated, grad_upward, out_own, out_peer),
            item,
            items,
            [grads_in[0][1]] if item == items - 1 else [],
        )
        grads_in.append((gin_own, swap(gin_peer, "grad_in_second%d" % item)))
        up_sums.append(up_sum)
        highs.append(high)

    def before_attention(item):
        _, _, attended, residual, _, _ = kept[item]
        grad_residual, low, sums_two = second_back(
            *grads_in[item], residual, attended, cots[0], mods, item
        )
        return grad_residual, low, sums_two, swap(low, "grad_attended%d" % item)

    bounds = highs[0]
    for high in highs[1:]:
        bounds = jnp.maximum(bounds, high)
    for axis in ("fsdp", "ctx"):
        bounds = butterfly_max(bounds, axis, "bounds")
    bounds = jnp.maximum(bounds[:, 0, 0], 1e-15)
    tokens = items * here * size_c * size_f
    up_scale = 32768.0 / (bounds[0] * bounds[3] * tokens)
    down_scale = 32768.0 / (bounds[1] * bounds[2] * tokens)
    scales = jnp.where(jnp.arange(2 * hidden) < hidden, up_scale, down_scale)
    middles = [before_attention(item) for item in range(items)]
    parts = outer(
        in_second, grad_upward, 0, 768, 0, 2 * hidden, [None, None], [grads_in[1][1]]
    )
    parts = outer(
        grad_feed, activated, 0, 768, hidden // 768, 2 * hidden, parts, [middles[0][3]]
    )
    feed_rows = reduce_rows(*parts, "grad_feed", scales)
    grad_feed_weights = ring_reduce(feed_rows, "grad_feed", scales)

    peers = swap(out_peer, "feed_out")
    gate_sums = []
    for item in range(items):
        out_half, gate_sum = finish(
            out_own, peers, bias_down, kept[item][3], cots[0], mods, out_half, item
        )
        gate_sums.append(gate_sum)
    output = order([out_half], [swap(out_half, "output")], items)

    grad_blocks = []
    for item in range(items):
        _, low, _, low_peer = middles[item]
        grad_attended, grad_mixed = grad_mixed_of(
            low, low_peer, proj_full, grad_attended, item, items
        )
        grad_blocks.append(
            exchange(grad_mixed.reshape(size_c, group, here), "grad_mixed%d" % item)
        )

    input_grads, input_peers, mod_terms = [], [], []
    for item in range(items):
        qkv_t, logs, _, _, _, _ = kept[item]
        grad_qkv, blocks = attend_back(
            qkv_t,
            grad_blocks[item],
            logs,
            grad_qkv,
            item,
            items,
            [parts[0]] if item == 0 else [],
        )
        own, peer = back_to_rows(
            exchange(blocks, "grad_qkv%d" % item),
            qkv_full,
            1,
            after=[feed_rows] if item == 1 else [],
        )
        grad_latent, sums_one = first_back(
            own,
            swap(peer, "grad_in_first%d" % item),
            *latent[item],
            middles[item][0],
            mods,
            item,
            input_peers[-1:],
        )
        input_grads.append(grad_latent)
        input_peers.append(swap(grad_latent, "grad_latent%d" % item))
        mod_terms.append(jnp.concatenate([sums_one, middles[item][2][:3], gate_sums[item]], 0))

    proj_parts = outer(grad_attended, mixed, 1, half_width, 0, half_width, [None, None])
    grad_proj = ring_reduce(reduce_rows(*proj_parts, "grad_proj"), "grad_proj").T
    grad_qkv = grad_qkv.reshape(3 * group, -1)
    qkv_rows = reduce_rows(*long_outer(in_first, grad_qkv, items), "grad_qkvw")
    grad_qkv_weight = (
        exchange(qkv_rows, "grad_qkvw_c")
        .reshape(size_c, rows, 3, group)
        .transpose(1, 2, 0, 3)
        .reshape(rows, 3, half_width)
    )

    down_sum = sum(
        jnp.sum(grad_feed[item * here : item * here + half].astype(F32), 0)
        for item in range(items)
    )
    qkv_sum = jnp.sum(grad_qkv.astype(F32), 1).reshape(3, group)
    pair_sum = jnp.stack([qkv_sum[0], qkv_sum[2]])
    up_total = lax.dynamic_update_slice_in_dim(
        jnp.zeros(up_bias.shape, F32), sum(up_sums)[0], t * hidden, 0
    )
    pair_total = lax.dynamic_update_slice_in_dim(
        jnp.zeros(qv_bias.shape, F32), pair_sum, first_column + c * group, 1
    )
    proj_sum = sum(middle[2][3] for middle in middles)
    sums = jnp.concatenate(
        [jnp.stack(mod_terms).reshape(-1), up_total, pair_total.reshape(-1), proj_sum, down_sum]
    ).reshape(-1, 128)
    sums = butterfly_sum(butterfly_sum(sums, "tp", "sums"), "ctx", "sums")
    sums = cube_gather(sums, "sums").reshape(size_f, -1)
    edge = items * 6 * model
    grad_mod_all = sums[:, :edge].astype(BF16).reshape(size_f, items, 6, model)
    ada_sum = tree_sum(jnp.sum(grad_mod_all.astype(F32), 1))
    bias_sum = tree_sum(sums[:, edge:])
    ends = [up_bias.shape[0], up_bias.shape[0] + qv_bias.size]

    mod_here = lax.dynamic_slice_in_dim(grad_mod_all, first_column, half_width, 3).reshape(
        size_f * items, -1
    )
    grad_ada = dot(silu_here, mod_here, ((0,), (0,))).reshape(rows, 6, half_width)
    cond_part = dot(mod_here, ada_weight.reshape(rows, -1), ((1,), (1,)))
    cond_part = lax.dynamic_update_slice_in_dim(
        jnp.zeros((size_f * items, model), F32), cond_part, first_row, 1
    ).reshape(size_f, items, model)
    cond_total = cube_reduce(cond_part, "grad_cond")
    for axis in ("ctx", "tp"):
        cond_total = butterfly_sum(cond_total, axis, "grad_cond")
    grad_cond = jax.vjp(jax.nn.silu, cond)[1](cond_total)[0]

    return (
        output.reshape(latents.shape),
        order(input_grads, input_peers, items).reshape(latents.shape),
        grad_cond.reshape(condition.shape),
        grad_ada,
        ada_sum,
        grad_qkv_weight,
        bias_sum[ends[0] : ends[1]].reshape(qv_bias.shape),
        grad_proj,
        bias_sum[ends[1] : ends[1] + model],
        grad_feed_weights[:, :hidden],
        bias_sum[: ends[0]],
        grad_feed_weights[:, hidden:].T,
        bias_sum[ends[1] + model :],
    )


def tree_sum(entries):
    while entries.shape[0] > 1:
        entries = entries[0::2] + entries[1::2]
    return entries[0]


def solution(mesh):
    in_specs = (
        P(None, "fsdp", "ctx", None),
        P(None, "fsdp", None),
        P(None, "fsdp", "ctx", None),
        P(("fsdp", "ctx"), None, "tp"),
        P(),
        P(("fsdp", "ctx"), None, "tp"),
        P(),
        P("tp", ("fsdp", "ctx")),
        P(),
        P(("fsdp", "ctx"), "tp"),
        P(),
        P("tp", ("fsdp", "ctx")),
        P(),
    )
    out_specs = (
        P(None, "fsdp", "ctx", None),
        P(None, "fsdp", "ctx", None),
        P(None, "fsdp", None),
        P(("fsdp", "ctx"), None, "tp"),
        P(),
        P(("fsdp", "ctx"), None, "tp"),
        P(),
        P("tp", ("fsdp", "ctx")),
        P(),
        P(("fsdp", "ctx"), "tp"),
        P(),
        P("tp", ("fsdp", "ctx")),
        P(),
    )
    return jax.shard_map(body, mesh=mesh, in_specs=in_specs, out_specs=out_specs, check_vma=False)
```

time: 919 us -> 677 us (0.74)
  local copies, waits for them, and re-layouts: 208 us -> 95.9 us
  Pallas kernels: 75.3 us -> 182 us
  matrix products: 82.9 us -> 1.74 us
  waiting for transfers between devices: 249 us -> 185 us
  other arithmetic: 112 us -> 48.9 us
  starting transfers between devices: 174 us -> 134 us
  between operations: 4.87 us -> 18.9 us
    pallas_call x6 -> x47, Pallas kernels: 49.8 us -> 175 us  [slab_call(): pl.pallas_call(run, in_specs=in_specs + [ANYWHERE] * more, input_output_a...]
    dot_general x35 -> x3, matrix products: 82.9 us -> 1.74 us  [dot(): return lax.dot_general(a, b, (dims, ((), ())), preferred_element_type=F32)]
    ppermute x60 -> x15, starting transfers between devices: 95 us -> 28.9 us  [shift(): return lax.ppermute(x, 'ctx', [(i, (i + k) % size) for i in range(size)])]
    all_to_all x0 -> x11, starting transfers between devices: none -> 55.8 us  [exchange(): return lax.all_to_all(x, 'ctx', 0, 0)]
    ppermute x102 -> x59, waiting for transfers between devices: 148 us -> 93.4 us  [flip(): return lax.ppermute(x, axis, [(i, i ^ 1 << bit) for i in range(size)])]
    reduce_sum x26 -> x2, other arithmetic: 31.3 us -> 1.97 us  [the longest x1 1.92 us: body(): jnp.sum(grad_feed[item * here:item * here + half].astype(F32), 0)]
    ppermute x102 -> x59, starting transfers between devices: 79 us -> 49.7 us  [flip(): return lax.ppermute(x, axis, [(i, i ^ 1 << bit) for i in range(size)])]
    ppermute x18 -> x0, local copies, waits for them, and re-layouts: 27.6 us -> none  [the longest x9 15.2 us: flip(): return lax.ppermute(x, axis, [(i, i ^ 1 << bit) for i in range(size)])]
  transfers between devices with their start and end apart: 162 -> 87, of which waited for: 55 -> 31; matrix products, arithmetic and copies ran while one was open for 40% -> 11% of each run, Pallas kernels for 7% -> 26%
where the time goes in v2:
time: 677 us; the launch traced here: 666 us
  waiting for transfers between devices  185 us (27%)
  Pallas kernels  182 us (27%)
  starting transfers between devices  134 us (20%)
  local copies, waits for them, and re-layouts  95.9 us (14%)
  other arithmetic  48.9 us (7%)
  between operations  18.9 us (3%)
    pallas_call x47, Pallas kernels, slab_call(): pl.pallas_call(run, in_specs=in_specs + [ANYWHERE] * more, input_output_a...  175 us
    ppermute x59, waiting for transfers between devices, flip(): return lax.ppermute(x, axis, [(i, i ^ 1 << bit) for i in range(size)])  93.4 us
    ppermute x15, waiting for transfers between devices, shift(): return lax.ppermute(x, 'ctx', [(i, (i + k) % size) for i in range(size)])  83 us
    unnamed x305, local copies, waits for them, and re-layouts  72.9 us
    all_to_all x11, starting transfers between devices, exchange(): return lax.all_to_all(x, 'ctx', 0, 0)  55.8 us
    ppermute x59, starting transfers between devices, flip(): return lax.ppermute(x, axis, [(i, i ^ 1 << bit) for i in range(size)])  49.7 us
    ppermute x15, starting transfers between devices, shift(): return lax.ppermute(x, 'ctx', [(i, (i + k) % size) for i in range(size)])  28.9 us
  transfers between devices with their start and end apart: 87, of which 31 were waited for; matrix products, arithmetic and copies ran while one was open for 11% of the time, Pallas kernels for 26%

profile of v2, /device:TPU:0, one launch (start us, length us, event | category | flops | bytes accessed | tf_op | source)
XLA Modules:
  0.0 666.2 jit_solution(9432348967048878862)
XLA Ops:
  10.7 4.6 collective-permute-start.4
  20.0 2.7 collective-permute-done.4.refs_2_.refs_6_
  22.6 6.9 %collective-permute-done.refs_1_.refs_2_ = bf16[1,128,1152]{2,1,0:T(8,128)(2,1)} collective-permute-done((bf16[1,128,1152]{2,1,0:T(8,128)(2,1)S(1)}, bf16[1,128,1152]{2,1,0:T(8,128)(2,1)}, u32[]{:S(2)}, u32[]{:S(2)}) %collective-permute-start) | collective-permute-done | bytes 294944 | tf_op jit(solution)/shard_map/latent0_right/ppermute | solution.py:38
  31.4 3.2 collective-permute-done.8
  39.3 3.5 all-to-all-start
  42.9 2.9 collective-permute-start.11
  45.9 9.2 %collective-permute-done.11 = f32[3,3456]{1,0:T(4,128)S(1)} collective-permute-done((f32[3,3456]{1,0:T(4,128)S(1)}, f32[3,3456]{1,0:T(4,128)S(1)}, u32[]{:S(2)}, u32[]{:S(2)}) %collective-permute-start.11) | collective-permute-done | bytes 41504 | tf_op jit(solution)/shard_map/mod_c/ppermute | solution.py:44
  64.6 4.6 collective-permute-done.2.refs_4_
  72.3 3.3 shard_map.231
  79.0 3.2 collective-permute-done.3.refs_5_
  83.1 5.1 shard_map.232
  88.4 3.8 collective-permute-start.20
  92.2 15.7 %collective-permute-done.16.refs_2_.refs_1_ = bf16[2,128,1152]{2,1,0:T(8,128)(2,1)S(1)} collective-permute-done((bf16[2,128,1152]{2,1,0:T(8,128)(2,1)S(1)}, bf16[2,128,1152]{2,1,0:T(8,128)(2,1)S(1)}, u32[]{:S(2)}, u32[]{:S(2)}) %collective-permute-start.16) | collective-permute-done | bytes 589856 | tf_op jit(solution)/shard_map/latent1_right/ppermute | solution.py:38
  107.9 21.8 %collective-permute-done.20.refs_6_.refs_2_ = bf16[2,128,1152]{2,1,0:T(8,128)(2,1)S(1)} collective-permute-done((bf16[2,128,1152]{2,1,0:T(8,128)(2,1)S(1)}, bf16[2,128,1152]{2,1,0:T(8,128)(2,1)S(1)}, u32[]{:S(2)}, u32[]{:S(2)}) %collective-permute-start.20) | collective-permute-done | bytes 589856 | tf_op jit(solution)/shard_map/latent1_left/ppermute | solution.py:38
  129.7 4.6 collective-permute-start.22
  136.2 14.5 %collective-permute-done.18.refs_4_ = bf16[2,128,1152]{2,1,0:T(8,128)(2,1)S(1)} collective-permute-done((bf16[2,128,1152]{2,1,0:T(8,128)(2,1)S(1)}, bf16[2,128,1152]{2,1,0:T(8,128)(2,1)S(1)}, u32[]{:S(2)}, u32[]{:S(2)}) %collective-permute-start.18) | collective-permute-done | bytes 589856 | tf_op jit(solution)/shard_map/latent1_right/ppermute | solution.py:38
  152.2 8.1 %collective-permute-start.24 = (bf16[72,576]{1,0:T(8,128)(2,1)S(1)}, bf16[72,576]{1,0:T(8,128)(2,1)S(1)}, u32[]{:S(2)}, u32[]{:S(2)}) collective-permute-start(bf16[72,576]{1,0:T(8,128)(2,1)S(1)} %shard_map.237), channel_id=1, source_target_pairs={{0,6},{2,0},{4,2},{6,4},{1,7},{3,1},{5,3},{7,5},{8,14},{10,8},{12,... | collective-permute-start | bytes 248840 | tf_op jit(solution)/shard_map/proj_left/ppermute | solution.py:38
  160.3 5.0 collective-permute-done.24
  165.3 5.0 collective-permute-done.23
  171.2 7.2 %shard_map.240 = (bf16[4,144,256]{2,1,0:T(8,128)(2,1)S(1)}, f32[2,1024]{1,0:T(2,128)S(1)}) custom-call(bf16[3,144,1024]{2,1,0:T(8,128)(2,1)S(1)} %bitcast.177, bf16[3,144,1024]{2,1,0:T(8,128)(2,1)S(1)} %bitcast.178, bf16[3,144,1024]{2,1,0:T(8,128)(2,1)S(1)} %bitcast.179), custom_call_target="tpu_custom_call" | custom-call | flops 3355443200 | bytes 1179648 | tf_op jit(solution)/shard_map/pallas_call | solution.py:247
  179.1 7.7 %all-to-all-start.3 = ((bf16[4,144,256]{2,1,0:T(8,128)(2,1)}), bf16[4,144,256]{2,1,0:T(8,128)(2,1)}, u32[]{:S(2)}, u32[]{:S(2)}) async-start(bf16[4,144,256]{2,1,0:T(8,128)(2,1)} %copy-done.97), calls=%async_computation.3 | async-start | bytes 589824 | tf_op jit(solution)/shard_map/mixed0/all_to_all | solution.py:49
  187.4 4.9 shard_map.234
  192.3 7.9 %shard_map.239 = (bf16[4,144,256]{2,1,0:T(8,128)(2,1)}, f32[2,1024]{1,0:T(2,128)S(1)}) custom-call(bf16[3,144,1024]{2,1,0:T(8,128)(2,1)S(1)} %bitcast.197, bf16[3,144,1024]{2,1,0:T(8,128)(2,1)S(1)} %bitcast.198, bf16[3,144,1024]{2,1,0:T(8,128)(2,1)S(1)} %bitcast.199), custom_call_target="tpu_custom_call" | custom-call | flops 3355443200 | bytes 1179648 | tf_op jit(solution)/shard_map/pallas_call | solution.py:247
  201.2 5.1 all-to-all-start.2
  206.3 3.1 shard_map.238
  210.5 2.6 shard_map.241
  218.0 4.9 shard_map.235
  227.3 7.2 %shard_map.236 = (bf16[4,144,256]{2,1,0:T(8,128)(2,1)S(1)}, f32[2,1024]{1,0:T(2,128)S(1)}) custom-call(bf16[3,144,1024]{2,1,0:T(8,128)(2,1)S(1)} %bitcast.191, bf16[3,144,1024]{2,1,0:T(8,128)(2,1)S(1)} %bitcast.192, bf16[3,144,1024]{2,1,0:T(8,128)(2,1)S(1)} %bitcast.193), custom_call_target="tpu_custom_call" | custom-call | flops 3355443200 | bytes 1179648 | tf_op jit(solution)/shard_map/pallas_call | solution.py:247
  235.3 5.1 all-to-all-start.1
  249.4 2.7 shard_map.243
  261.8 12.4 %shard_map.249 = (bf16[768,1152]{1,0:T(8,128)(2,1)}, bf16[768,1152]{1,0:T(8,128)(2,1)}, bf16[768,2304]{1,0:T(8,128)(2,1)}, bf16[768,2304]{1,0:T(8,128)(2,1)}, f3...) custom-call(bf16[128,1152]{1,0:T(8,128)(2,1)} %get-tuple-element.150, ...), custom_call_target="tpu_custom_call" | custom-call | flops 5435817984 | bytes 12976128 | tf_op jit(solution)/shard_map/pallas_call | solution.py:247
  279.4 12.0 %shard_map.250 = (bf16[768,1152]{1,0:T(8,128)(2,1)}, bf16[768,1152]{1,0:T(8,128)(2,1)}, bf16[768,2304]{1,0:T(8,128)(2,1)}, bf16[768,2304]{1,0:T(8,128)(2,1)}, f3...) custom-call(bf16[128,1152]{1,0:T(8,128)(2,1)} %get-tuple-element.147, ...), custom_call_target="tpu_custom_call", output_to_operand_aliasing={{0}: (8, {}), {1}: (9, {}), {2}: (10, {}), {3}: (11, {}), {... | custom-call | flops 5435817984 | bytes 12976128 | tf_op jit(solution)/shard_map/pallas_call | solution.py:247
  296.4 11.8 %shard_map.251 = (bf16[768,1152]{1,0:T(8,128)(2,1)}, bf16[768,1152]{1,0:T(8,128)(2,1)}, bf16[768,2304]{1,0:T(8,128)(2,1)}, bf16[768,2304]{1,0:T(8,128)(2,1)}, f3...) custom-call(bf16[128,1152]{1,0:T(8,128)(2,1)S(1)} %get-tuple-element, ...), custom_call_target="tpu_custom_call", output_to_operand_aliasing={{0}: (8, {}), {1}: (9, {}), {2}: (10, {}), {3}: (11, {}), {... | custom-call | flops 5435817984 | bytes 12976128 | tf_op jit(solution)/shard_map/pallas_call | solution.py:247
  313.6 7.1 %shard_map.258 = (f32[2,288,4608]{2,1,0:T(8,128)}, f32[2,288,4608]{2,1,0:T(8,128)}) custom-call(bf16[768,1152]{1,0:T(8,128)(2,1)S(1)} %copy-done.19, bf16[768,2304]{1,0:T(8,128)(2,1)S(1)} %copy-done.6, f32[128,1152]{1,0:T(8,128)S(1)} %collective-permute-done.38.refs_2_.refs_1_), custom_call_target="tpu_custom_call" | custom-call | flops 4076863488 | bytes 14155776 | tf_op jit(solution)/shard_map/pallas_call | solution.py:247
  320.8 7.3 %shard_map.259 = (f32[2,288,4608]{2,1,0:T(8,128)}, f32[2,288,4608]{2,1,0:T(8,128)}) custom-call(bf16[768,1152]{1,0:T(8,128)(2,1)S(1)} %copy-done.5, bf16[768,2304]{1,0:T(8,128)(2,1)S(1)} %copy-done.4, f32[2,288,4608]{2,1,0:T(8,128)} %get-tuple-element.182.refs_2_, ...), custom_call_target="tpu_custom_call", output_to_operand_aliasing={{0}: (2, {}), {1}: (3, {})} | custom-call | flops 4076863488 | bytes 14155776 | tf_op jit(solution)/shard_map/pallas_call | solution.py:247
  333.6 11.2 %collective-permute-done.42 = f32[4,8,128]{2,1,0:T(8,128)} collective-permute-done((f32[4,8,128]{2,1,0:T(8,128)}, f32[4,8,128]{2,1,0:T(8,128)}, u32[]{:S(2)}, u32[]{:S(2)}) %collective-permute-start.42) | collective-permute-done | bytes 16416 | tf_op jit(solution)/shard_map/bounds/ppermute | solution.py:44
  369.7 4.2 all-to-all-start.4
  388.8 5.1 all-to-all-start.6
  395.0 12.0 %shard_map.260 = (bf16[3,144,3072]{2,1,0:T(8,128)(2,1)S(1)}, bf16[4,3,144,256]{3,2,1,0:T(8,128)(2,1)}) custom-call(bf16[3,144,1024]{2,1,0:T(8,128)(2,1)S(1)} %bitcast.180, bf16[3,144,1024]{2,1,0:T(8,128)(2,1)S(1)} %bitcast.181, bf16[3,144,1024]{2,1,0:T(8,128)(2,1)S(1)} %bitcast.182, f32[2,1024]{1,0:T(2,128)S(1)} %get-tuple-element.172.refs_3_, ...), custom_call_target="tpu_custom_call" | custom-call | flops 8388608000 | bytes 2359296 | tf_op jit(solution)/shard_map/pallas_call | solution.py:247
  412.1 5.1 all-to-all-start.8
  420.1 10.9 %shard_map.266 = (bf16[3,144,3072]{2,1,0:T(8,128)(2,1)S(1)}, bf16[4,3,144,256]{3,2,1,0:T(8,128)(2,1)S(1)}) custom-call(bf16[3,144,1024]{2,1,0:T(8,128)(2,1)S(1)} %bitcast.200, bf16[3,144,1024]{2,1,0:T(8,128)(2,1)S(1)} %bitcast.201, bf16[3,144,1024]{2,1,0:T(8,128)(2,1)S(1)} %bitcast.202, f32[2,1024]{1,0:T(2,128)S(1)} %copy-done.128, ...), custom_call_target="tpu_custom_call", output_to_operand_aliasing={{0}: (5, {})} | custom-call | flops 8388608000 | bytes 2359296 | tf_op jit(solution)/shard_map/pallas_call | solution.py:247
  433.5 5.5 all-to-all-start.5
  439.0 6.8 %multiply_convert_fusion = f16[1,288,4608]{2,1,0:T(8,128)(2,1)} fusion(f32[2,288,4608]{2,1,0:T(8,128)} %collective-permute-done.41, s32[]{:T(128)S(6)} %select_n.122, f32[2,288,4608]{2,1,0:T(8,128)} %get-tuple-element.198, f32[4608]{0:T(1024)S(1)} %copy-done.137), kind=kLoop, calls=%fused_computation.2 | loop fusion | flops 3981312 | bytes 13289476 | tf_op jit(solution)/shard_map/convert_element_type | solution.py:173
  447.8 2.8 shard_map.276
  456.0 9.9 %shard_map.271 = (bf16[3,144,3072]{2,1,0:T(8,128)(2,1)S(1)}, bf16[4,3,144,256]{3,2,1,0:T(8,128)(2,1)S(1)}) custom-call(bf16[3,144,1024]{2,1,0:T(8,128)(2,1)S(1)} %bitcast.194, bf16[3,144,1024]{2,1,0:T(8,128)(2,1)S(1)} %bitcast.195, bf16[3,144,1024]{2,1,0:T(8,128)(2,1)S(1)} %bitcast.196, f32[2,1024]{1,0:T(2,128)S(1)} %copy-done.126, ...), custom_call_target="tpu_custom_call", output_to_operand_aliasing={{0}: (5, {})} | custom-call | flops 8388608000 | bytes 2359296 | tf_op jit(solution)/shard_map/pallas_call | solution.py:247
  468.4 5.1 all-to-all-start.9
  475.3 7.9 %shard_map.275 = (f32[2,288,432]{2,1,0:T(8,128)}, f32[2,288,432]{2,1,0:T(8,128)S(1)}) custom-call(bf16[3072,1152]{1,0:T(8,128)(2,1)} %get-tuple-element.232.refs_0_, bf16[432,3072]{1,0:T(8,128)(2,1)S(1)} %bitcast.175), custom_call_target="tpu_custom_call" | custom-call | flops 3057647616 | bytes 9732096 | tf_op jit(solution)/shard_map/pallas_call | solution.py:247
  487.5 3.4 shard_map.262
  501.8 6.0 collective-permute-done.39.refs_1_
  511.1 5.3 all-to-all-start.7
  522.9 8.3 %multiply_add_fusion = f32[1,288,4608]{2,1,0:T(8,128)} fusion(f16[1,288,4608]{2,1,0:T(8,128)(2,1)} %collective-permute-done.46, f32[2,288,4608]{2,1,0:T(8,128)} %collective-permute-done.41, s32[]{:T(128)S(6)} %select_n.121, f32[2,288,4608]{2,1,0:T(8,128)} %get-tuple-element.198, f32[4608]{0:T(1024)S(1)} %broadcast_divide_fusion), kind=kLoop, calls=%fused_computation.1 | loop fusion | flops 5308416 | bytes 18597892 | tf_op jit(solution)/shard_map/add | solution.py:192
  531.2 7.1 %all-to-all-done.7.refs_0_ = bf16[4,3,144,256]{3,2,1,0:T(8,128)(2,1)S(1)} async-done(((bf16[4,3,144,256]{3,2,1,0:T(8,128)(2,1)}), bf16[4,3,144,256]{3,2,1,0:T(8,128)(2,1)S(1)}, u32[]{:S(2)}, u32[]{:S(2)}) %all-to-all-start.7) | async-done | bytes 884768 | tf_op jit(solution)/shard_map/grad_qkv1/all_to_all | solution.py:49
  546.8 4.2 all-to-all-start.10
  563.2 10.0 %collective-permute-done.52.refs_5_.refs_4_ = f32[128,1152]{1,0:T(8,128)S(1)} collective-permute-done((f32[128,1152]{1,0:T(8,128)S(1)}, f32[128,1152]{1,0:T(8,128)S(1)}, u32[]{:S(2)}, u32[]{:S(2)}) %collective-permute-start.52) | collective-permute-done | bytes 589856 | tf_op jit(solution)/shard_map/grad_latent1/ppermute | solution.py:44
  578.7 2.7 collective-permute-done.54
  581.5 6.9 %collective-permute-done.71 = f16[72,4608]{1,0:T(8,128)(2,1)} collective-permute-done((f16[72,4608]{1,0:T(8,128)(2,1)}, f16[72,4608]{1,0:T(8,128)(2,1)}, u32[]{:S(2)}, u32[]{:S(2)}) %collective-permute-start.71) | collective-permute-done | bytes 663584 | tf_op jit(solution)/shard_map/grad_feed_ring/ppermute | solution.py:38
  588.3 3.1 fusion.3
  591.7 3.6 collective-permute-start.73
  605.7 20.4 %collective-permute-done.56 = f32[234,128]{1,0:T(8,128)} collective-permute-done((f32[234,128]{1,0:T(8,128)S(1)}, f32[234,128]{1,0:T(8,128)}, u32[]{:S(2)}, u32[]{:S(2)}) %collective-permute-start.56) | collective-permute-done | bytes 119840 | tf_op jit(solution)/shard_map/sums/ppermute | solution.py:44
  630.7 3.1 shard_map.274
  633.8 3.8 collective-permute-done.58
  641.7 2.8 collective-permute-done.59
  646.8 3.1 collective-permute-done.61
  650.3 4.2 collective-permute-done.62
  (578 shorter events, 226.5 us)
Async XLA Ops:
  15.3 14.3 %collective-permute-start = (bf16[1,128,1152]{2,1,0:T(8,128)(2,1)S(1)}, bf16[1,128,1152]{2,1,0:T(8,128)(2,1)}, u32[]{:S(2)}, u32[]{:S(2)}) collective-permute-start(bf16[1,128,1152]{2,1,0:T(8,128)(2,1)S(1)} %get-tuple-element.126.refs_0_.refs_3_.refs_2_), channel_id=1, source_target_pairs={{0,2},{2,4},{4,6},{6,0},{1,3},{3,5},{5,7},{7,1},{8,10},{10,12},{12... | collective-permute-start | bytes 884744 | tf_op jit(solution)/shard_map/latent0_right/ppermute | solution.py:38
  39.3 19.9 %all-to-all-start = ((bf16[4,72,432]{2,1,0:T(8,128)(2,1)}), bf16[4,72,432]{2,1,0:T(8,128)(2,1)S(1)}, u32[]{:S(2)}, u32[]{:S(2)}) async-start(bf16[4,72,432]{2,1,0:T(8,128)(2,1)} %copy.88), calls=%async_computation | async-start | bytes 589824 | tf_op jit(solution)/shard_map/qkv_c/all_to_all | solution.py:49
  42.8 217.8 %all-gather.3.cloned.1.call-start = ((), (), s32[]{:S(2)}) async-start(), calls=%async_computation.11 | async-start | bytes 11280384 | tf_op jit(solution)/shard_map/feed_weights/all_gather | solution.py:54
  42.9 12.2 %collective-permute-start.11 = (f32[3,3456]{1,0:T(4,128)S(1)}, f32[3,3456]{1,0:T(4,128)S(1)}, u32[]{:S(2)}, u32[]{:S(2)}) collective-permute-start(f32[3,3456]{1,0:T(4,128)S(1)} %add.250), channel_id=1, source_target_pairs={{0,4},{2,6},{4,0},{6,2},{1,5},{3,7},{5,1},{7,3},{8,12},{10,14},{12... | collective-permute-start | bytes 124424 | tf_op jit(solution)/shard_map/mod_c/ppermute | solution.py:44
  62.6 13.9 %collective-permute-start.5 = (bf16[1,128,1152]{2,1,0:T(8,128)(2,1)}, bf16[1,128,1152]{2,1,0:T(8,128)(2,1)}, u32[]{:S(2)}, u32[]{:S(2)}) collective-permute-start(bf16[1,128,1152]{2,1,0:T(8,128)(2,1)} %collective-permute-done.4.refs_2_.refs_6_), channel_id=1, source_target_pairs={{0,1},{1,0},{2,3},{3,2},{4,5},{5,4},{6,7},{7,6},{8,9},{9,8},{10,11... | collective-permute-start | bytes 884744 | tf_op jit(solution)/shard_map/latent0_t/ppermute | solution.py:44
  64.1 14.9 %collective-permute-start.1 = (bf16[1,128,1152]{2,1,0:T(8,128)(2,1)}, bf16[1,128,1152]{2,1,0:T(8,128)(2,1)}, u32[]{:S(2)}, u32[]{:S(2)}) collective-permute-start(bf16[1,128,1152]{2,1,0:T(8,128)(2,1)} %collective-permute-done.refs_1_.refs_2_), channel_id=1, source_target_pairs={{0,1},{1,0},{2,3},{3,2},{4,5},{5,4},{6,7},{7,6},{8,9},{9,8},{10,11... | collective-permute-start | bytes 884744 | tf_op jit(solution)/shard_map/latent0_t/ppermute | solution.py:44
  69.2 12.9 %collective-permute-start.3 = (bf16[1,128,1152]{2,1,0:T(8,128)(2,1)}, bf16[1,128,1152]{2,1,0:T(8,128)(2,1)}, u32[]{:S(2)}, u32[]{:S(2)}) collective-permute-start(bf16[1,128,1152]{2,1,0:T(8,128)(2,1)} %collective-permute-done.2.refs_4_), channel_id=1, source_target_pairs={{0,1},{1,0},{2,3},{3,2},{4,5},{5,4},{6,7},{7,6},{8,9},{9,8},{10,11... | collective-permute-start | bytes 884744 | tf_op jit(solution)/shard_map/latent0_t/ppermute | solution.py:44
  88.3 19.5 %collective-permute-start.16 = (bf16[2,128,1152]{2,1,0:T(8,128)(2,1)S(1)}, bf16[2,128,1152]{2,1,0:T(8,128)(2,1)S(1)}, u32[]{:S(2)}, u32[]{:S(2)}) collective-permute-start(bf16[2,128,1152]{2,1,0:T(8,128)(2,1)S(1)} %get-tuple-element.129.refs_0_.refs_3_.refs_2_), channel_id=1, source_target_pairs={{0,2},{2,4},{4,6},{6,0},{1,3},{3,5},{5,7},{7,1},{8,10},{10,12},{12... | collective-permute-start | bytes 1769480 | tf_op jit(solution)/shard_map/latent1_right/ppermute | solution.py:38
  88.4 41.3 %collective-permute-start.20 = (bf16[2,128,1152]{2,1,0:T(8,128)(2,1)S(1)}, bf16[2,128,1152]{2,1,0:T(8,128)(2,1)S(1)}, u32[]{:S(2)}, u32[]{:S(2)}) collective-permute-start(bf16[2,128,1152]{2,1,0:T(8,128)(2,1)S(1)} %get-tuple-element.129.refs_0_.refs_3_.refs_2_), channel_id=1, source_target_pairs={{0,6},{2,0},{4,2},{6,4},{1,7},{3,1},{5,3},{7,5},{8,14},{10,8},{12,... | collective-permute-start | bytes 1769480 | tf_op jit(solution)/shard_map/latent1_left/ppermute | solution.py:38
  107.8 42.8 %collective-permute-start.18 = (bf16[2,128,1152]{2,1,0:T(8,128)(2,1)S(1)}, bf16[2,128,1152]{2,1,0:T(8,128)(2,1)S(1)}, u32[]{:S(2)}, u32[]{:S(2)}) collective-permute-start(bf16[2,128,1152]{2,1,0:T(8,128)(2,1)S(1)} %collective-permute-done.16.refs_2_.refs_1_), channel_id=1, source_target_pairs={{0,2},{2,4},{4,6},{6,0},{1,3},{3,5},{5,7},{7,1},{8,10},{10,12},{12... | collective-permute-start | bytes 1769480 | tf_op jit(solution)/shard_map/latent1_right/ppermute | solution.py:38
  129.7 30.6 %collective-permute-start.22 = (bf16[72,576]{1,0:T(8,128)(2,1)S(1)}, bf16[72,576]{1,0:T(8,128)(2,1)S(1)}, u32[]{:S(2)}, u32[]{:S(2)}) collective-permute-start(bf16[72,576]{1,0:T(8,128)(2,1)S(1)} %shard_map.237), channel_id=1, source_target_pairs={{0,2},{2,4},{4,6},{6,0},{1,3},{3,5},{5,7},{7,1},{8,10},{10,12},{12... | collective-permute-start | bytes 248840 | tf_op jit(solution)/shard_map/proj_right/ppermute | solution.py:38
  134.2 53.2 %collective-permute-start.21 = (bf16[2,128,1152]{2,1,0:T(8,128)(2,1)S(1)}, bf16[2,128,1152]{2,1,0:T(8,128)(2,1)}, u32[]{:S(2)}, u32[]{:S(2)}) collective-permute-start(bf16[2,128,1152]{2,1,0:T(8,128)(2,1)S(1)} %collective-permute-done.20.refs_6_.refs_2_), channel_id=1, source_target_pairs={{0,1},{1,0},{2,3},{3,2},{4,5},{5,4},{6,7},{7,6},{8,9},{9,8},{10,11... | collective-permute-start | bytes 1769480 | tf_op jit(solution)/shard_map/latent1_t/ppermute | solution.py:44
  135.7 51.7 %collective-permute-start.17 = (bf16[2,128,1152]{2,1,0:T(8,128)(2,1)S(1)}, bf16[2,128,1152]{2,1,0:T(8,128)(2,1)}, u32[]{:S(2)}, u32[]{:S(2)}) collective-permute-start(bf16[2,128,1152]{2,1,0:T(8,128)(2,1)S(1)} %collective-permute-done.16.refs_2_.refs_1_), channel_id=1, source_target_pairs={{0,1},{1,0},{2,3},{3,2},{4,5},{5,4},{6,7},{7,6},{8,9},{9,8},{10,11... | collective-permute-start | bytes 1769480 | tf_op jit(solution)/shard_map/latent1_t/ppermute | solution.py:44
  150.7 36.7 %collective-permute-start.19 = (bf16[2,128,1152]{2,1,0:T(8,128)(2,1)S(1)}, bf16[2,128,1152]{2,1,0:T(8,128)(2,1)}, u32[]{:S(2)}, u32[]{:S(2)}) collective-permute-start(bf16[2,128,1152]{2,1,0:T(8,128)(2,1)S(1)} %collective-permute-done.18.refs_4_), channel_id=1, source_target_pairs={{0,1},{1,0},{2,3},{3,2},{4,5},{5,4},{6,7},{7,6},{8,9},{9,8},{10,11... | collective-permute-start | bytes 1769480 | tf_op jit(solution)/shard_map/latent1_t/ppermute | solution.py:44
  152.2 13.1 %collective-permute-start.24 = (bf16[72,576]{1,0:T(8,128)(2,1)S(1)}, bf16[72,576]{1,0:T(8,128)(2,1)S(1)}, u32[]{:S(2)}, u32[]{:S(2)}) collective-permute-start(bf16[72,576]{1,0:T(8,128)(2,1)S(1)} %shard_map.237), channel_id=1, source_target_pairs={{0,6},{2,0},{4,2},{6,4},{1,7},{3,1},{5,3},{7,5},{8,14},{10,8},{12,... | collective-permute-start | bytes 248840 | tf_op jit(solution)/shard_map/proj_left/ppermute | solution.py:38
  171.2 15.7 %collective-permute-start.25 = (bf16[4,72,576]{2,1,0:T(8,128)(2,1)}, bf16[4,72,576]{2,1,0:T(8,128)(2,1)}, u32[]{:S(2)}, u32[]{:S(2)}) collective-permute-start(bf16[4,72,576]{2,1,0:T(8,128)(2,1)} %pad_maximum_fusion.2.refs_0_), channel_id=1, source_target_pairs={{0,16},{8,24},{16,0},{24,8},{1,17},{9,25},{17,1},{25,9},{2,18},{10... | collective-permute-start | bytes 995336 | tf_op jit(solution)/shard_map/proj_1/ppermute | solution.py:44
  179.1 22.1 %all-to-all-start.3 = ((bf16[4,144,256]{2,1,0:T(8,128)(2,1)}), bf16[4,144,256]{2,1,0:T(8,128)(2,1)}, u32[]{:S(2)}, u32[]{:S(2)}) async-start(bf16[4,144,256]{2,1,0:T(8,128)(2,1)} %copy-done.97), calls=%async_computation.3 | async-start | bytes 589824 | tf_op jit(solution)/shard_map/mixed0/all_to_all | solution.py:49
  186.8 19.5 %collective-permute-start.26 = (bf16[4,72,576]{2,1,0:T(8,128)(2,1)}, bf16[4,72,576]{2,1,0:T(8,128)(2,1)}, u32[]{:S(2)}, u32[]{:S(2)}) collective-permute-start(bf16[4,72,576]{2,1,0:T(8,128)(2,1)} %pad_maximum_fusion.2.refs_0_), channel_id=1, source_target_pairs={{0,8},{8,0},{16,24},{24,16},{1,9},{9,1},{17,25},{25,17},{2,10},{10... | collective-permute-start | bytes 995336 | tf_op jit(solution)/shard_map/proj_0/ppermute | solution.py:44
  186.9 19.4 %collective-permute-start.27 = (bf16[4,72,576]{2,1,0:T(8,128)(2,1)}, bf16[4,72,576]{2,1,0:T(8,128)(2,1)}, u32[]{:S(2)}, u32[]{:S(2)}) collective-permute-start(bf16[4,72,576]{2,1,0:T(8,128)(2,1)} %collective-permute-done.25.refs_1_), channel_id=1, source_target_pairs={{0,8},{8,0},{16,24},{24,16},{1,9},{9,1},{17,25},{25,17},{2,10},{10... | collective-permute-start | bytes 995336 | tf_op jit(solution)/shard_map/proj_0/ppermute | solution.py:44
  201.2 22.7 %all-to-all-start.2 = ((bf16[4,144,256]{2,1,0:T(8,128)(2,1)}), bf16[4,144,256]{2,1,0:T(8,128)(2,1)}, u32[]{:S(2)}, u32[]{:S(2)}) async-start(bf16[4,144,256]{2,1,0:T(8,128)(2,1)} %get-tuple-element.136), calls=%async_computation.2 | async-start | bytes 589824 | tf_op jit(solution)/shard_map/mixed1/all_to_all | solution.py:49
  213.9 26.5 %collective-permute-start.32 = (f32[128,1152]{1,0:T(8,128)}, f32[128,1152]{1,0:T(8,128)S(1)}, u32[]{:S(2)}, u32[]{:S(2)}) collective-permute-start(f32[128,1152]{1,0:T(8,128)} %get-tuple-element.149), channel_id=1, source_target_pairs={{0,1},{1,0},{2,3},{3,2},{4,5},{5,4},{6,7},{7,6},{8,9},{9,8},{10,11... | collective-permute-start | bytes 1769480 | tf_op jit(solution)/shard_map/attended0/ppermute | solution.py:44
  227.2 29.3 %collective-permute-start.30 = (f32[128,1152]{1,0:T(8,128)}, f32[128,1152]{1,0:T(8,128)}, u32[]{:S(2)}, u32[]{:S(2)}) collective-permute-start(f32[128,1152]{1,0:T(8,128)} %get-tuple-element.146), channel_id=1, source_target_pairs={{0,1},{1,0},{2,3},{3,2},{4,5},{5,4},{6,7},{7,6},{8,9},{9,8},{10,11... | collective-permute-start | bytes 1769480 | tf_op jit(solution)/shard_map/attended1/ppermute | solution.py:44
  235.3 14.1 %all-to-all-start.1 = ((bf16[4,144,256]{2,1,0:T(8,128)(2,1)}), bf16[4,144,256]{2,1,0:T(8,128)(2,1)}, u32[]{:S(2)}, u32[]{:S(2)}) async-start(bf16[4,144,256]{2,1,0:T(8,128)(2,1)} %copy-done.98), calls=%async_computation.1 | async-start | bytes 589824 | tf_op jit(solution)/shard_map/mixed2/all_to_all | solution.py:49
  240.4 245.0 %all-gather.5.cloned.1.call-start = ((), (), s32[]{:S(2)}) async-start(), calls=%async_computation.12 | async-start | bytes 4386816 | tf_op jit(solution)/shard_map/qkv_weights/all_gather | solution.py:54
  246.1 14.5 %collective-permute-start.33 = (bf16[128,1152]{1,0:T(8,128)(2,1)}, bf16[128,1152]{1,0:T(8,128)(2,1)}, u32[]{:S(2)}, u32[]{:S(2)}) collective-permute-start(bf16[128,1152]{1,0:T(8,128)(2,1)} %get-tuple-element.150.refs_0_), channel_id=1, source_target_pairs={{0,1},{1,0},{2,3},{3,2},{4,5},{5,4},{6,7},{7,6},{8,9},{9,8},{10,11... | collective-permute-start | bytes 884744 | tf_op jit(solution)/shard_map/in_second0/ppermute | solution.py:44
  252.9 23.0 %collective-permute-start.28 = (f32[128,1152]{1,0:T(8,128)}, f32[128,1152]{1,0:T(8,128)}, u32[]{:S(2)}, u32[]{:S(2)}) collective-permute-start(f32[128,1152]{1,0:T(8,128)} %get-tuple-element.141), channel_id=1, source_target_pairs={{0,1},{1,0},{2,3},{3,2},{4,5},{5,4},{6,7},{7,6},{8,9},{9,8},{10,11... | collective-permute-start | bytes 1769480 | tf_op jit(solution)/shard_map/attended2/ppermute | solution.py:44
  260.3 19.0 %collective-permute-start.31 = (bf16[128,1152]{1,0:T(8,128)(2,1)}, bf16[128,1152]{1,0:T(8,128)(2,1)}, u32[]{:S(2)}, u32[]{:S(2)}) collective-permute-start(bf16[128,1152]{1,0:T(8,128)(2,1)} %get-tuple-element.147.refs_0_), channel_id=1, source_target_pairs={{0,1},{1,0},{2,3},{3,2},{4,5},{5,4},{6,7},{7,6},{8,9},{9,8},{10,11... | collective-permute-start | bytes 884744 | tf_op jit(solution)/shard_map/in_second1/ppermute | solution.py:44
  274.2 20.4 %collective-permute-start.34 = (f32[128,1152]{1,0:T(8,128)S(1)}, f32[128,1152]{1,0:T(8,128)S(1)}, u32[]{:S(2)}, u32[]{:S(2)}) collective-permute-start(f32[128,1152]{1,0:T(8,128)S(1)} %get-tuple-element.163), channel_id=1, source_target_pairs={{0,1},{1,0},{2,3},{3,2},{4,5},{5,4},{6,7},{7,6},{8,9},{9,8},{10,11... | collective-permute-start | bytes 1769480 | tf_op jit(solution)/shard_map/grad_in_second0/ppermute | solution.py:44
  279.1 17.4 %collective-permute-start.29 = (bf16[128,1152]{1,0:T(8,128)(2,1)S(1)}, bf16[128,1152]{1,0:T(8,128)(2,1)S(1)}, u32[]{:S(2)}, u32[]{:S(2)}) collective-permute-start(bf16[128,1152]{1,0:T(8,128)(2,1)S(1)} %get-tuple-element.142.refs_0_), channel_id=1, source_target_pairs={{0,1},{1,0},{2,3},{3,2},{4,5},{5,4},{6,7},{7,6},{8,9},{9,8},{10,11... | collective-permute-start | bytes 884744 | tf_op jit(solution)/shard_map/in_second2/ppermute | solution.py:44
  292.9 17.1 %collective-permute-start.38 = (f32[128,1152]{1,0:T(8,128)S(1)}, f32[128,1152]{1,0:T(8,128)S(1)}, u32[]{:S(2)}, u32[]{:S(2)}) collective-permute-start(f32[128,1152]{1,0:T(8,128)S(1)} %get-tuple-element.181), channel_id=1, source_target_pairs={{0,1},{1,0},{2,3},{3,2},{4,5},{5,4},{6,7},{7,6},{8,9},{9,8},{10,11... | collective-permute-start | bytes 1769480 | tf_op jit(solution)/shard_map/grad_in_second1/ppermute | solution.py:44
  296.1 24.6 %collective-permute-start.37 = (bf16[128,1152]{1,0:T(8,128)(2,1)S(1)}, bf16[128,1152]{1,0:T(8,128)(2,1)S(1)}, u32[]{:S(2)}, u32[]{:S(2)}) collective-permute-start(bf16[128,1152]{1,0:T(8,128)(2,1)S(1)} %get-tuple-element.175.refs_0_), channel_id=1, source_target_pairs={{0,1},{1,0},{2,3},{3,2},{4,5},{5,4},{6,7},{7,6},{8,9},{9,8},{10,11... | collective-permute-start | bytes 884744 | tf_op jit(solution)/shard_map/grad_attended0/ppermute | solution.py:44
  328.0 111.0 %collective-permute-start.41 = (f32[2,288,4608]{2,1,0:T(8,128)}, f32[2,288,4608]{2,1,0:T(8,128)}, u32[]{:S(2)}, u32[]{:S(2)}) collective-permute-start(f32[2,288,4608]{2,1,0:T(8,128)} %get-tuple-element.184.refs_5_), channel_id=1, source_target_pairs={{0,8},{8,0},{16,24},{24,16},{1,9},{9,1},{17,25},{25,17},{2,10},{10... | collective-permute-start | bytes 31850504 | tf_op jit(solution)/shard_map/grad_feed_0/ppermute | solution.py:44
  345.5 12.9 %collective-permute-start.43 = (f32[4,8,128]{2,1,0:T(8,128)S(1)}, f32[4,8,128]{2,1,0:T(8,128)S(1)}, u32[]{:S(2)}, u32[]{:S(2)}) collective-permute-start(f32[4,8,128]{2,1,0:T(8,128)S(1)} %max.24), channel_id=1, source_target_pairs={{0,16},{8,24},{16,0},{24,8},{1,17},{9,25},{17,1},{25,9},{2,18},{10... | collective-permute-start | bytes 49160 | tf_op jit(solution)/shard_map/bounds/ppermute | solution.py:44
  347.6 36.2 %collective-permute-start.49 = (f32[128,1152]{1,0:T(8,128)}, f32[128,1152]{1,0:T(8,128)}, u32[]{:S(2)}, u32[]{:S(2)}) collective-permute-start(f32[128,1152]{1,0:T(8,128)} %copy-done.122), channel_id=1, source_target_pairs={{0,1},{1,0},{2,3},{3,2},{4,5},{5,4},{6,7},{7,6},{8,9},{9,8},{10,11... | collective-permute-start | bytes 1769480 | tf_op jit(solution)/shard_map/grad_in_second2/ppermute | solution.py:44
  356.4 22.1 %collective-permute-start.40 = (bf16[128,1152]{1,0:T(8,128)(2,1)}, bf16[128,1152]{1,0:T(8,128)(2,1)}, u32[]{:S(2)}, u32[]{:S(2)}) collective-permute-start(bf16[128,1152]{1,0:T(8,128)(2,1)} %get-tuple-element.193.refs_0_), channel_id=1, source_target_pairs={{0,1},{1,0},{2,3},{3,2},{4,5},{5,4},{6,7},{7,6},{8,9},{9,8},{10,11... | collective-permute-start | bytes 884744 | tf_op jit(solution)/shard_map/grad_attended1/ppermute | solution.py:44
  356.6 93.9 %collective-permute-start.35 = (bf16[384,1152]{1,0:T(8,128)(2,1)}, bf16[384,1152]{1,0:T(8,128)(2,1)}, u32[]{:S(2)}, u32[]{:S(2)}) collective-permute-start(bf16[384,1152]{1,0:T(8,128)(2,1)} %get-tuple-element.165), channel_id=1, source_target_pairs={{0,1},{1,0},{2,3},{3,2},{4,5},{5,4},{6,7},{7,6},{8,9},{9,8},{10,11... | collective-permute-start | bytes 2654216 | tf_op jit(solution)/shard_map/feed_out/ppermute | solution.py:44
  369.7 19.0 %all-to-all-start.4 = ((bf16[4,144,256]{2,1,0:T(8,128)(2,1)}), bf16[4,144,256]{2,1,0:T(8,128)(2,1)}, u32[]{:S(2)}, u32[]{:S(2)}) async-start(bf16[4,144,256]{2,1,0:T(8,128)(2,1)} %bitcast.184), calls=%async_computation.4 | async-start | bytes 589824 | tf_op jit(solution)/shard_map/grad_mixed0/all_to_all | solution.py:49
  387.6 20.9 %collective-permute-start.50 = (bf16[128,1152]{1,0:T(8,128)(2,1)}, bf16[128,1152]{1,0:T(8,128)(2,1)}, u32[]{:S(2)}, u32[]{:S(2)}) collective-permute-start(bf16[128,1152]{1,0:T(8,128)(2,1)} %get-tuple-element.210.refs_0_), channel_id=1, source_target_pairs={{0,1},{1,0},{2,3},{3,2},{4,5},{5,4},{6,7},{7,6},{8,9},{9,8},{10,11... | collective-permute-start | bytes 884744 | tf_op jit(solution)/shard_map/grad_attended2/ppermute | solution.py:44
  388.8 23.4 %all-to-all-start.6 = ((bf16[4,144,256]{2,1,0:T(8,128)(2,1)}), bf16[4,144,256]{2,1,0:T(8,128)(2,1)}, u32[]{:S(2)}, u32[]{:S(2)}) async-start(bf16[4,144,256]{2,1,0:T(8,128)(2,1)} %bitcast.185), calls=%async_computation.6 | async-start | bytes 589824 | tf_op jit(solution)/shard_map/grad_mixed1/all_to_all | solution.py:49
  412.1 21.4 %all-to-all-start.8 = ((bf16[4,144,256]{2,1,0:T(8,128)(2,1)}), bf16[4,144,256]{2,1,0:T(8,128)(2,1)S(1)}, u32[]{:S(2)}, u32[]{:S(2)}) async-start(bf16[4,144,256]{2,1,0:T(8,128)(2,1)} %bitcast.186), calls=%async_computation.8 | async-start | bytes 589824 | tf_op jit(solution)/shard_map/grad_mixed2/all_to_all | solution.py:49
  433.5 34.9 %all-to-all-start.5 = ((bf16[4,3,144,256]{3,2,1,0:T(8,128)(2,1)}), bf16[4,3,144,256]{3,2,1,0:T(8,128)(2,1)}, u32[]{:S(2)}, u32[]{:S(2)}) async-start(bf16[4,3,144,256]{3,2,1,0:T(8,128)(2,1)} %get-tuple-element.185), calls=%async_computation.5 | async-start | bytes 1769472 | tf_op jit(solution)/shard_map/grad_qkv0/all_to_all | solution.py:49
  445.8 77.1 %collective-permute-start.46 = (f16[1,288,4608]{2,1,0:T(8,128)(2,1)}, f16[1,288,4608]{2,1,0:T(8,128)(2,1)}, u32[]{:S(2)}, u32[]{:S(2)}) collective-permute-start(f16[1,288,4608]{2,1,0:T(8,128)(2,1)} %multiply_convert_fusion), channel_id=1, source_target_pairs={{0,16},{8,24},{16,0},{24,8},{1,17},{9,25},{17,1},{25,9},{2,18},{10... | collective-permute-start | bytes 7962632 | tf_op jit(solution)/shard_map/grad_feed_1/ppermute | solution.py:44
  450.6 44.3 %collective-permute-start.66 = (f32[2,288,576]{2,1,0:T(8,128)}, f32[2,288,576]{2,1,0:T(8,128)}, u32[]{:S(2)}, u32[]{:S(2)}) collective-permute-start(f32[2,288,576]{2,1,0:T(8,128)} %get-tuple-element.238), channel_id=1, source_target_pairs={{0,8},{8,0},{16,24},{24,16},{1,9},{9,1},{17,25},{25,17},{2,10},{10... | collective-permute-start | bytes 3981320 | tf_op jit(solution)/shard_map/grad_proj_0/ppermute | solution.py:44
  454.8 38.6 %collective-permute-start.36 = (bf16[384,1152]{1,0:T(8,128)(2,1)S(1)}, bf16[384,1152]{1,0:T(8,128)(2,1)S(1)}, u32[]{:S(2)}, u32[]{:S(2)}) collective-permute-start(bf16[384,1152]{1,0:T(8,128)(2,1)S(1)} %get-tuple-element.171.refs_0_), channel_id=1, source_target_pairs={{0,1},{1,0},{2,3},{3,2},{4,5},{5,4},{6,7},{7,6},{8,9},{9,8},{10,11... | collective-permute-start | bytes 2654216 | tf_op jit(solution)/shard_map/output/ppermute | solution.py:44
  468.4 42.7 %all-to-all-start.9 = ((bf16[4,3,144,256]{3,2,1,0:T(8,128)(2,1)}), bf16[4,3,144,256]{3,2,1,0:T(8,128)(2,1)S(1)}, u32[]{:S(2)}, u32[]{:S(2)}) async-start(bf16[4,3,144,256]{3,2,1,0:T(8,128)(2,1)} %copy-done.60), calls=%async_computation.9 | async-start | bytes 1769472 | tf_op jit(solution)/shard_map/grad_qkv2/all_to_all | solution.py:49
  484.2 13.6 %collective-permute-start.64 = (f32[2,288,432]{2,1,0:T(8,128)}, f32[2,288,432]{2,1,0:T(8,128)}, u32[]{:S(2)}, u32[]{:S(2)}) collective-permute-start(f32[2,288,432]{2,1,0:T(8,128)} %get-tuple-element.234), channel_id=1, source_target_pairs={{0,8},{8,0},{16,24},{24,16},{1,9},{9,1},{17,25},{25,17},{2,10},{10... | collective-permute-start | bytes 2985992 | tf_op jit(solution)/shard_map/grad_qkvw_0/ppermute | solution.py:44
  491.7 16.1 %collective-permute-start.39 = (f32[128,1152]{1,0:T(8,128)}, f32[128,1152]{1,0:T(8,128)}, u32[]{:S(2)}, u32[]{:S(2)}) collective-permute-start(f32[128,1152]{1,0:T(8,128)} %get-tuple-element.187), channel_id=1, source_target_pairs={{0,1},{1,0},{2,3},{3,2},{4,5},{5,4},{6,7},{7,6},{8,9},{9,8},{10,11... | collective-permute-start | bytes 1769480 | tf_op jit(solution)/shard_map/grad_in_first0/ppermute | solution.py:44
  497.7 53.3 %collective-permute-start.67 = (f32[1,288,576]{2,1,0:T(8,128)}, f32[1,288,576]{2,1,0:T(8,128)}, u32[]{:S(2)}, u32[]{:S(2)}) collective-permute-start(f32[1,288,576]{2,1,0:T(8,128)} %dynamic-slice_add_fusion), channel_id=1, source_target_pairs={{0,16},{8,24},{16,0},{24,8},{1,17},{9,25},{17,1},{25,9},{2,18},{10... | collective-permute-start | bytes 1990664 | tf_op jit(solution)/shard_map/grad_proj_1/ppermute | solution.py:44
  499.8 44.8 %collective-permute-start.65 = (f32[1,288,432]{2,1,0:T(8,128)}, f32[1,288,432]{2,1,0:T(8,128)}, u32[]{:S(2)}, u32[]{:S(2)}) collective-permute-start(f32[1,288,432]{2,1,0:T(8,128)} %dynamic-slice_add_fusion.1), channel_id=1, source_target_pairs={{0,16},{8,24},{16,0},{24,8},{1,17},{9,25},{17,1},{25,9},{2,18},{10... | collective-permute-start | bytes 1493000 | tf_op jit(solution)/shard_map/grad_qkvw_1/ppermute | solution.py:44
  510.2 47.1 %collective-permute-start.48 = (f32[128,1152]{1,0:T(8,128)}, f32[128,1152]{1,0:T(8,128)S(1)}, u32[]{:S(2)}, u32[]{:S(2)}) collective-permute-start(f32[128,1152]{1,0:T(8,128)} %get-tuple-element.189.refs_0_), channel_id=1, source_target_pairs={{0,1},{1,0},{2,3},{3,2},{4,5},{5,4},{6,7},{7,6},{8,9},{9,8},{10,11... | collective-permute-start | bytes 1769480 | tf_op jit(solution)/shard_map/grad_latent0/ppermute | solution.py:44
  511.1 27.2 %all-to-all-start.7 = ((bf16[4,3,144,256]{3,2,1,0:T(8,128)(2,1)}), bf16[4,3,144,256]{3,2,1,0:T(8,128)(2,1)S(1)}, u32[]{:S(2)}, u32[]{:S(2)}) async-start(bf16[4,3,144,256]{3,2,1,0:T(8,128)(2,1)} %copy-done.59), calls=%async_computation.7 | async-start | bytes 1769472 | tf_op jit(solution)/shard_map/grad_qkv1/all_to_all | solution.py:49
  521.8 41.5 %collective-permute-start.51 = (f32[128,1152]{1,0:T(8,128)}, f32[128,1152]{1,0:T(8,128)}, u32[]{:S(2)}, u32[]{:S(2)}) collective-permute-start(f32[128,1152]{1,0:T(8,128)} %get-tuple-element.216), channel_id=1, source_target_pairs={{0,1},{1,0},{2,3},{3,2},{4,5},{5,4},{6,7},{7,6},{8,9},{9,8},{10,11... | collective-permute-start | bytes 1769480 | tf_op jit(solution)/shard_map/grad_in_first2/ppermute | solution.py:44
  543.5 14.6 %collective-permute-start.47 = (f32[128,1152]{1,0:T(8,128)}, f32[128,1152]{1,0:T(8,128)}, u32[]{:S(2)}, u32[]{:S(2)}) collective-permute-start(f32[128,1152]{1,0:T(8,128)} %get-tuple-element.203), channel_id=1, source_target_pairs={{0,1},{1,0},{2,3},{3,2},{4,5},{5,4},{6,7},{7,6},{8,9},{9,8},{10,11... | collective-permute-start | bytes 1769480 | tf_op jit(solution)/shard_map/grad_in_first1/ppermute | solution.py:44
  546.8 50.6 %all-to-all-start.10 = ((f32[4,72,432]{2,1,0:T(8,128)}), f32[4,72,432]{2,1,0:T(8,128)}, u32[]{:S(2)}, u32[]{:S(2)}) async-start(f32[4,72,432]{2,1,0:T(8,128)} %bitcast.214), calls=%async_computation.10 | async-start | bytes 1179648 | tf_op jit(solution)/shard_map/grad_qkvw_c/all_to_all | solution.py:49
  553.5 24.1 %collective-permute-start.68 = (f32[72,576]{1,0:T(8,128)}, f32[72,576]{1,0:T(8,128)}, u32[]{:S(2)}, u32[]{:S(2)}) collective-permute-start(f32[72,576]{1,0:T(8,128)} %get-tuple-element.300), channel_id=1, source_target_pairs={{0,2},{2,4},{4,6},{6,0},{1,3},{3,5},{5,7},{7,1},{8,10},{10,12},{12... | collective-permute-start | bytes 497672 | tf_op jit(solution)/shard_map/grad_proj_ring/ppermute | solution.py:38
  555.5 40.3 %collective-permute-start.70 = (f32[72,576]{1,0:T(8,128)}, f32[72,576]{1,0:T(8,128)}, u32[]{:S(2)}, u32[]{:S(2)}) collective-permute-start(f32[72,576]{1,0:T(8,128)} %get-tuple-element.301), channel_id=1, source_target_pairs={{0,6},{2,0},{4,2},{6,4},{1,7},{3,1},{5,3},{7,5},{8,14},{10,8},{12,... | collective-permute-start | bytes 497672 | tf_op jit(solution)/shard_map/grad_proj_ring/ppermute | solution.py:38
  559.7 13.4 %collective-permute-start.52 = (f32[128,1152]{1,0:T(8,128)S(1)}, f32[128,1152]{1,0:T(8,128)S(1)}, u32[]{:S(2)}, u32[]{:S(2)}) collective-permute-start(f32[128,1152]{1,0:T(8,128)S(1)} %get-tuple-element.205.refs_1_), channel_id=1, source_target_pairs={{0,1},{1,0},{2,3},{3,2},{4,5},{5,4},{6,7},{7,6},{8,9},{9,8},{10,11... | collective-permute-start | bytes 1769480 | tf_op jit(solution)/shard_map/grad_latent1/ppermute | solution.py:44
  563.2 25.2 %collective-permute-start.71 = (f16[72,4608]{1,0:T(8,128)(2,1)}, f16[72,4608]{1,0:T(8,128)(2,1)}, u32[]{:S(2)}, u32[]{:S(2)}) collective-permute-start(f16[72,4608]{1,0:T(8,128)(2,1)} %fusion.1), channel_id=1, source_target_pairs={{0,2},{2,4},{4,6},{6,0},{1,3},{3,5},{5,7},{7,1},{8,10},{10,12},{12... | collective-permute-start | bytes 1990664 | tf_op jit(solution)/shard_map/grad_feed_ring/ppermute | solution.py:38
  578.6 17.1 %collective-permute-start.69 = (f32[72,576]{1,0:T(8,128)S(1)}, f32[72,576]{1,0:T(8,128)S(1)}, u32[]{:S(2)}, u32[]{:S(2)}) collective-permute-start(f32[72,576]{1,0:T(8,128)S(1)} %bitcast_add_fusion.2), channel_id=1, source_target_pairs={{0,2},{2,4},{4,6},{6,0},{1,3},{3,5},{5,7},{7,1},{8,10},{10,12},{12... | collective-permute-start | bytes 497672 | tf_op jit(solution)/shard_map/grad_proj_ring/ppermute | solution.py:38
  581.4 13.9 %collective-permute-start.55 = (f32[234,128]{1,0:T(8,128)S(1)}, f32[234,128]{1,0:T(8,128)S(1)}, u32[]{:S(2)}, u32[]{:S(2)}) collective-permute-start(f32[234,128]{1,0:T(8,128)S(1)} %bitcast_add_fusion.4), channel_id=1, source_target_pairs={{0,2},{2,0},{4,6},{6,4},{1,3},{3,1},{5,7},{7,5},{8,10},{10,8},{12,... | collective-permute-start | bytes 359432 | tf_op jit(solution)/shard_map/sums/ppermute | solution.py:44
  591.5 35.7 %collective-permute-start.72 = (f16[72,4608]{1,0:T(8,128)(2,1)}, f16[72,4608]{1,0:T(8,128)(2,1)}, u32[]{:S(2)}, u32[]{:S(2)}) collective-permute-start(f16[72,4608]{1,0:T(8,128)(2,1)} %get-tuple-element.296), channel_id=1, source_target_pairs={{0,2},{2,4},{4,6},{6,0},{1,3},{3,5},{5,7},{7,1},{8,10},{10,12},{12... | collective-permute-start | bytes 1990664 | tf_op jit(solution)/shard_map/grad_feed_ring/ppermute | solution.py:38
  591.7 35.5 %collective-permute-start.73 = (f16[72,4608]{1,0:T(8,128)(2,1)S(1)}, f16[72,4608]{1,0:T(8,128)(2,1)}, u32[]{:S(2)}, u32[]{:S(2)}) collective-permute-start(f16[72,4608]{1,0:T(8,128)(2,1)S(1)} %get-tuple-element.297), channel_id=1, source_target_pairs={{0,6},{2,0},{4,2},{6,4},{1,7},{3,1},{5,3},{7,5},{8,14},{10,8},{12,... | collective-permute-start | bytes 1990664 | tf_op jit(solution)/shard_map/grad_feed_ring/ppermute | solution.py:38
  595.3 30.8 %collective-permute-start.56 = (f32[234,128]{1,0:T(8,128)S(1)}, f32[234,128]{1,0:T(8,128)}, u32[]{:S(2)}, u32[]{:S(2)}) collective-permute-start(f32[234,128]{1,0:T(8,128)S(1)} %fusion.43), channel_id=1, source_target_pairs={{0,4},{2,6},{4,0},{6,2},{1,5},{3,7},{5,1},{7,3},{8,12},{10,14},{12... | collective-permute-start | bytes 359432 | tf_op jit(solution)/shard_map/sums/ppermute | solution.py:44
  604.8 25.9 %collective-permute-start.53 = (f32[128,1152]{1,0:T(8,128)S(1)}, f32[128,1152]{1,0:T(8,128)S(1)}, u32[]{:S(2)}, u32[]{:S(2)}) collective-permute-start(f32[128,1152]{1,0:T(8,128)S(1)} %get-tuple-element.218.refs_2_), channel_id=1, source_target_pairs={{0,1},{1,0},{2,3},{3,2},{4,5},{5,4},{6,7},{7,6},{8,9},{9,8},{10,11... | collective-permute-start | bytes 1769480 | tf_op jit(solution)/shard_map/grad_latent2/ppermute | solution.py:44
  (171 other events, 1358.5 us)
Sparse Core Ops, SparseCore 0:
  60.3 121.3 all-gather.2
  331.8 52.7 all-gather.4

commit v3 on v2

--- a/solution.py
+++ b/solution.py
@@ -58,12 +58,12 @@
     return lax.axis_size(axis).bit_length() - 1
 
 
-def ring_gather(x, name):
+def ring_gather(x, name, second=lambda x: x):
     size = lax.axis_size("ctx")
     blocks = [x] * size
     moving = x
     for step in range(1, size // 2 + 1):
-        moving = shift(moving, 1, name + "_right")
+        moving = shift(second(moving) if step == 2 else moving, 1, name + "_right")
         blocks[step] = moving
     moving = x
     for step in range(1, (size - 1) // 2 + 1):
@@ -200,16 +200,18 @@
         return lax.dynamic_index_in_dim(blocks, (own + offset) % size, 0, False)
 
     total = block(0)
+    hops = []
     for sign, reach in ((1, size // 2), (-1, (size - 1) // 2)):
         moving = None
         for distance in range(reach, 0, -1):
             term = block(sign * distance)
             if moving is not None:
                 term = term + moving
-            moving = higher(shift(lower(term, scale), sign, name + "_ring"), scale)
+            hops.append(shift(lower(term, scale), sign, name + "_ring"))
+            moving = higher(hops[-1], scale)
         if moving is not None:
             total = total + moving
-    return total
+    return total, hops
 
 
 def whole(shape):
@@ -953,10 +955,10 @@
 
     flat_latents = latents.reshape(items, here, model)
 
-    def swapped_ring(first, count, after=()):
+    def swapped_ring(first, count, after=(), second=lambda x: x):
         own, peer = halves(flat_latents, first, count, after)
         pairs = [own, peer]
-        for piece in ring_gather(own, "latent%d" % first)[1:]:
+        for piece in ring_gather(own, "latent%d" % first, second)[1:]:
             pairs += [piece, swap(piece, "latent%d_t" % first)]
         return pairs
 
@@ -986,14 +988,14 @@
 
     in_first, qkv_t = project(rings[0], 0, mods, 0, items, qkv_mine, bias_mine, None)
     qkv_ts = [qkv_t]
-    rings.append(swapped_ring(1, items - 1, [qkv_t]))
+    outs, logs = attend(qkv_t, here)
+    first_attended = exchange(outs, "mixed0"), logs
+    rings.append(swapped_ring(1, items - 1, [mods], lambda x: once_after(x, [logs])))
     latent = [(pairs[0], at) for pairs in rings for at in range(pairs[0].shape[0])]
 
-    hop = [rings[1][2], rings[1][-2]]
-    (proj_full,) = place(gather_stacked(once_after(proj_weight.T, hop), "proj"), [half_width])
-    proj_full = proj_full.T
+    proj_full = gather_rows(proj_weight.T, "proj_weights").T
     feed_shard = jnp.concatenate([up_weight, down_weight.T], 1)
-    feed_full = gather_rows(once_after(feed_shard, [mods]), "feed_weights")
+    feed_full = gather_rows(once_after(feed_shard, [logs, rings[1][2], rings[1][-2]]), "feed_weights")
     cots = halves(grad_out.reshape(items, here, model), 0, items)
 
     bias_proj = proj_bias.astype(F32).reshape(1, -1)
@@ -1011,10 +1013,12 @@
             )
             qkv_ts.append(qkv_t)
         qkv_t = qkv_ts[item]
-        outs, logs = attend(qkv_t, here)
-        mixed, own, peer = back_to_rows(
-            exchange(outs, "mixed%d" % item), proj_full, 0, True, mixed, item, items
-        )
+        if item:
+            outs, logs = attend(qkv_t, here)
+            came = exchange(outs, "mixed%d" % item)
+        else:
+            came, logs = first_attended
+        mixed, own, peer = back_to_rows(came, proj_full, 0, True, mixed, item, items)
         attended, residual, in_half = second(
             own, swap(peer, "attended%d" % item), bias_proj, *latent[item], mods, item
         )
@@ -1079,7 +1083,7 @@
         grad_feed, activated, 0, 768, hidden // 768, 2 * hidden, parts, [middles[0][3]]
     )
     feed_rows = reduce_rows(*parts, "grad_feed", scales)
-    grad_feed_weights = ring_reduce(feed_rows, "grad_feed", scales)
+    grad_feed_weights, feed_hops = ring_reduce(feed_rows, "grad_feed", scales)
 
     peers = swap(out_peer, "feed_out")
     gate_sums = []
@@ -1099,6 +1103,9 @@
         grad_blocks.append(
             exchange(grad_mixed.reshape(size_c, group, here), "grad_mixed%d" % item)
         )
+
+    def mark(x):
+        return x.reshape(-1, x.shape[-1])[:8, :128].astype(F32)
 
     input_grads, input_peers, mod_terms = [], [], []
     for item in range(items):
@@ -1116,7 +1123,7 @@
             exchange(blocks, "grad_qkv%d" % item),
             qkv_full,
             1,
-            after=[feed_rows] if item == 1 else [],
+            after=[feed_rows] if item == 0 else [],
         )
         grad_latent, sums_one = first_back(
             own,
@@ -1125,14 +1132,14 @@
             middles[item][0],
             mods,
             item,
-            input_peers[-1:],
+            [],
         )
         input_grads.append(grad_latent)
         input_peers.append(swap(grad_latent, "grad_latent%d" % item))
         mod_terms.append(jnp.concatenate([sums_one, middles[item][2][:3], gate_sums[item]], 0))
 
     proj_parts = outer(grad_attended, mixed, 1, half_width, 0, half_width, [None, None])
-    grad_proj = ring_reduce(reduce_rows(*proj_parts, "grad_proj"), "grad_proj").T
+    grad_proj = ring_reduce(reduce_rows(*proj_parts, "grad_proj"), "grad_proj")[0].T
     grad_qkv = grad_qkv.reshape(3 * group, -1)
     qkv_rows = reduce_rows(*long_outer(in_first, grad_qkv, items), "grad_qkvw")
     grad_qkv_weight = (

time: 677 us -> 633 us (0.935)
  waiting for transfers between devices: 185 us -> 164 us
  starting transfers between devices: 134 us -> 116 us
    ppermute x15 -> x12, waiting for transfers between devices: 83 us -> 32.9 us  [shift(): return lax.ppermute(x, 'ctx', [(i, (i + k) % size) for i in range(size)])]
    all_to_all x11, waiting for transfers between devices: 8.43 us -> 27.2 us  [exchange(): return lax.all_to_all(x, 'ctx', 0, 0)]
    ppermute x15 -> x12, starting transfers between devices: 28.9 us -> 18.6 us  [shift(): return lax.ppermute(x, 'ctx', [(i, (i + k) % size) for i in range(size)])]
    ppermute x59 -> x56, waiting for transfers between devices: 93.4 us -> 103 us  [flip(): return lax.ppermute(x, axis, [(i, i ^ 1 << bit) for i in range(size)])]
    ppermute x59 -> x56, starting transfers between devices: 49.7 us -> 46.6 us  [flip(): return lax.ppermute(x, axis, [(i, i ^ 1 << bit) for i in range(size)])]
    unnamed x305 -> x289, local copies, waits for them, and re-layouts: 72.9 us -> 73.2 us
  transfers between devices with their start and end apart: 87 -> 82, of which waited for: 31 -> 25; matrix products, arithmetic and copies ran while one was open for 11% -> 12% of each run, Pallas kernels for 26% -> 27%
where the time goes in v3:
time: 633 us; the launch traced here: 623 us
  Pallas kernels  177 us (28%)
  waiting for transfers between devices  164 us (26%)
  starting transfers between devices  116 us (18%)
  local copies, waits for them, and re-layouts  98.6 us (16%)
  other arithmetic  46.6 us (7%)
  between operations  18.6 us (3%)
    pallas_call x47, Pallas kernels, slab_call(): pl.pallas_call(run, in_specs=in_specs + [ANYWHERE] * more, input_output_a...  175 us
    ppermute x56, waiting for transfers between devices, flip(): return lax.ppermute(x, axis, [(i, i ^ 1 << bit) for i in range(size)])  103 us
    unnamed x289, local copies, waits for them, and re-layouts  73.2 us
    all_to_all x11, starting transfers between devices, exchange(): return lax.all_to_all(x, 'ctx', 0, 0)  51.1 us
    ppermute x56, starting transfers between devices, flip(): return lax.ppermute(x, axis, [(i, i ^ 1 << bit) for i in range(size)])  46.6 us
    ppermute x12, waiting for transfers between devices, shift(): return lax.ppermute(x, 'ctx', [(i, (i + k) % size) for i in range(size)])  32.9 us
    all_to_all x11, waiting for transfers between devices, exchange(): return lax.all_to_all(x, 'ctx', 0, 0)  27.2 us
    ppermute x12, starting transfers between devices, shift(): return lax.ppermute(x, 'ctx', [(i, (i + k) % size) for i in range(size)])  18.6 us
  transfers between devices with their start and end apart: 82, of which 25 were waited for; matrix products, arithmetic and copies ran while one was open for 12% of the time, Pallas kernels for 27%

profile of v3, /device:TPU:0, one launch (start us, length us, event | category | flops | bytes accessed | tf_op | source)
XLA Modules:
  0.0 622.8 jit_solution(5646682251291228830)
XLA Ops:
  10.7 4.6 collective-permute-start.3
  20.0 2.7 collective-permute-done.3.refs_2_.refs_6_
  22.7 6.9 %collective-permute-done.2.refs_1_.refs_2_ = bf16[1,128,1152]{2,1,0:T(8,128)(2,1)} collective-permute-done((bf16[1,128,1152]{2,1,0:T(8,128)(2,1)S(1)}, bf16[1,128,1152]{2,1,0:T(8,128)(2,1)}, u32[]{:S(2)}, u32[]{:S(2)}) %collective-permute-start.2) | collective-permute-done | bytes 294944 | tf_op jit(solution)/shard_map/latent0_right/ppermute | solution.py:38
  31.5 3.2 collective-permute-done.4
  36.5 3.6 all-to-all-start
  43.3 9.0 %all-to-all-done.refs_1_.refs_0_ = bf16[4,72,432]{2,1,0:T(8,128)(2,1)S(1)} async-done(((bf16[4,72,432]{2,1,0:T(8,128)(2,1)}), bf16[4,72,432]{2,1,0:T(8,128)(2,1)S(1)}, u32[]{:S(2)}, u32[]{:S(2)}) %all-to-all-start) | async-done | bytes 248864 | tf_op jit(solution)/shard_map/qkv_c/all_to_all | solution.py:49
  56.1 9.2 %collective-permute-done.7 = f32[3,3456]{1,0:T(4,128)S(1)} collective-permute-done((f32[3,3456]{1,0:T(4,128)S(1)}, f32[3,3456]{1,0:T(4,128)S(1)}, u32[]{:S(2)}, u32[]{:S(2)}) %collective-permute-start.7) | collective-permute-done | bytes 41504 | tf_op jit(solution)/shard_map/mod_c/ppermute | solution.py:44
  75.4 2.7 shard_map.232
  81.0 3.3 collective-permute-done.11.refs_3_
  84.2 5.9 collective-permute-done.13.refs_5_
  93.0 4.9 shard_map.233
  97.9 7.2 %shard_map.234 = (bf16[4,144,256]{2,1,0:T(8,128)(2,1)S(1)}, f32[2,1024]{1,0:T(2,128)S(1)}) custom-call(bf16[3,144,1024]{2,1,0:T(8,128)(2,1)S(1)} %bitcast.189, bf16[3,144,1024]{2,1,0:T(8,128)(2,1)S(1)} %bitcast.190, bf16[3,144,1024]{2,1,0:T(8,128)(2,1)S(1)} %bitcast.191), custom_call_target="tpu_custom_call" | custom-call | flops 3355443200 | bytes 1179648 | tf_op jit(solution)/shard_map/pallas_call | solution.py:249
  109.0 23.4 %collective-permute-done.18.refs_4_ = bf16[2,128,1152]{2,1,0:T(8,128)(2,1)S(1)} collective-permute-done((bf16[2,128,1152]{2,1,0:T(8,128)(2,1)S(1)}, bf16[2,128,1152]{2,1,0:T(8,128)(2,1)S(1)}, u32[]{:S(2)}, u32[]{:S(2)}) %collective-permute-start.18) | collective-permute-done | bytes 589856 | tf_op jit(solution)/shard_map/latent1_right/ppermute | solution.py:38
  132.4 4.3 all-to-all-start.3
  136.7 10.6 %collective-permute-done.19.refs_5_ = bf16[2,128,1152]{2,1,0:T(8,128)(2,1)} collective-permute-done((bf16[2,128,1152]{2,1,0:T(8,128)(2,1)S(1)}, bf16[2,128,1152]{2,1,0:T(8,128)(2,1)}, u32[]{:S(2)}, u32[]{:S(2)}) %collective-permute-start.19) | collective-permute-done | bytes 589856 | tf_op jit(solution)/shard_map/latent1_t/ppermute | solution.py:44
  147.3 4.9 shard_map.236
  152.2 7.2 %shard_map.239 = (bf16[4,144,256]{2,1,0:T(8,128)(2,1)S(1)}, f32[2,1024]{1,0:T(2,128)S(1)}) custom-call(bf16[3,144,1024]{2,1,0:T(8,128)(2,1)S(1)} %bitcast.183, bf16[3,144,1024]{2,1,0:T(8,128)(2,1)S(1)} %bitcast.184, bf16[3,144,1024]{2,1,0:T(8,128)(2,1)S(1)} %bitcast.185), custom_call_target="tpu_custom_call" | custom-call | flops 3355443200 | bytes 1179648 | tf_op jit(solution)/shard_map/pallas_call | solution.py:249
  161.1 4.7 all-to-all-start.2
  165.9 4.9 shard_map.237
  173.6 2.5 shard_map.240
  177.4 5.6 all-to-all-done.2.refs_0_
  183.1 2.6 shard_map.241
  187.5 7.2 %shard_map.238 = (bf16[4,144,256]{2,1,0:T(8,128)(2,1)S(1)}, f32[2,1024]{1,0:T(2,128)S(1)}) custom-call(bf16[3,144,1024]{2,1,0:T(8,128)(2,1)S(1)} %bitcast.177, bf16[3,144,1024]{2,1,0:T(8,128)(2,1)S(1)} %bitcast.178, bf16[3,144,1024]{2,1,0:T(8,128)(2,1)S(1)} %bitcast.179), custom_call_target="tpu_custom_call" | custom-call | flops 3355443200 | bytes 1179648 | tf_op jit(solution)/shard_map/pallas_call | solution.py:249
  195.4 4.1 all-to-all-start.1
  206.7 5.4 all-to-all-done.1.refs_0_
  212.0 2.6 shard_map.242
  224.5 12.4 %shard_map.248 = (bf16[768,1152]{1,0:T(8,128)(2,1)}, bf16[768,1152]{1,0:T(8,128)(2,1)}, bf16[768,2304]{1,0:T(8,128)(2,1)}, bf16[768,2304]{1,0:T(8,128)(2,1)}, f3...) custom-call(bf16[128,1152]{1,0:T(8,128)(2,1)} %get-tuple-element.151, ...), custom_call_target="tpu_custom_call" | custom-call | flops 5435817984 | bytes 12976128 | tf_op jit(solution)/shard_map/pallas_call | solution.py:249
  242.0 12.0 %shard_map.249 = (bf16[768,1152]{1,0:T(8,128)(2,1)}, bf16[768,1152]{1,0:T(8,128)(2,1)}, bf16[768,2304]{1,0:T(8,128)(2,1)}, bf16[768,2304]{1,0:T(8,128)(2,1)}, f3...) custom-call(bf16[128,1152]{1,0:T(8,128)(2,1)} %get-tuple-element.148, ...), custom_call_target="tpu_custom_call", output_to_operand_aliasing={{0}: (8, {}), {1}: (9, {}), {2}: (10, {}), {3}: (11, {}), {... | custom-call | flops 5435817984 | bytes 12976128 | tf_op jit(solution)/shard_map/pallas_call | solution.py:249
  259.0 11.8 %shard_map.250 = (bf16[768,1152]{1,0:T(8,128)(2,1)}, bf16[768,1152]{1,0:T(8,128)(2,1)}, bf16[768,2304]{1,0:T(8,128)(2,1)}, bf16[768,2304]{1,0:T(8,128)(2,1)}, f3...) custom-call(bf16[128,1152]{1,0:T(8,128)(2,1)S(1)} %get-tuple-element, ...), custom_call_target="tpu_custom_call", output_to_operand_aliasing={{0}: (8, {}), {1}: (9, {}), {2}: (10, {}), {3}: (11, {}), {... | custom-call | flops 5435817984 | bytes 12976128 | tf_op jit(solution)/shard_map/pallas_call | solution.py:249
  276.2 7.2 %shard_map.257 = (f32[2,288,4608]{2,1,0:T(8,128)}, f32[2,288,4608]{2,1,0:T(8,128)}) custom-call(bf16[768,1152]{1,0:T(8,128)(2,1)S(1)} %copy-done.19, bf16[768,2304]{1,0:T(8,128)(2,1)S(1)} %copy-done.6, f32[128,1152]{1,0:T(8,128)S(1)} %collective-permute-done.32.refs_2_.refs_1_), custom_call_target="tpu_custom_call" | custom-call | flops 4076863488 | bytes 14155776 | tf_op jit(solution)/shard_map/pallas_call | solution.py:249
  283.5 7.3 %shard_map.258 = (f32[2,288,4608]{2,1,0:T(8,128)}, f32[2,288,4608]{2,1,0:T(8,128)}) custom-call(bf16[768,1152]{1,0:T(8,128)(2,1)S(1)} %copy-done.5, bf16[768,2304]{1,0:T(8,128)(2,1)S(1)} %copy-done.4, f32[2,288,4608]{2,1,0:T(8,128)} %get-tuple-element.182.refs_2_, ...), custom_call_target="tpu_custom_call", output_to_operand_aliasing={{0}: (2, {}), {1}: (3, {})} | custom-call | flops 4076863488 | bytes 14155776 | tf_op jit(solution)/shard_map/pallas_call | solution.py:249
  296.4 11.2 %collective-permute-done.34 = f32[4,8,128]{2,1,0:T(8,128)} collective-permute-done((f32[4,8,128]{2,1,0:T(8,128)}, f32[4,8,128]{2,1,0:T(8,128)}, u32[]{:S(2)}, u32[]{:S(2)}) %collective-permute-start.34) | collective-permute-done | bytes 16416 | tf_op jit(solution)/shard_map/bounds/ppermute | solution.py:44
  325.5 2.4 collective-permute-done.36
  333.8 4.2 all-to-all-start.4
  347.8 2.4 shard_map.268
  351.6 5.1 all-to-all-start.6
  357.9 12.0 %shard_map.259 = (bf16[3,144,3072]{2,1,0:T(8,128)(2,1)S(1)}, bf16[4,3,144,256]{3,2,1,0:T(8,128)(2,1)}) custom-call(bf16[3,144,1024]{2,1,0:T(8,128)(2,1)S(1)} %bitcast.192, bf16[3,144,1024]{2,1,0:T(8,128)(2,1)S(1)} %bitcast.193, bf16[3,144,1024]{2,1,0:T(8,128)(2,1)S(1)} %bitcast.194, f32[2,1024]{1,0:T(2,128)S(1)} %get-tuple-element.131.refs_1_.refs_3_, ...), custom_call_target="tpu_custom_call" | custom-call | flops 8388608000 | bytes 2359296 | tf_op jit(solution)/shard_map/pallas_call | solution.py:249
  375.0 5.1 all-to-all-start.8
  383.0 11.8 %shard_map.265 = (bf16[3,144,3072]{2,1,0:T(8,128)(2,1)S(1)}, bf16[4,3,144,256]{3,2,1,0:T(8,128)(2,1)}) custom-call(bf16[3,144,1024]{2,1,0:T(8,128)(2,1)S(1)} %bitcast.186, bf16[3,144,1024]{2,1,0:T(8,128)(2,1)S(1)} %bitcast.187, bf16[3,144,1024]{2,1,0:T(8,128)(2,1)S(1)} %bitcast.188, f32[2,1024]{1,0:T(2,128)S(1)} %copy-done.121, ...), custom_call_target="tpu_custom_call", output_to_operand_aliasing={{0}: (5, {})} | custom-call | flops 8388608000 | bytes 2359296 | tf_op jit(solution)/shard_map/pallas_call | solution.py:249
  396.3 5.4 all-to-all-start.7
  401.8 6.8 %multiply_convert_fusion = f16[1,288,4608]{2,1,0:T(8,128)(2,1)} fusion(f32[2,288,4608]{2,1,0:T(8,128)} %collective-permute-done.33, s32[]{:T(128)S(6)} %select_n.122, f32[2,288,4608]{2,1,0:T(8,128)} %get-tuple-element.186, f32[4608]{0:T(1024)S(1)} %copy-done.128), kind=kLoop, calls=%fused_computation.2 | loop fusion | flops 3981312 | bytes 13289476 | tf_op jit(solution)/shard_map/convert_element_type | solution.py:173
  409.5 2.8 shard_map.275
  417.7 9.9 %shard_map.270 = (bf16[3,144,3072]{2,1,0:T(8,128)(2,1)S(1)}, bf16[4,3,144,256]{3,2,1,0:T(8,128)(2,1)S(1)}) custom-call(bf16[3,144,1024]{2,1,0:T(8,128)(2,1)S(1)} %bitcast.180, bf16[3,144,1024]{2,1,0:T(8,128)(2,1)S(1)} %bitcast.181, bf16[3,144,1024]{2,1,0:T(8,128)(2,1)S(1)} %bitcast.182, f32[2,1024]{1,0:T(2,128)S(1)} %copy-done.119, ...), custom_call_target="tpu_custom_call", output_to_operand_aliasing={{0}: (5, {})} | custom-call | flops 8388608000 | bytes 2359296 | tf_op jit(solution)/shard_map/pallas_call | solution.py:249
  430.1 5.1 all-to-all-start.9
  437.0 7.9 %shard_map.274 = (f32[2,288,432]{2,1,0:T(8,128)}, f32[2,288,432]{2,1,0:T(8,128)S(1)}) custom-call(bf16[3072,1152]{1,0:T(8,128)(2,1)} %get-tuple-element.232.refs_0_, bf16[432,3072]{1,0:T(8,128)(2,1)S(1)} %bitcast.169), custom_call_target="tpu_custom_call" | custom-call | flops 3057647616 | bytes 9732096 | tf_op jit(solution)/shard_map/pallas_call | solution.py:249
  449.1 3.4 shard_map.266
  462.7 6.7 %collective-permute-done.41.refs_1_ = f32[128,1152]{1,0:T(8,128)} collective-permute-done((f32[128,1152]{1,0:T(8,128)}, f32[128,1152]{1,0:T(8,128)}, u32[]{:S(2)}, u32[]{:S(2)}) %collective-permute-start.41) | collective-permute-done | bytes 589856 | tf_op jit(solution)/shard_map/grad_in_first1/ppermute | solution.py:44
  472.0 5.3 all-to-all-start.5
  483.7 8.3 %multiply_add_fusion = f32[1,288,4608]{2,1,0:T(8,128)} fusion(f16[1,288,4608]{2,1,0:T(8,128)(2,1)} %collective-permute-done.38, f32[2,288,4608]{2,1,0:T(8,128)} %collective-permute-done.33, s32[]{:T(128)S(6)} %select_n.121, f32[2,288,4608]{2,1,0:T(8,128)} %get-tuple-element.186, f32[4608]{0:T(1024)S(1)} %broadcast_divide_fusion), kind=kLoop, calls=%fused_computation.1 | loop fusion | flops 5308416 | bytes 18597892 | tf_op jit(solution)/shard_map/add | solution.py:192
  492.0 7.1 %all-to-all-done.5.refs_0_ = bf16[4,3,144,256]{3,2,1,0:T(8,128)(2,1)S(1)} async-done(((bf16[4,3,144,256]{3,2,1,0:T(8,128)(2,1)}), bf16[4,3,144,256]{3,2,1,0:T(8,128)(2,1)S(1)}, u32[]{:S(2)}, u32[]{:S(2)}) %all-to-all-start.5) | async-done | bytes 884768 | tf_op jit(solution)/shard_map/grad_qkv0/all_to_all | solution.py:49
  507.7 4.2 all-to-all-start.10
  511.9 2.4 add_add_fusion
  516.2 2.8 collective-permute-done.39.refs_1_
  523.2 3.8 collective-permute-start.64
  531.4 16.4 %collective-permute-done.49 = f32[234,128]{1,0:T(8,128)S(1)} collective-permute-done((f32[234,128]{1,0:T(8,128)S(1)}, f32[234,128]{1,0:T(8,128)S(1)}, u32[]{:S(2)}, u32[]{:S(2)}) %collective-permute-start.49) | collective-permute-done | bytes 119840 | tf_op jit(solution)/shard_map/sums/ppermute | solution.py:44
  548.0 11.5 %collective-permute-done.50 = f32[234,128]{1,0:T(8,128)S(1)} collective-permute-done((f32[234,128]{1,0:T(8,128)S(1)}, f32[234,128]{1,0:T(8,128)S(1)}, u32[]{:S(2)}, u32[]{:S(2)}) %collective-permute-start.50) | collective-permute-done | bytes 119840 | tf_op jit(solution)/shard_map/sums/ppermute | solution.py:44
  561.2 2.3 copy.96
  563.5 2.5 copy.97
  566.0 2.5 reshape.335
  571.8 3.3 fusion.3
  575.4 3.9 collective-permute-start.67
  579.2 9.4 %collective-permute-done.45.refs_3_ = f32[128,1152]{1,0:T(8,128)S(1)} collective-permute-done((f32[128,1152]{1,0:T(8,128)S(1)}, f32[128,1152]{1,0:T(8,128)S(1)}, u32[]{:S(2)}, u32[]{:S(2)}) %collective-permute-start.45) | collective-permute-done | bytes 589856 | tf_op jit(solution)/shard_map/grad_latent0/ppermute | solution.py:44
  588.6 3.1 shard_map.273
  602.4 4.3 collective-permute-done.55
  (551 shorter events, 205.1 us)
Async XLA Ops:
  7.2 164.5 %all-gather.4.cloned.1.call-start = ((), (), s32[]{:S(2)}) async-start(), calls=%async_computation.11 | async-start | bytes 1566720 | tf_op jit(solution)/shard_map/proj_weights/all_gather | solution.py:54
  10.7 12.0 %collective-permute-start.3 = (bf16[1,128,1152]{2,1,0:T(8,128)(2,1)S(1)}, bf16[1,128,1152]{2,1,0:T(8,128)(2,1)}, u32[]{:S(2)}, u32[]{:S(2)}) collective-permute-start(bf16[1,128,1152]{2,1,0:T(8,128)(2,1)S(1)} %get-tuple-element.126.refs_0_.refs_3_.refs_2_), channel_id=1, source_target_pairs={{0,6},{2,0},{4,2},{6,4},{1,7},{3,1},{5,3},{7,5},{8,14},{10,8},{12,... | collective-permute-start | bytes 884744 | tf_op jit(solution)/shard_map/latent0_left/ppermute | solution.py:38
  15.3 14.3 %collective-permute-start.2 = (bf16[1,128,1152]{2,1,0:T(8,128)(2,1)S(1)}, bf16[1,128,1152]{2,1,0:T(8,128)(2,1)}, u32[]{:S(2)}, u32[]{:S(2)}) collective-permute-start(bf16[1,128,1152]{2,1,0:T(8,128)(2,1)S(1)} %get-tuple-element.126.refs_0_.refs_3_.refs_2_), channel_id=1, source_target_pairs={{0,2},{2,4},{4,6},{6,0},{1,3},{3,5},{5,7},{7,1},{8,10},{10,12},{12... | collective-permute-start | bytes 884744 | tf_op jit(solution)/shard_map/latent0_right/ppermute | solution.py:38
  36.5 15.8 %all-to-all-start = ((bf16[4,72,432]{2,1,0:T(8,128)(2,1)}), bf16[4,72,432]{2,1,0:T(8,128)(2,1)S(1)}, u32[]{:S(2)}, u32[]{:S(2)}) async-start(bf16[4,72,432]{2,1,0:T(8,128)(2,1)} %copy.88), calls=%async_computation | async-start | bytes 589824 | tf_op jit(solution)/shard_map/qkv_c/all_to_all | solution.py:49
  40.1 183.3 %all-gather.6.cloned.1.call-start = ((), (), s32[]{:S(2)}) async-start(), calls=%async_computation.12 | async-start | bytes 11280384 | tf_op jit(solution)/shard_map/feed_weights/all_gather | solution.py:54
  40.1 13.7 %collective-permute-start.6 = (f32[3,3456]{1,0:T(4,128)S(1)}, f32[3,3456]{1,0:T(4,128)S(1)}, u32[]{:S(2)}, u32[]{:S(2)}) collective-permute-start(f32[3,3456]{1,0:T(4,128)S(1)} %fusion.9), channel_id=1, source_target_pairs={{0,2},{2,0},{4,6},{6,4},{1,3},{3,1},{5,7},{7,5},{8,10},{10,8},{12,... | collective-permute-start | bytes 124424 | tf_op jit(solution)/shard_map/mod_c/ppermute | solution.py:44
  52.3 14.7 %collective-permute-start.15 = (bf16[4,72,432]{2,1,0:T(8,128)(2,1)S(1)}, bf16[4,72,432]{2,1,0:T(8,128)(2,1)}, u32[]{:S(2)}, u32[]{:S(2)}) collective-permute-start(bf16[4,72,432]{2,1,0:T(8,128)(2,1)S(1)} %all-to-all-done.refs_1_.refs_0_), channel_id=1, source_target_pairs={{0,16},{8,24},{16,0},{24,8},{1,17},{9,25},{17,1},{25,9},{2,18},{10... | collective-permute-start | bytes 746504 | tf_op jit(solution)/shard_map/qkv_1/ppermute | solution.py:44
  54.0 18.0 %collective-permute-start.12 = (bf16[1,128,1152]{2,1,0:T(8,128)(2,1)}, bf16[1,128,1152]{2,1,0:T(8,128)(2,1)}, u32[]{:S(2)}, u32[]{:S(2)}) collective-permute-start(bf16[1,128,1152]{2,1,0:T(8,128)(2,1)} %collective-permute-done.2.refs_1_.refs_2_), channel_id=1, source_target_pairs={{0,2},{2,4},{4,6},{6,0},{1,3},{3,5},{5,7},{7,1},{8,10},{10,12},{12... | collective-permute-start | bytes 884744 | tf_op jit(solution)/shard_map/latent0_right/ppermute | solution.py:38
  56.1 15.9 %collective-permute-start.16 = (bf16[4,72,432]{2,1,0:T(8,128)(2,1)S(1)}, bf16[4,72,432]{2,1,0:T(8,128)(2,1)}, u32[]{:S(2)}, u32[]{:S(2)}) collective-permute-start(bf16[4,72,432]{2,1,0:T(8,128)(2,1)S(1)} %all-to-all-done.refs_1_.refs_0_), channel_id=1, source_target_pairs={{0,8},{8,0},{16,24},{24,16},{1,9},{9,1},{17,25},{25,17},{2,10},{10... | collective-permute-start | bytes 746504 | tf_op jit(solution)/shard_map/qkv_0/ppermute | solution.py:44
  67.8 13.2 %collective-permute-start.14 = (bf16[1,128,1152]{2,1,0:T(8,128)(2,1)}, bf16[1,128,1152]{2,1,0:T(8,128)(2,1)}, u32[]{:S(2)}, u32[]{:S(2)}) collective-permute-start(bf16[1,128,1152]{2,1,0:T(8,128)(2,1)} %collective-permute-done.3.refs_2_.refs_6_), channel_id=1, source_target_pairs={{0,1},{1,0},{2,3},{3,2},{4,5},{5,4},{6,7},{7,6},{8,9},{9,8},{10,11... | collective-permute-start | bytes 884744 | tf_op jit(solution)/shard_map/latent0_t/ppermute | solution.py:44
  69.4 14.9 %collective-permute-start.11 = (bf16[1,128,1152]{2,1,0:T(8,128)(2,1)}, bf16[1,128,1152]{2,1,0:T(8,128)(2,1)}, u32[]{:S(2)}, u32[]{:S(2)}) collective-permute-start(bf16[1,128,1152]{2,1,0:T(8,128)(2,1)} %collective-permute-done.2.refs_1_.refs_2_), channel_id=1, source_target_pairs={{0,1},{1,0},{2,3},{3,2},{4,5},{5,4},{6,7},{7,6},{8,9},{9,8},{10,11... | collective-permute-start | bytes 884744 | tf_op jit(solution)/shard_map/latent0_t/ppermute | solution.py:44
  72.0 33.9 %collective-permute-start.20 = (bf16[2,128,1152]{2,1,0:T(8,128)(2,1)S(1)}, bf16[2,128,1152]{2,1,0:T(8,128)(2,1)S(1)}, u32[]{:S(2)}, u32[]{:S(2)}) collective-permute-start(bf16[2,128,1152]{2,1,0:T(8,128)(2,1)S(1)} %get-tuple-element.127.refs_0_.refs_3_.refs_2_), channel_id=1, source_target_pairs={{0,6},{2,0},{4,2},{6,4},{1,7},{3,1},{5,3},{7,5},{8,14},{10,8},{12,... | collective-permute-start | bytes 1769480 | tf_op jit(solution)/shard_map/latent1_left/ppermute | solution.py:38
  72.0 33.9 %collective-permute-start.9 = (bf16[2,128,1152]{2,1,0:T(8,128)(2,1)S(1)}, bf16[2,128,1152]{2,1,0:T(8,128)(2,1)S(1)}, u32[]{:S(2)}, u32[]{:S(2)}) collective-permute-start(bf16[2,128,1152]{2,1,0:T(8,128)(2,1)S(1)} %get-tuple-element.127.refs_0_.refs_3_.refs_2_), channel_id=1, source_target_pairs={{0,2},{2,4},{4,6},{6,0},{1,3},{3,5},{5,7},{7,1},{8,10},{10,12},{12... | collective-permute-start | bytes 1769480 | tf_op jit(solution)/shard_map/latent1_right/ppermute | solution.py:38
  74.0 16.2 %collective-permute-start.13 = (bf16[1,128,1152]{2,1,0:T(8,128)(2,1)}, bf16[1,128,1152]{2,1,0:T(8,128)(2,1)}, u32[]{:S(2)}, u32[]{:S(2)}) collective-permute-start(bf16[1,128,1152]{2,1,0:T(8,128)(2,1)} %collective-permute-done.12.refs_4_), channel_id=1, source_target_pairs={{0,1},{1,0},{2,3},{3,2},{4,5},{5,4},{6,7},{7,6},{8,9},{9,8},{10,11... | collective-permute-start | bytes 884744 | tf_op jit(solution)/shard_map/latent0_t/ppermute | solution.py:44
  106.8 25.5 %collective-permute-start.18 = (bf16[2,128,1152]{2,1,0:T(8,128)(2,1)S(1)}, bf16[2,128,1152]{2,1,0:T(8,128)(2,1)S(1)}, u32[]{:S(2)}, u32[]{:S(2)}) collective-permute-start(bf16[2,128,1152]{2,1,0:T(8,128)(2,1)S(1)} %shard_map.235), channel_id=1, source_target_pairs={{0,2},{2,4},{4,6},{6,0},{1,3},{3,5},{5,7},{7,1},{8,10},{10,12},{12... | collective-permute-start | bytes 1769480 | tf_op jit(solution)/shard_map/latent1_right/ppermute | solution.py:38
  106.9 29.8 %collective-permute-start.21 = (bf16[2,128,1152]{2,1,0:T(8,128)(2,1)S(1)}, bf16[2,128,1152]{2,1,0:T(8,128)(2,1)}, u32[]{:S(2)}, u32[]{:S(2)}) collective-permute-start(bf16[2,128,1152]{2,1,0:T(8,128)(2,1)S(1)} %collective-permute-done.20.refs_6_.refs_3_), channel_id=1, source_target_pairs={{0,1},{1,0},{2,3},{3,2},{4,5},{5,4},{6,7},{7,6},{8,9},{9,8},{10,11... | collective-permute-start | bytes 1769480 | tf_op jit(solution)/shard_map/latent1_t/ppermute | solution.py:44
  107.5 29.2 %collective-permute-start.10 = (bf16[2,128,1152]{2,1,0:T(8,128)(2,1)S(1)}, bf16[2,128,1152]{2,1,0:T(8,128)(2,1)}, u32[]{:S(2)}, u32[]{:S(2)}) collective-permute-start(bf16[2,128,1152]{2,1,0:T(8,128)(2,1)S(1)} %collective-permute-done.9.refs_0_.refs_2_), channel_id=1, source_target_pairs={{0,1},{1,0},{2,3},{3,2},{4,5},{5,4},{6,7},{7,6},{8,9},{9,8},{10,11... | collective-permute-start | bytes 1769480 | tf_op jit(solution)/shard_map/latent1_t/ppermute | solution.py:44
  132.4 15.0 %collective-permute-start.19 = (bf16[2,128,1152]{2,1,0:T(8,128)(2,1)S(1)}, bf16[2,128,1152]{2,1,0:T(8,128)(2,1)}, u32[]{:S(2)}, u32[]{:S(2)}) collective-permute-start(bf16[2,128,1152]{2,1,0:T(8,128)(2,1)S(1)} %collective-permute-done.18.refs_4_), channel_id=1, source_target_pairs={{0,1},{1,0},{2,3},{3,2},{4,5},{5,4},{6,7},{7,6},{8,9},{9,8},{10,11... | collective-permute-start | bytes 1769480 | tf_op jit(solution)/shard_map/latent1_t/ppermute | solution.py:44
  132.4 28.8 %all-to-all-start.3 = ((bf16[4,144,256]{2,1,0:T(8,128)(2,1)}), bf16[4,144,256]{2,1,0:T(8,128)(2,1)}, u32[]{:S(2)}, u32[]{:S(2)}) async-start(bf16[4,144,256]{2,1,0:T(8,128)(2,1)} %copy-done.88), calls=%async_computation.3 | async-start | bytes 589824 | tf_op jit(solution)/shard_map/mixed0/all_to_all | solution.py:49
  161.1 21.9 %all-to-all-start.2 = ((bf16[4,144,256]{2,1,0:T(8,128)(2,1)}), bf16[4,144,256]{2,1,0:T(8,128)(2,1)}, u32[]{:S(2)}, u32[]{:S(2)}) async-start(bf16[4,144,256]{2,1,0:T(8,128)(2,1)} %copy-done.90), calls=%async_computation.2 | async-start | bytes 589824 | tf_op jit(solution)/shard_map/mixed1/all_to_all | solution.py:49
  176.9 22.6 %collective-permute-start.26 = (f32[128,1152]{1,0:T(8,128)}, f32[128,1152]{1,0:T(8,128)S(1)}, u32[]{:S(2)}, u32[]{:S(2)}) collective-permute-start(f32[128,1152]{1,0:T(8,128)} %get-tuple-element.150), channel_id=1, source_target_pairs={{0,1},{1,0},{2,3},{3,2},{4,5},{5,4},{6,7},{7,6},{8,9},{9,8},{10,11... | collective-permute-start | bytes 1769480 | tf_op jit(solution)/shard_map/attended0/ppermute | solution.py:44
  186.4 32.5 %collective-permute-start.24 = (f32[128,1152]{1,0:T(8,128)}, f32[128,1152]{1,0:T(8,128)}, u32[]{:S(2)}, u32[]{:S(2)}) collective-permute-start(f32[128,1152]{1,0:T(8,128)} %get-tuple-element.147), channel_id=1, source_target_pairs={{0,1},{1,0},{2,3},{3,2},{4,5},{5,4},{6,7},{7,6},{8,9},{9,8},{10,11... | collective-permute-start | bytes 1769480 | tf_op jit(solution)/shard_map/attended1/ppermute | solution.py:44
  195.4 16.7 %all-to-all-start.1 = ((bf16[4,144,256]{2,1,0:T(8,128)(2,1)}), bf16[4,144,256]{2,1,0:T(8,128)(2,1)}, u32[]{:S(2)}, u32[]{:S(2)}) async-start(bf16[4,144,256]{2,1,0:T(8,128)(2,1)} %copy-done.91), calls=%async_computation.1 | async-start | bytes 589824 | tf_op jit(solution)/shard_map/mixed2/all_to_all | solution.py:49
  199.5 247.5 %all-gather.8.cloned.1.call-start = ((), (), s32[]{:S(2)}) async-start(), calls=%async_computation.13 | async-start | bytes 4386816 | tf_op jit(solution)/shard_map/qkv_weights/all_gather | solution.py:54
  205.3 18.0 %collective-permute-start.27 = (bf16[128,1152]{1,0:T(8,128)(2,1)}, bf16[128,1152]{1,0:T(8,128)(2,1)}, u32[]{:S(2)}, u32[]{:S(2)}) collective-permute-start(bf16[128,1152]{1,0:T(8,128)(2,1)} %get-tuple-element.151.refs_0_), channel_id=1, source_target_pairs={{0,1},{1,0},{2,3},{3,2},{4,5},{5,4},{6,7},{7,6},{8,9},{9,8},{10,11... | collective-permute-start | bytes 884744 | tf_op jit(solution)/shard_map/in_second0/ppermute | solution.py:44
  215.6 22.7 %collective-permute-start.22 = (f32[128,1152]{1,0:T(8,128)}, f32[128,1152]{1,0:T(8,128)}, u32[]{:S(2)}, u32[]{:S(2)}) collective-permute-start(f32[128,1152]{1,0:T(8,128)} %get-tuple-element.142), channel_id=1, source_target_pairs={{0,1},{1,0},{2,3},{3,2},{4,5},{5,4},{6,7},{7,6},{8,9},{9,8},{10,11... | collective-permute-start | bytes 1769480 | tf_op jit(solution)/shard_map/attended2/ppermute | solution.py:44
  222.7 19.3 %collective-permute-start.25 = (bf16[128,1152]{1,0:T(8,128)(2,1)}, bf16[128,1152]{1,0:T(8,128)(2,1)}, u32[]{:S(2)}, u32[]{:S(2)}) collective-permute-start(bf16[128,1152]{1,0:T(8,128)(2,1)} %get-tuple-element.148.refs_0_), channel_id=1, source_target_pairs={{0,1},{1,0},{2,3},{3,2},{4,5},{5,4},{6,7},{7,6},{8,9},{9,8},{10,11... | collective-permute-start | bytes 884744 | tf_op jit(solution)/shard_map/in_second1/ppermute | solution.py:44
  236.9 20.0 %collective-permute-start.28 = (f32[128,1152]{1,0:T(8,128)S(1)}, f32[128,1152]{1,0:T(8,128)S(1)}, u32[]{:S(2)}, u32[]{:S(2)}) collective-permute-start(f32[128,1152]{1,0:T(8,128)S(1)} %get-tuple-element.164), channel_id=1, source_target_pairs={{0,1},{1,0},{2,3},{3,2},{4,5},{5,4},{6,7},{7,6},{8,9},{9,8},{10,11... | collective-permute-start | bytes 1769480 | tf_op jit(solution)/shard_map/grad_in_second0/ppermute | solution.py:44
  241.4 17.6 %collective-permute-start.23 = (bf16[128,1152]{1,0:T(8,128)(2,1)S(1)}, bf16[128,1152]{1,0:T(8,128)(2,1)S(1)}, u32[]{:S(2)}, u32[]{:S(2)}) collective-permute-start(bf16[128,1152]{1,0:T(8,128)(2,1)S(1)} %get-tuple-element.143.refs_0_), channel_id=1, source_target_pairs={{0,1},{1,0},{2,3},{3,2},{4,5},{5,4},{6,7},{7,6},{8,9},{9,8},{10,11... | collective-permute-start | bytes 884744 | tf_op jit(solution)/shard_map/in_second2/ppermute | solution.py:44
  255.5 17.0 %collective-permute-start.32 = (f32[128,1152]{1,0:T(8,128)S(1)}, f32[128,1152]{1,0:T(8,128)S(1)}, u32[]{:S(2)}, u32[]{:S(2)}) collective-permute-start(f32[128,1152]{1,0:T(8,128)S(1)} %get-tuple-element.181), channel_id=1, source_target_pairs={{0,1},{1,0},{2,3},{3,2},{4,5},{5,4},{6,7},{7,6},{8,9},{9,8},{10,11... | collective-permute-start | bytes 1769480 | tf_op jit(solution)/shard_map/grad_in_second1/ppermute | solution.py:44
  258.4 25.1 %collective-permute-start.31 = (bf16[128,1152]{1,0:T(8,128)(2,1)S(1)}, bf16[128,1152]{1,0:T(8,128)(2,1)S(1)}, u32[]{:S(2)}, u32[]{:S(2)}) collective-permute-start(bf16[128,1152]{1,0:T(8,128)(2,1)S(1)} %get-tuple-element.175.refs_0_), channel_id=1, source_target_pairs={{0,1},{1,0},{2,3},{3,2},{4,5},{5,4},{6,7},{7,6},{8,9},{9,8},{10,11... | collective-permute-start | bytes 884744 | tf_op jit(solution)/shard_map/grad_attended0/ppermute | solution.py:44
  290.8 110.9 %collective-permute-start.33 = (f32[2,288,4608]{2,1,0:T(8,128)}, f32[2,288,4608]{2,1,0:T(8,128)}, u32[]{:S(2)}, u32[]{:S(2)}) collective-permute-start(f32[2,288,4608]{2,1,0:T(8,128)} %get-tuple-element.184.refs_5_), channel_id=1, source_target_pairs={{0,8},{8,0},{16,24},{24,16},{1,9},{9,1},{17,25},{25,17},{2,10},{10... | collective-permute-start | bytes 31850504 | tf_op jit(solution)/shard_map/grad_feed_0/ppermute | solution.py:44
  295.8 11.7 %collective-permute-start.34 = (f32[4,8,128]{2,1,0:T(8,128)}, f32[4,8,128]{2,1,0:T(8,128)}, u32[]{:S(2)}, u32[]{:S(2)}) collective-permute-start(f32[4,8,128]{2,1,0:T(8,128)} %maximum_maximum_fusion), channel_id=1, source_target_pairs={{0,8},{8,0},{16,24},{24,16},{1,9},{9,1},{17,25},{25,17},{2,10},{10... | collective-permute-start | bytes 49160 | tf_op jit(solution)/shard_map/bounds/ppermute | solution.py:44
  308.3 13.9 %collective-permute-start.35 = (f32[4,8,128]{2,1,0:T(8,128)S(1)}, f32[4,8,128]{2,1,0:T(8,128)S(1)}, u32[]{:S(2)}, u32[]{:S(2)}) collective-permute-start(f32[4,8,128]{2,1,0:T(8,128)S(1)} %max.24), channel_id=1, source_target_pairs={{0,16},{8,24},{16,0},{24,8},{1,17},{9,25},{17,1},{25,9},{2,18},{10... | collective-permute-start | bytes 49160 | tf_op jit(solution)/shard_map/bounds/ppermute | solution.py:44
  311.7 36.1 %collective-permute-start.42 = (f32[128,1152]{1,0:T(8,128)}, f32[128,1152]{1,0:T(8,128)}, u32[]{:S(2)}, u32[]{:S(2)}) collective-permute-start(f32[128,1152]{1,0:T(8,128)} %copy-done.113), channel_id=1, source_target_pairs={{0,1},{1,0},{2,3},{3,2},{4,5},{5,4},{6,7},{7,6},{8,9},{9,8},{10,11... | collective-permute-start | bytes 1769480 | tf_op jit(solution)/shard_map/grad_in_second2/ppermute | solution.py:44
  320.2 22.4 %collective-permute-start.40 = (bf16[128,1152]{1,0:T(8,128)(2,1)}, bf16[128,1152]{1,0:T(8,128)(2,1)}, u32[]{:S(2)}, u32[]{:S(2)}) collective-permute-start(bf16[128,1152]{1,0:T(8,128)(2,1)} %get-tuple-element.197.refs_0_), channel_id=1, source_target_pairs={{0,1},{1,0},{2,3},{3,2},{4,5},{5,4},{6,7},{7,6},{8,9},{9,8},{10,11... | collective-permute-start | bytes 884744 | tf_op jit(solution)/shard_map/grad_attended1/ppermute | solution.py:44
  320.7 91.6 %collective-permute-start.29 = (bf16[384,1152]{1,0:T(8,128)(2,1)}, bf16[384,1152]{1,0:T(8,128)(2,1)}, u32[]{:S(2)}, u32[]{:S(2)}) collective-permute-start(bf16[384,1152]{1,0:T(8,128)(2,1)} %get-tuple-element.166), channel_id=1, source_target_pairs={{0,1},{1,0},{2,3},{3,2},{4,5},{5,4},{6,7},{7,6},{8,9},{9,8},{10,11... | collective-permute-start | bytes 2654216 | tf_op jit(solution)/shard_map/feed_out/ppermute | solution.py:44
  333.8 17.9 %all-to-all-start.4 = ((bf16[4,144,256]{2,1,0:T(8,128)(2,1)}), bf16[4,144,256]{2,1,0:T(8,128)(2,1)}, u32[]{:S(2)}, u32[]{:S(2)}) async-start(bf16[4,144,256]{2,1,0:T(8,128)(2,1)} %bitcast.171), calls=%async_computation.4 | async-start | bytes 589824 | tf_op jit(solution)/shard_map/grad_mixed0/all_to_all | solution.py:49
  351.6 19.8 %collective-permute-start.43 = (bf16[128,1152]{1,0:T(8,128)(2,1)}, bf16[128,1152]{1,0:T(8,128)(2,1)}, u32[]{:S(2)}, u32[]{:S(2)}) collective-permute-start(bf16[128,1152]{1,0:T(8,128)(2,1)} %get-tuple-element.210.refs_0_), channel_id=1, source_target_pairs={{0,1},{1,0},{2,3},{3,2},{4,5},{5,4},{6,7},{7,6},{8,9},{9,8},{10,11... | collective-permute-start | bytes 884744 | tf_op jit(solution)/shard_map/grad_attended2/ppermute | solution.py:44
  351.6 23.3 %all-to-all-start.6 = ((bf16[4,144,256]{2,1,0:T(8,128)(2,1)}), bf16[4,144,256]{2,1,0:T(8,128)(2,1)}, u32[]{:S(2)}, u32[]{:S(2)}) async-start(bf16[4,144,256]{2,1,0:T(8,128)(2,1)} %bitcast.172), calls=%async_computation.6 | async-start | bytes 589824 | tf_op jit(solution)/shard_map/grad_mixed1/all_to_all | solution.py:49
  375.0 21.3 %all-to-all-start.8 = ((bf16[4,144,256]{2,1,0:T(8,128)(2,1)}), bf16[4,144,256]{2,1,0:T(8,128)(2,1)S(1)}, u32[]{:S(2)}, u32[]{:S(2)}) async-start(bf16[4,144,256]{2,1,0:T(8,128)(2,1)} %bitcast.173), calls=%async_computation.8 | async-start | bytes 589824 | tf_op jit(solution)/shard_map/grad_mixed2/all_to_all | solution.py:49
  396.3 33.8 %all-to-all-start.7 = ((bf16[4,3,144,256]{3,2,1,0:T(8,128)(2,1)}), bf16[4,3,144,256]{3,2,1,0:T(8,128)(2,1)}, u32[]{:S(2)}, u32[]{:S(2)}) async-start(bf16[4,3,144,256]{3,2,1,0:T(8,128)(2,1)} %get-tuple-element.201), calls=%async_computation.7 | async-start | bytes 1769472 | tf_op jit(solution)/shard_map/grad_qkv1/all_to_all | solution.py:49
  408.6 75.1 %collective-permute-start.38 = (f16[1,288,4608]{2,1,0:T(8,128)(2,1)}, f16[1,288,4608]{2,1,0:T(8,128)(2,1)}, u32[]{:S(2)}, u32[]{:S(2)}) collective-permute-start(f16[1,288,4608]{2,1,0:T(8,128)(2,1)} %multiply_convert_fusion), channel_id=1, source_target_pairs={{0,16},{8,24},{16,0},{24,8},{1,17},{9,25},{17,1},{25,9},{2,18},{10... | collective-permute-start | bytes 7962632 | tf_op jit(solution)/shard_map/grad_feed_1/ppermute | solution.py:44
  412.3 43.6 %collective-permute-start.60 = (f32[2,288,576]{2,1,0:T(8,128)}, f32[2,288,576]{2,1,0:T(8,128)}, u32[]{:S(2)}, u32[]{:S(2)}) collective-permute-start(f32[2,288,576]{2,1,0:T(8,128)} %get-tuple-element.238), channel_id=1, source_target_pairs={{0,8},{8,0},{16,24},{24,16},{1,9},{9,1},{17,25},{25,17},{2,10},{10... | collective-permute-start | bytes 3981320 | tf_op jit(solution)/shard_map/grad_proj_0/ppermute | solution.py:44
  416.5 37.9 %collective-permute-start.30 = (bf16[384,1152]{1,0:T(8,128)(2,1)S(1)}, bf16[384,1152]{1,0:T(8,128)(2,1)S(1)}, u32[]{:S(2)}, u32[]{:S(2)}) collective-permute-start(bf16[384,1152]{1,0:T(8,128)(2,1)S(1)} %get-tuple-element.172.refs_0_), channel_id=1, source_target_pairs={{0,1},{1,0},{2,3},{3,2},{4,5},{5,4},{6,7},{7,6},{8,9},{9,8},{10,11... | collective-permute-start | bytes 2654216 | tf_op jit(solution)/shard_map/output/ppermute | solution.py:44
  430.1 41.9 %all-to-all-start.9 = ((bf16[4,3,144,256]{3,2,1,0:T(8,128)(2,1)}), bf16[4,3,144,256]{3,2,1,0:T(8,128)(2,1)S(1)}, u32[]{:S(2)}, u32[]{:S(2)}) async-start(bf16[4,3,144,256]{3,2,1,0:T(8,128)(2,1)} %copy-done.54), calls=%async_computation.9 | async-start | bytes 1769472 | tf_op jit(solution)/shard_map/grad_qkv2/all_to_all | solution.py:49
  445.9 14.6 %collective-permute-start.58 = (f32[2,288,432]{2,1,0:T(8,128)}, f32[2,288,432]{2,1,0:T(8,128)}, u32[]{:S(2)}, u32[]{:S(2)}) collective-permute-start(f32[2,288,432]{2,1,0:T(8,128)} %get-tuple-element.234), channel_id=1, source_target_pairs={{0,8},{8,0},{16,24},{24,16},{1,9},{9,1},{17,25},{25,17},{2,10},{10... | collective-permute-start | bytes 2985992 | tf_op jit(solution)/shard_map/grad_qkvw_0/ppermute | solution.py:44
  453.3 16.0 %collective-permute-start.41 = (f32[128,1152]{1,0:T(8,128)}, f32[128,1152]{1,0:T(8,128)}, u32[]{:S(2)}, u32[]{:S(2)}) collective-permute-start(f32[128,1152]{1,0:T(8,128)} %get-tuple-element.203), channel_id=1, source_target_pairs={{0,1},{1,0},{2,3},{3,2},{4,5},{5,4},{6,7},{7,6},{8,9},{9,8},{10,11... | collective-permute-start | bytes 1769480 | tf_op jit(solution)/shard_map/grad_in_first1/ppermute | solution.py:44
  458.7 53.2 %collective-permute-start.61 = (f32[1,288,576]{2,1,0:T(8,128)}, f32[1,288,576]{2,1,0:T(8,128)}, u32[]{:S(2)}, u32[]{:S(2)}) collective-permute-start(f32[1,288,576]{2,1,0:T(8,128)} %dynamic-slice_add_fusion), channel_id=1, source_target_pairs={{0,16},{8,24},{16,0},{24,8},{1,17},{9,25},{17,1},{25,9},{2,18},{10... | collective-permute-start | bytes 1990664 | tf_op jit(solution)/shard_map/grad_proj_1/ppermute | solution.py:44
  462.5 43.0 %collective-permute-start.59 = (f32[1,288,432]{2,1,0:T(8,128)}, f32[1,288,432]{2,1,0:T(8,128)}, u32[]{:S(2)}, u32[]{:S(2)}) collective-permute-start(f32[1,288,432]{2,1,0:T(8,128)} %dynamic-slice_add_fusion.1), channel_id=1, source_target_pairs={{0,16},{8,24},{16,0},{24,8},{1,17},{9,25},{17,1},{25,9},{2,18},{10... | collective-permute-start | bytes 1493000 | tf_op jit(solution)/shard_map/grad_qkvw_1/ppermute | solution.py:44
  471.0 104.3 %collective-permute-start.46 = (f32[128,1152]{1,0:T(8,128)S(1)}, f32[128,1152]{1,0:T(8,128)}, u32[]{:S(2)}, u32[]{:S(2)}) collective-permute-start(f32[128,1152]{1,0:T(8,128)S(1)} %get-tuple-element.205.refs_1_), channel_id=1, source_target_pairs={{0,1},{1,0},{2,3},{3,2},{4,5},{5,4},{6,7},{7,6},{8,9},{9,8},{10,11... | collective-permute-start | bytes 1769480 | tf_op jit(solution)/shard_map/grad_latent1/ppermute | solution.py:44
  472.0 27.2 %all-to-all-start.5 = ((bf16[4,3,144,256]{3,2,1,0:T(8,128)(2,1)}), bf16[4,3,144,256]{3,2,1,0:T(8,128)(2,1)S(1)}, u32[]{:S(2)}, u32[]{:S(2)}) async-start(bf16[4,3,144,256]{3,2,1,0:T(8,128)(2,1)} %get-tuple-element.185), calls=%async_computation.5 | async-start | bytes 1769472 | tf_op jit(solution)/shard_map/grad_qkv0/all_to_all | solution.py:49
  482.6 31.7 %collective-permute-start.44 = (f32[128,1152]{1,0:T(8,128)}, f32[128,1152]{1,0:T(8,128)}, u32[]{:S(2)}, u32[]{:S(2)}) collective-permute-start(f32[128,1152]{1,0:T(8,128)} %get-tuple-element.216), channel_id=1, source_target_pairs={{0,1},{1,0},{2,3},{3,2},{4,5},{5,4},{6,7},{7,6},{8,9},{9,8},{10,11... | collective-permute-start | bytes 1769480 | tf_op jit(solution)/shard_map/grad_in_first2/ppermute | solution.py:44
  504.3 14.6 %collective-permute-start.39 = (f32[128,1152]{1,0:T(8,128)}, f32[128,1152]{1,0:T(8,128)}, u32[]{:S(2)}, u32[]{:S(2)}) collective-permute-start(f32[128,1152]{1,0:T(8,128)} %get-tuple-element.191), channel_id=1, source_target_pairs={{0,1},{1,0},{2,3},{3,2},{4,5},{5,4},{6,7},{7,6},{8,9},{9,8},{10,11... | collective-permute-start | bytes 1769480 | tf_op jit(solution)/shard_map/grad_in_first0/ppermute | solution.py:44
  507.7 53.5 %all-to-all-start.10 = ((f32[4,72,432]{2,1,0:T(8,128)}), f32[4,72,432]{2,1,0:T(8,128)}, u32[]{:S(2)}, u32[]{:S(2)}) async-start(f32[4,72,432]{2,1,0:T(8,128)} %bitcast.206), calls=%async_computation.10 | async-start | bytes 1179648 | tf_op jit(solution)/shard_map/grad_qkvw_c/all_to_all | solution.py:49
  523.1 24.7 %collective-permute-start.62 = (f32[72,576]{1,0:T(8,128)S(1)}, f32[72,576]{1,0:T(8,128)S(1)}, u32[]{:S(2)}, u32[]{:S(2)}) collective-permute-start(f32[72,576]{1,0:T(8,128)S(1)} %get-tuple-element.300), channel_id=1, source_target_pairs={{0,2},{2,4},{4,6},{6,0},{1,3},{3,5},{5,7},{7,1},{8,10},{10,12},{12... | collective-permute-start | bytes 497672 | tf_op jit(solution)/shard_map/grad_proj_ring/ppermute | solution.py:38
  523.2 36.4 %collective-permute-start.64 = (f32[72,576]{1,0:T(8,128)S(1)}, f32[72,576]{1,0:T(8,128)S(1)}, u32[]{:S(2)}, u32[]{:S(2)}) collective-permute-start(f32[72,576]{1,0:T(8,128)S(1)} %get-tuple-element.301), channel_id=1, source_target_pairs={{0,6},{2,0},{4,2},{6,4},{1,7},{3,1},{5,3},{7,5},{8,14},{10,8},{12,... | collective-permute-start | bytes 497672 | tf_op jit(solution)/shard_map/grad_proj_ring/ppermute | solution.py:38
  527.0 20.7 %collective-permute-start.49 = (f32[234,128]{1,0:T(8,128)S(1)}, f32[234,128]{1,0:T(8,128)S(1)}, u32[]{:S(2)}, u32[]{:S(2)}) collective-permute-start(f32[234,128]{1,0:T(8,128)S(1)} %bitcast_add_fusion.4), channel_id=1, source_target_pairs={{0,2},{2,0},{4,6},{6,4},{1,3},{3,1},{5,7},{7,5},{8,10},{10,8},{12,... | collective-permute-start | bytes 359432 | tf_op jit(solution)/shard_map/sums/ppermute | solution.py:44
  529.4 42.4 %collective-permute-start.65 = (f16[72,4608]{1,0:T(8,128)(2,1)}, f16[72,4608]{1,0:T(8,128)(2,1)}, u32[]{:S(2)}, u32[]{:S(2)}) collective-permute-start(f16[72,4608]{1,0:T(8,128)(2,1)} %fusion.1), channel_id=1, source_target_pairs={{0,2},{2,4},{4,6},{6,0},{1,3},{3,5},{5,7},{7,1},{8,10},{10,12},{12... | collective-permute-start | bytes 1990664 | tf_op jit(solution)/shard_map/grad_feed_ring/ppermute | solution.py:38
  560.3 18.9 %collective-permute-start.47 = (f32[128,1152]{1,0:T(8,128)S(1)}, f32[128,1152]{1,0:T(8,128)S(1)}, u32[]{:S(2)}, u32[]{:S(2)}) collective-permute-start(f32[128,1152]{1,0:T(8,128)S(1)} %get-tuple-element.218.refs_2_), channel_id=1, source_target_pairs={{0,1},{1,0},{2,3},{3,2},{4,5},{5,4},{6,7},{7,6},{8,9},{9,8},{10,11... | collective-permute-start | bytes 1769480 | tf_op jit(solution)/shard_map/grad_latent2/ppermute | solution.py:44
  568.5 20.1 %collective-permute-start.45 = (f32[128,1152]{1,0:T(8,128)S(1)}, f32[128,1152]{1,0:T(8,128)S(1)}, u32[]{:S(2)}, u32[]{:S(2)}) collective-permute-start(f32[128,1152]{1,0:T(8,128)S(1)} %get-tuple-element.193.refs_0_), channel_id=1, source_target_pairs={{0,1},{1,0},{2,3},{3,2},{4,5},{5,4},{6,7},{7,6},{8,9},{9,8},{10,11... | collective-permute-start | bytes 1769480 | tf_op jit(solution)/shard_map/grad_latent0/ppermute | solution.py:44
  569.7 22.1 %collective-permute-start.52 = (f32[2,234,128]{2,1,0:T(8,128)S(1)}, f32[2,234,128]{2,1,0:T(8,128)S(1)}, u32[]{:S(2)}, u32[]{:S(2)}) collective-permute-start(f32[2,234,128]{2,1,0:T(8,128)S(1)} %pad_maximum_fusion.2), channel_id=1, source_target_pairs={{0,16},{8,24},{16,0},{24,8},{1,17},{9,25},{17,1},{25,9},{2,18},{10... | collective-permute-start | bytes 718856 | tf_op jit(solution)/shard_map/sums/ppermute | solution.py:44
  575.1 33.7 %collective-permute-start.66 = (f16[72,4608]{1,0:T(8,128)(2,1)}, f16[72,4608]{1,0:T(8,128)(2,1)}, u32[]{:S(2)}, u32[]{:S(2)}) collective-permute-start(f16[72,4608]{1,0:T(8,128)(2,1)} %get-tuple-element.296), channel_id=1, source_target_pairs={{0,2},{2,4},{4,6},{6,0},{1,3},{3,5},{5,7},{7,1},{8,10},{10,12},{12... | collective-permute-start | bytes 1990664 | tf_op jit(solution)/shard_map/grad_feed_ring/ppermute | solution.py:38
  575.4 33.4 %collective-permute-start.67 = (f16[72,4608]{1,0:T(8,128)(2,1)}, f16[72,4608]{1,0:T(8,128)(2,1)}, u32[]{:S(2)}, u32[]{:S(2)}) collective-permute-start(f16[72,4608]{1,0:T(8,128)(2,1)} %get-tuple-element.297), channel_id=1, source_target_pairs={{0,6},{2,0},{4,2},{6,4},{1,7},{3,1},{5,3},{7,5},{8,14},{10,8},{12,... | collective-permute-start | bytes 1990664 | tf_op jit(solution)/shard_map/grad_feed_ring/ppermute | solution.py:38
  (158 other events, 888.6 us)
Sparse Core Ops, SparseCore 0:
  34.9 42.9 all-gather.3
  106.9 106.2 all-gather.5
  294.6 52.9 all-gather.7

commit v4 on v3

--- a/solution.py
+++ b/solution.py
@@ -968,14 +968,13 @@
     silu_all = cube_gather(jax.nn.silu(cond).astype(BF16), "cond")
     first_row = (f * size_c + c) * rows
     silu_here = lax.dynamic_slice_in_dim(silu_all, first_row, rows, 2).reshape(-1, rows)
-    silu_here = once_after(silu_here, [rings[0][2], rings[0][-2]])
     mod_part = dot(silu_here, ada_weight.reshape(rows, -1), ((1,), (0,)))
     mod_part = cube_reduce(mod_part.reshape(size_f, items, -1), "mod_f")
     mod_part = butterfly_sum(mod_part, "ctx", "mod_c")
     bias_mod = lax.dynamic_slice_in_dim(ada_bias.astype(F32), first_column, half_width, 1)
     mod_half = (mod_part.reshape(items, 6, half_width) + bias_mod).astype(BF16)
     mods = both(mod_half, swap(mod_half, "mod_t"), 2).astype(F32)
-    mods = once_after(mods, [qkv_came])
+    mods = once_after(mods, [qkv_came, rings[0][4], rings[0][3], rings[0][-1]])
 
     pieces = spread([(0, "own", qkv_came)], "qkv")
     (qkv_mine,) = place(pieces, [3 * group])
@@ -1077,7 +1076,7 @@
     scales = jnp.where(jnp.arange(2 * hidden) < hidden, up_scale, down_scale)
     middles = [before_attention(item) for item in range(items)]
     parts = outer(
-        in_second, grad_upward, 0, 768, 0, 2 * hidden, [None, None], [grads_in[1][1]]
+        in_second, grad_upward, 0, 768, 0, 2 * hidden, [None, None]
     )
     parts = outer(
         grad_feed, activated, 0, 768, hidden // 768, 2 * hidden, parts, [middles[0][3]]
@@ -1092,7 +1091,8 @@
             out_own, peers, bias_down, kept[item][3], cots[0], mods, out_half, item
         )
         gate_sums.append(gate_sum)
-    output = order([out_half], [swap(out_half, "output")], items)
+    out_swapped = swap(out_half, "output")
+    output = order([out_half], [out_swapped], items)
 
     grad_blocks = []
     for item in range(items):
@@ -1132,7 +1132,7 @@
             middles[item][0],
             mods,
             item,
-            [],
+            [out_swapped] if item == 1 else [],
         )
         input_grads.append(grad_latent)
         input_peers.append(swap(grad_latent, "grad_latent%d" % item))

time: 633 us -> 619 us (0.978)
  waiting for transfers between devices: 164 us -> 144 us
  starting transfers between devices: 116 us -> 127 us
    ppermute x12, waiting for transfers between devices: 32.9 us -> 16.9 us  [shift(): return lax.ppermute(x, 'ctx', [(i, (i + k) % size) for i in range(size)])]
    all_to_all x11, waiting for transfers between devices: 27.2 us -> 18.1 us  [exchange(): return lax.all_to_all(x, 'ctx', 0, 0)]
    pallas_call x47 -> x46, Pallas kernels: 175 us -> 177 us  [slab_call(): pl.pallas_call(run, in_specs=in_specs + [ANYWHERE] * more, input_output_a...]
    unnamed x289 -> x277, local copies, waits for them, and re-layouts: 73.2 us -> 75.5 us
  transfers between devices with their start and end apart: 82 -> 82, of which waited for: 25 -> 26; matrix products, arithmetic and copies ran while one was open for 12% -> 11% of each run, Pallas kernels for 27% -> 28%
where the time goes in v4:
time: 619 us; the launch traced here: 608 us
  Pallas kernels  180 us (29%)
  waiting for transfers between devices  144 us (23%)
  starting transfers between devices  127 us (21%)
  local copies, waits for them, and re-layouts  95.7 us (15%)
  other arithmetic  41.2 us (7%)
  between operations  18.5 us (3%)
    pallas_call x46, Pallas kernels, slab_call(): pl.pallas_call(run, in_specs=in_specs + [ANYWHERE] * more, input_output_a...  177 us
    ppermute x56, waiting for transfers between devices, flip(): return lax.ppermute(x, axis, [(i, i ^ 1 << bit) for i in range(size)])  109 us
    unnamed x277, local copies, waits for them, and re-layouts  75.5 us
    all_to_all x11, starting transfers between devices, exchange(): return lax.all_to_all(x, 'ctx', 0, 0)  56.5 us
    ppermute x56, starting transfers between devices, flip(): return lax.ppermute(x, axis, [(i, i ^ 1 << bit) for i in range(size)])  49.4 us
    ppermute x12, starting transfers between devices, shift(): return lax.ppermute(x, 'ctx', [(i, (i + k) % size) for i in range(size)])  21 us
    all_to_all x11, waiting for transfers between devices, exchange(): return lax.all_to_all(x, 'ctx', 0, 0)  18.1 us
    ppermute x12, waiting for transfers between devices, shift(): return lax.ppermute(x, 'ctx', [(i, (i + k) % size) for i in range(size)])  16.9 us
  transfers between devices with their start and end apart: 82, of which 26 were waited for; matrix products, arithmetic and copies ran while one was open for 11% of the time, Pallas kernels for 28%

profile of v4, /device:TPU:0, one launch (start us, length us, event | category | flops | bytes accessed | tf_op | source)
XLA Modules:
  0.0 608.5 jit_solution(10499454283978933401)
XLA Ops:
  9.3 2.9 collective-permute-start.1
  16.5 2.7 collective-permute-done.2
  20.1 4.1 collective-permute-start.10
  26.8 5.1 all-to-all-start
  35.9 10.5 %collective-permute-done.4 = f32[3,3456]{1,0:T(4,128)S(1)} collective-permute-done((f32[3,3456]{1,0:T(4,128)S(1)}, f32[3,3456]{1,0:T(4,128)S(1)}, u32[]{:S(2)}, u32[]{:S(2)}) %collective-permute-start.4) | collective-permute-done | bytes 41504 | tf_op jit(solution)/shard_map/mod_c/ppermute | solution.py:44
  47.4 4.1 collective-permute-done.5
  53.7 2.5 collective-permute-start.8
  60.2 7.1 %collective-permute-done.11.refs_4_.refs_7_ = bf16[1,128,1152]{2,1,0:T(8,128)(2,1)S(1)} collective-permute-done((bf16[1,128,1152]{2,1,0:T(8,128)(2,1)}, bf16[1,128,1152]{2,1,0:T(8,128)(2,1)S(1)}, u32[]{:S(2)}, u32[]{:S(2)}) %collective-permute-start.11) | collective-permute-done | bytes 294944 | tf_op jit(solution)/shard_map/latent0_t/ppermute | solution.py:44
  69.7 2.5 collective-permute-start.20
  74.6 2.7 shard_map.231
  85.2 4.6 shard_map.232
  89.8 7.2 %shard_map.233 = (bf16[4,144,256]{2,1,0:T(8,128)(2,1)S(1)}, f32[2,1024]{1,0:T(2,128)S(1)}) custom-call(bf16[3,144,1024]{2,1,0:T(8,128)(2,1)S(1)} %bitcast.187, bf16[3,144,1024]{2,1,0:T(8,128)(2,1)S(1)} %bitcast.188, bf16[3,144,1024]{2,1,0:T(8,128)(2,1)S(1)} %bitcast.189), custom_call_target="tpu_custom_call" | custom-call | flops 3355443200 | bytes 1179648 | tf_op jit(solution)/shard_map/pallas_call | solution.py:249
  102.9 16.9 %collective-permute-done.18.refs_4_ = bf16[2,128,1152]{2,1,0:T(8,128)(2,1)} collective-permute-done((bf16[2,128,1152]{2,1,0:T(8,128)(2,1)S(1)}, bf16[2,128,1152]{2,1,0:T(8,128)(2,1)}, u32[]{:S(2)}, u32[]{:S(2)}) %collective-permute-start.18) | collective-permute-done | bytes 589856 | tf_op jit(solution)/shard_map/latent1_right/ppermute | solution.py:38
  121.3 11.1 %all-to-all-start.3 = ((bf16[4,144,256]{2,1,0:T(8,128)(2,1)}), bf16[4,144,256]{2,1,0:T(8,128)(2,1)S(1)}, u32[]{:S(2)}, u32[]{:S(2)}) async-start(bf16[4,144,256]{2,1,0:T(8,128)(2,1)} %copy-done.91), calls=%async_computation.3 | async-start | bytes 589824 | tf_op jit(solution)/shard_map/mixed0/all_to_all | solution.py:49
  132.4 8.9 %collective-permute-done.19.refs_5_ = bf16[2,128,1152]{2,1,0:T(8,128)(2,1)} collective-permute-done((bf16[2,128,1152]{2,1,0:T(8,128)(2,1)}, bf16[2,128,1152]{2,1,0:T(8,128)(2,1)}, u32[]{:S(2)}, u32[]{:S(2)}) %collective-permute-start.19) | collective-permute-done | bytes 589856 | tf_op jit(solution)/shard_map/latent1_t/ppermute | solution.py:44
  141.3 5.0 shard_map.235
  146.3 7.9 %shard_map.238 = (bf16[4,144,256]{2,1,0:T(8,128)(2,1)}, f32[2,1024]{1,0:T(2,128)S(1)}) custom-call(bf16[3,144,1024]{2,1,0:T(8,128)(2,1)S(1)} %bitcast.181, bf16[3,144,1024]{2,1,0:T(8,128)(2,1)S(1)} %bitcast.182, bf16[3,144,1024]{2,1,0:T(8,128)(2,1)S(1)} %bitcast.183), custom_call_target="tpu_custom_call" | custom-call | flops 3355443200 | bytes 1179648 | tf_op jit(solution)/shard_map/pallas_call | solution.py:249
  155.2 3.5 all-to-all-start.2
  168.4 5.0 shard_map.236
  174.3 2.6 all-to-all-done.2.refs_0_
  182.8 7.2 %shard_map.237 = (bf16[4,144,256]{2,1,0:T(8,128)(2,1)S(1)}, f32[2,1024]{1,0:T(2,128)S(1)}) custom-call(bf16[3,144,1024]{2,1,0:T(8,128)(2,1)S(1)} %bitcast.175, bf16[3,144,1024]{2,1,0:T(8,128)(2,1)S(1)} %bitcast.176, bf16[3,144,1024]{2,1,0:T(8,128)(2,1)S(1)} %bitcast.177), custom_call_target="tpu_custom_call" | custom-call | flops 3355443200 | bytes 1179648 | tf_op jit(solution)/shard_map/pallas_call | solution.py:249
  190.7 3.6 all-to-all-start.1
  200.9 5.4 all-to-all-done.1.refs_0_
  216.9 12.4 %shard_map.247 = (bf16[768,1152]{1,0:T(8,128)(2,1)}, bf16[768,1152]{1,0:T(8,128)(2,1)}, bf16[768,2304]{1,0:T(8,128)(2,1)}, bf16[768,2304]{1,0:T(8,128)(2,1)}, f3...) custom-call(bf16[128,1152]{1,0:T(8,128)(2,1)} %get-tuple-element.151, ...), custom_call_target="tpu_custom_call" | custom-call | flops 5435817984 | bytes 12976128 | tf_op jit(solution)/shard_map/pallas_call | solution.py:249
  234.4 12.0 %shard_map.248 = (bf16[768,1152]{1,0:T(8,128)(2,1)}, bf16[768,1152]{1,0:T(8,128)(2,1)}, bf16[768,2304]{1,0:T(8,128)(2,1)}, bf16[768,2304]{1,0:T(8,128)(2,1)}, f3...) custom-call(bf16[128,1152]{1,0:T(8,128)(2,1)S(1)} %get-tuple-element, ...), custom_call_target="tpu_custom_call", output_to_operand_aliasing={{0}: (8, {}), {1}: (9, {}), {2}: (10, {}), {3}: (11, {}), {... | custom-call | flops 5435817984 | bytes 12976128 | tf_op jit(solution)/shard_map/pallas_call | solution.py:249
  250.3 11.8 %shard_map.249 = (bf16[768,1152]{1,0:T(8,128)(2,1)}, bf16[768,1152]{1,0:T(8,128)(2,1)}, bf16[768,2304]{1,0:T(8,128)(2,1)}, bf16[768,2304]{1,0:T(8,128)(2,1)}, f3...) custom-call(bf16[128,1152]{1,0:T(8,128)(2,1)S(1)} %get-tuple-element, ...), custom_call_target="tpu_custom_call", output_to_operand_aliasing={{0}: (8, {}), {1}: (9, {}), {2}: (10, {}), {3}: (11, {}), {... | custom-call | flops 5435817984 | bytes 12976128 | tf_op jit(solution)/shard_map/pallas_call | solution.py:249
  267.2 7.2 %shard_map.256 = (f32[2,288,4608]{2,1,0:T(8,128)}, f32[2,288,4608]{2,1,0:T(8,128)}) custom-call(bf16[768,1152]{1,0:T(8,128)(2,1)S(1)} %copy-done.18, bf16[768,2304]{1,0:T(8,128)(2,1)S(1)} %copy-done.6), custom_call_target="tpu_custom_call" | custom-call | flops 4076863488 | bytes 14155776 | tf_op jit(solution)/shard_map/pallas_call | solution.py:249
  274.4 7.3 %shard_map.257 = (f32[2,288,4608]{2,1,0:T(8,128)}, f32[2,288,4608]{2,1,0:T(8,128)}) custom-call(bf16[768,1152]{1,0:T(8,128)(2,1)S(1)} %copy-done.5, bf16[768,2304]{1,0:T(8,128)(2,1)S(1)} %copy-done.4, f32[2,288,4608]{2,1,0:T(8,128)} %get-tuple-element.181.refs_2_, ...), custom_call_target="tpu_custom_call", output_to_operand_aliasing={{0}: (2, {}), {1}: (3, {})} | custom-call | flops 4076863488 | bytes 14155776 | tf_op jit(solution)/shard_map/pallas_call | solution.py:249
  287.4 10.6 %collective-permute-done.33 = f32[4,8,128]{2,1,0:T(8,128)S(1)} collective-permute-done((f32[4,8,128]{2,1,0:T(8,128)S(1)}, f32[4,8,128]{2,1,0:T(8,128)S(1)}, u32[]{:S(2)}, u32[]{:S(2)}) %collective-permute-start.33) | collective-permute-done | bytes 16416 | tf_op jit(solution)/shard_map/bounds/ppermute | solution.py:44
  305.8 2.4 shard_map.262
  311.5 3.9 collective-permute-done.35
  318.9 4.2 all-to-all-start.4
  335.4 2.4 all-to-all-done.4.refs_4_
  337.8 4.1 all-to-all-start.6
  343.1 11.9 %shard_map.258 = (bf16[3,144,3072]{2,1,0:T(8,128)(2,1)S(1)}, bf16[4,3,144,256]{3,2,1,0:T(8,128)(2,1)}) custom-call(bf16[3,144,1024]{2,1,0:T(8,128)(2,1)S(1)} %bitcast.190, bf16[3,144,1024]{2,1,0:T(8,128)(2,1)S(1)} %bitcast.191, bf16[3,144,1024]{2,1,0:T(8,128)(2,1)S(1)} %bitcast.192, f32[2,1024]{1,0:T(2,128)S(1)} %get-tuple-element.131.refs_1_.refs_3_, ...), custom_call_target="tpu_custom_call" | custom-call | flops 8388608000 | bytes 2359296 | tf_op jit(solution)/shard_map/pallas_call | solution.py:249
  360.0 5.0 all-to-all-start.8
  368.0 11.0 %shard_map.264 = (bf16[3,144,3072]{2,1,0:T(8,128)(2,1)S(1)}, bf16[4,3,144,256]{3,2,1,0:T(8,128)(2,1)S(1)}) custom-call(bf16[3,144,1024]{2,1,0:T(8,128)(2,1)S(1)} %bitcast.184, bf16[3,144,1024]{2,1,0:T(8,128)(2,1)S(1)} %bitcast.185, bf16[3,144,1024]{2,1,0:T(8,128)(2,1)S(1)} %bitcast.186, ...), custom_call_target="tpu_custom_call", output_to_operand_aliasing={{0}: (5, {})} | custom-call | flops 8388608000 | bytes 2359296 | tf_op jit(solution)/shard_map/pallas_call | solution.py:249
  383.3 5.3 all-to-all-start.7
  388.6 6.7 %multiply_convert_fusion = f16[1,288,4608]{2,1,0:T(8,128)(2,1)} fusion(f32[2,288,4608]{2,1,0:T(8,128)} %collective-permute-done.32, s32[]{:T(128)S(6)} %select_n.122, f32[2,288,4608]{2,1,0:T(8,128)} %get-tuple-element.185, f32[4608]{0:T(1024)S(1)} %fusion.16), kind=kLoop, calls=%fused_computation.2 | loop fusion | flops 3981312 | bytes 13289476 | tf_op jit(solution)/shard_map/convert_element_type | solution.py:173
  401.8 2.8 shard_map.274
  405.7 11.8 %shard_map.269 = (bf16[3,144,3072]{2,1,0:T(8,128)(2,1)S(1)}, bf16[4,3,144,256]{3,2,1,0:T(8,128)(2,1)}) custom-call(bf16[3,144,1024]{2,1,0:T(8,128)(2,1)S(1)} %bitcast.178, bf16[3,144,1024]{2,1,0:T(8,128)(2,1)S(1)} %bitcast.179, bf16[3,144,1024]{2,1,0:T(8,128)(2,1)S(1)} %bitcast.180, ...), custom_call_target="tpu_custom_call", output_to_operand_aliasing={{0}: (5, {})} | custom-call | flops 8388608000 | bytes 2359296 | tf_op jit(solution)/shard_map/pallas_call | solution.py:249
  419.0 5.1 all-to-all-start.9
  425.8 7.9 %shard_map.273 = (f32[2,288,432]{2,1,0:T(8,128)}, f32[2,288,432]{2,1,0:T(8,128)S(1)}) custom-call(bf16[3072,1152]{1,0:T(8,128)(2,1)} %get-tuple-element.232.refs_0_, bf16[432,3072]{1,0:T(8,128)(2,1)S(1)} %bitcast.167), custom_call_target="tpu_custom_call" | custom-call | flops 3057647616 | bytes 9732096 | tf_op jit(solution)/shard_map/pallas_call | solution.py:249
  437.6 3.4 shard_map.265
  441.9 2.6 shard_map.253
  450.8 6.1 %collective-permute-done.41.refs_1_ = f32[128,1152]{1,0:T(8,128)} collective-permute-done((f32[128,1152]{1,0:T(8,128)}, f32[128,1152]{1,0:T(8,128)}, u32[]{:S(2)}, u32[]{:S(2)}) %collective-permute-start.41) | collective-permute-done | bytes 589856 | tf_op jit(solution)/shard_map/grad_in_first1/ppermute | solution.py:44
  456.8 2.4 shard_map.266
  459.9 5.3 all-to-all-start.5
  471.0 8.3 %multiply_add_fusion = f32[1,288,4608]{2,1,0:T(8,128)} fusion(f16[1,288,4608]{2,1,0:T(8,128)(2,1)} %collective-permute-done.37, f32[2,288,4608]{2,1,0:T(8,128)} %collective-permute-done.32, s32[]{:T(128)S(6)} %select_n.121, f32[2,288,4608]{2,1,0:T(8,128)} %get-tuple-element.185, f32[4608]{0:T(1024)S(1)} %broadcast_divide_fusion), kind=kLoop, calls=%fused_computation.1 | loop fusion | flops 5308416 | bytes 18597892 | tf_op jit(solution)/shard_map/add | solution.py:192
  479.4 7.7 %all-to-all-done.5.refs_0_ = bf16[4,3,144,256]{3,2,1,0:T(8,128)(2,1)S(1)} async-done(((bf16[4,3,144,256]{3,2,1,0:T(8,128)(2,1)}), bf16[4,3,144,256]{3,2,1,0:T(8,128)(2,1)S(1)}, u32[]{:S(2)}, u32[]{:S(2)}) %all-to-all-start.5) | async-done | bytes 884768 | tf_op jit(solution)/shard_map/grad_qkv0/all_to_all | solution.py:49
  492.8 2.2 add_add_fusion.1
  495.1 4.2 all-to-all-start.10
  499.3 2.4 add_add_fusion
  503.5 2.6 collective-permute-done.38.refs_1_
  509.4 3.8 collective-permute-start.64
  513.3 2.3 fusion.1
  517.6 17.1 %collective-permute-done.49 = f32[234,128]{1,0:T(8,128)S(1)} collective-permute-done((f32[234,128]{1,0:T(8,128)S(1)}, f32[234,128]{1,0:T(8,128)S(1)}, u32[]{:S(2)}, u32[]{:S(2)}) %collective-permute-start.49) | collective-permute-done | bytes 119840 | tf_op jit(solution)/shard_map/sums/ppermute | solution.py:44
  534.9 11.3 %collective-permute-done.50 = f32[234,128]{1,0:T(8,128)S(1)} collective-permute-done((f32[234,128]{1,0:T(8,128)S(1)}, f32[234,128]{1,0:T(8,128)S(1)}, u32[]{:S(2)}, u32[]{:S(2)}) %collective-permute-start.50) | collective-permute-done | bytes 119840 | tf_op jit(solution)/shard_map/sums/ppermute | solution.py:44
  554.7 3.1 fusion.3
  559.0 3.9 collective-permute-start.67
  563.7 12.2 %collective-permute-done.45.refs_3_ = f32[128,1152]{1,0:T(8,128)S(1)} collective-permute-done((f32[128,1152]{1,0:T(8,128)S(1)}, f32[128,1152]{1,0:T(8,128)S(1)}, u32[]{:S(2)}, u32[]{:S(2)}) %collective-permute-start.45) | collective-permute-done | bytes 589856 | tf_op jit(solution)/shard_map/grad_latent0/ppermute | solution.py:44
  576.0 3.3 shard_map.272
  589.9 2.5 collective-permute-done.55
  594.3 2.7 collective-permute-done.56
  (539 shorter events, 201.9 us)
Async XLA Ops:
  7.2 151.5 %all-gather.4.cloned.1.call-start = ((), (), s32[]{:S(2)}) async-start(), calls=%async_computation.11 | async-start | bytes 1566720 | tf_op jit(solution)/shard_map/proj_weights/all_gather | solution.py:54
  19.2 12.7 %collective-permute-start.3 = (f32[1,3,3456]{2,1,0:T(4,128)S(1)}, f32[1,3,3456]{2,1,0:T(4,128)S(1)}, u32[]{:S(2)}, u32[]{:S(2)}) collective-permute-start(f32[1,3,3456]{2,1,0:T(4,128)S(1)} %slice.213), channel_id=1, source_target_pairs={{0,8},{8,0},{16,24},{24,16},{1,9},{9,1},{17,25},{25,17},{2,10},{10... | collective-permute-start | bytes 124424 | tf_op jit(solution)/shard_map/mod_f/ppermute | solution.py:44
  20.1 36.1 %collective-permute-start.10 = (bf16[1,128,1152]{2,1,0:T(8,128)(2,1)S(1)}, bf16[1,128,1152]{2,1,0:T(8,128)(2,1)}, u32[]{:S(2)}, u32[]{:S(2)}) collective-permute-start(bf16[1,128,1152]{2,1,0:T(8,128)(2,1)S(1)} %get-tuple-element.126.refs_0_.refs_3_.refs_2_), channel_id=1, source_target_pairs={{0,6},{2,0},{4,2},{6,4},{1,7},{3,1},{5,3},{7,5},{8,14},{10,8},{12,... | collective-permute-start | bytes 884744 | tf_op jit(solution)/shard_map/latent0_left/ppermute | solution.py:38
  24.2 29.0 %collective-permute-start.7 = (bf16[1,128,1152]{2,1,0:T(8,128)(2,1)S(1)}, bf16[1,128,1152]{2,1,0:T(8,128)(2,1)}, u32[]{:S(2)}, u32[]{:S(2)}) collective-permute-start(bf16[1,128,1152]{2,1,0:T(8,128)(2,1)S(1)} %get-tuple-element.126.refs_0_.refs_3_.refs_2_), channel_id=1, source_target_pairs={{0,2},{2,4},{4,6},{6,0},{1,3},{3,5},{5,7},{7,1},{8,10},{10,12},{12... | collective-permute-start | bytes 884744 | tf_op jit(solution)/shard_map/latent0_right/ppermute | solution.py:38
  26.8 30.9 %all-to-all-start = ((bf16[4,72,432]{2,1,0:T(8,128)(2,1)}), bf16[4,72,432]{2,1,0:T(8,128)(2,1)S(1)}, u32[]{:S(2)}, u32[]{:S(2)}) async-start(bf16[4,72,432]{2,1,0:T(8,128)(2,1)} %copy.88), calls=%async_computation | async-start | bytes 589824 | tf_op jit(solution)/shard_map/qkv_c/all_to_all | solution.py:49
  31.9 183.9 %all-gather.6.cloned.1.call-start = ((), (), s32[]{:S(2)}) async-start(), calls=%async_computation.12 | async-start | bytes 11280384 | tf_op jit(solution)/shard_map/feed_weights/all_gather | solution.py:54
  31.9 14.4 %collective-permute-start.4 = (f32[3,3456]{1,0:T(4,128)S(1)}, f32[3,3456]{1,0:T(4,128)S(1)}, u32[]{:S(2)}, u32[]{:S(2)}) collective-permute-start(f32[3,3456]{1,0:T(4,128)S(1)} %fusion.9), channel_id=1, source_target_pairs={{0,2},{2,0},{4,6},{6,4},{1,3},{3,1},{5,7},{7,5},{8,10},{10,8},{12,... | collective-permute-start | bytes 124424 | tf_op jit(solution)/shard_map/mod_c/ppermute | solution.py:44
  53.2 14.0 %collective-permute-start.9 = (bf16[1,128,1152]{2,1,0:T(8,128)(2,1)}, bf16[1,128,1152]{2,1,0:T(8,128)(2,1)S(1)}, u32[]{:S(2)}, u32[]{:S(2)}) collective-permute-start(bf16[1,128,1152]{2,1,0:T(8,128)(2,1)} %collective-permute-done.7.refs_2_), channel_id=1, source_target_pairs={{0,1},{1,0},{2,3},{3,2},{4,5},{5,4},{6,7},{7,6},{8,9},{9,8},{10,11... | collective-permute-start | bytes 884744 | tf_op jit(solution)/shard_map/latent0_t/ppermute | solution.py:44
  53.7 13.5 %collective-permute-start.8 = (bf16[1,128,1152]{2,1,0:T(8,128)(2,1)}, bf16[1,128,1152]{2,1,0:T(8,128)(2,1)S(1)}, u32[]{:S(2)}, u32[]{:S(2)}) collective-permute-start(bf16[1,128,1152]{2,1,0:T(8,128)(2,1)} %collective-permute-done.7.refs_2_), channel_id=1, source_target_pairs={{0,2},{2,4},{4,6},{6,0},{1,3},{3,5},{5,7},{7,1},{8,10},{10,12},{12... | collective-permute-start | bytes 884744 | tf_op jit(solution)/shard_map/latent0_right/ppermute | solution.py:38
  57.7 15.1 %collective-permute-start.15 = (bf16[4,72,432]{2,1,0:T(8,128)(2,1)S(1)}, bf16[4,72,432]{2,1,0:T(8,128)(2,1)}, u32[]{:S(2)}, u32[]{:S(2)}) collective-permute-start(bf16[4,72,432]{2,1,0:T(8,128)(2,1)S(1)} %all-to-all-done.refs_1_.refs_0_), channel_id=1, source_target_pairs={{0,16},{8,24},{16,0},{24,8},{1,17},{9,25},{17,1},{25,9},{2,18},{10... | collective-permute-start | bytes 746504 | tf_op jit(solution)/shard_map/qkv_1/ppermute | solution.py:44
  60.1 13.6 %collective-permute-start.16 = (bf16[4,72,432]{2,1,0:T(8,128)(2,1)S(1)}, bf16[4,72,432]{2,1,0:T(8,128)(2,1)}, u32[]{:S(2)}, u32[]{:S(2)}) collective-permute-start(bf16[4,72,432]{2,1,0:T(8,128)(2,1)S(1)} %all-to-all-done.refs_1_.refs_0_), channel_id=1, source_target_pairs={{0,8},{8,0},{16,24},{24,16},{1,9},{9,1},{17,25},{25,17},{2,10},{10... | collective-permute-start | bytes 746504 | tf_op jit(solution)/shard_map/qkv_0/ppermute | solution.py:44
  69.7 28.1 %collective-permute-start.20 = (bf16[2,128,1152]{2,1,0:T(8,128)(2,1)S(1)}, bf16[2,128,1152]{2,1,0:T(8,128)(2,1)S(1)}, u32[]{:S(2)}, u32[]{:S(2)}) collective-permute-start(bf16[2,128,1152]{2,1,0:T(8,128)(2,1)S(1)} %get-tuple-element.127.refs_0_.refs_3_.refs_2_), channel_id=1, source_target_pairs={{0,6},{2,0},{4,2},{6,4},{1,7},{3,1},{5,3},{7,5},{8,14},{10,8},{12,... | collective-permute-start | bytes 1769480 | tf_op jit(solution)/shard_map/latent1_left/ppermute | solution.py:38
  72.1 25.6 %collective-permute-start.12 = (bf16[2,128,1152]{2,1,0:T(8,128)(2,1)S(1)}, bf16[2,128,1152]{2,1,0:T(8,128)(2,1)S(1)}, u32[]{:S(2)}, u32[]{:S(2)}) collective-permute-start(bf16[2,128,1152]{2,1,0:T(8,128)(2,1)S(1)} %get-tuple-element.127.refs_0_.refs_3_.refs_2_), channel_id=1, source_target_pairs={{0,2},{2,4},{4,6},{6,0},{1,3},{3,5},{5,7},{7,1},{8,10},{10,12},{12... | collective-permute-start | bytes 1769480 | tf_op jit(solution)/shard_map/latent1_right/ppermute | solution.py:38
  98.8 21.0 %collective-permute-start.18 = (bf16[2,128,1152]{2,1,0:T(8,128)(2,1)S(1)}, bf16[2,128,1152]{2,1,0:T(8,128)(2,1)}, u32[]{:S(2)}, u32[]{:S(2)}) collective-permute-start(bf16[2,128,1152]{2,1,0:T(8,128)(2,1)S(1)} %shard_map.234), channel_id=1, source_target_pairs={{0,2},{2,4},{4,6},{6,0},{1,3},{3,5},{5,7},{7,1},{8,10},{10,12},{12... | collective-permute-start | bytes 1769480 | tf_op jit(solution)/shard_map/latent1_right/ppermute | solution.py:38
  100.9 31.5 %collective-permute-start.21 = (bf16[2,128,1152]{2,1,0:T(8,128)(2,1)S(1)}, bf16[2,128,1152]{2,1,0:T(8,128)(2,1)}, u32[]{:S(2)}, u32[]{:S(2)}) collective-permute-start(bf16[2,128,1152]{2,1,0:T(8,128)(2,1)S(1)} %collective-permute-done.20.refs_6_.refs_3_), channel_id=1, source_target_pairs={{0,1},{1,0},{2,3},{3,2},{4,5},{5,4},{6,7},{7,6},{8,9},{9,8},{10,11... | collective-permute-start | bytes 1769480 | tf_op jit(solution)/shard_map/latent1_t/ppermute | solution.py:44
  102.4 30.0 %collective-permute-start.13 = (bf16[2,128,1152]{2,1,0:T(8,128)(2,1)S(1)}, bf16[2,128,1152]{2,1,0:T(8,128)(2,1)}, u32[]{:S(2)}, u32[]{:S(2)}) collective-permute-start(bf16[2,128,1152]{2,1,0:T(8,128)(2,1)S(1)} %collective-permute-done.12.refs_0_.refs_2_), channel_id=1, source_target_pairs={{0,1},{1,0},{2,3},{3,2},{4,5},{5,4},{6,7},{7,6},{8,9},{9,8},{10,11... | collective-permute-start | bytes 1769480 | tf_op jit(solution)/shard_map/latent1_t/ppermute | solution.py:44
  119.8 21.5 %collective-permute-start.19 = (bf16[2,128,1152]{2,1,0:T(8,128)(2,1)}, bf16[2,128,1152]{2,1,0:T(8,128)(2,1)}, u32[]{:S(2)}, u32[]{:S(2)}) collective-permute-start(bf16[2,128,1152]{2,1,0:T(8,128)(2,1)} %collective-permute-done.18.refs_4_), channel_id=1, source_target_pairs={{0,1},{1,0},{2,3},{3,2},{4,5},{5,4},{6,7},{7,6},{8,9},{9,8},{10,11... | collective-permute-start | bytes 1769480 | tf_op jit(solution)/shard_map/latent1_t/ppermute | solution.py:44
  121.3 33.9 %all-to-all-start.3 = ((bf16[4,144,256]{2,1,0:T(8,128)(2,1)}), bf16[4,144,256]{2,1,0:T(8,128)(2,1)S(1)}, u32[]{:S(2)}, u32[]{:S(2)}) async-start(bf16[4,144,256]{2,1,0:T(8,128)(2,1)} %copy-done.91), calls=%async_computation.3 | async-start | bytes 589824 | tf_op jit(solution)/shard_map/mixed0/all_to_all | solution.py:49
  155.2 21.8 %all-to-all-start.2 = ((bf16[4,144,256]{2,1,0:T(8,128)(2,1)}), bf16[4,144,256]{2,1,0:T(8,128)(2,1)S(1)}, u32[]{:S(2)}, u32[]{:S(2)}) async-start(bf16[4,144,256]{2,1,0:T(8,128)(2,1)} %get-tuple-element.137), calls=%async_computation.2 | async-start | bytes 589824 | tf_op jit(solution)/shard_map/mixed1/all_to_all | solution.py:49
  164.8 29.6 %collective-permute-start.26 = (f32[128,1152]{1,0:T(8,128)}, f32[128,1152]{1,0:T(8,128)}, u32[]{:S(2)}, u32[]{:S(2)}) collective-permute-start(f32[128,1152]{1,0:T(8,128)} %get-tuple-element.150), channel_id=1, source_target_pairs={{0,1},{1,0},{2,3},{3,2},{4,5},{5,4},{6,7},{7,6},{8,9},{9,8},{10,11... | collective-permute-start | bytes 1769480 | tf_op jit(solution)/shard_map/attended0/ppermute | solution.py:44
  181.3 30.8 %collective-permute-start.24 = (f32[128,1152]{1,0:T(8,128)}, f32[128,1152]{1,0:T(8,128)}, u32[]{:S(2)}, u32[]{:S(2)}) collective-permute-start(f32[128,1152]{1,0:T(8,128)} %get-tuple-element.147), channel_id=1, source_target_pairs={{0,1},{1,0},{2,3},{3,2},{4,5},{5,4},{6,7},{7,6},{8,9},{9,8},{10,11... | collective-permute-start | bytes 1769480 | tf_op jit(solution)/shard_map/attended1/ppermute | solution.py:44
  190.7 15.6 %all-to-all-start.1 = ((bf16[4,144,256]{2,1,0:T(8,128)(2,1)}), bf16[4,144,256]{2,1,0:T(8,128)(2,1)S(1)}, u32[]{:S(2)}, u32[]{:S(2)}) async-start(bf16[4,144,256]{2,1,0:T(8,128)(2,1)} %copy-done.93), calls=%async_computation.1 | async-start | bytes 589824 | tf_op jit(solution)/shard_map/mixed2/all_to_all | solution.py:49
  194.3 241.1 %all-gather.8.cloned.1.call-start = ((), (), s32[]{:S(2)}) async-start(), calls=%async_computation.13 | async-start | bytes 4386816 | tf_op jit(solution)/shard_map/qkv_weights/all_gather | solution.py:54
  200.3 15.4 %collective-permute-start.27 = (bf16[128,1152]{1,0:T(8,128)(2,1)}, bf16[128,1152]{1,0:T(8,128)(2,1)}, u32[]{:S(2)}, u32[]{:S(2)}) collective-permute-start(bf16[128,1152]{1,0:T(8,128)(2,1)} %get-tuple-element.151.refs_0_), channel_id=1, source_target_pairs={{0,1},{1,0},{2,3},{3,2},{4,5},{5,4},{6,7},{7,6},{8,9},{9,8},{10,11... | collective-permute-start | bytes 884744 | tf_op jit(solution)/shard_map/in_second0/ppermute | solution.py:44
  209.6 21.2 %collective-permute-start.22 = (f32[128,1152]{1,0:T(8,128)}, f32[128,1152]{1,0:T(8,128)}, u32[]{:S(2)}, u32[]{:S(2)}) collective-permute-start(f32[128,1152]{1,0:T(8,128)} %get-tuple-element.142), channel_id=1, source_target_pairs={{0,1},{1,0},{2,3},{3,2},{4,5},{5,4},{6,7},{7,6},{8,9},{9,8},{10,11... | collective-permute-start | bytes 1769480 | tf_op jit(solution)/shard_map/attended2/ppermute | solution.py:44
  215.2 19.3 %collective-permute-start.25 = (bf16[128,1152]{1,0:T(8,128)(2,1)S(1)}, bf16[128,1152]{1,0:T(8,128)(2,1)}, u32[]{:S(2)}, u32[]{:S(2)}) collective-permute-start(bf16[128,1152]{1,0:T(8,128)(2,1)S(1)} %get-tuple-element.148.refs_0_), channel_id=1, source_target_pairs={{0,1},{1,0},{2,3},{3,2},{4,5},{5,4},{6,7},{7,6},{8,9},{9,8},{10,11... | collective-permute-start | bytes 884744 | tf_op jit(solution)/shard_map/in_second1/ppermute | solution.py:44
  229.3 18.8 %collective-permute-start.28 = (f32[128,1152]{1,0:T(8,128)S(1)}, f32[128,1152]{1,0:T(8,128)S(1)}, u32[]{:S(2)}, u32[]{:S(2)}) collective-permute-start(f32[128,1152]{1,0:T(8,128)S(1)} %get-tuple-element.164), channel_id=1, source_target_pairs={{0,1},{1,0},{2,3},{3,2},{4,5},{5,4},{6,7},{7,6},{8,9},{9,8},{10,11... | collective-permute-start | bytes 1769480 | tf_op jit(solution)/shard_map/grad_in_second0/ppermute | solution.py:44
  233.9 16.4 %collective-permute-start.23 = (bf16[128,1152]{1,0:T(8,128)(2,1)S(1)}, bf16[128,1152]{1,0:T(8,128)(2,1)S(1)}, u32[]{:S(2)}, u32[]{:S(2)}) collective-permute-start(bf16[128,1152]{1,0:T(8,128)(2,1)S(1)} %get-tuple-element.143.refs_0_), channel_id=1, source_target_pairs={{0,1},{1,0},{2,3},{3,2},{4,5},{5,4},{6,7},{7,6},{8,9},{9,8},{10,11... | collective-permute-start | bytes 884744 | tf_op jit(solution)/shard_map/in_second2/ppermute | solution.py:44
  248.7 25.7 %collective-permute-start.31 = (bf16[128,1152]{1,0:T(8,128)(2,1)S(1)}, bf16[128,1152]{1,0:T(8,128)(2,1)S(1)}, u32[]{:S(2)}, u32[]{:S(2)}) collective-permute-start(bf16[128,1152]{1,0:T(8,128)(2,1)S(1)} %get-tuple-element.175.refs_0_), channel_id=1, source_target_pairs={{0,1},{1,0},{2,3},{3,2},{4,5},{5,4},{6,7},{7,6},{8,9},{9,8},{10,11... | collective-permute-start | bytes 884744 | tf_op jit(solution)/shard_map/grad_attended0/ppermute | solution.py:44
  281.7 106.9 %collective-permute-start.32 = (f32[2,288,4608]{2,1,0:T(8,128)}, f32[2,288,4608]{2,1,0:T(8,128)}, u32[]{:S(2)}, u32[]{:S(2)}) collective-permute-start(f32[2,288,4608]{2,1,0:T(8,128)} %get-tuple-element.183.refs_5_), channel_id=1, source_target_pairs={{0,8},{8,0},{16,24},{24,16},{1,9},{9,1},{17,25},{25,17},{2,10},{10... | collective-permute-start | bytes 31850504 | tf_op jit(solution)/shard_map/grad_feed_0/ppermute | solution.py:44
  285.3 17.3 %collective-permute-start.39 = (f32[128,1152]{1,0:T(8,128)}, f32[128,1152]{1,0:T(8,128)}, u32[]{:S(2)}, u32[]{:S(2)}) collective-permute-start(f32[128,1152]{1,0:T(8,128)} %copy-done.109), channel_id=1, source_target_pairs={{0,1},{1,0},{2,3},{3,2},{4,5},{5,4},{6,7},{7,6},{8,9},{9,8},{10,11... | collective-permute-start | bytes 1769480 | tf_op jit(solution)/shard_map/grad_in_second1/ppermute | solution.py:44
  286.6 11.5 %collective-permute-start.33 = (f32[4,8,128]{2,1,0:T(8,128)S(1)}, f32[4,8,128]{2,1,0:T(8,128)S(1)}, u32[]{:S(2)}, u32[]{:S(2)}) collective-permute-start(f32[4,8,128]{2,1,0:T(8,128)S(1)} %maximum_maximum_fusion), channel_id=1, source_target_pairs={{0,8},{8,0},{16,24},{24,16},{1,9},{9,1},{17,25},{25,17},{2,10},{10... | collective-permute-start | bytes 49160 | tf_op jit(solution)/shard_map/bounds/ppermute | solution.py:44
  298.1 13.0 %collective-permute-start.34 = (f32[4,8,128]{2,1,0:T(8,128)S(1)}, f32[4,8,128]{2,1,0:T(8,128)S(1)}, u32[]{:S(2)}, u32[]{:S(2)}) collective-permute-start(f32[4,8,128]{2,1,0:T(8,128)S(1)} %max.24), channel_id=1, source_target_pairs={{0,16},{8,24},{16,0},{24,8},{1,17},{9,25},{17,1},{25,9},{2,18},{10... | collective-permute-start | bytes 49160 | tf_op jit(solution)/shard_map/bounds/ppermute | solution.py:44
  301.4 30.1 %collective-permute-start.42 = (f32[128,1152]{1,0:T(8,128)}, f32[128,1152]{1,0:T(8,128)}, u32[]{:S(2)}, u32[]{:S(2)}) collective-permute-start(f32[128,1152]{1,0:T(8,128)} %copy-done.108), channel_id=1, source_target_pairs={{0,1},{1,0},{2,3},{3,2},{4,5},{5,4},{6,7},{7,6},{8,9},{9,8},{10,11... | collective-permute-start | bytes 1769480 | tf_op jit(solution)/shard_map/grad_in_second2/ppermute | solution.py:44
  309.0 17.3 %collective-permute-start.40 = (bf16[128,1152]{1,0:T(8,128)(2,1)}, bf16[128,1152]{1,0:T(8,128)(2,1)}, u32[]{:S(2)}, u32[]{:S(2)}) collective-permute-start(bf16[128,1152]{1,0:T(8,128)(2,1)} %get-tuple-element.197.refs_0_), channel_id=1, source_target_pairs={{0,1},{1,0},{2,3},{3,2},{4,5},{5,4},{6,7},{7,6},{8,9},{9,8},{10,11... | collective-permute-start | bytes 884744 | tf_op jit(solution)/shard_map/grad_attended1/ppermute | solution.py:44
  309.9 71.5 %collective-permute-start.29 = (bf16[384,1152]{1,0:T(8,128)(2,1)}, bf16[384,1152]{1,0:T(8,128)(2,1)}, u32[]{:S(2)}, u32[]{:S(2)}) collective-permute-start(bf16[384,1152]{1,0:T(8,128)(2,1)} %get-tuple-element.166), channel_id=1, source_target_pairs={{0,1},{1,0},{2,3},{3,2},{4,5},{5,4},{6,7},{7,6},{8,9},{9,8},{10,11... | collective-permute-start | bytes 2654216 | tf_op jit(solution)/shard_map/feed_out/ppermute | solution.py:44
  318.9 18.9 %all-to-all-start.4 = ((bf16[4,144,256]{2,1,0:T(8,128)(2,1)}), bf16[4,144,256]{2,1,0:T(8,128)(2,1)}, u32[]{:S(2)}, u32[]{:S(2)}) async-start(bf16[4,144,256]{2,1,0:T(8,128)(2,1)} %bitcast.169), calls=%async_computation.4 | async-start | bytes 589824 | tf_op jit(solution)/shard_map/grad_mixed0/all_to_all | solution.py:49
  334.1 22.4 %collective-permute-start.43 = (bf16[128,1152]{1,0:T(8,128)(2,1)S(1)}, bf16[128,1152]{1,0:T(8,128)(2,1)}, u32[]{:S(2)}, u32[]{:S(2)}) collective-permute-start(bf16[128,1152]{1,0:T(8,128)(2,1)S(1)} %get-tuple-element.210.refs_0_), channel_id=1, source_target_pairs={{0,1},{1,0},{2,3},{3,2},{4,5},{5,4},{6,7},{7,6},{8,9},{9,8},{10,11... | collective-permute-start | bytes 884744 | tf_op jit(solution)/shard_map/grad_attended2/ppermute | solution.py:44
  337.8 22.2 %all-to-all-start.6 = ((bf16[4,144,256]{2,1,0:T(8,128)(2,1)}), bf16[4,144,256]{2,1,0:T(8,128)(2,1)}, u32[]{:S(2)}, u32[]{:S(2)}) async-start(bf16[4,144,256]{2,1,0:T(8,128)(2,1)} %bitcast.170), calls=%async_computation.6 | async-start | bytes 589824 | tf_op jit(solution)/shard_map/grad_mixed1/all_to_all | solution.py:49
  360.0 23.3 %all-to-all-start.8 = ((bf16[4,144,256]{2,1,0:T(8,128)(2,1)}), bf16[4,144,256]{2,1,0:T(8,128)(2,1)}, u32[]{:S(2)}, u32[]{:S(2)}) async-start(bf16[4,144,256]{2,1,0:T(8,128)(2,1)} %bitcast.171), calls=%async_computation.8 | async-start | bytes 589824 | tf_op jit(solution)/shard_map/grad_mixed2/all_to_all | solution.py:49
  383.3 35.7 %all-to-all-start.7 = ((bf16[4,3,144,256]{3,2,1,0:T(8,128)(2,1)}), bf16[4,3,144,256]{3,2,1,0:T(8,128)(2,1)}, u32[]{:S(2)}, u32[]{:S(2)}) async-start(bf16[4,3,144,256]{3,2,1,0:T(8,128)(2,1)} %copy-done.63), calls=%async_computation.7 | async-start | bytes 1769472 | tf_op jit(solution)/shard_map/grad_qkv1/all_to_all | solution.py:49
  395.3 75.7 %collective-permute-start.37 = (f16[1,288,4608]{2,1,0:T(8,128)(2,1)}, f16[1,288,4608]{2,1,0:T(8,128)(2,1)}, u32[]{:S(2)}, u32[]{:S(2)}) collective-permute-start(f16[1,288,4608]{2,1,0:T(8,128)(2,1)} %multiply_convert_fusion), channel_id=1, source_target_pairs={{0,16},{8,24},{16,0},{24,8},{1,17},{9,25},{17,1},{25,9},{2,18},{10... | collective-permute-start | bytes 7962632 | tf_op jit(solution)/shard_map/grad_feed_1/ppermute | solution.py:44
  400.4 41.5 %collective-permute-start.30 = (bf16[384,1152]{1,0:T(8,128)(2,1)}, bf16[384,1152]{1,0:T(8,128)(2,1)S(1)}, u32[]{:S(2)}, u32[]{:S(2)}) collective-permute-start(bf16[384,1152]{1,0:T(8,128)(2,1)} %get-tuple-element.172.refs_0_), channel_id=1, source_target_pairs={{0,1},{1,0},{2,3},{3,2},{4,5},{5,4},{6,7},{7,6},{8,9},{9,8},{10,11... | collective-permute-start | bytes 2654216 | tf_op jit(solution)/shard_map/output/ppermute | solution.py:44
  405.7 38.9 %collective-permute-start.60 = (f32[2,288,576]{2,1,0:T(8,128)}, f32[2,288,576]{2,1,0:T(8,128)}, u32[]{:S(2)}, u32[]{:S(2)}) collective-permute-start(f32[2,288,576]{2,1,0:T(8,128)} %get-tuple-element.238), channel_id=1, source_target_pairs={{0,8},{8,0},{16,24},{24,16},{1,9},{9,1},{17,25},{25,17},{2,10},{10... | collective-permute-start | bytes 3981320 | tf_op jit(solution)/shard_map/grad_proj_0/ppermute | solution.py:44
  419.0 40.9 %all-to-all-start.9 = ((bf16[4,3,144,256]{3,2,1,0:T(8,128)(2,1)}), bf16[4,3,144,256]{3,2,1,0:T(8,128)(2,1)S(1)}, u32[]{:S(2)}, u32[]{:S(2)}) async-start(bf16[4,3,144,256]{3,2,1,0:T(8,128)(2,1)} %get-tuple-element.214), calls=%async_computation.9 | async-start | bytes 1769472 | tf_op jit(solution)/shard_map/grad_qkv2/all_to_all | solution.py:49
  434.7 12.9 %collective-permute-start.58 = (f32[2,288,432]{2,1,0:T(8,128)}, f32[2,288,432]{2,1,0:T(8,128)}, u32[]{:S(2)}, u32[]{:S(2)}) collective-permute-start(f32[2,288,432]{2,1,0:T(8,128)} %get-tuple-element.234), channel_id=1, source_target_pairs={{0,8},{8,0},{16,24},{24,16},{1,9},{9,1},{17,25},{25,17},{2,10},{10... | collective-permute-start | bytes 2985992 | tf_op jit(solution)/shard_map/grad_qkvw_0/ppermute | solution.py:44
  441.0 15.8 %collective-permute-start.41 = (f32[128,1152]{1,0:T(8,128)}, f32[128,1152]{1,0:T(8,128)}, u32[]{:S(2)}, u32[]{:S(2)}) collective-permute-start(f32[128,1152]{1,0:T(8,128)} %get-tuple-element.203), channel_id=1, source_target_pairs={{0,1},{1,0},{2,3},{3,2},{4,5},{5,4},{6,7},{7,6},{8,9},{9,8},{10,11... | collective-permute-start | bytes 1769480 | tf_op jit(solution)/shard_map/grad_in_first1/ppermute | solution.py:44
  446.8 52.5 %collective-permute-start.61 = (f32[1,288,576]{2,1,0:T(8,128)}, f32[1,288,576]{2,1,0:T(8,128)}, u32[]{:S(2)}, u32[]{:S(2)}) collective-permute-start(f32[1,288,576]{2,1,0:T(8,128)} %dynamic-slice_add_fusion), channel_id=1, source_target_pairs={{0,16},{8,24},{16,0},{24,8},{1,17},{9,25},{17,1},{25,9},{2,18},{10... | collective-permute-start | bytes 1990664 | tf_op jit(solution)/shard_map/grad_proj_1/ppermute | solution.py:44
  449.5 43.3 %collective-permute-start.59 = (f32[1,288,432]{2,1,0:T(8,128)}, f32[1,288,432]{2,1,0:T(8,128)}, u32[]{:S(2)}, u32[]{:S(2)}) collective-permute-start(f32[1,288,432]{2,1,0:T(8,128)} %dynamic-slice_add_fusion.1), channel_id=1, source_target_pairs={{0,16},{8,24},{16,0},{24,8},{1,17},{9,25},{17,1},{25,9},{2,18},{10... | collective-permute-start | bytes 1493000 | tf_op jit(solution)/shard_map/grad_qkvw_1/ppermute | solution.py:44
  459.2 99.8 %collective-permute-start.46 = (f32[128,1152]{1,0:T(8,128)}, f32[128,1152]{1,0:T(8,128)}, u32[]{:S(2)}, u32[]{:S(2)}) collective-permute-start(f32[128,1152]{1,0:T(8,128)} %get-tuple-element.205.refs_1_), channel_id=1, source_target_pairs={{0,1},{1,0},{2,3},{3,2},{4,5},{5,4},{6,7},{7,6},{8,9},{9,8},{10,11... | collective-permute-start | bytes 1769480 | tf_op jit(solution)/shard_map/grad_latent1/ppermute | solution.py:44
  459.9 27.2 %all-to-all-start.5 = ((bf16[4,3,144,256]{3,2,1,0:T(8,128)(2,1)}), bf16[4,3,144,256]{3,2,1,0:T(8,128)(2,1)S(1)}, u32[]{:S(2)}, u32[]{:S(2)}) async-start(bf16[4,3,144,256]{3,2,1,0:T(8,128)(2,1)} %get-tuple-element.184), calls=%async_computation.5 | async-start | bytes 1769472 | tf_op jit(solution)/shard_map/grad_qkv0/all_to_all | solution.py:49
  469.7 32.0 %collective-permute-start.44 = (f32[128,1152]{1,0:T(8,128)}, f32[128,1152]{1,0:T(8,128)}, u32[]{:S(2)}, u32[]{:S(2)}) collective-permute-start(f32[128,1152]{1,0:T(8,128)} %get-tuple-element.216), channel_id=1, source_target_pairs={{0,1},{1,0},{2,3},{3,2},{4,5},{5,4},{6,7},{7,6},{8,9},{9,8},{10,11... | collective-permute-start | bytes 1769480 | tf_op jit(solution)/shard_map/grad_in_first2/ppermute | solution.py:44
  491.5 14.6 %collective-permute-start.38 = (f32[128,1152]{1,0:T(8,128)}, f32[128,1152]{1,0:T(8,128)}, u32[]{:S(2)}, u32[]{:S(2)}) collective-permute-start(f32[128,1152]{1,0:T(8,128)} %get-tuple-element.190), channel_id=1, source_target_pairs={{0,1},{1,0},{2,3},{3,2},{4,5},{5,4},{6,7},{7,6},{8,9},{9,8},{10,11... | collective-permute-start | bytes 1769480 | tf_op jit(solution)/shard_map/grad_in_first0/ppermute | solution.py:44
  495.1 53.4 %all-to-all-start.10 = ((f32[4,72,432]{2,1,0:T(8,128)}), f32[4,72,432]{2,1,0:T(8,128)}, u32[]{:S(2)}, u32[]{:S(2)}) async-start(f32[4,72,432]{2,1,0:T(8,128)} %bitcast.204), calls=%async_computation.10 | async-start | bytes 1179648 | tf_op jit(solution)/shard_map/grad_qkvw_c/all_to_all | solution.py:49
  509.3 25.5 %collective-permute-start.62 = (f32[72,576]{1,0:T(8,128)S(1)}, f32[72,576]{1,0:T(8,128)S(1)}, u32[]{:S(2)}, u32[]{:S(2)}) collective-permute-start(f32[72,576]{1,0:T(8,128)S(1)} %get-tuple-element.300), channel_id=1, source_target_pairs={{0,2},{2,4},{4,6},{6,0},{1,3},{3,5},{5,7},{7,1},{8,10},{10,12},{12... | collective-permute-start | bytes 497672 | tf_op jit(solution)/shard_map/grad_proj_ring/ppermute | solution.py:38
  509.4 37.5 %collective-permute-start.64 = (f32[72,576]{1,0:T(8,128)S(1)}, f32[72,576]{1,0:T(8,128)S(1)}, u32[]{:S(2)}, u32[]{:S(2)}) collective-permute-start(f32[72,576]{1,0:T(8,128)S(1)} %get-tuple-element.301), channel_id=1, source_target_pairs={{0,6},{2,0},{4,2},{6,4},{1,7},{3,1},{5,3},{7,5},{8,14},{10,8},{12,... | collective-permute-start | bytes 497672 | tf_op jit(solution)/shard_map/grad_proj_ring/ppermute | solution.py:38
  513.2 21.5 %collective-permute-start.49 = (f32[234,128]{1,0:T(8,128)S(1)}, f32[234,128]{1,0:T(8,128)S(1)}, u32[]{:S(2)}, u32[]{:S(2)}) collective-permute-start(f32[234,128]{1,0:T(8,128)S(1)} %bitcast_add_fusion.4), channel_id=1, source_target_pairs={{0,2},{2,0},{4,6},{6,4},{1,3},{3,1},{5,7},{7,5},{8,10},{10,8},{12,... | collective-permute-start | bytes 359432 | tf_op jit(solution)/shard_map/sums/ppermute | solution.py:44
  515.6 39.1 %collective-permute-start.65 = (f16[72,4608]{1,0:T(8,128)(2,1)}, f16[72,4608]{1,0:T(8,128)(2,1)}, u32[]{:S(2)}, u32[]{:S(2)}) collective-permute-start(f16[72,4608]{1,0:T(8,128)(2,1)} %fusion.1), channel_id=1, source_target_pairs={{0,2},{2,4},{4,6},{6,0},{1,3},{3,5},{5,7},{7,1},{8,10},{10,12},{12... | collective-permute-start | bytes 1990664 | tf_op jit(solution)/shard_map/grad_feed_ring/ppermute | solution.py:38
  534.8 12.1 %collective-permute-start.63 = (f32[72,576]{1,0:T(8,128)S(1)}, f32[72,576]{1,0:T(8,128)S(1)}, u32[]{:S(2)}, u32[]{:S(2)}) collective-permute-start(f32[72,576]{1,0:T(8,128)S(1)} %bitcast_add_fusion.2), channel_id=1, source_target_pairs={{0,2},{2,4},{4,6},{6,0},{1,3},{3,5},{5,7},{7,1},{8,10},{10,12},{12... | collective-permute-start | bytes 497672 | tf_op jit(solution)/shard_map/grad_proj_ring/ppermute | solution.py:38
  547.6 16.1 %collective-permute-start.47 = (f32[128,1152]{1,0:T(8,128)S(1)}, f32[128,1152]{1,0:T(8,128)S(1)}, u32[]{:S(2)}, u32[]{:S(2)}) collective-permute-start(f32[128,1152]{1,0:T(8,128)S(1)} %get-tuple-element.218.refs_2_), channel_id=1, source_target_pairs={{0,1},{1,0},{2,3},{3,2},{4,5},{5,4},{6,7},{7,6},{8,9},{9,8},{10,11... | collective-permute-start | bytes 1769480 | tf_op jit(solution)/shard_map/grad_latent2/ppermute | solution.py:44
  551.7 24.3 %collective-permute-start.45 = (f32[128,1152]{1,0:T(8,128)S(1)}, f32[128,1152]{1,0:T(8,128)S(1)}, u32[]{:S(2)}, u32[]{:S(2)}) collective-permute-start(f32[128,1152]{1,0:T(8,128)S(1)} %get-tuple-element.192.refs_0_), channel_id=1, source_target_pairs={{0,1},{1,0},{2,3},{3,2},{4,5},{5,4},{6,7},{7,6},{8,9},{9,8},{10,11... | collective-permute-start | bytes 1769480 | tf_op jit(solution)/shard_map/grad_latent0/ppermute | solution.py:44
  553.9 25.4 %collective-permute-start.52 = (f32[2,234,128]{2,1,0:T(8,128)S(1)}, f32[2,234,128]{2,1,0:T(8,128)S(1)}, u32[]{:S(2)}, u32[]{:S(2)}) collective-permute-start(f32[2,234,128]{2,1,0:T(8,128)S(1)} %pad_maximum_fusion.2), channel_id=1, source_target_pairs={{0,16},{8,24},{16,0},{24,8},{1,17},{9,25},{17,1},{25,9},{2,18},{10... | collective-permute-start | bytes 718856 | tf_op jit(solution)/shard_map/sums/ppermute | solution.py:44
  557.8 34.6 %collective-permute-start.66 = (f16[72,4608]{1,0:T(8,128)(2,1)}, f16[72,4608]{1,0:T(8,128)(2,1)S(1)}, u32[]{:S(2)}, u32[]{:S(2)}) collective-permute-start(f16[72,4608]{1,0:T(8,128)(2,1)} %get-tuple-element.296), channel_id=1, source_target_pairs={{0,2},{2,4},{4,6},{6,0},{1,3},{3,5},{5,7},{7,1},{8,10},{10,12},{12... | collective-permute-start | bytes 1990664 | tf_op jit(solution)/shard_map/grad_feed_ring/ppermute | solution.py:38
  559.0 33.4 %collective-permute-start.67 = (f16[72,4608]{1,0:T(8,128)(2,1)S(1)}, f16[72,4608]{1,0:T(8,128)(2,1)}, u32[]{:S(2)}, u32[]{:S(2)}) collective-permute-start(f16[72,4608]{1,0:T(8,128)(2,1)S(1)} %get-tuple-element.297), channel_id=1, source_target_pairs={{0,6},{2,0},{4,2},{6,4},{1,7},{3,1},{5,3},{7,5},{8,14},{10,8},{12,... | collective-permute-start | bytes 1990664 | tf_op jit(solution)/shard_map/grad_feed_ring/ppermute | solution.py:38
  (152 other events, 919.7 us)
Sparse Core Ops, SparseCore 0:
  24.4 46.0 all-gather.3
  98.9 108.7 all-gather.5
  285.4 53.8 all-gather.7

commit v5 on v4

--- a/solution.py
+++ b/solution.py
@@ -625,7 +625,7 @@
     half, model = own.shape
     here, hidden = 2 * half, weights.shape[1] // 2
     cot = pl.BlockSpec((None, half, model), lambda j: (item, 0, 0))
-    tile = 768
+    tile = 1152
     steps = hidden // tile
     rows = pl.BlockSpec((here, model), lambda j: (item, 0))
     slab = pl.BlockSpec((here, tile), lambda j: (item, j))

time: 619 us -> 621 us (level)
  transfers between devices with their start and end apart: 82 -> 82, of which waited for: 26 -> 26; matrix products, arithmetic and copies ran while one was open for 11% -> 10% of each run, Pallas kernels for 28% -> 29%
where the time goes in v5:
time: 621 us; the launch traced here: 611 us
  Pallas kernels  183 us (29%)
  waiting for transfers between devices  144 us (23%)
  starting transfers between devices  127 us (20%)
  local copies, waits for them, and re-layouts  95.2 us (15%)
  other arithmetic  41.1 us (7%)
  between operations  18.4 us (3%)
    pallas_call x46, Pallas kernels, slab_call(): pl.pallas_call(run, in_specs=in_specs + [ANYWHERE] * more, input_output_a...  180 us
    ppermute x56, waiting for transfers between devices, flip(): return lax.ppermute(x, axis, [(i, i ^ 1 << bit) for i in range(size)])  109 us
    unnamed x277, local copies, waits for them, and re-layouts  75.4 us
    all_to_all x11, starting transfers between devices, exchange(): return lax.all_to_all(x, 'ctx', 0, 0)  56.4 us
    ppermute x56, starting transfers between devices, flip(): return lax.ppermute(x, axis, [(i, i ^ 1 << bit) for i in range(size)])  48.9 us
    ppermute x12, starting transfers between devices, shift(): return lax.ppermute(x, 'ctx', [(i, (i + k) % size) for i in range(size)])  21.3 us
    all_to_all x11, waiting for transfers between devices, exchange(): return lax.all_to_all(x, 'ctx', 0, 0)  17.8 us
    ppermute x12, waiting for transfers between devices, shift(): return lax.ppermute(x, 'ctx', [(i, (i + k) % size) for i in range(size)])  16.9 us
  transfers between devices with their start and end apart: 82, of which 26 were waited for; matrix products, arithmetic and copies ran while one was open for 10% of the time, Pallas kernels for 29%

profile of v5, /device:TPU:0, one launch (start us, length us, event | category | flops | bytes accessed | tf_op | source)
XLA Modules:
  0.0 610.5 jit_solution(14335591956987599999)
XLA Ops:
  9.3 2.9 collective-permute-start.1
  16.5 2.7 collective-permute-done.2
  20.1 4.1 collective-permute-start.10
  26.8 5.1 all-to-all-start
  35.9 10.5 %collective-permute-done.4 = f32[3,3456]{1,0:T(4,128)S(1)} collective-permute-done((f32[3,3456]{1,0:T(4,128)S(1)}, f32[3,3456]{1,0:T(4,128)S(1)}, u32[]{:S(2)}, u32[]{:S(2)}) %collective-permute-start.4) | collective-permute-done | bytes 41504 | tf_op jit(solution)/shard_map/mod_c/ppermute | solution.py:44
  47.4 4.1 collective-permute-done.5
  53.7 2.5 collective-permute-start.8
  60.2 7.1 %collective-permute-done.11.refs_4_.refs_7_ = bf16[1,128,1152]{2,1,0:T(8,128)(2,1)S(1)} collective-permute-done((bf16[1,128,1152]{2,1,0:T(8,128)(2,1)}, bf16[1,128,1152]{2,1,0:T(8,128)(2,1)S(1)}, u32[]{:S(2)}, u32[]{:S(2)}) %collective-permute-start.11) | collective-permute-done | bytes 294944 | tf_op jit(solution)/shard_map/latent0_t/ppermute | solution.py:44
  69.7 2.5 collective-permute-start.20
  74.6 2.7 shard_map.231
  85.2 4.6 shard_map.232
  89.8 7.2 %shard_map.233 = (bf16[4,144,256]{2,1,0:T(8,128)(2,1)S(1)}, f32[2,1024]{1,0:T(2,128)S(1)}) custom-call(bf16[3,144,1024]{2,1,0:T(8,128)(2,1)S(1)} %bitcast.187, bf16[3,144,1024]{2,1,0:T(8,128)(2,1)S(1)} %bitcast.188, bf16[3,144,1024]{2,1,0:T(8,128)(2,1)S(1)} %bitcast.189), custom_call_target="tpu_custom_call" | custom-call | flops 3355443200 | bytes 1179648 | tf_op jit(solution)/shard_map/pallas_call | solution.py:249
  102.9 16.9 %collective-permute-done.18.refs_4_ = bf16[2,128,1152]{2,1,0:T(8,128)(2,1)} collective-permute-done((bf16[2,128,1152]{2,1,0:T(8,128)(2,1)S(1)}, bf16[2,128,1152]{2,1,0:T(8,128)(2,1)}, u32[]{:S(2)}, u32[]{:S(2)}) %collective-permute-start.18) | collective-permute-done | bytes 589856 | tf_op jit(solution)/shard_map/latent1_right/ppermute | solution.py:38
  121.3 11.0 %all-to-all-start.3 = ((bf16[4,144,256]{2,1,0:T(8,128)(2,1)}), bf16[4,144,256]{2,1,0:T(8,128)(2,1)S(1)}, u32[]{:S(2)}, u32[]{:S(2)}) async-start(bf16[4,144,256]{2,1,0:T(8,128)(2,1)} %copy-done.91), calls=%async_computation.3 | async-start | bytes 589824 | tf_op jit(solution)/shard_map/mixed0/all_to_all | solution.py:49
  132.4 9.0 %collective-permute-done.19.refs_5_ = bf16[2,128,1152]{2,1,0:T(8,128)(2,1)} collective-permute-done((bf16[2,128,1152]{2,1,0:T(8,128)(2,1)}, bf16[2,128,1152]{2,1,0:T(8,128)(2,1)}, u32[]{:S(2)}, u32[]{:S(2)}) %collective-permute-start.19) | collective-permute-done | bytes 589856 | tf_op jit(solution)/shard_map/latent1_t/ppermute | solution.py:44
  141.3 5.0 shard_map.235
  146.3 7.9 %shard_map.238 = (bf16[4,144,256]{2,1,0:T(8,128)(2,1)}, f32[2,1024]{1,0:T(2,128)S(1)}) custom-call(bf16[3,144,1024]{2,1,0:T(8,128)(2,1)S(1)} %bitcast.181, bf16[3,144,1024]{2,1,0:T(8,128)(2,1)S(1)} %bitcast.182, bf16[3,144,1024]{2,1,0:T(8,128)(2,1)S(1)} %bitcast.183), custom_call_target="tpu_custom_call" | custom-call | flops 3355443200 | bytes 1179648 | tf_op jit(solution)/shard_map/pallas_call | solution.py:249
  155.2 3.5 all-to-all-start.2
  168.4 5.0 shard_map.236
  174.3 2.6 all-to-all-done.2.refs_0_
  182.8 7.2 %shard_map.237 = (bf16[4,144,256]{2,1,0:T(8,128)(2,1)S(1)}, f32[2,1024]{1,0:T(2,128)S(1)}) custom-call(bf16[3,144,1024]{2,1,0:T(8,128)(2,1)S(1)} %bitcast.175, bf16[3,144,1024]{2,1,0:T(8,128)(2,1)S(1)} %bitcast.176, bf16[3,144,1024]{2,1,0:T(8,128)(2,1)S(1)} %bitcast.177), custom_call_target="tpu_custom_call" | custom-call | flops 3355443200 | bytes 1179648 | tf_op jit(solution)/shard_map/pallas_call | solution.py:249
  190.7 3.6 all-to-all-start.1
  201.0 5.2 all-to-all-done.1.refs_0_
  216.9 13.0 %shard_map.247 = (bf16[768,1152]{1,0:T(8,128)(2,1)}, bf16[768,1152]{1,0:T(8,128)(2,1)}, bf16[768,2304]{1,0:T(8,128)(2,1)}, bf16[768,2304]{1,0:T(8,128)(2,1)}, f3...) custom-call(bf16[128,1152]{1,0:T(8,128)(2,1)} %get-tuple-element.151, ...), custom_call_target="tpu_custom_call" | custom-call | flops 5435817984 | bytes 12976128 | tf_op jit(solution)/shard_map/pallas_call | solution.py:249
  235.1 13.0 %shard_map.248 = (bf16[768,1152]{1,0:T(8,128)(2,1)}, bf16[768,1152]{1,0:T(8,128)(2,1)}, bf16[768,2304]{1,0:T(8,128)(2,1)}, bf16[768,2304]{1,0:T(8,128)(2,1)}, f3...) custom-call(bf16[128,1152]{1,0:T(8,128)(2,1)S(1)} %get-tuple-element, ...), custom_call_target="tpu_custom_call", output_to_operand_aliasing={{0}: (8, {}), {1}: (9, {}), {2}: (10, {}), {3}: (11, {}), {... | custom-call | flops 5435817984 | bytes 12976128 | tf_op jit(solution)/shard_map/pallas_call | solution.py:249
  251.9 13.2 %shard_map.249 = (bf16[768,1152]{1,0:T(8,128)(2,1)}, bf16[768,1152]{1,0:T(8,128)(2,1)}, bf16[768,2304]{1,0:T(8,128)(2,1)}, bf16[768,2304]{1,0:T(8,128)(2,1)}, f3...) custom-call(bf16[128,1152]{1,0:T(8,128)(2,1)S(1)} %get-tuple-element, ...), custom_call_target="tpu_custom_call", output_to_operand_aliasing={{0}: (8, {}), {1}: (9, {}), {2}: (10, {}), {3}: (11, {}), {... | custom-call | flops 5435817984 | bytes 12976128 | tf_op jit(solution)/shard_map/pallas_call | solution.py:249
  270.3 7.2 %shard_map.256 = (f32[2,288,4608]{2,1,0:T(8,128)}, f32[2,288,4608]{2,1,0:T(8,128)}) custom-call(bf16[768,1152]{1,0:T(8,128)(2,1)S(1)} %copy-done.18, bf16[768,2304]{1,0:T(8,128)(2,1)S(1)} %copy-done.6), custom_call_target="tpu_custom_call" | custom-call | flops 4076863488 | bytes 14155776 | tf_op jit(solution)/shard_map/pallas_call | solution.py:249
  277.5 7.1 %shard_map.257 = (f32[2,288,4608]{2,1,0:T(8,128)}, f32[2,288,4608]{2,1,0:T(8,128)}) custom-call(bf16[768,1152]{1,0:T(8,128)(2,1)S(1)} %copy-done.5, bf16[768,2304]{1,0:T(8,128)(2,1)S(1)} %copy-done.4, f32[2,288,4608]{2,1,0:T(8,128)} %get-tuple-element.181.refs_2_, ...), custom_call_target="tpu_custom_call", output_to_operand_aliasing={{0}: (2, {}), {1}: (3, {})} | custom-call | flops 4076863488 | bytes 14155776 | tf_op jit(solution)/shard_map/pallas_call | solution.py:249
  289.7 11.2 %collective-permute-done.33 = f32[4,8,128]{2,1,0:T(8,128)S(1)} collective-permute-done((f32[4,8,128]{2,1,0:T(8,128)S(1)}, f32[4,8,128]{2,1,0:T(8,128)S(1)}, u32[]{:S(2)}, u32[]{:S(2)}) %collective-permute-start.33) | collective-permute-done | bytes 16416 | tf_op jit(solution)/shard_map/bounds/ppermute | solution.py:44
  308.2 2.4 shard_map.262
  313.9 3.9 collective-permute-done.35
  321.3 4.2 all-to-all-start.4
  338.0 2.2 all-to-all-done.4.refs_4_
  340.2 4.3 all-to-all-start.6
  345.7 11.9 %shard_map.258 = (bf16[3,144,3072]{2,1,0:T(8,128)(2,1)S(1)}, bf16[4,3,144,256]{3,2,1,0:T(8,128)(2,1)}) custom-call(bf16[3,144,1024]{2,1,0:T(8,128)(2,1)S(1)} %bitcast.190, bf16[3,144,1024]{2,1,0:T(8,128)(2,1)S(1)} %bitcast.191, bf16[3,144,1024]{2,1,0:T(8,128)(2,1)S(1)} %bitcast.192, f32[2,1024]{1,0:T(2,128)S(1)} %get-tuple-element.131.refs_1_.refs_3_, ...), custom_call_target="tpu_custom_call" | custom-call | flops 8388608000 | bytes 2359296 | tf_op jit(solution)/shard_map/pallas_call | solution.py:249
  362.6 5.1 all-to-all-start.8
  370.6 11.0 %shard_map.264 = (bf16[3,144,3072]{2,1,0:T(8,128)(2,1)S(1)}, bf16[4,3,144,256]{3,2,1,0:T(8,128)(2,1)S(1)}) custom-call(bf16[3,144,1024]{2,1,0:T(8,128)(2,1)S(1)} %bitcast.184, bf16[3,144,1024]{2,1,0:T(8,128)(2,1)S(1)} %bitcast.185, bf16[3,144,1024]{2,1,0:T(8,128)(2,1)S(1)} %bitcast.186, ...), custom_call_target="tpu_custom_call", output_to_operand_aliasing={{0}: (5, {})} | custom-call | flops 8388608000 | bytes 2359296 | tf_op jit(solution)/shard_map/pallas_call | solution.py:249
  385.9 5.1 all-to-all-start.7
  391.0 6.7 %multiply_convert_fusion = f16[1,288,4608]{2,1,0:T(8,128)(2,1)} fusion(f32[2,288,4608]{2,1,0:T(8,128)} %collective-permute-done.32, s32[]{:T(128)S(6)} %select_n.122, f32[2,288,4608]{2,1,0:T(8,128)} %get-tuple-element.185, f32[4608]{0:T(1024)S(1)} %fusion.16), kind=kLoop, calls=%fused_computation.2 | loop fusion | flops 3981312 | bytes 13289476 | tf_op jit(solution)/shard_map/convert_element_type | solution.py:173
  404.2 2.8 shard_map.274
  408.1 11.8 %shard_map.269 = (bf16[3,144,3072]{2,1,0:T(8,128)(2,1)S(1)}, bf16[4,3,144,256]{3,2,1,0:T(8,128)(2,1)}) custom-call(bf16[3,144,1024]{2,1,0:T(8,128)(2,1)S(1)} %bitcast.178, bf16[3,144,1024]{2,1,0:T(8,128)(2,1)S(1)} %bitcast.179, bf16[3,144,1024]{2,1,0:T(8,128)(2,1)S(1)} %bitcast.180, ...), custom_call_target="tpu_custom_call", output_to_operand_aliasing={{0}: (5, {})} | custom-call | flops 8388608000 | bytes 2359296 | tf_op jit(solution)/shard_map/pallas_call | solution.py:249
  421.4 5.3 all-to-all-start.9
  428.5 7.9 %shard_map.273 = (f32[2,288,432]{2,1,0:T(8,128)}, f32[2,288,432]{2,1,0:T(8,128)S(1)}) custom-call(bf16[3072,1152]{1,0:T(8,128)(2,1)} %get-tuple-element.232.refs_0_, bf16[432,3072]{1,0:T(8,128)(2,1)S(1)} %bitcast.167), custom_call_target="tpu_custom_call" | custom-call | flops 3057647616 | bytes 9732096 | tf_op jit(solution)/shard_map/pallas_call | solution.py:249
  440.3 3.4 shard_map.265
  444.5 2.6 shard_map.253
  453.4 6.1 %collective-permute-done.41.refs_1_ = f32[128,1152]{1,0:T(8,128)} collective-permute-done((f32[128,1152]{1,0:T(8,128)}, f32[128,1152]{1,0:T(8,128)}, u32[]{:S(2)}, u32[]{:S(2)}) %collective-permute-start.41) | collective-permute-done | bytes 589856 | tf_op jit(solution)/shard_map/grad_in_first1/ppermute | solution.py:44
  459.5 2.4 shard_map.266
  462.6 5.1 all-to-all-start.5
  473.4 8.3 %multiply_add_fusion = f32[1,288,4608]{2,1,0:T(8,128)} fusion(f16[1,288,4608]{2,1,0:T(8,128)(2,1)} %collective-permute-done.37, f32[2,288,4608]{2,1,0:T(8,128)} %collective-permute-done.32, s32[]{:T(128)S(6)} %select_n.121, f32[2,288,4608]{2,1,0:T(8,128)} %get-tuple-element.185, f32[4608]{0:T(1024)S(1)} %broadcast_divide_fusion), kind=kLoop, calls=%fused_computation.1 | loop fusion | flops 5308416 | bytes 18597892 | tf_op jit(solution)/shard_map/add | solution.py:192
  481.8 7.7 %all-to-all-done.5.refs_0_ = bf16[4,3,144,256]{3,2,1,0:T(8,128)(2,1)S(1)} async-done(((bf16[4,3,144,256]{3,2,1,0:T(8,128)(2,1)}), bf16[4,3,144,256]{3,2,1,0:T(8,128)(2,1)S(1)}, u32[]{:S(2)}, u32[]{:S(2)}) %all-to-all-start.5) | async-done | bytes 884768 | tf_op jit(solution)/shard_map/grad_qkv0/all_to_all | solution.py:49
  495.2 2.2 add_add_fusion.1
  497.5 4.2 all-to-all-start.10
  501.7 2.4 add_add_fusion
  505.9 2.6 collective-permute-done.38.refs_1_
  511.8 3.8 collective-permute-start.64
  515.7 2.3 fusion.1
  520.0 17.1 %collective-permute-done.49 = f32[234,128]{1,0:T(8,128)S(1)} collective-permute-done((f32[234,128]{1,0:T(8,128)S(1)}, f32[234,128]{1,0:T(8,128)S(1)}, u32[]{:S(2)}, u32[]{:S(2)}) %collective-permute-start.49) | collective-permute-done | bytes 119840 | tf_op jit(solution)/shard_map/sums/ppermute | solution.py:44
  537.6 11.0 %collective-permute-done.50 = f32[234,128]{1,0:T(8,128)S(1)} collective-permute-done((f32[234,128]{1,0:T(8,128)S(1)}, f32[234,128]{1,0:T(8,128)S(1)}, u32[]{:S(2)}, u32[]{:S(2)}) %collective-permute-start.50) | collective-permute-done | bytes 119840 | tf_op jit(solution)/shard_map/sums/ppermute | solution.py:44
  557.2 3.1 fusion.3
  561.5 3.9 collective-permute-start.67
  566.1 12.2 %collective-permute-done.45.refs_3_ = f32[128,1152]{1,0:T(8,128)S(1)} collective-permute-done((f32[128,1152]{1,0:T(8,128)S(1)}, f32[128,1152]{1,0:T(8,128)S(1)}, u32[]{:S(2)}, u32[]{:S(2)}) %collective-permute-start.45) | collective-permute-done | bytes 589856 | tf_op jit(solution)/shard_map/grad_latent0/ppermute | solution.py:44
  578.4 3.3 shard_map.272
  591.9 2.5 collective-permute-done.55
  596.4 2.7 collective-permute-done.56
  (539 shorter events, 201.2 us)
Async XLA Ops:
  7.2 151.5 %all-gather.4.cloned.1.call-start = ((), (), s32[]{:S(2)}) async-start(), calls=%async_computation.11 | async-start | bytes 1566720 | tf_op jit(solution)/shard_map/proj_weights/all_gather | solution.py:54
  19.2 12.7 %collective-permute-start.3 = (f32[1,3,3456]{2,1,0:T(4,128)S(1)}, f32[1,3,3456]{2,1,0:T(4,128)S(1)}, u32[]{:S(2)}, u32[]{:S(2)}) collective-permute-start(f32[1,3,3456]{2,1,0:T(4,128)S(1)} %slice.213), channel_id=1, source_target_pairs={{0,8},{8,0},{16,24},{24,16},{1,9},{9,1},{17,25},{25,17},{2,10},{10... | collective-permute-start | bytes 124424 | tf_op jit(solution)/shard_map/mod_f/ppermute | solution.py:44
  20.1 36.1 %collective-permute-start.10 = (bf16[1,128,1152]{2,1,0:T(8,128)(2,1)S(1)}, bf16[1,128,1152]{2,1,0:T(8,128)(2,1)}, u32[]{:S(2)}, u32[]{:S(2)}) collective-permute-start(bf16[1,128,1152]{2,1,0:T(8,128)(2,1)S(1)} %get-tuple-element.126.refs_0_.refs_3_.refs_2_), channel_id=1, source_target_pairs={{0,6},{2,0},{4,2},{6,4},{1,7},{3,1},{5,3},{7,5},{8,14},{10,8},{12,... | collective-permute-start | bytes 884744 | tf_op jit(solution)/shard_map/latent0_left/ppermute | solution.py:38
  24.2 29.0 %collective-permute-start.7 = (bf16[1,128,1152]{2,1,0:T(8,128)(2,1)S(1)}, bf16[1,128,1152]{2,1,0:T(8,128)(2,1)}, u32[]{:S(2)}, u32[]{:S(2)}) collective-permute-start(bf16[1,128,1152]{2,1,0:T(8,128)(2,1)S(1)} %get-tuple-element.126.refs_0_.refs_3_.refs_2_), channel_id=1, source_target_pairs={{0,2},{2,4},{4,6},{6,0},{1,3},{3,5},{5,7},{7,1},{8,10},{10,12},{12... | collective-permute-start | bytes 884744 | tf_op jit(solution)/shard_map/latent0_right/ppermute | solution.py:38
  26.8 30.9 %all-to-all-start = ((bf16[4,72,432]{2,1,0:T(8,128)(2,1)}), bf16[4,72,432]{2,1,0:T(8,128)(2,1)S(1)}, u32[]{:S(2)}, u32[]{:S(2)}) async-start(bf16[4,72,432]{2,1,0:T(8,128)(2,1)} %copy.88), calls=%async_computation | async-start | bytes 589824 | tf_op jit(solution)/shard_map/qkv_c/all_to_all | solution.py:49
  31.9 183.9 %all-gather.6.cloned.1.call-start = ((), (), s32[]{:S(2)}) async-start(), calls=%async_computation.12 | async-start | bytes 11280384 | tf_op jit(solution)/shard_map/feed_weights/all_gather | solution.py:54
  31.9 14.4 %collective-permute-start.4 = (f32[3,3456]{1,0:T(4,128)S(1)}, f32[3,3456]{1,0:T(4,128)S(1)}, u32[]{:S(2)}, u32[]{:S(2)}) collective-permute-start(f32[3,3456]{1,0:T(4,128)S(1)} %fusion.9), channel_id=1, source_target_pairs={{0,2},{2,0},{4,6},{6,4},{1,3},{3,1},{5,7},{7,5},{8,10},{10,8},{12,... | collective-permute-start | bytes 124424 | tf_op jit(solution)/shard_map/mod_c/ppermute | solution.py:44
  53.2 14.0 %collective-permute-start.9 = (bf16[1,128,1152]{2,1,0:T(8,128)(2,1)}, bf16[1,128,1152]{2,1,0:T(8,128)(2,1)S(1)}, u32[]{:S(2)}, u32[]{:S(2)}) collective-permute-start(bf16[1,128,1152]{2,1,0:T(8,128)(2,1)} %collective-permute-done.7.refs_2_), channel_id=1, source_target_pairs={{0,1},{1,0},{2,3},{3,2},{4,5},{5,4},{6,7},{7,6},{8,9},{9,8},{10,11... | collective-permute-start | bytes 884744 | tf_op jit(solution)/shard_map/latent0_t/ppermute | solution.py:44
  53.7 13.5 %collective-permute-start.8 = (bf16[1,128,1152]{2,1,0:T(8,128)(2,1)}, bf16[1,128,1152]{2,1,0:T(8,128)(2,1)S(1)}, u32[]{:S(2)}, u32[]{:S(2)}) collective-permute-start(bf16[1,128,1152]{2,1,0:T(8,128)(2,1)} %collective-permute-done.7.refs_2_), channel_id=1, source_target_pairs={{0,2},{2,4},{4,6},{6,0},{1,3},{3,5},{5,7},{7,1},{8,10},{10,12},{12... | collective-permute-start | bytes 884744 | tf_op jit(solution)/shard_map/latent0_right/ppermute | solution.py:38
  57.7 15.1 %collective-permute-start.15 = (bf16[4,72,432]{2,1,0:T(8,128)(2,1)S(1)}, bf16[4,72,432]{2,1,0:T(8,128)(2,1)}, u32[]{:S(2)}, u32[]{:S(2)}) collective-permute-start(bf16[4,72,432]{2,1,0:T(8,128)(2,1)S(1)} %all-to-all-done.refs_1_.refs_0_), channel_id=1, source_target_pairs={{0,16},{8,24},{16,0},{24,8},{1,17},{9,25},{17,1},{25,9},{2,18},{10... | collective-permute-start | bytes 746504 | tf_op jit(solution)/shard_map/qkv_1/ppermute | solution.py:44
  60.1 13.6 %collective-permute-start.16 = (bf16[4,72,432]{2,1,0:T(8,128)(2,1)S(1)}, bf16[4,72,432]{2,1,0:T(8,128)(2,1)}, u32[]{:S(2)}, u32[]{:S(2)}) collective-permute-start(bf16[4,72,432]{2,1,0:T(8,128)(2,1)S(1)} %all-to-all-done.refs_1_.refs_0_), channel_id=1, source_target_pairs={{0,8},{8,0},{16,24},{24,16},{1,9},{9,1},{17,25},{25,17},{2,10},{10... | collective-permute-start | bytes 746504 | tf_op jit(solution)/shard_map/qkv_0/ppermute | solution.py:44
  69.7 28.1 %collective-permute-start.20 = (bf16[2,128,1152]{2,1,0:T(8,128)(2,1)S(1)}, bf16[2,128,1152]{2,1,0:T(8,128)(2,1)S(1)}, u32[]{:S(2)}, u32[]{:S(2)}) collective-permute-start(bf16[2,128,1152]{2,1,0:T(8,128)(2,1)S(1)} %get-tuple-element.127.refs_0_.refs_3_.refs_2_), channel_id=1, source_target_pairs={{0,6},{2,0},{4,2},{6,4},{1,7},{3,1},{5,3},{7,5},{8,14},{10,8},{12,... | collective-permute-start | bytes 1769480 | tf_op jit(solution)/shard_map/latent1_left/ppermute | solution.py:38
  72.1 25.6 %collective-permute-start.12 = (bf16[2,128,1152]{2,1,0:T(8,128)(2,1)S(1)}, bf16[2,128,1152]{2,1,0:T(8,128)(2,1)S(1)}, u32[]{:S(2)}, u32[]{:S(2)}) collective-permute-start(bf16[2,128,1152]{2,1,0:T(8,128)(2,1)S(1)} %get-tuple-element.127.refs_0_.refs_3_.refs_2_), channel_id=1, source_target_pairs={{0,2},{2,4},{4,6},{6,0},{1,3},{3,5},{5,7},{7,1},{8,10},{10,12},{12... | collective-permute-start | bytes 1769480 | tf_op jit(solution)/shard_map/latent1_right/ppermute | solution.py:38
  98.8 21.0 %collective-permute-start.18 = (bf16[2,128,1152]{2,1,0:T(8,128)(2,1)S(1)}, bf16[2,128,1152]{2,1,0:T(8,128)(2,1)}, u32[]{:S(2)}, u32[]{:S(2)}) collective-permute-start(bf16[2,128,1152]{2,1,0:T(8,128)(2,1)S(1)} %shard_map.234), channel_id=1, source_target_pairs={{0,2},{2,4},{4,6},{6,0},{1,3},{3,5},{5,7},{7,1},{8,10},{10,12},{12... | collective-permute-start | bytes 1769480 | tf_op jit(solution)/shard_map/latent1_right/ppermute | solution.py:38
  100.9 31.5 %collective-permute-start.21 = (bf16[2,128,1152]{2,1,0:T(8,128)(2,1)S(1)}, bf16[2,128,1152]{2,1,0:T(8,128)(2,1)}, u32[]{:S(2)}, u32[]{:S(2)}) collective-permute-start(bf16[2,128,1152]{2,1,0:T(8,128)(2,1)S(1)} %collective-permute-done.20.refs_6_.refs_3_), channel_id=1, source_target_pairs={{0,1},{1,0},{2,3},{3,2},{4,5},{5,4},{6,7},{7,6},{8,9},{9,8},{10,11... | collective-permute-start | bytes 1769480 | tf_op jit(solution)/shard_map/latent1_t/ppermute | solution.py:44
  102.4 30.0 %collective-permute-start.13 = (bf16[2,128,1152]{2,1,0:T(8,128)(2,1)S(1)}, bf16[2,128,1152]{2,1,0:T(8,128)(2,1)}, u32[]{:S(2)}, u32[]{:S(2)}) collective-permute-start(bf16[2,128,1152]{2,1,0:T(8,128)(2,1)S(1)} %collective-permute-done.12.refs_0_.refs_2_), channel_id=1, source_target_pairs={{0,1},{1,0},{2,3},{3,2},{4,5},{5,4},{6,7},{7,6},{8,9},{9,8},{10,11... | collective-permute-start | bytes 1769480 | tf_op jit(solution)/shard_map/latent1_t/ppermute | solution.py:44
  119.8 21.5 %collective-permute-start.19 = (bf16[2,128,1152]{2,1,0:T(8,128)(2,1)}, bf16[2,128,1152]{2,1,0:T(8,128)(2,1)}, u32[]{:S(2)}, u32[]{:S(2)}) collective-permute-start(bf16[2,128,1152]{2,1,0:T(8,128)(2,1)} %collective-permute-done.18.refs_4_), channel_id=1, source_target_pairs={{0,1},{1,0},{2,3},{3,2},{4,5},{5,4},{6,7},{7,6},{8,9},{9,8},{10,11... | collective-permute-start | bytes 1769480 | tf_op jit(solution)/shard_map/latent1_t/ppermute | solution.py:44
  121.3 33.8 %all-to-all-start.3 = ((bf16[4,144,256]{2,1,0:T(8,128)(2,1)}), bf16[4,144,256]{2,1,0:T(8,128)(2,1)S(1)}, u32[]{:S(2)}, u32[]{:S(2)}) async-start(bf16[4,144,256]{2,1,0:T(8,128)(2,1)} %copy-done.91), calls=%async_computation.3 | async-start | bytes 589824 | tf_op jit(solution)/shard_map/mixed0/all_to_all | solution.py:49
  155.2 21.7 %all-to-all-start.2 = ((bf16[4,144,256]{2,1,0:T(8,128)(2,1)}), bf16[4,144,256]{2,1,0:T(8,128)(2,1)S(1)}, u32[]{:S(2)}, u32[]{:S(2)}) async-start(bf16[4,144,256]{2,1,0:T(8,128)(2,1)} %get-tuple-element.137), calls=%async_computation.2 | async-start | bytes 589824 | tf_op jit(solution)/shard_map/mixed1/all_to_all | solution.py:49
  164.8 29.8 %collective-permute-start.26 = (f32[128,1152]{1,0:T(8,128)}, f32[128,1152]{1,0:T(8,128)}, u32[]{:S(2)}, u32[]{:S(2)}) collective-permute-start(f32[128,1152]{1,0:T(8,128)} %get-tuple-element.150), channel_id=1, source_target_pairs={{0,1},{1,0},{2,3},{3,2},{4,5},{5,4},{6,7},{7,6},{8,9},{9,8},{10,11... | collective-permute-start | bytes 1769480 | tf_op jit(solution)/shard_map/attended0/ppermute | solution.py:44
  181.3 30.8 %collective-permute-start.24 = (f32[128,1152]{1,0:T(8,128)}, f32[128,1152]{1,0:T(8,128)}, u32[]{:S(2)}, u32[]{:S(2)}) collective-permute-start(f32[128,1152]{1,0:T(8,128)} %get-tuple-element.147), channel_id=1, source_target_pairs={{0,1},{1,0},{2,3},{3,2},{4,5},{5,4},{6,7},{7,6},{8,9},{9,8},{10,11... | collective-permute-start | bytes 1769480 | tf_op jit(solution)/shard_map/attended1/ppermute | solution.py:44
  190.7 15.6 %all-to-all-start.1 = ((bf16[4,144,256]{2,1,0:T(8,128)(2,1)}), bf16[4,144,256]{2,1,0:T(8,128)(2,1)S(1)}, u32[]{:S(2)}, u32[]{:S(2)}) async-start(bf16[4,144,256]{2,1,0:T(8,128)(2,1)} %copy-done.93), calls=%async_computation.1 | async-start | bytes 589824 | tf_op jit(solution)/shard_map/mixed2/all_to_all | solution.py:49
  194.3 243.8 %all-gather.8.cloned.1.call-start = ((), (), s32[]{:S(2)}) async-start(), calls=%async_computation.13 | async-start | bytes 4386816 | tf_op jit(solution)/shard_map/qkv_weights/all_gather | solution.py:54
  200.4 15.4 %collective-permute-start.27 = (bf16[128,1152]{1,0:T(8,128)(2,1)}, bf16[128,1152]{1,0:T(8,128)(2,1)}, u32[]{:S(2)}, u32[]{:S(2)}) collective-permute-start(bf16[128,1152]{1,0:T(8,128)(2,1)} %get-tuple-element.151.refs_0_), channel_id=1, source_target_pairs={{0,1},{1,0},{2,3},{3,2},{4,5},{5,4},{6,7},{7,6},{8,9},{9,8},{10,11... | collective-permute-start | bytes 884744 | tf_op jit(solution)/shard_map/in_second0/ppermute | solution.py:44
  209.6 21.9 %collective-permute-start.22 = (f32[128,1152]{1,0:T(8,128)}, f32[128,1152]{1,0:T(8,128)}, u32[]{:S(2)}, u32[]{:S(2)}) collective-permute-start(f32[128,1152]{1,0:T(8,128)} %get-tuple-element.142), channel_id=1, source_target_pairs={{0,1},{1,0},{2,3},{3,2},{4,5},{5,4},{6,7},{7,6},{8,9},{9,8},{10,11... | collective-permute-start | bytes 1769480 | tf_op jit(solution)/shard_map/attended2/ppermute | solution.py:44
  215.2 19.9 %collective-permute-start.25 = (bf16[128,1152]{1,0:T(8,128)(2,1)S(1)}, bf16[128,1152]{1,0:T(8,128)(2,1)}, u32[]{:S(2)}, u32[]{:S(2)}) collective-permute-start(bf16[128,1152]{1,0:T(8,128)(2,1)S(1)} %get-tuple-element.148.refs_0_), channel_id=1, source_target_pairs={{0,1},{1,0},{2,3},{3,2},{4,5},{5,4},{6,7},{7,6},{8,9},{9,8},{10,11... | collective-permute-start | bytes 884744 | tf_op jit(solution)/shard_map/in_second1/ppermute | solution.py:44
  229.9 19.8 %collective-permute-start.28 = (f32[128,1152]{1,0:T(8,128)S(1)}, f32[128,1152]{1,0:T(8,128)S(1)}, u32[]{:S(2)}, u32[]{:S(2)}) collective-permute-start(f32[128,1152]{1,0:T(8,128)S(1)} %get-tuple-element.164), channel_id=1, source_target_pairs={{0,1},{1,0},{2,3},{3,2},{4,5},{5,4},{6,7},{7,6},{8,9},{9,8},{10,11... | collective-permute-start | bytes 1769480 | tf_op jit(solution)/shard_map/grad_in_second0/ppermute | solution.py:44
  234.5 17.4 %collective-permute-start.23 = (bf16[128,1152]{1,0:T(8,128)(2,1)S(1)}, bf16[128,1152]{1,0:T(8,128)(2,1)S(1)}, u32[]{:S(2)}, u32[]{:S(2)}) collective-permute-start(bf16[128,1152]{1,0:T(8,128)(2,1)S(1)} %get-tuple-element.143.refs_0_), channel_id=1, source_target_pairs={{0,1},{1,0},{2,3},{3,2},{4,5},{5,4},{6,7},{7,6},{8,9},{9,8},{10,11... | collective-permute-start | bytes 884744 | tf_op jit(solution)/shard_map/in_second2/ppermute | solution.py:44
  250.4 27.1 %collective-permute-start.31 = (bf16[128,1152]{1,0:T(8,128)(2,1)S(1)}, bf16[128,1152]{1,0:T(8,128)(2,1)S(1)}, u32[]{:S(2)}, u32[]{:S(2)}) collective-permute-start(bf16[128,1152]{1,0:T(8,128)(2,1)S(1)} %get-tuple-element.175.refs_0_), channel_id=1, source_target_pairs={{0,1},{1,0},{2,3},{3,2},{4,5},{5,4},{6,7},{7,6},{8,9},{9,8},{10,11... | collective-permute-start | bytes 884744 | tf_op jit(solution)/shard_map/grad_attended0/ppermute | solution.py:44
  284.6 106.4 %collective-permute-start.32 = (f32[2,288,4608]{2,1,0:T(8,128)}, f32[2,288,4608]{2,1,0:T(8,128)}, u32[]{:S(2)}, u32[]{:S(2)}) collective-permute-start(f32[2,288,4608]{2,1,0:T(8,128)} %get-tuple-element.183.refs_5_), channel_id=1, source_target_pairs={{0,8},{8,0},{16,24},{24,16},{1,9},{9,1},{17,25},{25,17},{2,10},{10... | collective-permute-start | bytes 31850504 | tf_op jit(solution)/shard_map/grad_feed_0/ppermute | solution.py:44
  288.2 16.8 %collective-permute-start.39 = (f32[128,1152]{1,0:T(8,128)}, f32[128,1152]{1,0:T(8,128)}, u32[]{:S(2)}, u32[]{:S(2)}) collective-permute-start(f32[128,1152]{1,0:T(8,128)} %copy-done.109), channel_id=1, source_target_pairs={{0,1},{1,0},{2,3},{3,2},{4,5},{5,4},{6,7},{7,6},{8,9},{9,8},{10,11... | collective-permute-start | bytes 1769480 | tf_op jit(solution)/shard_map/grad_in_second1/ppermute | solution.py:44
  288.8 12.1 %collective-permute-start.33 = (f32[4,8,128]{2,1,0:T(8,128)S(1)}, f32[4,8,128]{2,1,0:T(8,128)S(1)}, u32[]{:S(2)}, u32[]{:S(2)}) collective-permute-start(f32[4,8,128]{2,1,0:T(8,128)S(1)} %maximum_maximum_fusion), channel_id=1, source_target_pairs={{0,8},{8,0},{16,24},{24,16},{1,9},{9,1},{17,25},{25,17},{2,10},{10... | collective-permute-start | bytes 49160 | tf_op jit(solution)/shard_map/bounds/ppermute | solution.py:44
  301.0 12.5 %collective-permute-start.34 = (f32[4,8,128]{2,1,0:T(8,128)S(1)}, f32[4,8,128]{2,1,0:T(8,128)S(1)}, u32[]{:S(2)}, u32[]{:S(2)}) collective-permute-start(f32[4,8,128]{2,1,0:T(8,128)S(1)} %max.24), channel_id=1, source_target_pairs={{0,16},{8,24},{16,0},{24,8},{1,17},{9,25},{17,1},{25,9},{2,18},{10... | collective-permute-start | bytes 49160 | tf_op jit(solution)/shard_map/bounds/ppermute | solution.py:44
  304.3 29.6 %collective-permute-start.42 = (f32[128,1152]{1,0:T(8,128)}, f32[128,1152]{1,0:T(8,128)}, u32[]{:S(2)}, u32[]{:S(2)}) collective-permute-start(f32[128,1152]{1,0:T(8,128)} %copy-done.108), channel_id=1, source_target_pairs={{0,1},{1,0},{2,3},{3,2},{4,5},{5,4},{6,7},{7,6},{8,9},{9,8},{10,11... | collective-permute-start | bytes 1769480 | tf_op jit(solution)/shard_map/grad_in_second2/ppermute | solution.py:44
  311.4 17.3 %collective-permute-start.40 = (bf16[128,1152]{1,0:T(8,128)(2,1)}, bf16[128,1152]{1,0:T(8,128)(2,1)}, u32[]{:S(2)}, u32[]{:S(2)}) collective-permute-start(bf16[128,1152]{1,0:T(8,128)(2,1)} %get-tuple-element.197.refs_0_), channel_id=1, source_target_pairs={{0,1},{1,0},{2,3},{3,2},{4,5},{5,4},{6,7},{7,6},{8,9},{9,8},{10,11... | collective-permute-start | bytes 884744 | tf_op jit(solution)/shard_map/grad_attended1/ppermute | solution.py:44
  312.8 71.2 %collective-permute-start.29 = (bf16[384,1152]{1,0:T(8,128)(2,1)}, bf16[384,1152]{1,0:T(8,128)(2,1)}, u32[]{:S(2)}, u32[]{:S(2)}) collective-permute-start(bf16[384,1152]{1,0:T(8,128)(2,1)} %get-tuple-element.166), channel_id=1, source_target_pairs={{0,1},{1,0},{2,3},{3,2},{4,5},{5,4},{6,7},{7,6},{8,9},{9,8},{10,11... | collective-permute-start | bytes 2654216 | tf_op jit(solution)/shard_map/feed_out/ppermute | solution.py:44
  321.3 18.9 %all-to-all-start.4 = ((bf16[4,144,256]{2,1,0:T(8,128)(2,1)}), bf16[4,144,256]{2,1,0:T(8,128)(2,1)}, u32[]{:S(2)}, u32[]{:S(2)}) async-start(bf16[4,144,256]{2,1,0:T(8,128)(2,1)} %bitcast.169), calls=%async_computation.4 | async-start | bytes 589824 | tf_op jit(solution)/shard_map/grad_mixed0/all_to_all | solution.py:49
  336.5 22.5 %collective-permute-start.43 = (bf16[128,1152]{1,0:T(8,128)(2,1)S(1)}, bf16[128,1152]{1,0:T(8,128)(2,1)}, u32[]{:S(2)}, u32[]{:S(2)}) collective-permute-start(bf16[128,1152]{1,0:T(8,128)(2,1)S(1)} %get-tuple-element.210.refs_0_), channel_id=1, source_target_pairs={{0,1},{1,0},{2,3},{3,2},{4,5},{5,4},{6,7},{7,6},{8,9},{9,8},{10,11... | collective-permute-start | bytes 884744 | tf_op jit(solution)/shard_map/grad_attended2/ppermute | solution.py:44
  340.2 22.4 %all-to-all-start.6 = ((bf16[4,144,256]{2,1,0:T(8,128)(2,1)}), bf16[4,144,256]{2,1,0:T(8,128)(2,1)}, u32[]{:S(2)}, u32[]{:S(2)}) async-start(bf16[4,144,256]{2,1,0:T(8,128)(2,1)} %bitcast.170), calls=%async_computation.6 | async-start | bytes 589824 | tf_op jit(solution)/shard_map/grad_mixed1/all_to_all | solution.py:49
  362.6 23.3 %all-to-all-start.8 = ((bf16[4,144,256]{2,1,0:T(8,128)(2,1)}), bf16[4,144,256]{2,1,0:T(8,128)(2,1)}, u32[]{:S(2)}, u32[]{:S(2)}) async-start(bf16[4,144,256]{2,1,0:T(8,128)(2,1)} %bitcast.171), calls=%async_computation.8 | async-start | bytes 589824 | tf_op jit(solution)/shard_map/grad_mixed2/all_to_all | solution.py:49
  385.9 35.6 %all-to-all-start.7 = ((bf16[4,3,144,256]{3,2,1,0:T(8,128)(2,1)}), bf16[4,3,144,256]{3,2,1,0:T(8,128)(2,1)}, u32[]{:S(2)}, u32[]{:S(2)}) async-start(bf16[4,3,144,256]{3,2,1,0:T(8,128)(2,1)} %copy-done.63), calls=%async_computation.7 | async-start | bytes 1769472 | tf_op jit(solution)/shard_map/grad_qkv1/all_to_all | solution.py:49
  397.7 75.8 %collective-permute-start.37 = (f16[1,288,4608]{2,1,0:T(8,128)(2,1)}, f16[1,288,4608]{2,1,0:T(8,128)(2,1)}, u32[]{:S(2)}, u32[]{:S(2)}) collective-permute-start(f16[1,288,4608]{2,1,0:T(8,128)(2,1)} %multiply_convert_fusion), channel_id=1, source_target_pairs={{0,16},{8,24},{16,0},{24,8},{1,17},{9,25},{17,1},{25,9},{2,18},{10... | collective-permute-start | bytes 7962632 | tf_op jit(solution)/shard_map/grad_feed_1/ppermute | solution.py:44
  402.8 41.7 %collective-permute-start.30 = (bf16[384,1152]{1,0:T(8,128)(2,1)}, bf16[384,1152]{1,0:T(8,128)(2,1)S(1)}, u32[]{:S(2)}, u32[]{:S(2)}) collective-permute-start(bf16[384,1152]{1,0:T(8,128)(2,1)} %get-tuple-element.172.refs_0_), channel_id=1, source_target_pairs={{0,1},{1,0},{2,3},{3,2},{4,5},{5,4},{6,7},{7,6},{8,9},{9,8},{10,11... | collective-permute-start | bytes 2654216 | tf_op jit(solution)/shard_map/output/ppermute | solution.py:44
  408.1 39.0 %collective-permute-start.60 = (f32[2,288,576]{2,1,0:T(8,128)}, f32[2,288,576]{2,1,0:T(8,128)}, u32[]{:S(2)}, u32[]{:S(2)}) collective-permute-start(f32[2,288,576]{2,1,0:T(8,128)} %get-tuple-element.238), channel_id=1, source_target_pairs={{0,8},{8,0},{16,24},{24,16},{1,9},{9,1},{17,25},{25,17},{2,10},{10... | collective-permute-start | bytes 3981320 | tf_op jit(solution)/shard_map/grad_proj_0/ppermute | solution.py:44
  421.4 41.1 %all-to-all-start.9 = ((bf16[4,3,144,256]{3,2,1,0:T(8,128)(2,1)}), bf16[4,3,144,256]{3,2,1,0:T(8,128)(2,1)S(1)}, u32[]{:S(2)}, u32[]{:S(2)}) async-start(bf16[4,3,144,256]{3,2,1,0:T(8,128)(2,1)} %get-tuple-element.214), calls=%async_computation.9 | async-start | bytes 1769472 | tf_op jit(solution)/shard_map/grad_qkv2/all_to_all | solution.py:49
  437.4 12.7 %collective-permute-start.58 = (f32[2,288,432]{2,1,0:T(8,128)}, f32[2,288,432]{2,1,0:T(8,128)}, u32[]{:S(2)}, u32[]{:S(2)}) collective-permute-start(f32[2,288,432]{2,1,0:T(8,128)} %get-tuple-element.234), channel_id=1, source_target_pairs={{0,8},{8,0},{16,24},{24,16},{1,9},{9,1},{17,25},{25,17},{2,10},{10... | collective-permute-start | bytes 2985992 | tf_op jit(solution)/shard_map/grad_qkvw_0/ppermute | solution.py:44
  443.7 15.9 %collective-permute-start.41 = (f32[128,1152]{1,0:T(8,128)}, f32[128,1152]{1,0:T(8,128)}, u32[]{:S(2)}, u32[]{:S(2)}) collective-permute-start(f32[128,1152]{1,0:T(8,128)} %get-tuple-element.203), channel_id=1, source_target_pairs={{0,1},{1,0},{2,3},{3,2},{4,5},{5,4},{6,7},{7,6},{8,9},{9,8},{10,11... | collective-permute-start | bytes 1769480 | tf_op jit(solution)/shard_map/grad_in_first1/ppermute | solution.py:44
  449.4 52.3 %collective-permute-start.61 = (f32[1,288,576]{2,1,0:T(8,128)}, f32[1,288,576]{2,1,0:T(8,128)}, u32[]{:S(2)}, u32[]{:S(2)}) collective-permute-start(f32[1,288,576]{2,1,0:T(8,128)} %dynamic-slice_add_fusion), channel_id=1, source_target_pairs={{0,16},{8,24},{16,0},{24,8},{1,17},{9,25},{17,1},{25,9},{2,18},{10... | collective-permute-start | bytes 1990664 | tf_op jit(solution)/shard_map/grad_proj_1/ppermute | solution.py:44
  452.1 43.1 %collective-permute-start.59 = (f32[1,288,432]{2,1,0:T(8,128)}, f32[1,288,432]{2,1,0:T(8,128)}, u32[]{:S(2)}, u32[]{:S(2)}) collective-permute-start(f32[1,288,432]{2,1,0:T(8,128)} %dynamic-slice_add_fusion.1), channel_id=1, source_target_pairs={{0,16},{8,24},{16,0},{24,8},{1,17},{9,25},{17,1},{25,9},{2,18},{10... | collective-permute-start | bytes 1493000 | tf_op jit(solution)/shard_map/grad_qkvw_1/ppermute | solution.py:44
  461.9 99.6 %collective-permute-start.46 = (f32[128,1152]{1,0:T(8,128)}, f32[128,1152]{1,0:T(8,128)}, u32[]{:S(2)}, u32[]{:S(2)}) collective-permute-start(f32[128,1152]{1,0:T(8,128)} %get-tuple-element.205.refs_1_), channel_id=1, source_target_pairs={{0,1},{1,0},{2,3},{3,2},{4,5},{5,4},{6,7},{7,6},{8,9},{9,8},{10,11... | collective-permute-start | bytes 1769480 | tf_op jit(solution)/shard_map/grad_latent1/ppermute | solution.py:44
  462.6 26.9 %all-to-all-start.5 = ((bf16[4,3,144,256]{3,2,1,0:T(8,128)(2,1)}), bf16[4,3,144,256]{3,2,1,0:T(8,128)(2,1)S(1)}, u32[]{:S(2)}, u32[]{:S(2)}) async-start(bf16[4,3,144,256]{3,2,1,0:T(8,128)(2,1)} %get-tuple-element.184), calls=%async_computation.5 | async-start | bytes 1769472 | tf_op jit(solution)/shard_map/grad_qkv0/all_to_all | solution.py:49
  472.0 32.1 %collective-permute-start.44 = (f32[128,1152]{1,0:T(8,128)}, f32[128,1152]{1,0:T(8,128)}, u32[]{:S(2)}, u32[]{:S(2)}) collective-permute-start(f32[128,1152]{1,0:T(8,128)} %get-tuple-element.216), channel_id=1, source_target_pairs={{0,1},{1,0},{2,3},{3,2},{4,5},{5,4},{6,7},{7,6},{8,9},{9,8},{10,11... | collective-permute-start | bytes 1769480 | tf_op jit(solution)/shard_map/grad_in_first2/ppermute | solution.py:44
  493.9 14.6 %collective-permute-start.38 = (f32[128,1152]{1,0:T(8,128)}, f32[128,1152]{1,0:T(8,128)}, u32[]{:S(2)}, u32[]{:S(2)}) collective-permute-start(f32[128,1152]{1,0:T(8,128)} %get-tuple-element.190), channel_id=1, source_target_pairs={{0,1},{1,0},{2,3},{3,2},{4,5},{5,4},{6,7},{7,6},{8,9},{9,8},{10,11... | collective-permute-start | bytes 1769480 | tf_op jit(solution)/shard_map/grad_in_first0/ppermute | solution.py:44
  497.5 53.4 %all-to-all-start.10 = ((f32[4,72,432]{2,1,0:T(8,128)}), f32[4,72,432]{2,1,0:T(8,128)}, u32[]{:S(2)}, u32[]{:S(2)}) async-start(f32[4,72,432]{2,1,0:T(8,128)} %bitcast.204), calls=%async_computation.10 | async-start | bytes 1179648 | tf_op jit(solution)/shard_map/grad_qkvw_c/all_to_all | solution.py:49
  511.7 25.5 %collective-permute-start.62 = (f32[72,576]{1,0:T(8,128)S(1)}, f32[72,576]{1,0:T(8,128)S(1)}, u32[]{:S(2)}, u32[]{:S(2)}) collective-permute-start(f32[72,576]{1,0:T(8,128)S(1)} %get-tuple-element.300), channel_id=1, source_target_pairs={{0,2},{2,4},{4,6},{6,0},{1,3},{3,5},{5,7},{7,1},{8,10},{10,12},{12... | collective-permute-start | bytes 497672 | tf_op jit(solution)/shard_map/grad_proj_ring/ppermute | solution.py:38
  511.8 37.5 %collective-permute-start.64 = (f32[72,576]{1,0:T(8,128)S(1)}, f32[72,576]{1,0:T(8,128)S(1)}, u32[]{:S(2)}, u32[]{:S(2)}) collective-permute-start(f32[72,576]{1,0:T(8,128)S(1)} %get-tuple-element.301), channel_id=1, source_target_pairs={{0,6},{2,0},{4,2},{6,4},{1,7},{3,1},{5,3},{7,5},{8,14},{10,8},{12,... | collective-permute-start | bytes 497672 | tf_op jit(solution)/shard_map/grad_proj_ring/ppermute | solution.py:38
  515.6 21.5 %collective-permute-start.49 = (f32[234,128]{1,0:T(8,128)S(1)}, f32[234,128]{1,0:T(8,128)S(1)}, u32[]{:S(2)}, u32[]{:S(2)}) collective-permute-start(f32[234,128]{1,0:T(8,128)S(1)} %bitcast_add_fusion.4), channel_id=1, source_target_pairs={{0,2},{2,0},{4,6},{6,4},{1,3},{3,1},{5,7},{7,5},{8,10},{10,8},{12,... | collective-permute-start | bytes 359432 | tf_op jit(solution)/shard_map/sums/ppermute | solution.py:44
  518.0 39.2 %collective-permute-start.65 = (f16[72,4608]{1,0:T(8,128)(2,1)}, f16[72,4608]{1,0:T(8,128)(2,1)}, u32[]{:S(2)}, u32[]{:S(2)}) collective-permute-start(f16[72,4608]{1,0:T(8,128)(2,1)} %fusion.1), channel_id=1, source_target_pairs={{0,2},{2,4},{4,6},{6,0},{1,3},{3,5},{5,7},{7,1},{8,10},{10,12},{12... | collective-permute-start | bytes 1990664 | tf_op jit(solution)/shard_map/grad_feed_ring/ppermute | solution.py:38
  537.3 12.0 %collective-permute-start.63 = (f32[72,576]{1,0:T(8,128)S(1)}, f32[72,576]{1,0:T(8,128)S(1)}, u32[]{:S(2)}, u32[]{:S(2)}) collective-permute-start(f32[72,576]{1,0:T(8,128)S(1)} %bitcast_add_fusion.2), channel_id=1, source_target_pairs={{0,2},{2,4},{4,6},{6,0},{1,3},{3,5},{5,7},{7,1},{8,10},{10,12},{12... | collective-permute-start | bytes 497672 | tf_op jit(solution)/shard_map/grad_proj_ring/ppermute | solution.py:38
  550.0 16.1 %collective-permute-start.47 = (f32[128,1152]{1,0:T(8,128)S(1)}, f32[128,1152]{1,0:T(8,128)S(1)}, u32[]{:S(2)}, u32[]{:S(2)}) collective-permute-start(f32[128,1152]{1,0:T(8,128)S(1)} %get-tuple-element.218.refs_2_), channel_id=1, source_target_pairs={{0,1},{1,0},{2,3},{3,2},{4,5},{5,4},{6,7},{7,6},{8,9},{9,8},{10,11... | collective-permute-start | bytes 1769480 | tf_op jit(solution)/shard_map/grad_latent2/ppermute | solution.py:44
  554.1 24.2 %collective-permute-start.45 = (f32[128,1152]{1,0:T(8,128)S(1)}, f32[128,1152]{1,0:T(8,128)S(1)}, u32[]{:S(2)}, u32[]{:S(2)}) collective-permute-start(f32[128,1152]{1,0:T(8,128)S(1)} %get-tuple-element.192.refs_0_), channel_id=1, source_target_pairs={{0,1},{1,0},{2,3},{3,2},{4,5},{5,4},{6,7},{7,6},{8,9},{9,8},{10,11... | collective-permute-start | bytes 1769480 | tf_op jit(solution)/shard_map/grad_latent0/ppermute | solution.py:44
  556.3 25.4 %collective-permute-start.52 = (f32[2,234,128]{2,1,0:T(8,128)S(1)}, f32[2,234,128]{2,1,0:T(8,128)S(1)}, u32[]{:S(2)}, u32[]{:S(2)}) collective-permute-start(f32[2,234,128]{2,1,0:T(8,128)S(1)} %pad_maximum_fusion.2), channel_id=1, source_target_pairs={{0,16},{8,24},{16,0},{24,8},{1,17},{9,25},{17,1},{25,9},{2,18},{10... | collective-permute-start | bytes 718856 | tf_op jit(solution)/shard_map/sums/ppermute | solution.py:44
  560.3 34.2 %collective-permute-start.66 = (f16[72,4608]{1,0:T(8,128)(2,1)}, f16[72,4608]{1,0:T(8,128)(2,1)S(1)}, u32[]{:S(2)}, u32[]{:S(2)}) collective-permute-start(f16[72,4608]{1,0:T(8,128)(2,1)} %get-tuple-element.296), channel_id=1, source_target_pairs={{0,2},{2,4},{4,6},{6,0},{1,3},{3,5},{5,7},{7,1},{8,10},{10,12},{12... | collective-permute-start | bytes 1990664 | tf_op jit(solution)/shard_map/grad_feed_ring/ppermute | solution.py:38
  561.5 33.0 %collective-permute-start.67 = (f16[72,4608]{1,0:T(8,128)(2,1)S(1)}, f16[72,4608]{1,0:T(8,128)(2,1)}, u32[]{:S(2)}, u32[]{:S(2)}) collective-permute-start(f16[72,4608]{1,0:T(8,128)(2,1)S(1)} %get-tuple-element.297), channel_id=1, source_target_pairs={{0,6},{2,0},{4,2},{6,4},{1,7},{3,1},{5,3},{7,5},{8,14},{10,8},{12,... | collective-permute-start | bytes 1990664 | tf_op jit(solution)/shard_map/grad_feed_ring/ppermute | solution.py:38
  (152 other events, 924.4 us)
Sparse Core Ops, SparseCore 0:
  24.4 46.0 all-gather.3
  98.9 108.7 all-gather.5
  288.3 53.3 all-gather.7
